TPU v7x, 256 devices: a whole 4x4x8 slice. The times are simulated.
256 devices in a mesh: row: 16 (over z_lo, x, core), col: 16 (over z_hi, y).
Axes of the slice: x: 4, y: 4, z: 8 (z_hi: 4, z_lo: 2; z = z_hi * 2 + z_lo), core: 2. Of those that a mesh axis runs over, the one named last changes fastest.
Arguments:
- residual: bfloat16 [30720, 512], P('row', 'col'), may hold values from -4 to 4
- interaction: bfloat16 [30720, 5120], P('row', 'col'), may hold values from -0.078125 to 0.078125
- commands: bfloat16 [5120, 512], P('col'), may hold values from -6 to 6
- slope_valid: int32 [240], P('row'), may hold values 0 or 1
- frame_valid: int32 [512], P('col'), may hold values 0 or 1
Outputs:
- covariance: bfloat16 [30720, 30720], P('row', 'col')
All inputs are finite; a program needn't handle non-finite values. No bound on the sum of `slope_valid` or of `frame_valid` on one device may be relied on, other than what follows from the above.
Results may differ from a plain program's by a relative error of at most 0.02.
Values may be sent and summed in bfloat16 or wider, within the bound.
No kernel may reach another device: no remote copies, remote signals or barrier semaphores. Data moves between devices by JAX's collectives and lax.ppermute only.
A program may use at most 64 MiB of HBM per device.

v0:
```python
import jax
import jax.numpy as jnp
from jax import lax
from jax.sharding import PartitionSpec as P

SBLK = 128
FRAMES = 512


def per_device(residual, interaction, commands, slope_valid, frame_valid):
    block_rows = interaction.shape[0]
    product = jnp.dot(interaction, commands, preferred_element_type=jnp.float32)
    summed = lax.psum_scatter(
        product.astype(jnp.bfloat16), "col", scatter_dimension=1, tiled=True
    ).astype(jnp.float32)
    row_mask = (
        (slope_valid[:, None] * jnp.ones((1, SBLK), jnp.int32)).reshape(-1).astype(jnp.float32)
    )
    local_slopes = (
        (residual.astype(jnp.float32) + summed)
        * row_mask[:, None]
        * frame_valid[None, :].astype(jnp.float32)
    ).astype(jnp.bfloat16)
    row_copy = lax.all_gather(local_slopes, "col", axis=1, tiled=True)
    total_slopes = block_rows * lax.axis_size("row")
    block_cols = total_slopes // lax.axis_size("col")
    col_index = lax.axis_index("col")
    gathered = lax.all_gather(local_slopes, "row", axis=0, tiled=True)
    columns = lax.all_to_all(gathered, "col", split_axis=0, concat_axis=1, tiled=True)
    row_start = lax.axis_index("row") * block_rows
    col_start = col_index * block_cols
    row_ids = row_start + jnp.arange(block_rows, dtype=jnp.int32)[:, None]
    col_ids = col_start + jnp.arange(block_cols, dtype=jnp.int32)[None, :]
    tile = (
        lax.dot_general(
            row_copy, columns, (((1,), (1,)), ((), ())), preferred_element_type=jnp.float32
        )
        / FRAMES
    )
    return jnp.where(row_ids <= col_ids, tile, jnp.float32(0.0)).astype(jnp.bfloat16)


def solution(mesh):
    placed = (P("row", "col"), P("row", "col"), P("col", None), P("row"), P("col"))
    return jax.shard_map(
        per_device, mesh=mesh, in_specs=placed, out_specs=P("row", "col"), check_vma=False
    )
```

profile of v0, /device:TPU:24, one launch (start us, length us, event | category | flops | bytes accessed | tf_op | source)
XLA Modules:
  0.0 232.6 jit_solution(2607457852600107517)
XLA Ops:
  6.5 0.0 copy-start
  6.5 0.0 reduce-scatter.2.cloned.1.call-start
  6.5 1.3 copy-done
  7.8 3.5 %convolution_convert_fusion = bf16[1920,512]{0,1:T(8,128)(2,1)} fusion(bf16[1920,320]{0,1:T(8,128)(2,1)S(1)} %copy-done, bf16[320,512]{1,0:T(8,128)(2,1)} %param.7), kind=kOutput, calls=%fused_computation.1 | convolution fusion | flops 630128640 | bytes 3522560 | tf_op jit(solution)/shard_map/dot_general | solution.py:12
  11.3 0.0 copy-start.2
  11.3 0.0 copy-start.3
  11.3 0.0 copy-start.1
  11.3 0.0 reduce-scatter.2.cloned.1.call-update
  11.4 0.0 all-gather.5.cloned.1.call-start
  11.4 0.6 copy-done.2
  12.0 0.0 copy-done.3
  12.0 0.1 broadcast_bitcast_fusion
  12.1 89.3 %reduce-scatter.2.cloned.1.call-done = bf16[1920,32]{0,1:T(8,128)(2,1)} async-done(((bf16[1920,512]{0,1:T(8,128)(2,1)}), bf16[1920,32]{0,1:T(8,128)(2,1)}) %reduce-scatter.2.cloned.1.call-update) | async-done | bytes 122896 | tf_op jit(solution)/shard_map/reduce_scatter | solution.py:13
  101.3 0.0 copy-done.1
  101.4 1.6 multiply_convert_fusion
  103.0 0.0 all-gather.5.cloned.1.call-update
  103.0 0.0 all-gather.3.cloned.1.call-start
  103.1 0.7 all-gather.3.cloned.1.call-update
  103.8 34.4 %all-gather.5.cloned.1.call-done = bf16[30720,32]{0,1:T(8,128)(2,1)} async-done(((bf16[1920,32]{0,1:T(8,128)(2,1)}), bf16[30720,32]{0,1:T(8,128)(2,1)}) %all-gather.5.cloned.1.call-update) | async-done | bytes 1966096 | tf_op jit(solution)/shard_map/all_gather | solution.py:28
  138.1 3.0 %copy.9 = bf16[4,16,8,1920]{3,2,0,1:T(8,128)(2,1)} copy(bf16[4,16,8,1920]{3,2,1,0:T(8,128)(2,1)} %bitcast.14) | data formatting | bytes 3932160 | tf_op jit(solution)/shard_map/all_to_all | solution.py:29
  141.1 9.5 %all-to-all-start = ((bf16[16,1920,32]{1,2,0:T(8,128)(2,1)}), bf16[16,1920,32]{1,2,0:T(8,128)(2,1)S(1)}, u32[]{:S(2)}, u32[]{:S(2)}) async-start(bf16[16,1920,32]{1,2,0:T(8,128)(2,1)} %bitcast.12), calls=%async_computation.1 | async-start | bytes 3932160 | tf_op jit(solution)/shard_map/all_to_all | solution.py:29
  150.6 66.3 %all-gather.3.cloned.1.call-done = bf16[1920,512]{0,1:T(8,128)(2,1)} async-done(((bf16[1920,32]{0,1:T(8,128)(2,1)}), bf16[1920,512]{0,1:T(8,128)(2,1)}) %all-gather.3.cloned.1.call-update) | async-done | bytes 1966096 | tf_op jit(solution)/shard_map/all_gather | solution.py:24
  217.0 0.0 all-to-all-done
  217.0 9.1 %select_convert_fusion = bf16[1920,1920]{1,0:T(8,128)(2,1)} fusion(bf16[1920,512]{0,1:T(8,128)(2,1)} %all-gather.3.cloned.1.call-done, bf16[1920,512]{0,1:T(8,128)(2,1)S(1)} %bitcast.13, s32[1920]{0:T(1024)S(1)} %get-tuple-element.5, s32[1920]{0:T(1024)S(1)} %get-tuple-element.6), kind=kOutput, calls=%fused_computation | convolution fusion | flops 3789619200 | bytes 11320320 | tf_op jit(solution)/shard_map/dot_general | solution.py:35
  (3 shorter events, 0.0 us)
Async XLA Ops:
  6.5 1.3 copy-start
  6.5 94.8 %reduce-scatter.2.cloned.1.call-start = ((), (), s32[]{:S(2)}) async-start(), calls=%async_computation.2 | async-start | bytes 2088960 | tf_op jit(solution)/shard_map/reduce_scatter | solution.py:13
  11.3 0.7 copy-start.2
  11.3 0.7 copy-start.3
  11.3 90.0 %copy-start.1 = (bf16[1920,32]{0,1:T(8,128)(2,1)S(1)}, bf16[1920,32]{0,1:T(8,128)(2,1)}, u32[]{:S(2)}) copy-start(bf16[1920,32]{0,1:T(8,128)(2,1)} %param.5) | copy-start | bytes 368644
  11.4 126.8 %all-gather.5.cloned.1.call-start = ((), (), s32[]{:S(2)}) async-start(), calls=%async_computation.4 | async-start | bytes 2088960 | tf_op jit(solution)/shard_map/all_gather | solution.py:28
  103.0 114.0 %all-gather.3.cloned.1.call-start = ((), (), s32[]{:S(2)}) async-start(), calls=%async_computation.3 | async-start | bytes 2088960 | tf_op jit(solution)/shard_map/all_gather | solution.py:24
  141.1 75.9 %all-to-all-start = ((bf16[16,1920,32]{1,2,0:T(8,128)(2,1)}), bf16[16,1920,32]{1,2,0:T(8,128)(2,1)S(1)}, u32[]{:S(2)}, u32[]{:S(2)}) async-start(bf16[16,1920,32]{1,2,0:T(8,128)(2,1)} %bitcast.12), calls=%async_computation.1 | async-start | bytes 3932160 | tf_op jit(solution)/shard_map/all_to_all | solution.py:29
Sparse Core Ops, SparseCore 0:
  11.5 89.8 reduce-scatter.1
  103.3 34.7 all-gather.4
  140.9 76.0 all-gather.2
where the time goes:
time: 236 us; the launch traced here: 233 us
  waiting for transfers between devices  191 us (81%)
  between operations  13.1 us (6%)
  matrix products  12.6 us (5%)
  starting transfers between devices  9.6 us (4%)
  local copies, waits for them, and re-layouts  4.92 us (2%)
    reduce_scatter x1, waiting for transfers between devices, per_device(): lax.psum_scatter(product.astype(jnp.bfloat16), 'col', scatter_dimension=1...  89.3 us
    all_gather x1, waiting for transfers between devices, per_device(): row_copy = lax.all_gather(local_slopes, 'col', axis=1, tiled=True)  66.3 us
    all_gather x1, waiting for transfers between devices, per_device(): gathered = lax.all_gather(local_slopes, 'row', axis=0, tiled=True)  34.4 us
    all_to_all x1, starting transfers between devices, per_device(): lax.all_to_all(gathered, 'col', split_axis=0, concat_axis=1, tiled=True)  9.51 us
    dot_general x1, matrix products, per_device(): lax.dot_general(row_copy, columns, (((1,), (1,)), ((), ())), preferred_el...  9.07 us
  transfers between devices with their start and end apart: 4, of which 3 were waited for; matrix products, arithmetic and copies ran while one was open for 1% of the time, Pallas kernels for 0%

commit v1 on v0

v1 whole, which is shorter than its diff:
```python
import jax
import jax.numpy as jnp
from jax import lax
from jax.sharding import PartitionSpec as P

SBLK = 128
FRAMES = 512
MASKS_A = (0, 3, 1, 2)
MASKS_B = (0, 1, 3, 2)


def y_swap(mask):
    return [(c, c ^ mask) for c in range(16)]


def z_swap(mask):
    return [(c, c ^ (4 * mask)) for c in range(16)]


def y_turn(by):
    return [(c, (c & 12) | ((c + by) & 3)) for c in range(16)]


def z_turn(by):
    return [(c, (c + 4 * by) & 15) for c in range(16)]


def x_turn(by):
    return [(r, (r & 9) | ((r + 2 * by) & 6)) for r in range(16)]


def add(one, other):
    return (one.astype(jnp.float32) + other.astype(jnp.float32)).astype(jnp.bfloat16)


def ring_gather(own, axis, turn):
    half = own.shape[0] // 2
    left = lax.ppermute(own, axis, turn(1))
    right = lax.ppermute(own, axis, turn(-1))
    far_a = lax.ppermute(left[:half], axis, turn(1))
    far_b = lax.ppermute(right[half:], axis, turn(-1))
    return jnp.concatenate([own, left, right, far_a, far_b], axis=0)


def frame_order(col):
    half, y_at, z_at, low = jnp.meshgrid(
        jnp.arange(2), jnp.arange(4), jnp.arange(4), jnp.arange(16), indexing="ij"
    )
    masks = jnp.array([MASKS_A, MASKS_B])
    y_mask, z_mask = masks[half, y_at], masks[half, z_at]
    piece = col ^ (y_mask + 4 * z_mask)
    return (piece * 32 + half * 16 + low).reshape(-1).astype(jnp.int32)


def per_device(residual, interaction, commands, slope_valid, frame_valid):
    block_rows = interaction.shape[0]
    row, col = lax.axis_index("row"), lax.axis_index("col")
    order = frame_order(col)
    pick = (jnp.arange(FRAMES, dtype=jnp.int32)[None, :] == order[:, None]).astype(jnp.bfloat16)
    ordered = lax.dot_general(
        pick, commands, (((1,), (1,)), ((), ())), preferred_element_type=jnp.float32
    ).astype(jnp.bfloat16)
    product = lax.dot_general(
        ordered, interaction, (((1,), (1,)), ((), ())), preferred_element_type=jnp.float32
    ).astype(jnp.bfloat16)
    kept_a, sent_a, kept_b, sent_b = jnp.split(product, 4, axis=0)
    for swap, first, second in ((y_swap, 1, 3), (z_swap, 1, 3)):
        got_a = lax.ppermute(sent_a, "col", swap(first))
        got_b = lax.ppermute(sent_b, "col", swap(second))
        kept_a, kept_b = add(kept_a, got_a), add(kept_b, got_b)
        kept_a, sent_a = jnp.split(kept_a, 2, axis=0)
        kept_b, sent_b = jnp.split(kept_b, 2, axis=0)
        got_a = lax.ppermute(sent_a, "col", swap(second))
        got_b = lax.ppermute(sent_b, "col", swap(first))
        if swap is y_swap:
            kept_a, kept_b = add(kept_a, got_a), add(kept_b, got_b)
            kept_a, sent_a = jnp.split(kept_a, 2, axis=0)
            kept_b, sent_b = jnp.split(kept_b, 2, axis=0)
    summed = jnp.concatenate([kept_a, kept_b]).astype(jnp.float32) + jnp.concatenate(
        [got_a, got_b]
    ).astype(jnp.float32)
    row_mask = jnp.broadcast_to(slope_valid[:, None], (15, SBLK)).reshape(-1).astype(jnp.float32)
    slopes = (
        (residual.T.astype(jnp.float32) + summed)
        * row_mask[None, :]
        * frame_valid[:, None].astype(jnp.float32)
    ).astype(jnp.bfloat16)

    flip = [(r * 16 + c, c * 16 + r) for r in range(16) for c in range(16)]
    other = lax.ppermute(slopes, ("row", "col"), flip)
    mine = ring_gather(slopes, "col", z_turn)
    other = jnp.concatenate([other, lax.ppermute(other, "row", [(r, r ^ 8) for r in range(16)])])
    other = ring_gather(other, "row", x_turn)
    mine = ring_gather(mine, "col", y_turn)
    other = jnp.concatenate([other, lax.ppermute(other, "row", [(r, r ^ 1) for r in range(16)])])

    def turned(frames, step):
        half = frames.shape[0] // 2
        far = step(frames, 2)
        return jnp.concatenate([frames, step(frames, -1), step(frames, 1), far[:half], far[half:]])

    base = jnp.arange(32)
    def step_of(shift, width):
        low = (1 << shift) * 32
        def step(frames, by):
            digit = (frames // low) % width
            return frames + (((digit + by) % width) - digit) * low
        return step

    mine_at = turned(turned(base + col * 32, step_of(2, 4)), step_of(0, 4))
    other_at = base + row * 32
    other_at = jnp.concatenate([other_at, step_of(3, 2)(other_at, 1)])
    other_at = turned(other_at, step_of(1, 4))
    other_at = jnp.concatenate([other_at, step_of(0, 2)(other_at, 1)])
    match = (mine_at[:, None] == other_at[None, :]).astype(jnp.bfloat16)
    other = lax.dot_general(
        match, other, (((1,), (0,)), ((), ())), preferred_element_type=jnp.float32
    ).astype(jnp.bfloat16)
    row_ids = row * block_rows + jnp.arange(block_rows, dtype=jnp.int32)[:, None]
    col_ids = col * block_rows + jnp.arange(block_rows, dtype=jnp.int32)[None, :]
    tile = (
        lax.dot_general(mine, other, (((0,), (0,)), ((), ())), preferred_element_type=jnp.float32)
        / FRAMES
    )
    return jnp.where(row_ids <= col_ids, tile, jnp.float32(0.0)).astype(jnp.bfloat16)


def solution(mesh):
    placed = (P("row", "col"), P("row", "col"), P("col", None), P("row"), P("col"))
    return jax.shard_map(
        per_device, mesh=mesh, in_specs=placed, out_specs=P("row", "col"), check_vma=False
    )
```

time: 236 us -> 131 us (0.56)
  waiting for transfers between devices: 191 us -> 50.2 us
  starting transfers between devices: 9.6 us -> 38.4 us
  local copies, waits for them, and re-layouts: 4.92 us -> 25.3 us
  between operations: 13.1 us -> 0.28 us
    all_gather x2 -> x0, waiting for transfers between devices: 101 us -> none  [the longest x1 66.3 us: per_device(): row_copy = lax.all_gather(local_slopes, 'col', axis=1, tiled=True)]
    reduce_scatter x1 -> x0, waiting for transfers between devices: 89.3 us -> none  [per_device(): lax.psum_scatter(product.astype(jnp.bfloat16), 'col', scatter_dimension=1...]
    ppermute x0 -> x23, waiting for transfers between devices: none -> 50.2 us  [the longest x2 15.5 us: per_device(): got_a = lax.ppermute(sent_a, 'col', swap(first))]
    ppermute x0 -> x23, starting transfers between devices: none -> 38.4 us  [the longest x3 11.7 us: ring_gather(): right = lax.ppermute(own, axis, turn(-1))]
    unnamed x8 -> x30, local copies, waits for them, and re-layouts: 1.88 us -> 11.8 us
    all_to_all x1 -> x0, starting transfers between devices: 9.51 us -> none  [per_device(): lax.all_to_all(gathered, 'col', split_axis=0, concat_axis=1, tiled=True)]
    gather x0 -> x2, local copies, waits for them, and re-layouts: none -> 9.5 us  [frame_order(): y_mask, z_mask = (masks[half, y_at], masks[half, z_at])]
    all_to_all x1 -> x0, local copies, waits for them, and re-layouts: 2.98 us -> none  [per_device(): lax.all_to_all(gathered, 'col', split_axis=0, concat_axis=1, tiled=True)]
  transfers between devices with their start and end apart: 4 -> 23, of which waited for: 3 -> 11; matrix products, arithmetic and copies ran while one was open for 1% -> 9% of each run, Pallas kernels for 0% -> 0%
where the time goes in v1:
time: 131 us; the launch traced here: 129 us
  waiting for transfers between devices  50.2 us (38%)
  starting transfers between devices  38.4 us (29%)
  local copies, waits for them, and re-layouts  25.3 us (19%)
  matrix products  12.3 us (9%)
  other arithmetic  2.79 us (2%)
    ppermute x2, waiting for transfers between devices, per_device(): got_a = lax.ppermute(sent_a, 'col', swap(first))  15.5 us
    unnamed x30, local copies, waits for them, and re-layouts  11.8 us
    ppermute x3, starting transfers between devices, ring_gather(): right = lax.ppermute(own, axis, turn(-1))  11.7 us
    dot_general x1, matrix products, per_device(): lax.dot_general(mine, other, (((0,), (0,)), ((), ())), preferred_element_...  10.8 us
    ppermute x3, waiting for transfers between devices, ring_gather(): far_a = lax.ppermute(left[:half], axis, turn(1))  10.5 us
    gather x2, local copies, waits for them, and re-layouts, frame_order(): y_mask, z_mask = (masks[half, y_at], masks[half, z_at])  9.5 us
    ppermute x2, starting transfers between devices, per_device(): got_b = lax.ppermute(sent_b, 'col', swap(second))  7.61 us
    ppermute x3, starting transfers between devices, ring_gather(): far_b = lax.ppermute(right[half:], axis, turn(-1))  6.38 us
  transfers between devices with their start and end apart: 23, of which 11 were waited for; matrix products, arithmetic and copies ran while one was open for 9% of the time, Pallas kernels for 0%

profile of v1, /device:TPU:24, one launch (start us, length us, event | category | flops | bytes accessed | tf_op | source)
XLA Modules:
  0.0 129.3 jit_solution(7343398038950564939)
XLA Ops:
  0.8 4.7 %gather_fusion = s32[512]{0:T(512)S(1)} fusion(s32[2,4]{1,0:T(2,128)S(1)} %copy-done.1, s32[512]{0:T(512)S(1)} %reshape.57), kind=kCustom, calls=%fused_computation | custom fusion | bytes 8192 | tf_op jit(solution)/shard_map/gather | solution.py:50
  5.5 4.8 %gather_fusion.1 = s32[512]{0:T(512)S(1)} fusion(s32[2,4]{1,0:T(2,128)S(1)} %copy-done.1, s32[512]{0:T(512)S(1)} %reshape.63), kind=kCustom, calls=%fused_computation.1 | custom fusion | bytes 8192 | tf_op jit(solution)/shard_map/gather | solution.py:50
  10.6 1.6 %convolution_convert_fusion.1 = bf16[512,1920]{1,0:T(8,128)(2,1)S(1)} fusion(bf16[1920,320]{0,1:T(8,128)(2,1)S(1)} %copy-done, bf16[320,512]{1,0:T(8,128)(2,1)S(1)} %copy-done.6, s32[512]{0:T(512)S(1)} %reshape.56), kind=kOutput, calls=%fused_computation.4 | convolution fusion | flops 798326784 | bytes 3524608 | tf_op jit(solution)/shard_map/dot_general | solution.py:63
  12.2 1.0 fusion.39
  13.9 1.2 collective-permute-start.3
  15.5 11.0 %collective-permute-done = bf16[128,1920]{1,0:T(8,128)(2,1)} collective-permute-done((bf16[128,1920]{1,0:T(8,128)(2,1)}, bf16[128,1920]{1,0:T(8,128)(2,1)}, u32[]{:S(2)}, u32[]{:S(2)}) %collective-permute-start) | collective-permute-done | bytes 491552 | tf_op jit(solution)/shard_map/ppermute | solution.py:68
  26.5 1.7 %collective-permute-done.3 = bf16[128,1920]{1,0:T(8,128)(2,1)} collective-permute-done((bf16[128,1920]{1,0:T(8,128)(2,1)}, bf16[128,1920]{1,0:T(8,128)(2,1)}, u32[]{:S(2)}, u32[]{:S(2)}) %collective-permute-start.3) | collective-permute-done | bytes 491552 | tf_op jit(solution)/shard_map/ppermute | solution.py:69
  28.1 1.4 %add_convert_fusion.1 = (bf16[128,1920]{1,0:T(8,128)(2,1)S(1)}, bf16[128,1920]{1,0:T(8,128)(2,1)S(1)}) fusion(bf16[128,1920]{1,0:T(8,128)(2,1)} %collective-permute-done, bf16[512,1920]{1,0:T(8,128)(2,1)S(1)} %convolution_convert_fusion.1, bf16[128,1920]{1,0:T(8,128)(2,1)} %collective-permute-done.3), kind=kLoop, calls=%fused_computation.9 | loop fusion | flops 1966080 | bytes 2949120 | tf_op jit(solution)/shard_map/convert_element_type | solution.py:33
  30.0 1.1 collective-permute-start.1
  31.1 5.1 %collective-permute-done.4 = bf16[64,1920]{1,0:T(8,128)(2,1)S(1)} collective-permute-done((bf16[64,1920]{1,0:T(8,128)(2,1)S(1)}, bf16[64,1920]{1,0:T(8,128)(2,1)S(1)}, u32[]{:S(2)}, u32[]{:S(2)}) %collective-permute-start.4) | collective-permute-done | bytes 245792 | tf_op jit(solution)/shard_map/ppermute | solution.py:74
  36.3 6.4 %collective-permute-start.5 = (bf16[32,1920]{1,0:T(8,128)(2,1)S(1)}, bf16[32,1920]{1,0:T(8,128)(2,1)S(1)}, u32[]{:S(2)}, u32[]{:S(2)}) collective-permute-start(bf16[32,1920]{1,0:T(8,128)(2,1)S(1)} %split.76), channel_id=1, source_target_pairs={{0,12},{1,13},{2,14},{3,15},{4,8},{5,9},{6,10},{7,11},{8,4},{9,5},... | collective-permute-start | bytes 368648 | tf_op jit(solution)/shard_map/ppermute | solution.py:69
  42.8 1.5 %collective-permute-start.2 = (bf16[32,1920]{1,0:T(8,128)(2,1)S(1)}, bf16[32,1920]{1,0:T(8,128)(2,1)S(1)}, u32[]{:S(2)}, u32[]{:S(2)}) collective-permute-start(bf16[32,1920]{1,0:T(8,128)(2,1)S(1)} %split.69), channel_id=1, source_target_pairs={{0,4},{1,5},{2,6},{3,7},{4,0},{5,1},{6,2},{7,3},{8,12},{9,13},{10,... | collective-permute-start | bytes 368648 | tf_op jit(solution)/shard_map/ppermute | solution.py:68
  44.3 2.2 %collective-permute-done.5 = bf16[32,1920]{1,0:T(8,128)(2,1)S(1)} collective-permute-done((bf16[32,1920]{1,0:T(8,128)(2,1)S(1)}, bf16[32,1920]{1,0:T(8,128)(2,1)S(1)}, u32[]{:S(2)}, u32[]{:S(2)}) %collective-permute-start.5) | collective-permute-done | bytes 122912 | tf_op jit(solution)/shard_map/ppermute | solution.py:69
  47.4 4.5 %collective-permute-done.2 = bf16[32,1920]{1,0:T(8,128)(2,1)S(1)} collective-permute-done((bf16[32,1920]{1,0:T(8,128)(2,1)S(1)}, bf16[32,1920]{1,0:T(8,128)(2,1)S(1)}, u32[]{:S(2)}, u32[]{:S(2)}) %collective-permute-start.2) | collective-permute-done | bytes 122912 | tf_op jit(solution)/shard_map/ppermute | solution.py:68
  52.6 5.8 %collective-permute-done.6 = bf16[16,1920]{1,0:T(8,128)(2,1)S(1)} collective-permute-done((bf16[16,1920]{1,0:T(8,128)(2,1)S(1)}, bf16[16,1920]{1,0:T(8,128)(2,1)S(1)}, u32[]{:S(2)}, u32[]{:S(2)}) %collective-permute-start.6) | collective-permute-done | bytes 61472 | tf_op jit(solution)/shard_map/ppermute | solution.py:73
  59.2 1.9 %collective-permute-start.16 = (bf16[32,1920]{1,0:T(8,128)(2,1)S(1)}, bf16[32,1920]{1,0:T(8,128)(2,1)S(1)}, u32[]{:S(2)}, u32[]{:S(2)}) collective-permute-start(bf16[32,1920]{1,0:T(8,128)(2,1)S(1)} %get-tuple-element.12), channel_id=1, source_target_pairs={{0,0},{1,16},{2,32},{3,48},{4,64},{5,80},{6,96},{7,112},{8,128},{9... | collective-permute-start | bytes 368648 | tf_op jit(solution)/shard_map/ppermute | solution.py:90
  61.1 1.0 collective-permute-start.9
  62.1 2.0 %collective-permute-start.8 = (bf16[32,1920]{1,0:T(8,128)(2,1)S(1)}, bf16[32,1920]{1,0:T(8,128)(2,1)S(1)}, u32[]{:S(2)}, u32[]{:S(2)}) collective-permute-start(bf16[32,1920]{1,0:T(8,128)(2,1)S(1)} %get-tuple-element.12), channel_id=1, source_target_pairs={{0,4},{1,5},{2,6},{3,7},{4,8},{5,9},{6,10},{7,11},{8,12},{9,13},{1... | collective-permute-start | bytes 368648 | tf_op jit(solution)/shard_map/ppermute | solution.py:38
  64.8 6.2 %collective-permute-done.9 = bf16[32,1920]{1,0:T(8,128)(2,1)S(1)} collective-permute-done((bf16[32,1920]{1,0:T(8,128)(2,1)S(1)}, bf16[32,1920]{1,0:T(8,128)(2,1)S(1)}, u32[]{:S(2)}, u32[]{:S(2)}) %collective-permute-start.9) | collective-permute-done | bytes 122912 | tf_op jit(solution)/shard_map/ppermute | solution.py:39
  71.3 2.7 %collective-permute-start.10 = (bf16[16,1920]{1,0:T(8,128)(2,1)S(1)}, bf16[16,1920]{1,0:T(8,128)(2,1)S(1)}, u32[]{:S(2)}, u32[]{:S(2)}) collective-permute-start(bf16[16,1920]{1,0:T(8,128)(2,1)S(1)} %slice.39), channel_id=1, source_target_pairs={{0,4},{1,5},{2,6},{3,7},{4,8},{5,9},{6,10},{7,11},{8,12},{9,13},{1... | collective-permute-start | bytes 184328 | tf_op jit(solution)/shard_map/ppermute | solution.py:40
  76.1 2.7 %collective-permute-done.17 = bf16[32,1920]{1,0:T(8,128)(2,1)S(1)} collective-permute-done((bf16[32,1920]{1,0:T(8,128)(2,1)S(1)}, bf16[32,1920]{1,0:T(8,128)(2,1)S(1)}, u32[]{:S(2)}, u32[]{:S(2)}) %collective-permute-start.17) | collective-permute-done | bytes 122912 | tf_op jit(solution)/shard_map/ppermute | solution.py:92
  79.5 5.6 %collective-permute-start.19 = (bf16[64,1920]{1,0:T(8,128)(2,1)S(1)}, bf16[64,1920]{1,0:T(8,128)(2,1)S(1)}, u32[]{:S(2)}, u32[]{:S(2)}) collective-permute-start(bf16[64,1920]{1,0:T(8,128)(2,1)S(1)} %get-tuple-element.27), channel_id=1, source_target_pairs={{0,96},{16,112},{32,0},{48,16},{64,32},{80,48},{96,64},{112,80},{1... | collective-permute-start | bytes 737288 | tf_op jit(solution)/shard_map/ppermute | solution.py:39
  86.4 5.1 %collective-permute-start.13 = (bf16[128,1920]{1,0:T(8,128)(2,1)}, bf16[128,1920]{1,0:T(8,128)(2,1)S(1)}, u32[]{:S(2)}, u32[]{:S(2)}) collective-permute-start(bf16[128,1920]{1,0:T(8,128)(2,1)} %get-tuple-element.39), channel_id=1, source_target_pairs={{0,3},{1,0},{2,1},{3,2},{4,7},{5,4},{6,5},{7,6},{8,11},{9,8},{10,9... | collective-permute-start | bytes 1474568 | tf_op jit(solution)/shard_map/ppermute | solution.py:39
  91.5 0.9 collective-permute-start.12
  92.5 1.6 %collective-permute-start.21 = (bf16[32,1920]{1,0:T(8,128)(2,1)S(1)}, bf16[32,1920]{1,0:T(8,128)(2,1)S(1)}, u32[]{:S(2)}, u32[]{:S(2)}) collective-permute-start(bf16[32,1920]{1,0:T(8,128)(2,1)S(1)} %slice.44), channel_id=1, source_target_pairs={{0,96},{16,112},{32,0},{48,16},{64,32},{80,48},{96,64},{112,80},{1... | collective-permute-start | bytes 368648 | tf_op jit(solution)/shard_map/ppermute | solution.py:41
  96.2 4.1 %collective-permute-done.20 = bf16[32,1920]{1,0:T(8,128)(2,1)S(1)} collective-permute-done((bf16[32,1920]{1,0:T(8,128)(2,1)S(1)}, bf16[32,1920]{1,0:T(8,128)(2,1)S(1)}, u32[]{:S(2)}, u32[]{:S(2)}) %collective-permute-start.20) | collective-permute-done | bytes 122912 | tf_op jit(solution)/shard_map/ppermute | solution.py:40
  101.6 1.3 copy-done.3
  103.1 4.4 %collective-permute-start.15 = (bf16[64,1920]{1,0:T(8,128)(2,1)S(1)}, bf16[64,1920]{1,0:T(8,128)(2,1)S(1)}, u32[]{:S(2)}, u32[]{:S(2)}) collective-permute-start(bf16[64,1920]{1,0:T(8,128)(2,1)S(1)} %slice.42), channel_id=1, source_target_pairs={{0,3},{1,0},{2,1},{3,2},{4,7},{5,4},{6,5},{7,6},{8,11},{9,8},{10,9... | collective-permute-start | bytes 737288 | tf_op jit(solution)/shard_map/ppermute | solution.py:41
  107.6 0.9 constant_dynamic-update-slice_fusion.8
  109.3 6.4 %collective-permute-done.14 = bf16[64,1920]{1,0:T(8,128)(2,1)S(1)} collective-permute-done((bf16[64,1920]{1,0:T(8,128)(2,1)S(1)}, bf16[64,1920]{1,0:T(8,128)(2,1)S(1)}, u32[]{:S(2)}, u32[]{:S(2)}) %collective-permute-start.14) | collective-permute-done | bytes 245792 | tf_op jit(solution)/shard_map/ppermute | solution.py:40
  117.3 1.3 copy-done.5
  118.5 10.8 %select_convert_fusion = bf16[1920,1920]{1,0:T(8,128)(2,1)} fusion(bf16[512,1920]{1,0:T(8,128)(2,1)} %constant_dynamic-update-slice_fusion.5, s32[1920]{0:T(1024)S(1)} %get-tuple-element.53, s32[1920]{0:T(1024)S(1)} %get-tuple-element.54, bf16[512,1920]{1,0:T(8,128)(2,1)} %copy-done.5, s32[512]{0:T(512)S(1)} %concatenate.62, s32[512]{0:T(512)S(1)} %concatenate.59), kind=kOutput, calls=%fused_computation.2 | convolution fusion | flops 4797497344 | bytes 11324416 | tf_op jit(solution)/shard_map/dot_general | solution.py:122
  (95 shorter events, 16.2 us)
Async XLA Ops:
  0.0 10.6 %copy-start = (bf16[1920,320]{0,1:T(8,128)(2,1)S(1)}, bf16[1920,320]{0,1:T(8,128)(2,1)}, u32[]{:S(2)}) copy-start(bf16[1920,320]{0,1:T(8,128)(2,1)} %param.7) | copy-start | bytes 3686404
  0.0 0.8 copy-start.1
  5.5 5.0 %copy-start.6 = (bf16[320,512]{1,0:T(8,128)(2,1)S(1)}, bf16[320,512]{1,0:T(8,128)(2,1)}, u32[]{:S(2)}) copy-start(bf16[320,512]{1,0:T(8,128)(2,1)} %param.8) | copy-start | bytes 983044
  13.2 16.7 %copy-start.7 = (s32[15]{0:T(128)S(1)}, s32[15]{0:T(128)}, u32[]{:S(2)}) copy-start(s32[15]{0:T(128)} %param.9) | copy-start | bytes 184
  13.2 13.3 %collective-permute-start = (bf16[128,1920]{1,0:T(8,128)(2,1)}, bf16[128,1920]{1,0:T(8,128)(2,1)}, u32[]{:S(2)}, u32[]{:S(2)}) collective-permute-start(bf16[128,1920]{1,0:T(8,128)(2,1)} %get-tuple-element.15), channel_id=1, source_target_pairs={{0,1},{1,0},{2,3},{3,2},{4,5},{5,4},{6,7},{7,6},{8,9},{9,8},{10,11... | collective-permute-start | bytes 1474568 | tf_op jit(solution)/shard_map/ppermute | solution.py:68
  13.9 14.2 %collective-permute-start.3 = (bf16[128,1920]{1,0:T(8,128)(2,1)}, bf16[128,1920]{1,0:T(8,128)(2,1)}, u32[]{:S(2)}, u32[]{:S(2)}) collective-permute-start(bf16[128,1920]{1,0:T(8,128)(2,1)} %get-tuple-element.16), channel_id=1, source_target_pairs={{0,3},{1,2},{2,1},{3,0},{4,7},{5,6},{6,5},{7,4},{8,11},{9,10},{10,... | collective-permute-start | bytes 1474568 | tf_op jit(solution)/shard_map/ppermute | solution.py:69
  29.6 22.6 %copy-start.8 = (s32[32]{0:T(128)S(1)}, s32[32]{0:T(128)}, u32[]{:S(2)}) copy-start(s32[32]{0:T(128)} %param.10) | copy-start | bytes 388
  29.6 28.8 %copy-start.2 = (bf16[1920,32]{0,1:T(8,128)(2,1)S(1)}, bf16[1920,32]{0,1:T(8,128)(2,1)}, u32[]{:S(2)}) copy-start(bf16[1920,32]{0,1:T(8,128)(2,1)} %param.6) | copy-start | bytes 368644
  29.6 6.6 %collective-permute-start.4 = (bf16[64,1920]{1,0:T(8,128)(2,1)S(1)}, bf16[64,1920]{1,0:T(8,128)(2,1)S(1)}, u32[]{:S(2)}, u32[]{:S(2)}) collective-permute-start(bf16[64,1920]{1,0:T(8,128)(2,1)S(1)} %split.74), channel_id=1, source_target_pairs={{0,1},{1,0},{2,3},{3,2},{4,5},{5,4},{6,7},{7,6},{8,9},{9,8},{10,11... | collective-permute-start | bytes 737288 | tf_op jit(solution)/shard_map/ppermute | solution.py:74
  30.0 12.7 %collective-permute-start.1 = (bf16[64,1920]{1,0:T(8,128)(2,1)S(1)}, bf16[64,1920]{1,0:T(8,128)(2,1)S(1)}, u32[]{:S(2)}, u32[]{:S(2)}) collective-permute-start(bf16[64,1920]{1,0:T(8,128)(2,1)S(1)} %split.67), channel_id=1, source_target_pairs={{0,3},{1,2},{2,1},{3,0},{4,7},{5,6},{6,5},{7,4},{8,11},{9,10},{10,... | collective-permute-start | bytes 737288 | tf_op jit(solution)/shard_map/ppermute | solution.py:73
  36.3 10.2 %collective-permute-start.5 = (bf16[32,1920]{1,0:T(8,128)(2,1)S(1)}, bf16[32,1920]{1,0:T(8,128)(2,1)S(1)}, u32[]{:S(2)}, u32[]{:S(2)}) collective-permute-start(bf16[32,1920]{1,0:T(8,128)(2,1)S(1)} %split.76), channel_id=1, source_target_pairs={{0,12},{1,13},{2,14},{3,15},{4,8},{5,9},{6,10},{7,11},{8,4},{9,5},... | collective-permute-start | bytes 368648 | tf_op jit(solution)/shard_map/ppermute | solution.py:69
  42.8 9.2 %collective-permute-start.2 = (bf16[32,1920]{1,0:T(8,128)(2,1)S(1)}, bf16[32,1920]{1,0:T(8,128)(2,1)S(1)}, u32[]{:S(2)}, u32[]{:S(2)}) collective-permute-start(bf16[32,1920]{1,0:T(8,128)(2,1)S(1)} %split.69), channel_id=1, source_target_pairs={{0,4},{1,5},{2,6},{3,7},{4,0},{5,1},{6,2},{7,3},{8,12},{9,13},{10,... | collective-permute-start | bytes 368648 | tf_op jit(solution)/shard_map/ppermute | solution.py:68
  46.6 6.0 %collective-permute-start.7 = (bf16[16,1920]{1,0:T(8,128)(2,1)S(1)}, bf16[16,1920]{1,0:T(8,128)(2,1)S(1)}, u32[]{:S(2)}, u32[]{:S(2)}) collective-permute-start(bf16[16,1920]{1,0:T(8,128)(2,1)S(1)} %get-tuple-element.38), channel_id=1, source_target_pairs={{0,4},{1,5},{2,6},{3,7},{4,0},{5,1},{6,2},{7,3},{8,12},{9,13},{10,... | collective-permute-start | bytes 184328 | tf_op jit(solution)/shard_map/ppermute | solution.py:74
  52.0 6.4 %collective-permute-start.6 = (bf16[16,1920]{1,0:T(8,128)(2,1)S(1)}, bf16[16,1920]{1,0:T(8,128)(2,1)S(1)}, u32[]{:S(2)}, u32[]{:S(2)}) collective-permute-start(bf16[16,1920]{1,0:T(8,128)(2,1)S(1)} %get-tuple-element.36), channel_id=1, source_target_pairs={{0,12},{1,13},{2,14},{3,15},{4,8},{5,9},{6,10},{7,11},{8,4},{9,5},... | collective-permute-start | bytes 184328 | tf_op jit(solution)/shard_map/ppermute | solution.py:73
  59.2 14.8 %collective-permute-start.16 = (bf16[32,1920]{1,0:T(8,128)(2,1)S(1)}, bf16[32,1920]{1,0:T(8,128)(2,1)S(1)}, u32[]{:S(2)}, u32[]{:S(2)}) collective-permute-start(bf16[32,1920]{1,0:T(8,128)(2,1)S(1)} %get-tuple-element.12), channel_id=1, source_target_pairs={{0,0},{1,16},{2,32},{3,48},{4,64},{5,80},{6,96},{7,112},{8,128},{9... | collective-permute-start | bytes 368648 | tf_op jit(solution)/shard_map/ppermute | solution.py:90
  61.1 9.8 %collective-permute-start.9 = (bf16[32,1920]{1,0:T(8,128)(2,1)S(1)}, bf16[32,1920]{1,0:T(8,128)(2,1)S(1)}, u32[]{:S(2)}, u32[]{:S(2)}) collective-permute-start(bf16[32,1920]{1,0:T(8,128)(2,1)S(1)} %get-tuple-element.12), channel_id=1, source_target_pairs={{0,12},{1,13},{2,14},{3,15},{4,0},{5,1},{6,2},{7,3},{8,4},{9,5},{1... | collective-permute-start | bytes 368648 | tf_op jit(solution)/shard_map/ppermute | solution.py:39
  62.1 9.1 %collective-permute-start.8 = (bf16[32,1920]{1,0:T(8,128)(2,1)S(1)}, bf16[32,1920]{1,0:T(8,128)(2,1)S(1)}, u32[]{:S(2)}, u32[]{:S(2)}) collective-permute-start(bf16[32,1920]{1,0:T(8,128)(2,1)S(1)} %get-tuple-element.12), channel_id=1, source_target_pairs={{0,4},{1,5},{2,6},{3,7},{4,8},{5,9},{6,10},{7,11},{8,12},{9,13},{1... | collective-permute-start | bytes 368648 | tf_op jit(solution)/shard_map/ppermute | solution.py:38
  70.9 14.8 %collective-permute-start.11 = (bf16[16,1920]{1,0:T(8,128)(2,1)S(1)}, bf16[16,1920]{1,0:T(8,128)(2,1)S(1)}, u32[]{:S(2)}, u32[]{:S(2)}) collective-permute-start(bf16[16,1920]{1,0:T(8,128)(2,1)S(1)} %slice.40), channel_id=1, source_target_pairs={{0,12},{1,13},{2,14},{3,15},{4,0},{5,1},{6,2},{7,3},{8,4},{9,5},{1... | collective-permute-start | bytes 184328 | tf_op jit(solution)/shard_map/ppermute | solution.py:41
  71.3 13.8 %collective-permute-start.10 = (bf16[16,1920]{1,0:T(8,128)(2,1)S(1)}, bf16[16,1920]{1,0:T(8,128)(2,1)S(1)}, u32[]{:S(2)}, u32[]{:S(2)}) collective-permute-start(bf16[16,1920]{1,0:T(8,128)(2,1)S(1)} %slice.39), channel_id=1, source_target_pairs={{0,4},{1,5},{2,6},{3,7},{4,8},{5,9},{6,10},{7,11},{8,12},{9,13},{1... | collective-permute-start | bytes 184328 | tf_op jit(solution)/shard_map/ppermute | solution.py:40
  73.9 4.9 %collective-permute-start.17 = (bf16[32,1920]{1,0:T(8,128)(2,1)S(1)}, bf16[32,1920]{1,0:T(8,128)(2,1)S(1)}, u32[]{:S(2)}, u32[]{:S(2)}) collective-permute-start(bf16[32,1920]{1,0:T(8,128)(2,1)S(1)} %collective-permute-done.16), channel_id=1, source_target_pairs={{0,128},{16,144},{32,160},{48,176},{64,192},{80,208},{96,224},{112... | collective-permute-start | bytes 368648 | tf_op jit(solution)/shard_map/ppermute | solution.py:92
  79.5 12.9 %collective-permute-start.19 = (bf16[64,1920]{1,0:T(8,128)(2,1)S(1)}, bf16[64,1920]{1,0:T(8,128)(2,1)S(1)}, u32[]{:S(2)}, u32[]{:S(2)}) collective-permute-start(bf16[64,1920]{1,0:T(8,128)(2,1)S(1)} %get-tuple-element.27), channel_id=1, source_target_pairs={{0,96},{16,112},{32,0},{48,16},{64,32},{80,48},{96,64},{112,80},{1... | collective-permute-start | bytes 737288 | tf_op jit(solution)/shard_map/ppermute | solution.py:39
  85.1 9.0 %collective-permute-start.18 = (bf16[64,1920]{1,0:T(8,128)(2,1)S(1)}, bf16[64,1920]{1,0:T(8,128)(2,1)S(1)}, u32[]{:S(2)}, u32[]{:S(2)}) collective-permute-start(bf16[64,1920]{1,0:T(8,128)(2,1)S(1)} %get-tuple-element.27), channel_id=1, source_target_pairs={{0,32},{16,48},{32,64},{48,80},{64,96},{80,112},{96,0},{112,16},{1... | collective-permute-start | bytes 737288 | tf_op jit(solution)/shard_map/ppermute | solution.py:38
  86.4 16.6 %collective-permute-start.13 = (bf16[128,1920]{1,0:T(8,128)(2,1)}, bf16[128,1920]{1,0:T(8,128)(2,1)S(1)}, u32[]{:S(2)}, u32[]{:S(2)}) collective-permute-start(bf16[128,1920]{1,0:T(8,128)(2,1)} %get-tuple-element.39), channel_id=1, source_target_pairs={{0,3},{1,0},{2,1},{3,2},{4,7},{5,4},{6,5},{7,6},{8,11},{9,8},{10,9... | collective-permute-start | bytes 1474568 | tf_op jit(solution)/shard_map/ppermute | solution.py:39
  91.5 16.0 %collective-permute-start.12 = (bf16[128,1920]{1,0:T(8,128)(2,1)}, bf16[128,1920]{1,0:T(8,128)(2,1)S(1)}, u32[]{:S(2)}, u32[]{:S(2)}) collective-permute-start(bf16[128,1920]{1,0:T(8,128)(2,1)} %get-tuple-element.39), channel_id=1, source_target_pairs={{0,1},{1,2},{2,3},{3,0},{4,5},{5,6},{6,7},{7,4},{8,9},{9,10},{10,1... | collective-permute-start | bytes 1474568 | tf_op jit(solution)/shard_map/ppermute | solution.py:38
  92.5 8.5 %collective-permute-start.21 = (bf16[32,1920]{1,0:T(8,128)(2,1)S(1)}, bf16[32,1920]{1,0:T(8,128)(2,1)S(1)}, u32[]{:S(2)}, u32[]{:S(2)}) collective-permute-start(bf16[32,1920]{1,0:T(8,128)(2,1)S(1)} %slice.44), channel_id=1, source_target_pairs={{0,96},{16,112},{32,0},{48,16},{64,32},{80,48},{96,64},{112,80},{1... | collective-permute-start | bytes 368648 | tf_op jit(solution)/shard_map/ppermute | solution.py:41
  94.1 6.2 %collective-permute-start.20 = (bf16[32,1920]{1,0:T(8,128)(2,1)S(1)}, bf16[32,1920]{1,0:T(8,128)(2,1)S(1)}, u32[]{:S(2)}, u32[]{:S(2)}) collective-permute-start(bf16[32,1920]{1,0:T(8,128)(2,1)S(1)} %slice.43), channel_id=1, source_target_pairs={{0,32},{16,48},{32,64},{48,80},{64,96},{80,112},{96,0},{112,16},{1... | collective-permute-start | bytes 368648 | tf_op jit(solution)/shard_map/ppermute | solution.py:40
  101.6 1.3 copy-start.3
  102.9 14.2 %collective-permute-start.22 = (bf16[256,1920]{1,0:T(8,128)(2,1)}, bf16[256,1920]{1,0:T(8,128)(2,1)S(1)}, u32[]{:S(2)}, u32[]{:S(2)}) collective-permute-start(bf16[256,1920]{1,0:T(8,128)(2,1)} %get-tuple-element.21), channel_id=1, source_target_pairs={{0,16},{16,0},{32,48},{48,32},{64,80},{80,64},{96,112},{112,96},{1... | collective-permute-start | bytes 2949128 | tf_op jit(solution)/shard_map/ppermute | solution.py:95
  103.1 14.1 %copy-start.4 = (bf16[512,1920]{1,0:T(8,128)(2,1)S(1)}, bf16[512,1920]{1,0:T(8,128)(2,1)}, u32[]{:S(2)}) copy-start(bf16[512,1920]{1,0:T(8,128)(2,1)} %copy-done.3) | copy-start | bytes 5898244
  103.1 13.3 %collective-permute-start.15 = (bf16[64,1920]{1,0:T(8,128)(2,1)S(1)}, bf16[64,1920]{1,0:T(8,128)(2,1)S(1)}, u32[]{:S(2)}, u32[]{:S(2)}) collective-permute-start(bf16[64,1920]{1,0:T(8,128)(2,1)S(1)} %slice.42), channel_id=1, source_target_pairs={{0,3},{1,0},{2,1},{3,2},{4,7},{5,4},{6,5},{7,6},{8,11},{9,8},{10,9... | collective-permute-start | bytes 737288 | tf_op jit(solution)/shard_map/ppermute | solution.py:41
  107.5 8.2 %collective-permute-start.14 = (bf16[64,1920]{1,0:T(8,128)(2,1)S(1)}, bf16[64,1920]{1,0:T(8,128)(2,1)S(1)}, u32[]{:S(2)}, u32[]{:S(2)}) collective-permute-start(bf16[64,1920]{1,0:T(8,128)(2,1)S(1)} %slice.41), channel_id=1, source_target_pairs={{0,1},{1,2},{2,3},{3,0},{4,5},{5,6},{6,7},{7,4},{8,9},{9,10},{10,1... | collective-permute-start | bytes 737288 | tf_op jit(solution)/shard_map/ppermute | solution.py:40
  117.2 1.3 %copy-start.5 = (bf16[512,1920]{1,0:T(8,128)(2,1)}, bf16[512,1920]{1,0:T(8,128)(2,1)S(1)}, u32[]{:S(2)}) copy-start(bf16[512,1920]{1,0:T(8,128)(2,1)S(1)} %constant_dynamic-update-slice_fusion.22) | copy-start | bytes 5898244

commit v2 on v0

v2 whole, which is shorter than its diff:
```python
import functools

import jax
import jax.numpy as jnp
from jax import lax
from jax.experimental import pallas as pl
from jax.experimental.pallas import tpu as pltpu
from jax.sharding import PartitionSpec as P

SBLK = 128
FRAMES = 512
BF16 = jnp.bfloat16
F32 = jnp.float32
WHOLE = pl.BlockSpec(memory_space=pltpu.VMEM)
SCALAR = pl.BlockSpec(memory_space=pltpu.SMEM)


def y_swap(mask):
    return [(c, c ^ mask) for c in range(16)]


def z_swap(mask):
    return [(c, c ^ (4 * mask)) for c in range(16)]


def y_turn(by):
    return [(c, (c & 12) | ((c + by) & 3)) for c in range(16)]


def z_turn(by):
    return [(c, (c + 4 * by) & 15) for c in range(16)]


def x_turn(by):
    return [(r, (r & 9) | ((r + 2 * by) & 6)) for r in range(16)]


def flip_pairs():
    pairs = []
    for r in range(16):
        for c in range(16):
            z_hi, y = c >> 2, c & 3
            x = (((r >> 1) & 3) + y) & 3
            to = (z_hi >> 1) * 8 + x * 2 + (z_hi & 1)
            pairs.append((r * 16 + c, to * 16 + r))
    return pairs


def add(one, other):
    return (one.astype(F32) + other.astype(F32)).astype(BF16)


def shape(rows, cols):
    return jax.ShapeDtypeStruct((rows, cols), BF16)


def first_kernel(at_ref, commands_ref, interaction_ref, sent_a, sent_b, ordered_ref):
    col = at_ref[1]
    out = lax.broadcasted_iota(jnp.int32, (FRAMES, FRAMES), 0)
    src = lax.broadcasted_iota(jnp.int32, (FRAMES, FRAMES), 1)
    half = out >> 8
    low = out & 15

    def mask_of(at):
        one, two = at & 1, at >> 1
        return jnp.where(half == 0, (one << 1) | (one ^ two), at ^ two)

    piece = col ^ (mask_of((out >> 6) & 3) + 4 * mask_of((out >> 4) & 3))
    pick = (src == piece * 32 + half * 16 + low).astype(F32).astype(BF16)
    ordered = lax.dot_general(
        pick, commands_ref[...], (((1,), (1,)), ((), ())), preferred_element_type=F32
    ).astype(BF16)
    sent_a[...] = jnp.dot(
        ordered[128:256], interaction_ref[...], preferred_element_type=F32
    ).astype(BF16)
    sent_b[...] = jnp.dot(
        ordered[384:512], interaction_ref[...], preferred_element_type=F32
    ).astype(BF16)
    ordered_ref[:128] = ordered[:128]
    ordered_ref[128:] = ordered[256:384]


def second_kernel(ordered_ref, interaction_ref, kept_a, kept_b):
    kept_a[...] = jnp.dot(
        ordered_ref[:128], interaction_ref[...], preferred_element_type=F32
    ).astype(BF16)
    kept_b[...] = jnp.dot(
        ordered_ref[128:], interaction_ref[...], preferred_element_type=F32
    ).astype(BF16)


def halves_kernel(left, right, flipped, low, high, same):
    half = low.shape[0]
    low[...] = left[:half]
    high[...] = right[half:]
    same[...] = flipped[...]


def join_kernel(at_ref, own, left, right, far_a, far_b, flipped, pair, mine, near):
    z = at_ref[1] >> 2

    def put(by, start, ref):
        first = pl.multiple_of(((z + by) & 3) * 32 + start, 16)
        mine[pl.ds(first, ref.shape[0])] = ref[...]

    put(0, 0, own)
    put(3, 0, left)
    put(1, 0, right)
    put(2, 0, far_a)
    put(2, 16, far_b)
    z_lo = at_ref[0] >> 3
    near[pl.ds(pl.multiple_of(z_lo * 32, 32), 32)] = flipped[...]
    near[pl.ds(pl.multiple_of((1 - z_lo) * 32, 32), 32)] = pair[...]


def split_kernel(y_left, y_right, near, x_left, x_right, y_low, y_high, x_low, x_high, joined):
    y_low[...] = y_left[:64]
    y_high[...] = y_right[64:]
    x_low[...] = x_left[:32]
    x_high[...] = x_right[32:]
    joined[:64] = near[...]
    joined[64:128] = x_left[...]
    joined[128:] = x_right[...]


def stack_kernel(one, two, out):
    half = one.shape[0]
    out[:half] = one[...]
    out[half:] = two[...]


def turn_kernel(own, left, right, out):
    for at, ref in enumerate((own, left, right)):
        out[:, at * 128 : at * 128 + 128] = ref[...].T


def last_kernel(
    at_ref, early, far_a, far_b, near, near_far, other, other_far, out, lhs, rhs
):
    row, col = at_ref[0], at_ref[1]
    rows, columns = out.shape

    @pl.when(row <= col)
    def _():
        @pl.when(pl.program_id(0) == 0)
        def _():
            y = col & 3
            for at, by in enumerate((0, 3, 1)):
                lane = pl.multiple_of(((y + by) & 3) * 128, 128)
                lhs[:, pl.ds(lane, 128)] = early[:, at * 128 : at * 128 + 128]
            lane = pl.multiple_of(((y + 2) & 3) * 128, 128)
            far = jnp.concatenate([far_a[...], far_b[...]], axis=0)
            lhs[:, pl.ds(lane, 128)] = far.T
            x, core = (row >> 1) & 3, row & 1
            for swap, most, rest in ((0, near, near_far), (1, other, other_far)):
                for at, by in enumerate((0, 3, 1, 2)):
                    ref, at = (most, at) if at < 3 else (rest, 0)
                    y_from = (x + by - (col >> 1)) & 3
                    for z_lo in range(2):
                        z_from = z_lo * 2 + (core ^ swap)
                        first = pl.multiple_of(y_from * 128 + z_from * 32, 32)
                        rhs[pl.ds(first, 32)] = ref[at * 64 + z_lo * 32 : at * 64 + z_lo * 32 + 32]

        start = pl.multiple_of(pl.program_id(0) * rows, rows)
        tile = jnp.dot(lhs[pl.ds(start, rows)], rhs[...], preferred_element_type=F32) * (
            1.0 / FRAMES
        )

        @pl.when(row < col)
        def _():
            out[...] = tile.astype(BF16)

        @pl.when(row == col)
        def _():
            down = lax.broadcasted_iota(jnp.int32, tile.shape, 0) + start
            across = lax.broadcasted_iota(jnp.int32, tile.shape, 1)
            out[...] = jnp.where(down <= across, tile, 0.0).astype(BF16)

    @pl.when(row > col)
    def _():
        out[...] = jnp.zeros_like(out)


def per_device(residual, interaction, commands, slope_valid, frame_valid):
    rows, width = interaction.shape
    row, col = lax.axis_index("row"), lax.axis_index("col")
    at = jnp.stack([row, col]).astype(jnp.int32)
    limit = pltpu.CompilerParams(vmem_limit_bytes=48 * 1024 * 1024)
    call = functools.partial(pl.pallas_call, compiler_params=limit)
    turned = interaction.T
    sent_a, sent_b, ordered = call(
        first_kernel,
        out_shape=(shape(128, rows), shape(128, rows), shape(256, width)),
        in_specs=[SCALAR, WHOLE, WHOLE],
        out_specs=(WHOLE, WHOLE, WHOLE),
        cost_estimate=pl.CostEstimate(
            flops=2 * 256 * width * rows, bytes_accessed=1600000, transcendentals=0
        ),
    )(at, commands, turned)
    got_a = lax.ppermute(sent_a, "col", y_swap(1))
    got_b = lax.ppermute(sent_b, "col", y_swap(3))
    kept_a, kept_b = call(
        second_kernel,
        out_shape=(shape(128, rows), shape(128, rows)),
        in_specs=[WHOLE, WHOLE],
        out_specs=(WHOLE, WHOLE),
        cost_estimate=pl.CostEstimate(
            flops=2 * 256 * width * rows, bytes_accessed=1600000, transcendentals=0
        ),
    )(ordered, turned)
    for swap_a, swap_b in (
        (y_swap(3), y_swap(1)),
        (z_swap(1), z_swap(3)),
        (z_swap(3), z_swap(1)),
    ):
        half = kept_a.shape[0] // 2
        sent_a, sent_b = add(kept_a[half:], got_a[half:]), add(kept_b[half:], got_b[half:])
        next_a = lax.ppermute(sent_a, "col", swap_a)
        next_b = lax.ppermute(sent_b, "col", swap_b)
        kept_a, kept_b = add(kept_a[:half], got_a[:half]), add(kept_b[:half], got_b[:half])
        got_a, got_b = next_a, next_b
    summed = jnp.concatenate([kept_a, kept_b]).astype(F32) + jnp.concatenate(
        [got_a, got_b]
    ).astype(F32)
    row_mask = jnp.broadcast_to(slope_valid[:, None], (rows // SBLK, SBLK)).reshape(-1)
    slopes = (
        (residual.T.astype(F32) + summed)
        * row_mask[None, :].astype(F32)
        * frame_valid[:, None].astype(F32)
    ).astype(BF16)

    left = lax.ppermute(slopes, "col", z_turn(1))
    right = lax.ppermute(slopes, "col", z_turn(-1))
    flipped = lax.ppermute(slopes, ("row", "col"), flip_pairs())
    low, high, flipped = call(
        halves_kernel,
        out_shape=(shape(16, rows), shape(16, rows), shape(32, rows)),
        in_specs=[WHOLE] * 3,
        out_specs=(WHOLE,) * 3,
    )(left, right, flipped)
    far_a = lax.ppermute(low, "col", z_turn(1))
    far_b = lax.ppermute(high, "col", z_turn(-1))
    pair = lax.ppermute(flipped, "row", [(r, r ^ 8) for r in range(16)])
    mine, near = call(
        join_kernel,
        out_shape=(shape(128, rows), shape(64, rows)),
        in_specs=[SCALAR] + [WHOLE] * 7,
        out_specs=(WHOLE,) * 2,
    )(at, slopes, left, right, far_a, far_b, flipped, pair)
    left = lax.ppermute(mine, "col", y_turn(1))
    right = lax.ppermute(mine, "col", y_turn(-1))
    x_left = lax.ppermute(near, "row", x_turn(1))
    x_right = lax.ppermute(near, "row", x_turn(-1))
    low, high, x_low, x_high, near = call(
        split_kernel,
        out_shape=(shape(64, rows),) * 2 + (shape(32, rows),) * 2 + (shape(192, rows),),
        in_specs=[WHOLE] * 5,
        out_specs=(WHOLE,) * 5,
    )(left, right, near, x_left, x_right)
    far_a = lax.ppermute(low, "col", y_turn(1))
    far_b = lax.ppermute(high, "col", y_turn(-1))
    x_far_a = lax.ppermute(x_low, "row", x_turn(1))
    x_far_b = lax.ppermute(x_high, "row", x_turn(-1))
    cores = [(r, r ^ 1) for r in range(16)]
    other = lax.ppermute(near, "row", cores)
    near_far = call(
        stack_kernel, out_shape=shape(64, rows), in_specs=[WHOLE] * 2, out_specs=WHOLE
    )(x_far_a, x_far_b)
    other_far = lax.ppermute(near_far, "row", cores)
    early = call(
        turn_kernel,
        out_shape=shape(rows, 384),
        in_specs=[WHOLE] * 3,
        out_specs=WHOLE,
    )(mine, left, right)
    steps = 5
    return call(
        last_kernel,
        grid=(steps,),
        out_shape=shape(rows, rows),
        in_specs=[SCALAR] + [WHOLE] * 7,
        out_specs=pl.BlockSpec((rows // steps, rows), lambda i: (i, 0)),
        scratch_shapes=[pltpu.VMEM((rows, FRAMES), BF16), pltpu.VMEM((FRAMES, rows), BF16)],
        cost_estimate=pl.CostEstimate(
            flops=2 * FRAMES * rows * rows, bytes_accessed=2 * rows * rows, transcendentals=0
        ),
    )(at, early, far_a, far_b, near, near_far, other, other_far)


def solution(mesh):
    placed = (P("row", "col"), P("row", "col"), P("col", None), P("row"), P("col"))
    return jax.shard_map(
        per_device, mesh=mesh, in_specs=placed, out_specs=P("row", "col"), check_vma=False
    )
```

time: 236 us -> 110 us (0.47); the launches traced: 233 us -> 110 us
  waiting for transfers between devices: 191 us -> 57.4 us
  starting transfers between devices: 9.6 us -> 37.8 us
  between operations: 13.1 us -> 0.18 us
  matrix products: 12.6 us -> 0 us
  Pallas kernels: 0 us -> 11.7 us
  local copies, waits for them, and re-layouts: 4.92 us -> 2.35 us
    all_gather x2 -> x0, waiting for transfers between devices: 101 us -> none  [the longest x1 66.3 us: per_device(): row_copy = lax.all_gather(local_slopes, 'col', axis=1, tiled=True)]
    reduce_scatter x1 -> x0, waiting for transfers between devices: 89.3 us -> none  [per_device(): lax.psum_scatter(product.astype(jnp.bfloat16), 'col', scatter_dimension=1...]
    ppermute x0 -> x24, waiting for transfers between devices: none -> 57.4 us  [the longest x1 11.5 us: per_device(): got_b = lax.ppermute(sent_b, 'col', y_swap(3))]
    ppermute x0 -> x24, starting transfers between devices: none -> 37.8 us  [the longest x3 7.11 us: per_device(): next_b = lax.ppermute(sent_b, 'col', swap_b)]
    dot_general x2 -> x0, matrix products: 12.6 us -> none  [the longest x1 9.07 us: per_device(): lax.dot_general(row_copy, columns, (((1,), (1,)), ((), ())), preferred_el...]
    pallas_call x0 -> x8, Pallas kernels: none -> 11.7 us  [the longest x1 8.14 us: per_device(): call(last_kernel, grid=(steps,), out_shape=shape(rows, rows), in_specs=[S...]
    all_to_all x1 -> x0, starting transfers between devices: 9.51 us -> none  [per_device(): lax.all_to_all(gathered, 'col', split_axis=0, concat_axis=1, tiled=True)]
    all_to_all x1 -> x0, local copies, waits for them, and re-layouts: 2.98 us -> none  [per_device(): lax.all_to_all(gathered, 'col', split_axis=0, concat_axis=1, tiled=True)]
  transfers between devices with their start and end apart: 4 -> 24, of which waited for: 3 -> 16; matrix products, arithmetic and copies ran while one was open for 1% -> 0% of each run, Pallas kernels for 0% -> 1%
where the time goes in v2:
time: 110 us
  waiting for transfers between devices  57.4 us (52%)
  starting transfers between devices  37.8 us (34%)
  Pallas kernels  11.7 us (11%)
  local copies, waits for them, and re-layouts  2.35 us (2%)
    ppermute x1, waiting for transfers between devices, per_device(): got_b = lax.ppermute(sent_b, 'col', y_swap(3))  11.5 us
    ppermute x3, waiting for transfers between devices, per_device(): next_a = lax.ppermute(sent_a, 'col', swap_a)  10.9 us
    pallas_call x1, Pallas kernels, per_device(): call(last_kernel, grid=(steps,), out_shape=shape(rows, rows), in_specs=[S...  8.14 us
    ppermute x3, waiting for transfers between devices, per_device(): next_b = lax.ppermute(sent_b, 'col', swap_b)  7.37 us
    ppermute x3, starting transfers between devices, per_device(): next_b = lax.ppermute(sent_b, 'col', swap_b)  7.11 us
    ppermute x1, waiting for transfers between devices, per_device(): right = lax.ppermute(slopes, 'col', z_turn(-1))  5.87 us
    ppermute x1, waiting for transfers between devices, per_device(): x_right = lax.ppermute(near, 'row', x_turn(-1))  5.09 us
    ppermute x1, waiting for transfers between devices, per_device(): far_a = lax.ppermute(low, 'col', y_turn(1))  4 us
  transfers between devices with their start and end apart: 24, of which 16 were waited for; matrix products, arithmetic and copies ran while one was open for 0% of the time, Pallas kernels for 1%

profile of v2, /device:TPU:24, one launch (start us, length us, event | category | flops | bytes accessed | tf_op | source)
XLA Modules:
  0.0 110.0 jit_solution(1624780639489764540)
XLA Ops:
  0.1 1.3 %copy-done = bf16[1920,320]{0,1:T(8,128)(2,1)S(1)} copy-done((bf16[1920,320]{0,1:T(8,128)(2,1)S(1)}, bf16[1920,320]{0,1:T(8,128)(2,1)}, u32[]{:S(2)}) %copy-start) | copy-done | bytes 1228824
  1.4 1.0 copy-done.2
  2.3 1.7 %shard_map.55 = (bf16[128,1920]{1,0:T(8,128)(2,1)S(1)}, bf16[128,1920]{1,0:T(8,128)(2,1)S(1)}, bf16[256,320]{1,0:T(8,128)(2,1)S(1)}) custom-call(s32[2]{0:T(128)S(1)} %pad_add_fusion.at_ref, bf16[320,512]{1,0:T(8,128)(2,1)S(1)} %copy-done.2, bf16[320,1920]{1,0:T(8,128)(2,1)S(1)} %bitcast.13), custom_call_target="tpu_custom_call" | custom-call | flops 314572800 | bytes 1600000 | tf_op jit(solution)/shard_map/pallas_call | solution.py:191
  4.0 2.0 %collective-permute-start.3 = (bf16[128,1920]{1,0:T(8,128)(2,1)S(1)}, bf16[128,1920]{1,0:T(8,128)(2,1)S(1)}, u32[]{:S(2)}, u32[]{:S(2)}) collective-permute-start(bf16[128,1920]{1,0:T(8,128)(2,1)S(1)} %get-tuple-element.24), channel_id=1, source_target_pairs={{0,3},{1,2},{2,1},{3,0},{4,7},{5,6},{6,5},{7,4},{8,11},{9,10},{10,... | collective-permute-start | bytes 1474568 | tf_op jit(solution)/shard_map/ppermute | solution.py:201
  6.1 0.7 shard_map.56
  6.8 11.5 %collective-permute-done.3 = bf16[128,1920]{1,0:T(8,128)(2,1)S(1)} collective-permute-done((bf16[128,1920]{1,0:T(8,128)(2,1)S(1)}, bf16[128,1920]{1,0:T(8,128)(2,1)S(1)}, u32[]{:S(2)}, u32[]{:S(2)}) %collective-permute-start.3) | collective-permute-done | bytes 491552 | tf_op jit(solution)/shard_map/ppermute | solution.py:201
  18.7 2.0 %collective-permute-start.1 = (bf16[64,1920]{1,0:T(8,128)(2,1)S(1)}, bf16[64,1920]{1,0:T(8,128)(2,1)S(1)}, u32[]{:S(2)}, u32[]{:S(2)}) collective-permute-start(bf16[64,1920]{1,0:T(8,128)(2,1)S(1)} %get-tuple-element.36), channel_id=1, source_target_pairs={{0,3},{1,2},{2,1},{3,0},{4,7},{5,6},{6,5},{7,4},{8,11},{9,10},{10,... | collective-permute-start | bytes 737288 | tf_op jit(solution)/shard_map/ppermute | solution.py:218
  20.6 4.7 %collective-permute-done.4 = bf16[64,1920]{1,0:T(8,128)(2,1)S(1)} collective-permute-done((bf16[64,1920]{1,0:T(8,128)(2,1)S(1)}, bf16[64,1920]{1,0:T(8,128)(2,1)S(1)}, u32[]{:S(2)}, u32[]{:S(2)}) %collective-permute-start.4) | collective-permute-done | bytes 245792 | tf_op jit(solution)/shard_map/ppermute | solution.py:219
  25.4 6.4 %collective-permute-start.5 = (bf16[32,1920]{1,0:T(8,128)(2,1)S(1)}, bf16[32,1920]{1,0:T(8,128)(2,1)S(1)}, u32[]{:S(2)}, u32[]{:S(2)}) collective-permute-start(bf16[32,1920]{1,0:T(8,128)(2,1)S(1)} %get-tuple-element.42), channel_id=1, source_target_pairs={{0,12},{1,13},{2,14},{3,15},{4,8},{5,9},{6,10},{7,11},{8,4},{9,5},... | collective-permute-start | bytes 368648 | tf_op jit(solution)/shard_map/ppermute | solution.py:219
  31.9 1.5 %collective-permute-start.2 = (bf16[32,1920]{1,0:T(8,128)(2,1)S(1)}, bf16[32,1920]{1,0:T(8,128)(2,1)S(1)}, u32[]{:S(2)}, u32[]{:S(2)}) collective-permute-start(bf16[32,1920]{1,0:T(8,128)(2,1)S(1)} %get-tuple-element.40), channel_id=1, source_target_pairs={{0,4},{1,5},{2,6},{3,7},{4,0},{5,1},{6,2},{7,3},{8,12},{9,13},{10,... | collective-permute-start | bytes 368648 | tf_op jit(solution)/shard_map/ppermute | solution.py:218
  33.4 2.2 %collective-permute-done.5 = bf16[32,1920]{1,0:T(8,128)(2,1)S(1)} collective-permute-done((bf16[32,1920]{1,0:T(8,128)(2,1)S(1)}, bf16[32,1920]{1,0:T(8,128)(2,1)S(1)}, u32[]{:S(2)}, u32[]{:S(2)}) %collective-permute-start.5) | collective-permute-done | bytes 122912 | tf_op jit(solution)/shard_map/ppermute | solution.py:219
  36.3 5.1 %collective-permute-done.2 = bf16[32,1920]{1,0:T(8,128)(2,1)S(1)} collective-permute-done((bf16[32,1920]{1,0:T(8,128)(2,1)S(1)}, bf16[32,1920]{1,0:T(8,128)(2,1)S(1)}, u32[]{:S(2)}, u32[]{:S(2)}) %collective-permute-start.2) | collective-permute-done | bytes 122912 | tf_op jit(solution)/shard_map/ppermute | solution.py:218
  42.0 5.8 %collective-permute-done.6 = bf16[16,1920]{1,0:T(8,128)(2,1)S(1)} collective-permute-done((bf16[16,1920]{1,0:T(8,128)(2,1)S(1)}, bf16[16,1920]{1,0:T(8,128)(2,1)S(1)}, u32[]{:S(2)}, u32[]{:S(2)}) %collective-permute-start.6) | collective-permute-done | bytes 61472 | tf_op jit(solution)/shard_map/ppermute | solution.py:218
  47.9 3.9 %collective-permute-start.10 = (bf16[32,1920]{1,0:T(8,128)(2,1)S(1)}, bf16[32,1920]{1,0:T(8,128)(2,1)S(1)}, u32[]{:S(2)}, u32[]{:S(2)}) collective-permute-start(bf16[32,1920]{1,0:T(8,128)(2,1)S(1)} %fusion.2.own), channel_id=1, source_target_pairs={{0,0},{1,32},{2,64},{3,96},{4,16},{5,48},{6,80},{7,112},{8,128},{9... | collective-permute-start | bytes 368648 | tf_op jit(solution)/shard_map/ppermute | solution.py:234
  52.0 2.9 %collective-permute-start.8 = (bf16[32,1920]{1,0:T(8,128)(2,1)S(1)}, bf16[32,1920]{1,0:T(8,128)(2,1)S(1)}, u32[]{:S(2)}, u32[]{:S(2)}) collective-permute-start(bf16[32,1920]{1,0:T(8,128)(2,1)S(1)} %fusion.2.own), channel_id=1, source_target_pairs={{0,4},{1,5},{2,6},{3,7},{4,8},{5,9},{6,10},{7,11},{8,12},{9,13},{1... | collective-permute-start | bytes 368648 | tf_op jit(solution)/shard_map/ppermute | solution.py:232
  54.9 1.0 collective-permute-done.10.flipped
  55.8 5.9 %collective-permute-done.9.right = bf16[32,1920]{1,0:T(8,128)(2,1)S(1)} collective-permute-done((bf16[32,1920]{1,0:T(8,128)(2,1)S(1)}, bf16[32,1920]{1,0:T(8,128)(2,1)S(1)}, u32[]{:S(2)}, u32[]{:S(2)}) %collective-permute-start.9) | collective-permute-done | bytes 122912 | tf_op jit(solution)/shard_map/ppermute | solution.py:233
  61.7 2.2 %collective-permute-start.13 = (bf16[32,1920]{1,0:T(8,128)(2,1)S(1)}, bf16[32,1920]{1,0:T(8,128)(2,1)S(1)}, u32[]{:S(2)}, u32[]{:S(2)}) collective-permute-start(bf16[32,1920]{1,0:T(8,128)(2,1)S(1)} %get-tuple-element.27.flipped), channel_id=1, source_target_pairs={{0,128},{16,144},{32,160},{48,176},{64,192},{80,208},{96,224},{112... | collective-permute-start | bytes 368648 | tf_op jit(solution)/shard_map/ppermute | solution.py:243
  63.9 1.8 %collective-permute-start.11 = (bf16[16,1920]{1,0:T(8,128)(2,1)S(1)}, bf16[16,1920]{1,0:T(8,128)(2,1)S(1)}, u32[]{:S(2)}, u32[]{:S(2)}) collective-permute-start(bf16[16,1920]{1,0:T(8,128)(2,1)S(1)} %get-tuple-element.25), channel_id=1, source_target_pairs={{0,4},{1,5},{2,6},{3,7},{4,8},{5,9},{6,10},{7,11},{8,12},{9,13},{1... | collective-permute-start | bytes 184328 | tf_op jit(solution)/shard_map/ppermute | solution.py:241
  65.8 2.3 %collective-permute-start.12 = (bf16[16,1920]{1,0:T(8,128)(2,1)S(1)}, bf16[16,1920]{1,0:T(8,128)(2,1)S(1)}, u32[]{:S(2)}, u32[]{:S(2)}) collective-permute-start(bf16[16,1920]{1,0:T(8,128)(2,1)S(1)} %get-tuple-element.26), channel_id=1, source_target_pairs={{0,12},{1,13},{2,14},{3,15},{4,0},{5,1},{6,2},{7,3},{8,4},{9,5},{1... | collective-permute-start | bytes 184328 | tf_op jit(solution)/shard_map/ppermute | solution.py:242
  68.1 2.6 %collective-permute-done.11.far_a = bf16[16,1920]{1,0:T(8,128)(2,1)S(1)} collective-permute-done((bf16[16,1920]{1,0:T(8,128)(2,1)S(1)}, bf16[16,1920]{1,0:T(8,128)(2,1)S(1)}, u32[]{:S(2)}, u32[]{:S(2)}) %collective-permute-start.11) | collective-permute-done | bytes 61472 | tf_op jit(solution)/shard_map/ppermute | solution.py:241
  70.7 1.2 %collective-permute-done.12.far_b = bf16[16,1920]{1,0:T(8,128)(2,1)S(1)} collective-permute-done((bf16[16,1920]{1,0:T(8,128)(2,1)S(1)}, bf16[16,1920]{1,0:T(8,128)(2,1)S(1)}, u32[]{:S(2)}, u32[]{:S(2)}) %collective-permute-start.12) | collective-permute-done | bytes 61472 | tf_op jit(solution)/shard_map/ppermute | solution.py:242
  72.9 2.9 %collective-permute-start.14 = (bf16[128,1920]{1,0:T(8,128)(2,1)S(1)}, bf16[128,1920]{1,0:T(8,128)(2,1)S(1)}, u32[]{:S(2)}, u32[]{:S(2)}) collective-permute-start(bf16[128,1920]{1,0:T(8,128)(2,1)S(1)} %get-tuple-element.28.own), channel_id=1, source_target_pairs={{0,1},{1,2},{2,3},{3,0},{4,5},{5,6},{6,7},{7,4},{8,9},{9,10},{10,1... | collective-permute-start | bytes 1474568 | tf_op jit(solution)/shard_map/ppermute | solution.py:250
  75.8 1.4 %collective-permute-start.17 = (bf16[64,1920]{1,0:T(8,128)(2,1)S(1)}, bf16[64,1920]{1,0:T(8,128)(2,1)S(1)}, u32[]{:S(2)}, u32[]{:S(2)}) collective-permute-start(bf16[64,1920]{1,0:T(8,128)(2,1)S(1)} %get-tuple-element.29.near), channel_id=1, source_target_pairs={{0,96},{16,112},{32,0},{48,16},{64,32},{80,48},{96,64},{112,80},{1... | collective-permute-start | bytes 737288 | tf_op jit(solution)/shard_map/ppermute | solution.py:253
  77.8 5.1 %collective-permute-done.17.x_right = bf16[64,1920]{1,0:T(8,128)(2,1)S(1)} collective-permute-done((bf16[64,1920]{1,0:T(8,128)(2,1)S(1)}, bf16[64,1920]{1,0:T(8,128)(2,1)S(1)}, u32[]{:S(2)}, u32[]{:S(2)}) %collective-permute-start.17) | collective-permute-done | bytes 245792 | tf_op jit(solution)/shard_map/ppermute | solution.py:253
  82.9 1.6 %collective-permute-done.16.x_left = bf16[64,1920]{1,0:T(8,128)(2,1)S(1)} collective-permute-done((bf16[64,1920]{1,0:T(8,128)(2,1)S(1)}, bf16[64,1920]{1,0:T(8,128)(2,1)S(1)}, u32[]{:S(2)}, u32[]{:S(2)}) %collective-permute-start.16) | collective-permute-done | bytes 245792 | tf_op jit(solution)/shard_map/ppermute | solution.py:252
  84.6 2.2 %collective-permute-done.15.right.y_right = bf16[128,1920]{1,0:T(8,128)(2,1)S(1)} collective-permute-done((bf16[128,1920]{1,0:T(8,128)(2,1)S(1)}, bf16[128,1920]{1,0:T(8,128)(2,1)S(1)}, u32[]{:S(2)}, u32[]{:S(2)}) %collective-permute-start.15) | collective-permute-done | bytes 491552 | tf_op jit(solution)/shard_map/ppermute | solution.py:251
  87.5 2.7 %collective-permute-start.21 = (bf16[32,1920]{1,0:T(8,128)(2,1)S(1)}, bf16[32,1920]{1,0:T(8,128)(2,1)S(1)}, u32[]{:S(2)}, u32[]{:S(2)}) collective-permute-start(bf16[32,1920]{1,0:T(8,128)(2,1)S(1)} %get-tuple-element.34), channel_id=1, source_target_pairs={{0,96},{16,112},{32,0},{48,16},{64,32},{80,48},{96,64},{112,80},{1... | collective-permute-start | bytes 368648 | tf_op jit(solution)/shard_map/ppermute | solution.py:263
  90.2 3.0 %collective-permute-start.18 = (bf16[64,1920]{1,0:T(8,128)(2,1)S(1)}, bf16[64,1920]{1,0:T(8,128)(2,1)S(1)}, u32[]{:S(2)}, u32[]{:S(2)}) collective-permute-start(bf16[64,1920]{1,0:T(8,128)(2,1)S(1)} %get-tuple-element.30), channel_id=1, source_target_pairs={{0,1},{1,2},{2,3},{3,0},{4,5},{5,6},{6,7},{7,4},{8,9},{9,10},{10,1... | collective-permute-start | bytes 737288 | tf_op jit(solution)/shard_map/ppermute | solution.py:260
  94.4 4.0 %collective-permute-done.18.far_a = bf16[64,1920]{1,0:T(8,128)(2,1)S(1)} collective-permute-done((bf16[64,1920]{1,0:T(8,128)(2,1)S(1)}, bf16[64,1920]{1,0:T(8,128)(2,1)S(1)}, u32[]{:S(2)}, u32[]{:S(2)}) %collective-permute-start.18) | collective-permute-done | bytes 245792 | tf_op jit(solution)/shard_map/ppermute | solution.py:260
  98.4 3.4 %collective-permute-done.19.far_b = bf16[64,1920]{1,0:T(8,128)(2,1)S(1)} collective-permute-done((bf16[64,1920]{1,0:T(8,128)(2,1)S(1)}, bf16[64,1920]{1,0:T(8,128)(2,1)S(1)}, u32[]{:S(2)}, u32[]{:S(2)}) %collective-permute-start.19) | collective-permute-done | bytes 245792 | tf_op jit(solution)/shard_map/ppermute | solution.py:261
  101.9 8.1 %shard_map.62 = bf16[1920,1920]{1,0:T(8,128)(2,1)} custom-call(s32[2]{0:T(128)S(1)} %pad_add_fusion.at_ref, bf16[1920,384]{1,0:T(8,128)(2,1)S(1)} %shard_map.59.early, bf16[64,1920]{1,0:T(8,128)(2,1)S(1)} %collective-permute-done.18.far_a, bf16[64,1920]{1,0:T(8,128)(2,1)S(1)} %collective-permute-done.19.far_b, bf16[192,1920]{1,0:T(8,128)(2,1)S(1)} %get-tuple-element.32.near, ...), custom_call_target="tpu_custom_call" | custom-call | flops 3774873600 | bytes 7372800 | tf_op jit(solution)/shard_map/pallas_call | solution.py:277
  (47 shorter events, 5.8 us)
Async XLA Ops:
  0.0 6.1 %copy-start.4 = (s32[15]{0:T(128)S(1)}, s32[15]{0:T(128)}, u32[]{:S(2)}) copy-start(s32[15]{0:T(128)} %param.8) | copy-start | bytes 184
  0.1 1.3 %copy-start = (bf16[1920,320]{0,1:T(8,128)(2,1)S(1)}, bf16[1920,320]{0,1:T(8,128)(2,1)}, u32[]{:S(2)}) copy-start(bf16[1920,320]{0,1:T(8,128)(2,1)} %param.6) | copy-start | bytes 3686404
  1.4 1.0 copy-start.2
  2.3 3.8 %copy-start.1 = (bf16[1920,320]{0,1:T(8,128)(2,1)S(1)}, bf16[1920,320]{0,1:T(8,128)(2,1)}, u32[]{:S(2)}) copy-start(bf16[1920,320]{0,1:T(8,128)(2,1)} %param.6) | copy-start | bytes 3686404
  4.0 14.3 %collective-permute-start.3 = (bf16[128,1920]{1,0:T(8,128)(2,1)S(1)}, bf16[128,1920]{1,0:T(8,128)(2,1)S(1)}, u32[]{:S(2)}, u32[]{:S(2)}) collective-permute-start(bf16[128,1920]{1,0:T(8,128)(2,1)S(1)} %get-tuple-element.24), channel_id=1, source_target_pairs={{0,3},{1,2},{2,1},{3,0},{4,7},{5,6},{6,5},{7,4},{8,11},{9,10},{10,... | collective-permute-start | bytes 1474568 | tf_op jit(solution)/shard_map/ppermute | solution.py:201
  6.1 12.4 %collective-permute-start = (bf16[128,1920]{1,0:T(8,128)(2,1)S(1)}, bf16[128,1920]{1,0:T(8,128)(2,1)S(1)}, u32[]{:S(2)}, u32[]{:S(2)}) collective-permute-start(bf16[128,1920]{1,0:T(8,128)(2,1)S(1)} %get-tuple-element.22), channel_id=1, source_target_pairs={{0,1},{1,0},{2,3},{3,2},{4,5},{5,4},{6,7},{7,6},{8,9},{9,8},{10,11... | collective-permute-start | bytes 1474568 | tf_op jit(solution)/shard_map/ppermute | solution.py:200
  18.4 6.9 %collective-permute-start.4 = (bf16[64,1920]{1,0:T(8,128)(2,1)S(1)}, bf16[64,1920]{1,0:T(8,128)(2,1)S(1)}, u32[]{:S(2)}, u32[]{:S(2)}) collective-permute-start(bf16[64,1920]{1,0:T(8,128)(2,1)S(1)} %get-tuple-element.38), channel_id=1, source_target_pairs={{0,1},{1,0},{2,3},{3,2},{4,5},{5,4},{6,7},{7,6},{8,9},{9,8},{10,11... | collective-permute-start | bytes 737288 | tf_op jit(solution)/shard_map/ppermute | solution.py:219
  18.7 22.9 %copy-start.5 = (s32[32]{0:T(128)S(1)}, s32[32]{0:T(128)}, u32[]{:S(2)}) copy-start(s32[32]{0:T(128)} %param.9) | copy-start | bytes 388
  18.7 29.2 %copy-start.3 = (bf16[1920,32]{0,1:T(8,128)(2,1)S(1)}, bf16[1920,32]{0,1:T(8,128)(2,1)}, u32[]{:S(2)}) copy-start(bf16[1920,32]{0,1:T(8,128)(2,1)} %param.5) | copy-start | bytes 368644
  18.7 13.1 %collective-permute-start.1 = (bf16[64,1920]{1,0:T(8,128)(2,1)S(1)}, bf16[64,1920]{1,0:T(8,128)(2,1)S(1)}, u32[]{:S(2)}, u32[]{:S(2)}) collective-permute-start(bf16[64,1920]{1,0:T(8,128)(2,1)S(1)} %get-tuple-element.36), channel_id=1, source_target_pairs={{0,3},{1,2},{2,1},{3,0},{4,7},{5,6},{6,5},{7,4},{8,11},{9,10},{10,... | collective-permute-start | bytes 737288 | tf_op jit(solution)/shard_map/ppermute | solution.py:218
  25.4 10.2 %collective-permute-start.5 = (bf16[32,1920]{1,0:T(8,128)(2,1)S(1)}, bf16[32,1920]{1,0:T(8,128)(2,1)S(1)}, u32[]{:S(2)}, u32[]{:S(2)}) collective-permute-start(bf16[32,1920]{1,0:T(8,128)(2,1)S(1)} %get-tuple-element.42), channel_id=1, source_target_pairs={{0,12},{1,13},{2,14},{3,15},{4,8},{5,9},{6,10},{7,11},{8,4},{9,5},... | collective-permute-start | bytes 368648 | tf_op jit(solution)/shard_map/ppermute | solution.py:219
  31.9 9.5 %collective-permute-start.2 = (bf16[32,1920]{1,0:T(8,128)(2,1)S(1)}, bf16[32,1920]{1,0:T(8,128)(2,1)S(1)}, u32[]{:S(2)}, u32[]{:S(2)}) collective-permute-start(bf16[32,1920]{1,0:T(8,128)(2,1)S(1)} %get-tuple-element.40), channel_id=1, source_target_pairs={{0,4},{1,5},{2,6},{3,7},{4,0},{5,1},{6,2},{7,3},{8,12},{9,13},{10,... | collective-permute-start | bytes 368648 | tf_op jit(solution)/shard_map/ppermute | solution.py:218
  35.7 6.4 %collective-permute-start.7 = (bf16[16,1920]{1,0:T(8,128)(2,1)S(1)}, bf16[16,1920]{1,0:T(8,128)(2,1)S(1)}, u32[]{:S(2)}, u32[]{:S(2)}) collective-permute-start(bf16[16,1920]{1,0:T(8,128)(2,1)S(1)} %get-tuple-element.45), channel_id=1, source_target_pairs={{0,4},{1,5},{2,6},{3,7},{4,0},{5,1},{6,2},{7,3},{8,12},{9,13},{10,... | collective-permute-start | bytes 184328 | tf_op jit(solution)/shard_map/ppermute | solution.py:219
  41.4 6.4 %collective-permute-start.6 = (bf16[16,1920]{1,0:T(8,128)(2,1)S(1)}, bf16[16,1920]{1,0:T(8,128)(2,1)S(1)}, u32[]{:S(2)}, u32[]{:S(2)}) collective-permute-start(bf16[16,1920]{1,0:T(8,128)(2,1)S(1)} %get-tuple-element.43), channel_id=1, source_target_pairs={{0,12},{1,13},{2,14},{3,15},{4,8},{5,9},{6,10},{7,11},{8,4},{9,5},... | collective-permute-start | bytes 184328 | tf_op jit(solution)/shard_map/ppermute | solution.py:218
  47.9 7.9 %collective-permute-start.10 = (bf16[32,1920]{1,0:T(8,128)(2,1)S(1)}, bf16[32,1920]{1,0:T(8,128)(2,1)S(1)}, u32[]{:S(2)}, u32[]{:S(2)}) collective-permute-start(bf16[32,1920]{1,0:T(8,128)(2,1)S(1)} %fusion.2.own), channel_id=1, source_target_pairs={{0,0},{1,32},{2,64},{3,96},{4,16},{5,48},{6,80},{7,112},{8,128},{9... | collective-permute-start | bytes 368648 | tf_op jit(solution)/shard_map/ppermute | solution.py:234
  51.9 9.8 %collective-permute-start.9 = (bf16[32,1920]{1,0:T(8,128)(2,1)S(1)}, bf16[32,1920]{1,0:T(8,128)(2,1)S(1)}, u32[]{:S(2)}, u32[]{:S(2)}) collective-permute-start(bf16[32,1920]{1,0:T(8,128)(2,1)S(1)} %fusion.2.own), channel_id=1, source_target_pairs={{0,12},{1,13},{2,14},{3,15},{4,0},{5,1},{6,2},{7,3},{8,4},{9,5},{1... | collective-permute-start | bytes 368648 | tf_op jit(solution)/shard_map/ppermute | solution.py:233
  52.0 9.7 %collective-permute-start.8 = (bf16[32,1920]{1,0:T(8,128)(2,1)S(1)}, bf16[32,1920]{1,0:T(8,128)(2,1)S(1)}, u32[]{:S(2)}, u32[]{:S(2)}) collective-permute-start(bf16[32,1920]{1,0:T(8,128)(2,1)S(1)} %fusion.2.own), channel_id=1, source_target_pairs={{0,4},{1,5},{2,6},{3,7},{4,8},{5,9},{6,10},{7,11},{8,12},{9,13},{1... | collective-permute-start | bytes 368648 | tf_op jit(solution)/shard_map/ppermute | solution.py:232
  61.7 10.1 %collective-permute-start.13 = (bf16[32,1920]{1,0:T(8,128)(2,1)S(1)}, bf16[32,1920]{1,0:T(8,128)(2,1)S(1)}, u32[]{:S(2)}, u32[]{:S(2)}) collective-permute-start(bf16[32,1920]{1,0:T(8,128)(2,1)S(1)} %get-tuple-element.27.flipped), channel_id=1, source_target_pairs={{0,128},{16,144},{32,160},{48,176},{64,192},{80,208},{96,224},{112... | collective-permute-start | bytes 368648 | tf_op jit(solution)/shard_map/ppermute | solution.py:243
  63.9 6.8 %collective-permute-start.11 = (bf16[16,1920]{1,0:T(8,128)(2,1)S(1)}, bf16[16,1920]{1,0:T(8,128)(2,1)S(1)}, u32[]{:S(2)}, u32[]{:S(2)}) collective-permute-start(bf16[16,1920]{1,0:T(8,128)(2,1)S(1)} %get-tuple-element.25), channel_id=1, source_target_pairs={{0,4},{1,5},{2,6},{3,7},{4,8},{5,9},{6,10},{7,11},{8,12},{9,13},{1... | collective-permute-start | bytes 184328 | tf_op jit(solution)/shard_map/ppermute | solution.py:241
  65.8 6.1 %collective-permute-start.12 = (bf16[16,1920]{1,0:T(8,128)(2,1)S(1)}, bf16[16,1920]{1,0:T(8,128)(2,1)S(1)}, u32[]{:S(2)}, u32[]{:S(2)}) collective-permute-start(bf16[16,1920]{1,0:T(8,128)(2,1)S(1)} %get-tuple-element.26), channel_id=1, source_target_pairs={{0,12},{1,13},{2,14},{3,15},{4,0},{5,1},{6,2},{7,3},{8,4},{9,5},{1... | collective-permute-start | bytes 184328 | tf_op jit(solution)/shard_map/ppermute | solution.py:242
  72.5 14.2 %collective-permute-start.15 = (bf16[128,1920]{1,0:T(8,128)(2,1)S(1)}, bf16[128,1920]{1,0:T(8,128)(2,1)S(1)}, u32[]{:S(2)}, u32[]{:S(2)}) collective-permute-start(bf16[128,1920]{1,0:T(8,128)(2,1)S(1)} %get-tuple-element.28.own), channel_id=1, source_target_pairs={{0,3},{1,0},{2,1},{3,2},{4,7},{5,4},{6,5},{7,6},{8,11},{9,8},{10,9... | collective-permute-start | bytes 1474568 | tf_op jit(solution)/shard_map/ppermute | solution.py:251
  72.9 13.8 %collective-permute-start.14 = (bf16[128,1920]{1,0:T(8,128)(2,1)S(1)}, bf16[128,1920]{1,0:T(8,128)(2,1)S(1)}, u32[]{:S(2)}, u32[]{:S(2)}) collective-permute-start(bf16[128,1920]{1,0:T(8,128)(2,1)S(1)} %get-tuple-element.28.own), channel_id=1, source_target_pairs={{0,1},{1,2},{2,3},{3,0},{4,5},{5,6},{6,7},{7,4},{8,9},{9,10},{10,1... | collective-permute-start | bytes 1474568 | tf_op jit(solution)/shard_map/ppermute | solution.py:250
  75.8 7.1 %collective-permute-start.17 = (bf16[64,1920]{1,0:T(8,128)(2,1)S(1)}, bf16[64,1920]{1,0:T(8,128)(2,1)S(1)}, u32[]{:S(2)}, u32[]{:S(2)}) collective-permute-start(bf16[64,1920]{1,0:T(8,128)(2,1)S(1)} %get-tuple-element.29.near), channel_id=1, source_target_pairs={{0,96},{16,112},{32,0},{48,16},{64,32},{80,48},{96,64},{112,80},{1... | collective-permute-start | bytes 737288 | tf_op jit(solution)/shard_map/ppermute | solution.py:253
  77.1 7.4 %collective-permute-start.16 = (bf16[64,1920]{1,0:T(8,128)(2,1)S(1)}, bf16[64,1920]{1,0:T(8,128)(2,1)S(1)}, u32[]{:S(2)}, u32[]{:S(2)}) collective-permute-start(bf16[64,1920]{1,0:T(8,128)(2,1)S(1)} %get-tuple-element.29.near), channel_id=1, source_target_pairs={{0,32},{16,48},{32,64},{48,80},{64,96},{80,112},{96,0},{112,16},{1... | collective-permute-start | bytes 737288 | tf_op jit(solution)/shard_map/ppermute | solution.py:252
  86.8 15.0 %collective-permute-start.22 = (bf16[192,1920]{1,0:T(8,128)(2,1)S(1)}, bf16[192,1920]{1,0:T(8,128)(2,1)S(1)}, u32[]{:S(2)}, u32[]{:S(2)}) collective-permute-start(bf16[192,1920]{1,0:T(8,128)(2,1)S(1)} %get-tuple-element.32.near), channel_id=1, source_target_pairs={{0,16},{16,0},{32,48},{48,32},{64,80},{80,64},{96,112},{112,96},{1... | collective-permute-start | bytes 2211848 | tf_op jit(solution)/shard_map/ppermute | solution.py:265
  86.9 6.9 %collective-permute-start.20 = (bf16[32,1920]{1,0:T(8,128)(2,1)S(1)}, bf16[32,1920]{1,0:T(8,128)(2,1)S(1)}, u32[]{:S(2)}, u32[]{:S(2)}) collective-permute-start(bf16[32,1920]{1,0:T(8,128)(2,1)S(1)} %get-tuple-element.33), channel_id=1, source_target_pairs={{0,32},{16,48},{32,64},{48,80},{64,96},{80,112},{96,0},{112,16},{1... | collective-permute-start | bytes 368648 | tf_op jit(solution)/shard_map/ppermute | solution.py:262
  87.5 6.4 %collective-permute-start.21 = (bf16[32,1920]{1,0:T(8,128)(2,1)S(1)}, bf16[32,1920]{1,0:T(8,128)(2,1)S(1)}, u32[]{:S(2)}, u32[]{:S(2)}) collective-permute-start(bf16[32,1920]{1,0:T(8,128)(2,1)S(1)} %get-tuple-element.34), channel_id=1, source_target_pairs={{0,96},{16,112},{32,0},{48,16},{64,32},{80,48},{96,64},{112,80},{1... | collective-permute-start | bytes 368648 | tf_op jit(solution)/shard_map/ppermute | solution.py:263
  90.2 8.2 %collective-permute-start.18 = (bf16[64,1920]{1,0:T(8,128)(2,1)S(1)}, bf16[64,1920]{1,0:T(8,128)(2,1)S(1)}, u32[]{:S(2)}, u32[]{:S(2)}) collective-permute-start(bf16[64,1920]{1,0:T(8,128)(2,1)S(1)} %get-tuple-element.30), channel_id=1, source_target_pairs={{0,1},{1,2},{2,3},{3,0},{4,5},{5,6},{6,7},{7,4},{8,9},{9,10},{10,1... | collective-permute-start | bytes 737288 | tf_op jit(solution)/shard_map/ppermute | solution.py:260
  93.2 8.7 %collective-permute-start.19 = (bf16[64,1920]{1,0:T(8,128)(2,1)S(1)}, bf16[64,1920]{1,0:T(8,128)(2,1)S(1)}, u32[]{:S(2)}, u32[]{:S(2)}) collective-permute-start(bf16[64,1920]{1,0:T(8,128)(2,1)S(1)} %get-tuple-element.31), channel_id=1, source_target_pairs={{0,3},{1,0},{2,1},{3,2},{4,7},{5,4},{6,5},{7,6},{8,11},{9,8},{10,9... | collective-permute-start | bytes 737288 | tf_op jit(solution)/shard_map/ppermute | solution.py:261
  93.9 8.0 %collective-permute-start.23 = (bf16[64,1920]{1,0:T(8,128)(2,1)S(1)}, bf16[64,1920]{1,0:T(8,128)(2,1)S(1)}, u32[]{:S(2)}, u32[]{:S(2)}) collective-permute-start(bf16[64,1920]{1,0:T(8,128)(2,1)S(1)} %shard_map.61.near_far), channel_id=1, source_target_pairs={{0,16},{16,0},{32,48},{48,32},{64,80},{80,64},{96,112},{112,96},{1... | collective-permute-start | bytes 737288 | tf_op jit(solution)/shard_map/ppermute | solution.py:269

commit v3 on v2

--- a/solution.py
+++ b/solution.py
@@ -65,7 +65,7 @@
         one, two = at & 1, at >> 1
         return jnp.where(half == 0, (one << 1) | (one ^ two), at ^ two)
 
-    piece = col ^ (mask_of((out >> 6) & 3) + 4 * mask_of((out >> 4) & 3))
+    piece = ((out >> 4) & 3) * 4 + ((col & 3) ^ mask_of((out >> 6) & 3))
     pick = (src == piece * 32 + half * 16 + low).astype(F32).astype(BF16)
     ordered = lax.dot_general(
         pick, commands_ref[...], (((1,), (1,)), ((), ())), preferred_element_type=F32
@@ -89,33 +89,38 @@
     ).astype(BF16)
 
 
-def halves_kernel(left, right, flipped, low, high, same):
+def third_kernel(at_ref, kept_a, got_a, kept_b, got_b, residual, out_a, out_b):
+    own = pl.ds(pl.multiple_of((at_ref[1] >> 2) * 16, 16), 16)
+    for at, (kept, got, out) in enumerate(((kept_a, got_a, out_a), (kept_b, got_b, out_b))):
+        out[...] = (kept[...].astype(F32) + got[...].astype(F32)).astype(BF16)
+        extra = residual[at * 16 : at * 16 + 16].astype(F32)
+        out[own] = (kept[own].astype(F32) + got[own].astype(F32) + extra).astype(BF16)
+
+
+def slopes_kernel(
+    at_ref, kept_a, got_a, kept_b, got_b, row_mask, own, left, right, far, mine, turned
+):
+    z = at_ref[1] >> 2
+    across = row_mask[...]
+    for at, (kept, got) in enumerate(((kept_a, got_a), (kept_b, got_b))):
+        for by, frames in ((0, own), (3, left), (1, right), (2, far)):
+            first = pl.multiple_of(((z + by) & 3) * 16, 16)
+            part = pl.ds(first, 16)
+            total = kept[part].astype(F32) + got[part].astype(F32)
+            keep = frames[at * 16 : at * 16 + 16, :1]
+            mine[pl.ds(pl.multiple_of(first + at * 64, 16), 16)] = (total * across * keep).astype(
+                BF16
+            )
+    turned[...] = mine[pl.ds(pl.multiple_of((z & 1) * 64, 64), 64)]
+
+
+def halves_kernel(left, right, low, high):
     half = low.shape[0]
     low[...] = left[:half]
     high[...] = right[half:]
-    same[...] = flipped[...]
-
-
-def join_kernel(at_ref, own, left, right, far_a, far_b, flipped, pair, mine, near):
-    z = at_ref[1] >> 2
-
-    def put(by, start, ref):
-        first = pl.multiple_of(((z + by) & 3) * 32 + start, 16)
-        mine[pl.ds(first, ref.shape[0])] = ref[...]
-
-    put(0, 0, own)
-    put(3, 0, left)
-    put(1, 0, right)
-    put(2, 0, far_a)
-    put(2, 16, far_b)
-    z_lo = at_ref[0] >> 3
-    near[pl.ds(pl.multiple_of(z_lo * 32, 32), 32)] = flipped[...]
-    near[pl.ds(pl.multiple_of((1 - z_lo) * 32, 32), 32)] = pair[...]
-
-
-def split_kernel(y_left, y_right, near, x_left, x_right, y_low, y_high, x_low, x_high, joined):
-    y_low[...] = y_left[:64]
-    y_high[...] = y_right[64:]
+
+
+def split_kernel(near, x_left, x_right, x_low, x_high, joined):
     x_low[...] = x_left[:32]
     x_high[...] = x_right[32:]
     joined[:64] = near[...]
@@ -152,29 +157,37 @@
             far = jnp.concatenate([far_a[...], far_b[...]], axis=0)
             lhs[:, pl.ds(lane, 128)] = far.T
             x, core = (row >> 1) & 3, row & 1
-            for swap, most, rest in ((0, near, near_far), (1, other, other_far)):
+            for half, most, rest in ((core, near, near_far), (1 - core, other, other_far)):
                 for at, by in enumerate((0, 3, 1, 2)):
                     ref, at = (most, at) if at < 3 else (rest, 0)
                     y_from = (x + by - (col >> 1)) & 3
-                    for z_lo in range(2):
-                        z_from = z_lo * 2 + (core ^ swap)
-                        first = pl.multiple_of(y_from * 128 + z_from * 32, 32)
-                        rhs[pl.ds(first, 32)] = ref[at * 64 + z_lo * 32 : at * 64 + z_lo * 32 + 32]
+                    first = pl.multiple_of(y_from * 128 + half * 64, 64)
+                    rhs[pl.ds(first, 64)] = ref[at * 64 : at * 64 + 64]
 
         start = pl.multiple_of(pl.program_id(0) * rows, rows)
-        tile = jnp.dot(lhs[pl.ds(start, rows)], rhs[...], preferred_element_type=F32) * (
-            1.0 / FRAMES
-        )
-
-        @pl.when(row < col)
-        def _():
-            out[...] = tile.astype(BF16)
-
-        @pl.when(row == col)
-        def _():
-            down = lax.broadcasted_iota(jnp.int32, tile.shape, 0) + start
-            across = lax.broadcasted_iota(jnp.int32, tile.shape, 1)
-            out[...] = jnp.where(down <= across, tile, 0.0).astype(BF16)
+        for first in range(0, columns, 640):
+            span = slice(first, first + 640)
+
+            @pl.when(jnp.logical_or(row < col, start < first + 640))
+            def _():
+                tile = jnp.dot(
+                    lhs[pl.ds(start, rows)], rhs[:, span], preferred_element_type=F32
+                ) * (1.0 / FRAMES)
+                whole = jnp.logical_or(row < col, start + rows <= first)
+
+                @pl.when(whole)
+                def _():
+                    out[:, span] = tile.astype(BF16)
+
+                @pl.when(jnp.logical_not(whole))
+                def _():
+                    down = lax.broadcasted_iota(jnp.int32, tile.shape, 0) + start
+                    across = lax.broadcasted_iota(jnp.int32, tile.shape, 1) + first
+                    out[:, span] = jnp.where(down <= across, tile, 0.0).astype(BF16)
+
+            @pl.when(jnp.logical_not(jnp.logical_or(row < col, start < first + 640)))
+            def _():
+                out[:, span] = jnp.zeros((rows, 640), BF16)
 
     @pl.when(row > col)
     def _():
@@ -208,57 +221,64 @@
             flops=2 * 256 * width * rows, bytes_accessed=1600000, transcendentals=0
         ),
     )(ordered, turned)
-    for swap_a, swap_b in (
-        (y_swap(3), y_swap(1)),
-        (z_swap(1), z_swap(3)),
-        (z_swap(3), z_swap(1)),
-    ):
-        half = kept_a.shape[0] // 2
-        sent_a, sent_b = add(kept_a[half:], got_a[half:]), add(kept_b[half:], got_b[half:])
-        next_a = lax.ppermute(sent_a, "col", swap_a)
-        next_b = lax.ppermute(sent_b, "col", swap_b)
-        kept_a, kept_b = add(kept_a[:half], got_a[:half]), add(kept_b[:half], got_b[:half])
-        got_a, got_b = next_a, next_b
-    summed = jnp.concatenate([kept_a, kept_b]).astype(F32) + jnp.concatenate(
-        [got_a, got_b]
-    ).astype(F32)
-    row_mask = jnp.broadcast_to(slope_valid[:, None], (rows // SBLK, SBLK)).reshape(-1)
-    slopes = (
-        (residual.T.astype(F32) + summed)
-        * row_mask[None, :].astype(F32)
-        * frame_valid[:, None].astype(F32)
-    ).astype(BF16)
-
-    left = lax.ppermute(slopes, "col", z_turn(1))
-    right = lax.ppermute(slopes, "col", z_turn(-1))
-    flipped = lax.ppermute(slopes, ("row", "col"), flip_pairs())
-    low, high, flipped = call(
+    frames = jnp.broadcast_to(frame_valid[:, None], (32, 128)).astype(F32)
+    frames_left = lax.ppermute(frames, "col", z_turn(1))
+    frames_right = lax.ppermute(frames, "col", z_turn(-1))
+    frames_far = lax.ppermute(frames, "col", z_turn(2))
+    sent_a, sent_b = add(kept_a[64:], got_a[64:]), add(kept_b[64:], got_b[64:])
+    next_a = lax.ppermute(sent_a, "col", y_swap(3))
+    next_b = lax.ppermute(sent_b, "col", y_swap(1))
+    kept_a, kept_b = add(kept_a[:64], got_a[:64]), add(kept_b[:64], got_b[:64])
+    kept_a, kept_b = call(
+        third_kernel,
+        out_shape=(shape(64, rows),) * 2,
+        in_specs=[SCALAR] + [WHOLE] * 5,
+        out_specs=(WHOLE,) * 2,
+    )(at, kept_a, next_a, kept_b, next_b, residual.T)
+    got_a = lax.ppermute(kept_a, "col", z_swap(1))
+    got_b = lax.ppermute(kept_b, "col", z_swap(3))
+    kept_a, kept_b = add(kept_a, got_a), add(kept_b, got_b)
+    got_a = lax.ppermute(kept_a, "col", z_swap(3))
+    got_b = lax.ppermute(kept_b, "col", z_swap(1))
+    row_mask = jnp.broadcast_to(slope_valid[:, None], (rows // SBLK, SBLK)).reshape(1, rows)
+    mine, near = call(
+        slopes_kernel,
+        out_shape=(shape(128, rows), shape(64, rows)),
+        in_specs=[SCALAR] + [WHOLE] * 9,
+        out_specs=(WHOLE,) * 2,
+    )(
+        at,
+        kept_a,
+        got_a,
+        kept_b,
+        got_b,
+        row_mask.astype(F32),
+        frames,
+        frames_left,
+        frames_right,
+        frames_far,
+    )
+
+    left = lax.ppermute(mine, "col", y_turn(1))
+    right = lax.ppermute(mine, "col", y_turn(-1))
+    near = lax.ppermute(near, ("row", "col"), flip_pairs())
+    x_left = lax.ppermute(near, "row", x_turn(1))
+    x_right = lax.ppermute(near, "row", x_turn(-1))
+    low, high = call(
         halves_kernel,
-        out_shape=(shape(16, rows), shape(16, rows), shape(32, rows)),
+        out_shape=(shape(64, rows),) * 2,
+        in_specs=[WHOLE] * 2,
+        out_specs=(WHOLE,) * 2,
+        cost_estimate=pl.CostEstimate(flops=30000000000, bytes_accessed=983040, transcendentals=0),
+    )(left, right)
+    far_a = lax.ppermute(low, "col", y_turn(1))
+    far_b = lax.ppermute(high, "col", y_turn(-1))
+    x_low, x_high, near = call(
+        split_kernel,
+        out_shape=(shape(32, rows),) * 2 + (shape(192, rows),),
         in_specs=[WHOLE] * 3,
         out_specs=(WHOLE,) * 3,
-    )(left, right, flipped)
-    far_a = lax.ppermute(low, "col", z_turn(1))
-    far_b = lax.ppermute(high, "col", z_turn(-1))
-    pair = lax.ppermute(flipped, "row", [(r, r ^ 8) for r in range(16)])
-    mine, near = call(
-        join_kernel,
-        out_shape=(shape(128, rows), shape(64, rows)),
-        in_specs=[SCALAR] + [WHOLE] * 7,
-        out_specs=(WHOLE,) * 2,
-    )(at, slopes, left, right, far_a, far_b, flipped, pair)
-    left = lax.ppermute(mine, "col", y_turn(1))
-    right = lax.ppermute(mine, "col", y_turn(-1))
-    x_left = lax.ppermute(near, "row", x_turn(1))
-    x_right = lax.ppermute(near, "row", x_turn(-1))
-    low, high, x_low, x_high, near = call(
-        split_kernel,
-        out_shape=(shape(64, rows),) * 2 + (shape(32, rows),) * 2 + (shape(192, rows),),
-        in_specs=[WHOLE] * 5,
-        out_specs=(WHOLE,) * 5,
-    )(left, right, near, x_left, x_right)
-    far_a = lax.ppermute(low, "col", y_turn(1))
-    far_b = lax.ppermute(high, "col", y_turn(-1))
+    )(near, x_left, x_right)
     x_far_a = lax.ppermute(x_low, "row", x_turn(1))
     x_far_b = lax.ppermute(x_high, "row", x_turn(-1))
     cores = [(r, r ^ 1) for r in range(16)]
@@ -273,7 +293,7 @@
         in_specs=[WHOLE] * 3,
         out_specs=WHOLE,
     )(mine, left, right)
-    steps = 5
+    steps = 10
     return call(
         last_kernel,
         grid=(steps,),

time: 110 us -> 117 us (1.064)
  starting transfers between devices: 37.8 us -> 44.3 us
  waiting for transfers between devices: 57.4 us -> 51.5 us
  Pallas kernels: 11.7 us -> 17.5 us
    ppermute x12 -> x10, waiting for transfers between devices: 28.9 us -> 23.7 us  [the longest x1 7.66 us: per_device(): near = lax.ppermute(near, ('row', 'col'), flip_pairs())]
    pallas_call x1, Pallas kernels: 8.14 us -> 13.2 us  [per_device(): call(last_kernel, grid=(steps,), out_shape=shape(rows, rows), in_specs=[S...]
    ppermute x12 -> x10, starting transfers between devices: 24 us -> 28.1 us  [the longest x1 5.85 us: per_device(): got_a = lax.ppermute(kept_a, 'col', z_swap(3))]
    ppermute x1, starting transfers between devices: 1.35 us -> 4.05 us  [per_device(): x_right = lax.ppermute(near, 'row', x_turn(-1))]
    ppermute x1, waiting for transfers between devices: 1.64 us -> 3.97 us  [per_device(): x_left = lax.ppermute(near, 'row', x_turn(1))]
    ppermute x1, waiting for transfers between devices: 2.16 us -> 0.01 us  [per_device(): right = lax.ppermute(mine, 'col', y_turn(-1))]
    ppermute x1, waiting for transfers between devices: 5.09 us -> 3.82 us  [per_device(): x_right = lax.ppermute(near, 'row', x_turn(-1))]
    unnamed x12 -> x14, local copies, waits for them, and re-layouts: 2.28 us -> 2.36 us
  transfers between devices with their start and end apart: 24 -> 22, of which waited for: 16 -> 11; matrix products, arithmetic and copies ran while one was open for 0% -> 0% of each run, Pallas kernels for 1% -> 1%
where the time goes in v3:
time: 117 us; the launch traced here: 116 us
  waiting for transfers between devices  51.5 us (44%)
  starting transfers between devices  44.3 us (38%)
  Pallas kernels  17.5 us (15%)
  local copies, waits for them, and re-layouts  2.44 us (2%)
    pallas_call x1, Pallas kernels, per_device(): call(last_kernel, grid=(steps,), out_shape=shape(rows, rows), in_specs=[S...  13.2 us
    ppermute x1, waiting for transfers between devices, per_device(): got_b = lax.ppermute(sent_b, 'col', y_swap(3))  11.5 us
    ppermute x1, waiting for transfers between devices, per_device(): near = lax.ppermute(near, ('row', 'col'), flip_pairs())  7.66 us
    ppermute x1, starting transfers between devices, per_device(): got_a = lax.ppermute(kept_a, 'col', z_swap(3))  5.85 us
    ppermute x1, waiting for transfers between devices, per_device(): far_a = lax.ppermute(low, 'col', y_turn(1))  5.09 us
    ppermute x1, waiting for transfers between devices, per_device(): got_a = lax.ppermute(kept_a, 'col', z_swap(1))  5.05 us
    ppermute x1, waiting for transfers between devices, per_device(): next_b = lax.ppermute(sent_b, 'col', y_swap(1))  4.68 us
    ppermute x1, waiting for transfers between devices, per_device(): frames_far = lax.ppermute(frames, 'col', z_turn(2))  4.55 us
  transfers between devices with their start and end apart: 22, of which 11 were waited for; matrix products, arithmetic and copies ran while one was open for 0% of the time, Pallas kernels for 1%

profile of v3, /device:TPU:24, one launch (start us, length us, event | category | flops | bytes accessed | tf_op | source)
XLA Modules:
  0.0 116.4 jit_solution(3575369812744404681)
XLA Ops:
  0.1 1.3 %copy-done = bf16[1920,320]{0,1:T(8,128)(2,1)S(1)} copy-done((bf16[1920,320]{0,1:T(8,128)(2,1)S(1)}, bf16[1920,320]{0,1:T(8,128)(2,1)}, u32[]{:S(2)}) %copy-start) | copy-done | bytes 1228824
  1.4 1.0 copy-done.2
  2.3 1.6 %shard_map.55 = (bf16[128,1920]{1,0:T(8,128)(2,1)S(1)}, bf16[128,1920]{1,0:T(8,128)(2,1)S(1)}, bf16[256,320]{1,0:T(8,128)(2,1)S(1)}) custom-call(s32[2]{0:T(128)S(1)} %pad_add_fusion.at_ref, bf16[320,512]{1,0:T(8,128)(2,1)S(1)} %copy-done.2, bf16[320,1920]{1,0:T(8,128)(2,1)S(1)} %bitcast.10), custom_call_target="tpu_custom_call" | custom-call | flops 314572800 | bytes 1600000 | tf_op jit(solution)/shard_map/pallas_call | solution.py:204
  4.0 2.0 %collective-permute-start.2 = (bf16[128,1920]{1,0:T(8,128)(2,1)S(1)}, bf16[128,1920]{1,0:T(8,128)(2,1)S(1)}, u32[]{:S(2)}, u32[]{:S(2)}) collective-permute-start(bf16[128,1920]{1,0:T(8,128)(2,1)S(1)} %get-tuple-element.23), channel_id=1, source_target_pairs={{0,3},{1,2},{2,1},{3,0},{4,7},{5,6},{6,5},{7,4},{8,11},{9,10},{10,... | collective-permute-start | bytes 1474568 | tf_op jit(solution)/shard_map/ppermute | solution.py:214
  6.0 0.7 shard_map.56
  6.7 11.5 %collective-permute-done.2 = bf16[128,1920]{1,0:T(8,128)(2,1)S(1)} collective-permute-done((bf16[128,1920]{1,0:T(8,128)(2,1)S(1)}, bf16[128,1920]{1,0:T(8,128)(2,1)S(1)}, u32[]{:S(2)}, u32[]{:S(2)}) %collective-permute-start.2) | collective-permute-done | bytes 491552 | tf_op jit(solution)/shard_map/ppermute | solution.py:214
  18.6 2.0 %collective-permute-start.1 = (bf16[64,1920]{1,0:T(8,128)(2,1)S(1)}, bf16[64,1920]{1,0:T(8,128)(2,1)S(1)}, u32[]{:S(2)}, u32[]{:S(2)}) collective-permute-start(bf16[64,1920]{1,0:T(8,128)(2,1)S(1)} %get-tuple-element.35), channel_id=1, source_target_pairs={{0,3},{1,2},{2,1},{3,0},{4,7},{5,6},{6,5},{7,4},{8,11},{9,10},{10,... | collective-permute-start | bytes 737288 | tf_op jit(solution)/shard_map/ppermute | solution.py:229
  20.6 4.7 %collective-permute-done.3.got_b = bf16[64,1920]{1,0:T(8,128)(2,1)S(1)} collective-permute-done((bf16[64,1920]{1,0:T(8,128)(2,1)S(1)}, bf16[64,1920]{1,0:T(8,128)(2,1)S(1)}, u32[]{:S(2)}, u32[]{:S(2)}) %collective-permute-start.3) | collective-permute-done | bytes 245792 | tf_op jit(solution)/shard_map/ppermute | solution.py:230
  25.3 1.5 %collective-permute-done.1.got_a = bf16[64,1920]{1,0:T(8,128)(2,1)S(1)} collective-permute-done((bf16[64,1920]{1,0:T(8,128)(2,1)S(1)}, bf16[64,1920]{1,0:T(8,128)(2,1)S(1)}, u32[]{:S(2)}, u32[]{:S(2)}) %collective-permute-start.1) | collective-permute-done | bytes 245792 | tf_op jit(solution)/shard_map/ppermute | solution.py:229
  26.7 0.7 shard_map.57
  27.5 3.4 %collective-permute-start.4 = (bf16[64,1920]{1,0:T(8,128)(2,1)S(1)}, bf16[64,1920]{1,0:T(8,128)(2,1)S(1)}, u32[]{:S(2)}, u32[]{:S(2)}) collective-permute-start(bf16[64,1920]{1,0:T(8,128)(2,1)S(1)} %get-tuple-element.24), channel_id=1, source_target_pairs={{0,4},{1,5},{2,6},{3,7},{4,0},{5,1},{6,2},{7,3},{8,12},{9,13},{10,... | collective-permute-start | bytes 737288 | tf_op jit(solution)/shard_map/ppermute | solution.py:238
  30.8 4.5 %collective-permute-start.6 = (bf16[64,1920]{1,0:T(8,128)(2,1)S(1)}, bf16[64,1920]{1,0:T(8,128)(2,1)S(1)}, u32[]{:S(2)}, u32[]{:S(2)}) collective-permute-start(bf16[64,1920]{1,0:T(8,128)(2,1)S(1)} %get-tuple-element.25), channel_id=1, source_target_pairs={{0,12},{1,13},{2,14},{3,15},{4,8},{5,9},{6,10},{7,11},{8,4},{9,5},... | collective-permute-start | bytes 737288 | tf_op jit(solution)/shard_map/ppermute | solution.py:239
  35.3 5.1 %collective-permute-done.4 = bf16[64,1920]{1,0:T(8,128)(2,1)S(1)} collective-permute-done((bf16[64,1920]{1,0:T(8,128)(2,1)S(1)}, bf16[64,1920]{1,0:T(8,128)(2,1)S(1)}, u32[]{:S(2)}, u32[]{:S(2)}) %collective-permute-start.4) | collective-permute-done | bytes 245792 | tf_op jit(solution)/shard_map/ppermute | solution.py:238
  40.4 5.9 %collective-permute-start.5 = (bf16[64,1920]{1,0:T(8,128)(2,1)S(1)}, bf16[64,1920]{1,0:T(8,128)(2,1)S(1)}, u32[]{:S(2)}, u32[]{:S(2)}) collective-permute-start(bf16[64,1920]{1,0:T(8,128)(2,1)S(1)} %add_convert_fusion.1.kept_a), channel_id=1, source_target_pairs={{0,12},{1,13},{2,14},{3,15},{4,8},{5,9},{6,10},{7,11},{8,4},{9,5},... | collective-permute-start | bytes 737288 | tf_op jit(solution)/shard_map/ppermute | solution.py:241
  46.3 1.3 %collective-permute-start.7 = (bf16[64,1920]{1,0:T(8,128)(2,1)S(1)}, bf16[64,1920]{1,0:T(8,128)(2,1)S(1)}, u32[]{:S(2)}, u32[]{:S(2)}) collective-permute-start(bf16[64,1920]{1,0:T(8,128)(2,1)S(1)} %add_convert_fusion.kept_b), channel_id=1, source_target_pairs={{0,4},{1,5},{2,6},{3,7},{4,0},{5,1},{6,2},{7,3},{8,12},{9,13},{10,... | collective-permute-start | bytes 737288 | tf_op jit(solution)/shard_map/ppermute | solution.py:242
  47.7 3.8 %collective-permute-start.10 = (f32[32,128]{1,0:T(8,128)S(1)}, f32[32,128]{1,0:T(8,128)S(1)}, u32[]{:S(2)}, u32[]{:S(2)}) collective-permute-start(f32[32,128]{1,0:T(8,128)S(1)} %broadcast_in_dim.5.own), channel_id=1, source_target_pairs={{0,8},{1,9},{2,10},{3,11},{4,12},{5,13},{6,14},{7,15},{8,0},{9,1},... | collective-permute-start | bytes 49160 | tf_op jit(solution)/shard_map/ppermute | solution.py:227
  51.5 1.5 %collective-permute-start.9 = (f32[32,128]{1,0:T(8,128)S(1)}, f32[32,128]{1,0:T(8,128)S(1)}, u32[]{:S(2)}, u32[]{:S(2)}) collective-permute-start(f32[32,128]{1,0:T(8,128)S(1)} %broadcast_in_dim.5.own), channel_id=1, source_target_pairs={{0,12},{1,13},{2,14},{3,15},{4,0},{5,1},{6,2},{7,3},{8,4},{9,5},{1... | collective-permute-start | bytes 49160 | tf_op jit(solution)/shard_map/ppermute | solution.py:226
  53.0 1.5 %collective-permute-start.8 = (f32[32,128]{1,0:T(8,128)S(1)}, f32[32,128]{1,0:T(8,128)S(1)}, u32[]{:S(2)}, u32[]{:S(2)}) collective-permute-start(f32[32,128]{1,0:T(8,128)S(1)} %broadcast_in_dim.5.own), channel_id=1, source_target_pairs={{0,4},{1,5},{2,6},{3,7},{4,8},{5,9},{6,10},{7,11},{8,12},{9,13},{1... | collective-permute-start | bytes 49160 | tf_op jit(solution)/shard_map/ppermute | solution.py:225
  54.6 4.6 %collective-permute-done.10.far = f32[32,128]{1,0:T(8,128)S(1)} collective-permute-done((f32[32,128]{1,0:T(8,128)S(1)}, f32[32,128]{1,0:T(8,128)S(1)}, u32[]{:S(2)}, u32[]{:S(2)}) %collective-permute-start.10) | collective-permute-done | bytes 16416 | tf_op jit(solution)/shard_map/ppermute | solution.py:227
  59.4 0.7 shard_map.58
  60.1 4.3 %collective-permute-start.15 = (bf16[64,1920]{1,0:T(8,128)(2,1)S(1)}, bf16[64,1920]{1,0:T(8,128)(2,1)S(1)}, u32[]{:S(2)}, u32[]{:S(2)}) collective-permute-start(bf16[64,1920]{1,0:T(8,128)(2,1)S(1)} %get-tuple-element.29), channel_id=1, source_target_pairs={{0,0},{1,32},{2,64},{3,96},{4,16},{5,48},{6,80},{7,112},{8,128},{9... | collective-permute-start | bytes 737288 | tf_op jit(solution)/shard_map/ppermute | solution.py:264
  64.4 1.2 %collective-permute-start.12 = (bf16[128,1920]{1,0:T(8,128)(2,1)S(1)}, bf16[128,1920]{1,0:T(8,128)(2,1)S(1)}, u32[]{:S(2)}, u32[]{:S(2)}) collective-permute-start(bf16[128,1920]{1,0:T(8,128)(2,1)S(1)} %get-tuple-element.26.own), channel_id=1, source_target_pairs={{0,3},{1,0},{2,1},{3,2},{4,7},{5,4},{6,5},{7,6},{8,11},{9,8},{10,9... | collective-permute-start | bytes 1474568 | tf_op jit(solution)/shard_map/ppermute | solution.py:263
  65.6 2.1 %collective-permute-start.11 = (bf16[128,1920]{1,0:T(8,128)(2,1)S(1)}, bf16[128,1920]{1,0:T(8,128)(2,1)S(1)}, u32[]{:S(2)}, u32[]{:S(2)}) collective-permute-start(bf16[128,1920]{1,0:T(8,128)(2,1)S(1)} %get-tuple-element.26.own), channel_id=1, source_target_pairs={{0,1},{1,2},{2,3},{3,0},{4,5},{5,6},{6,7},{7,4},{8,9},{9,10},{10,1... | collective-permute-start | bytes 1474568 | tf_op jit(solution)/shard_map/ppermute | solution.py:262
  67.7 7.7 %collective-permute-done.15.near = bf16[64,1920]{1,0:T(8,128)(2,1)S(1)} collective-permute-done((bf16[64,1920]{1,0:T(8,128)(2,1)S(1)}, bf16[64,1920]{1,0:T(8,128)(2,1)S(1)}, u32[]{:S(2)}, u32[]{:S(2)}) %collective-permute-start.15) | collective-permute-done | bytes 245792 | tf_op jit(solution)/shard_map/ppermute | solution.py:264
  75.4 4.1 %collective-permute-start.17 = (bf16[64,1920]{1,0:T(8,128)(2,1)S(1)}, bf16[64,1920]{1,0:T(8,128)(2,1)S(1)}, u32[]{:S(2)}, u32[]{:S(2)}) collective-permute-start(bf16[64,1920]{1,0:T(8,128)(2,1)S(1)} %collective-permute-done.15.near), channel_id=1, source_target_pairs={{0,96},{16,112},{32,0},{48,16},{64,32},{80,48},{96,64},{112,80},{1... | collective-permute-start | bytes 737288 | tf_op jit(solution)/shard_map/ppermute | solution.py:266
  79.4 3.8 %collective-permute-done.17.x_right = bf16[64,1920]{1,0:T(8,128)(2,1)S(1)} collective-permute-done((bf16[64,1920]{1,0:T(8,128)(2,1)S(1)}, bf16[64,1920]{1,0:T(8,128)(2,1)S(1)}, u32[]{:S(2)}, u32[]{:S(2)}) %collective-permute-start.17) | collective-permute-done | bytes 245792 | tf_op jit(solution)/shard_map/ppermute | solution.py:266
  83.3 4.0 %collective-permute-done.16.x_left = bf16[64,1920]{1,0:T(8,128)(2,1)S(1)} collective-permute-done((bf16[64,1920]{1,0:T(8,128)(2,1)S(1)}, bf16[64,1920]{1,0:T(8,128)(2,1)S(1)}, u32[]{:S(2)}, u32[]{:S(2)}) %collective-permute-start.16) | collective-permute-done | bytes 245792 | tf_op jit(solution)/shard_map/ppermute | solution.py:265
  87.4 3.2 %collective-permute-start.19 = (bf16[32,1920]{1,0:T(8,128)(2,1)S(1)}, bf16[32,1920]{1,0:T(8,128)(2,1)S(1)}, u32[]{:S(2)}, u32[]{:S(2)}) collective-permute-start(bf16[32,1920]{1,0:T(8,128)(2,1)S(1)} %get-tuple-element.32), channel_id=1, source_target_pairs={{0,96},{16,112},{32,0},{48,16},{64,32},{80,48},{96,64},{112,80},{1... | collective-permute-start | bytes 368648 | tf_op jit(solution)/shard_map/ppermute | solution.py:283
  90.7 3.2 %collective-permute-start.13 = (bf16[64,1920]{1,0:T(8,128)(2,1)S(1)}, bf16[64,1920]{1,0:T(8,128)(2,1)S(1)}, u32[]{:S(2)}, u32[]{:S(2)}) collective-permute-start(bf16[64,1920]{1,0:T(8,128)(2,1)S(1)} %get-tuple-element.27), channel_id=1, source_target_pairs={{0,1},{1,2},{2,3},{3,0},{4,5},{5,6},{6,7},{7,4},{8,9},{9,10},{10,1... | collective-permute-start | bytes 737288 | tf_op jit(solution)/shard_map/ppermute | solution.py:274
  94.7 5.1 %collective-permute-done.13.far_a = bf16[64,1920]{1,0:T(8,128)(2,1)S(1)} collective-permute-done((bf16[64,1920]{1,0:T(8,128)(2,1)S(1)}, bf16[64,1920]{1,0:T(8,128)(2,1)S(1)}, u32[]{:S(2)}, u32[]{:S(2)}) %collective-permute-start.13) | collective-permute-done | bytes 245792 | tf_op jit(solution)/shard_map/ppermute | solution.py:274
  99.8 3.4 %collective-permute-done.14.far_b = bf16[64,1920]{1,0:T(8,128)(2,1)S(1)} collective-permute-done((bf16[64,1920]{1,0:T(8,128)(2,1)S(1)}, bf16[64,1920]{1,0:T(8,128)(2,1)S(1)}, u32[]{:S(2)}, u32[]{:S(2)}) %collective-permute-start.14) | collective-permute-done | bytes 245792 | tf_op jit(solution)/shard_map/ppermute | solution.py:275
  103.2 13.2 %shard_map.63 = bf16[1920,1920]{1,0:T(8,128)(2,1)} custom-call(s32[2]{0:T(128)S(1)} %pad_add_fusion.at_ref, bf16[1920,384]{1,0:T(8,128)(2,1)S(1)} %shard_map.59.early, bf16[64,1920]{1,0:T(8,128)(2,1)S(1)} %collective-permute-done.13.far_a, bf16[64,1920]{1,0:T(8,128)(2,1)S(1)} %collective-permute-done.14.far_b, bf16[192,1920]{1,0:T(8,128)(2,1)S(1)} %get-tuple-element.30.near, ...), custom_call_target="tpu_custom_call" | custom-call | flops 3774873600 | bytes 7372800 | tf_op jit(solution)/shard_map/pallas_call | solution.py:297
  (43 shorter events, 2.0 us)
Async XLA Ops:
  0.1 1.3 %copy-start = (bf16[1920,320]{0,1:T(8,128)(2,1)S(1)}, bf16[1920,320]{0,1:T(8,128)(2,1)}, u32[]{:S(2)}) copy-start(bf16[1920,320]{0,1:T(8,128)(2,1)} %param.6) | copy-start | bytes 3686404
  1.4 1.0 copy-start.2
  2.3 3.7 %copy-start.1 = (bf16[1920,320]{0,1:T(8,128)(2,1)S(1)}, bf16[1920,320]{0,1:T(8,128)(2,1)}, u32[]{:S(2)}) copy-start(bf16[1920,320]{0,1:T(8,128)(2,1)} %param.6) | copy-start | bytes 3686404
  4.0 14.3 %collective-permute-start.2 = (bf16[128,1920]{1,0:T(8,128)(2,1)S(1)}, bf16[128,1920]{1,0:T(8,128)(2,1)S(1)}, u32[]{:S(2)}, u32[]{:S(2)}) collective-permute-start(bf16[128,1920]{1,0:T(8,128)(2,1)S(1)} %get-tuple-element.23), channel_id=1, source_target_pairs={{0,3},{1,2},{2,1},{3,0},{4,7},{5,6},{6,5},{7,4},{8,11},{9,10},{10,... | collective-permute-start | bytes 1474568 | tf_op jit(solution)/shard_map/ppermute | solution.py:214
  6.0 12.4 %collective-permute-start = (bf16[128,1920]{1,0:T(8,128)(2,1)S(1)}, bf16[128,1920]{1,0:T(8,128)(2,1)S(1)}, u32[]{:S(2)}, u32[]{:S(2)}) collective-permute-start(bf16[128,1920]{1,0:T(8,128)(2,1)S(1)} %get-tuple-element.21), channel_id=1, source_target_pairs={{0,1},{1,0},{2,3},{3,2},{4,5},{5,4},{6,7},{7,6},{8,9},{9,8},{10,11... | collective-permute-start | bytes 1474568 | tf_op jit(solution)/shard_map/ppermute | solution.py:213
  18.2 8.5 %copy-start.3 = (bf16[1920,32]{0,1:T(8,128)(2,1)S(1)}, bf16[1920,32]{0,1:T(8,128)(2,1)}, u32[]{:S(2)}) copy-start(bf16[1920,32]{0,1:T(8,128)(2,1)} %param.5) | copy-start | bytes 368644
  18.4 6.9 %collective-permute-start.3 = (bf16[64,1920]{1,0:T(8,128)(2,1)S(1)}, bf16[64,1920]{1,0:T(8,128)(2,1)S(1)}, u32[]{:S(2)}, u32[]{:S(2)}) collective-permute-start(bf16[64,1920]{1,0:T(8,128)(2,1)S(1)} %get-tuple-element.33), channel_id=1, source_target_pairs={{0,1},{1,0},{2,3},{3,2},{4,5},{5,4},{6,7},{7,6},{8,9},{9,8},{10,11... | collective-permute-start | bytes 737288 | tf_op jit(solution)/shard_map/ppermute | solution.py:230
  18.6 29.1 %copy-start.4 = (s32[32]{0:T(128)S(1)}, s32[32]{0:T(128)}, u32[]{:S(2)}) copy-start(s32[32]{0:T(128)} %param.9) | copy-start | bytes 388
  18.6 35.9 %copy-start.5 = (s32[15]{0:T(128)S(1)}, s32[15]{0:T(128)}, u32[]{:S(2)}) copy-start(s32[15]{0:T(128)} %param.8) | copy-start | bytes 184
  18.6 8.1 %collective-permute-start.1 = (bf16[64,1920]{1,0:T(8,128)(2,1)S(1)}, bf16[64,1920]{1,0:T(8,128)(2,1)S(1)}, u32[]{:S(2)}, u32[]{:S(2)}) collective-permute-start(bf16[64,1920]{1,0:T(8,128)(2,1)S(1)} %get-tuple-element.35), channel_id=1, source_target_pairs={{0,3},{1,2},{2,1},{3,0},{4,7},{5,6},{6,5},{7,4},{8,11},{9,10},{10,... | collective-permute-start | bytes 737288 | tf_op jit(solution)/shard_map/ppermute | solution.py:229
  27.5 12.9 %collective-permute-start.4 = (bf16[64,1920]{1,0:T(8,128)(2,1)S(1)}, bf16[64,1920]{1,0:T(8,128)(2,1)S(1)}, u32[]{:S(2)}, u32[]{:S(2)}) collective-permute-start(bf16[64,1920]{1,0:T(8,128)(2,1)S(1)} %get-tuple-element.24), channel_id=1, source_target_pairs={{0,4},{1,5},{2,6},{3,7},{4,0},{5,1},{6,2},{7,3},{8,12},{9,13},{10,... | collective-permute-start | bytes 737288 | tf_op jit(solution)/shard_map/ppermute | solution.py:238
  30.8 15.5 %collective-permute-start.6 = (bf16[64,1920]{1,0:T(8,128)(2,1)S(1)}, bf16[64,1920]{1,0:T(8,128)(2,1)S(1)}, u32[]{:S(2)}, u32[]{:S(2)}) collective-permute-start(bf16[64,1920]{1,0:T(8,128)(2,1)S(1)} %get-tuple-element.25), channel_id=1, source_target_pairs={{0,12},{1,13},{2,14},{3,15},{4,8},{5,9},{6,10},{7,11},{8,4},{9,5},... | collective-permute-start | bytes 737288 | tf_op jit(solution)/shard_map/ppermute | solution.py:239
  40.4 19.0 %collective-permute-start.5 = (bf16[64,1920]{1,0:T(8,128)(2,1)S(1)}, bf16[64,1920]{1,0:T(8,128)(2,1)S(1)}, u32[]{:S(2)}, u32[]{:S(2)}) collective-permute-start(bf16[64,1920]{1,0:T(8,128)(2,1)S(1)} %add_convert_fusion.1.kept_a), channel_id=1, source_target_pairs={{0,12},{1,13},{2,14},{3,15},{4,8},{5,9},{6,10},{7,11},{8,4},{9,5},... | collective-permute-start | bytes 737288 | tf_op jit(solution)/shard_map/ppermute | solution.py:241
  46.3 13.0 %collective-permute-start.7 = (bf16[64,1920]{1,0:T(8,128)(2,1)S(1)}, bf16[64,1920]{1,0:T(8,128)(2,1)S(1)}, u32[]{:S(2)}, u32[]{:S(2)}) collective-permute-start(bf16[64,1920]{1,0:T(8,128)(2,1)S(1)} %add_convert_fusion.kept_b), channel_id=1, source_target_pairs={{0,4},{1,5},{2,6},{3,7},{4,0},{5,1},{6,2},{7,3},{8,12},{9,13},{10,... | collective-permute-start | bytes 737288 | tf_op jit(solution)/shard_map/ppermute | solution.py:242
  47.7 11.4 %collective-permute-start.10 = (f32[32,128]{1,0:T(8,128)S(1)}, f32[32,128]{1,0:T(8,128)S(1)}, u32[]{:S(2)}, u32[]{:S(2)}) collective-permute-start(f32[32,128]{1,0:T(8,128)S(1)} %broadcast_in_dim.5.own), channel_id=1, source_target_pairs={{0,8},{1,9},{2,10},{3,11},{4,12},{5,13},{6,14},{7,15},{8,0},{9,1},... | collective-permute-start | bytes 49160 | tf_op jit(solution)/shard_map/ppermute | solution.py:227
  51.5 7.8 %collective-permute-start.9 = (f32[32,128]{1,0:T(8,128)S(1)}, f32[32,128]{1,0:T(8,128)S(1)}, u32[]{:S(2)}, u32[]{:S(2)}) collective-permute-start(f32[32,128]{1,0:T(8,128)S(1)} %broadcast_in_dim.5.own), channel_id=1, source_target_pairs={{0,12},{1,13},{2,14},{3,15},{4,0},{5,1},{6,2},{7,3},{8,4},{9,5},{1... | collective-permute-start | bytes 49160 | tf_op jit(solution)/shard_map/ppermute | solution.py:226
  53.0 6.4 %collective-permute-start.8 = (f32[32,128]{1,0:T(8,128)S(1)}, f32[32,128]{1,0:T(8,128)S(1)}, u32[]{:S(2)}, u32[]{:S(2)}) collective-permute-start(f32[32,128]{1,0:T(8,128)S(1)} %broadcast_in_dim.5.own), channel_id=1, source_target_pairs={{0,4},{1,5},{2,6},{3,7},{4,8},{5,9},{6,10},{7,11},{8,12},{9,13},{1... | collective-permute-start | bytes 49160 | tf_op jit(solution)/shard_map/ppermute | solution.py:225
  60.1 15.3 %collective-permute-start.15 = (bf16[64,1920]{1,0:T(8,128)(2,1)S(1)}, bf16[64,1920]{1,0:T(8,128)(2,1)S(1)}, u32[]{:S(2)}, u32[]{:S(2)}) collective-permute-start(bf16[64,1920]{1,0:T(8,128)(2,1)S(1)} %get-tuple-element.29), channel_id=1, source_target_pairs={{0,0},{1,32},{2,64},{3,96},{4,16},{5,48},{6,80},{7,112},{8,128},{9... | collective-permute-start | bytes 737288 | tf_op jit(solution)/shard_map/ppermute | solution.py:264
  64.4 26.2 %collective-permute-start.12 = (bf16[128,1920]{1,0:T(8,128)(2,1)S(1)}, bf16[128,1920]{1,0:T(8,128)(2,1)S(1)}, u32[]{:S(2)}, u32[]{:S(2)}) collective-permute-start(bf16[128,1920]{1,0:T(8,128)(2,1)S(1)} %get-tuple-element.26.own), channel_id=1, source_target_pairs={{0,3},{1,0},{2,1},{3,2},{4,7},{5,4},{6,5},{7,6},{8,11},{9,8},{10,9... | collective-permute-start | bytes 1474568 | tf_op jit(solution)/shard_map/ppermute | solution.py:263
  65.6 25.0 %collective-permute-start.11 = (bf16[128,1920]{1,0:T(8,128)(2,1)S(1)}, bf16[128,1920]{1,0:T(8,128)(2,1)S(1)}, u32[]{:S(2)}, u32[]{:S(2)}) collective-permute-start(bf16[128,1920]{1,0:T(8,128)(2,1)S(1)} %get-tuple-element.26.own), channel_id=1, source_target_pairs={{0,1},{1,2},{2,3},{3,0},{4,5},{5,6},{6,7},{7,4},{8,9},{9,10},{10,1... | collective-permute-start | bytes 1474568 | tf_op jit(solution)/shard_map/ppermute | solution.py:262
  75.4 7.9 %collective-permute-start.17 = (bf16[64,1920]{1,0:T(8,128)(2,1)S(1)}, bf16[64,1920]{1,0:T(8,128)(2,1)S(1)}, u32[]{:S(2)}, u32[]{:S(2)}) collective-permute-start(bf16[64,1920]{1,0:T(8,128)(2,1)S(1)} %collective-permute-done.15.near), channel_id=1, source_target_pairs={{0,96},{16,112},{32,0},{48,16},{64,32},{80,48},{96,64},{112,80},{1... | collective-permute-start | bytes 737288 | tf_op jit(solution)/shard_map/ppermute | solution.py:266
  79.4 7.8 %collective-permute-start.16 = (bf16[64,1920]{1,0:T(8,128)(2,1)S(1)}, bf16[64,1920]{1,0:T(8,128)(2,1)S(1)}, u32[]{:S(2)}, u32[]{:S(2)}) collective-permute-start(bf16[64,1920]{1,0:T(8,128)(2,1)S(1)} %collective-permute-done.15.near), channel_id=1, source_target_pairs={{0,32},{16,48},{32,64},{48,80},{64,96},{80,112},{96,0},{112,16},{1... | collective-permute-start | bytes 737288 | tf_op jit(solution)/shard_map/ppermute | solution.py:265
  87.3 6.6 %collective-permute-start.18 = (bf16[32,1920]{1,0:T(8,128)(2,1)S(1)}, bf16[32,1920]{1,0:T(8,128)(2,1)S(1)}, u32[]{:S(2)}, u32[]{:S(2)}) collective-permute-start(bf16[32,1920]{1,0:T(8,128)(2,1)S(1)} %get-tuple-element.31), channel_id=1, source_target_pairs={{0,32},{16,48},{32,64},{48,80},{64,96},{80,112},{96,0},{112,16},{1... | collective-permute-start | bytes 368648 | tf_op jit(solution)/shard_map/ppermute | solution.py:282
  87.4 6.5 %collective-permute-start.19 = (bf16[32,1920]{1,0:T(8,128)(2,1)S(1)}, bf16[32,1920]{1,0:T(8,128)(2,1)S(1)}, u32[]{:S(2)}, u32[]{:S(2)}) collective-permute-start(bf16[32,1920]{1,0:T(8,128)(2,1)S(1)} %get-tuple-element.32), channel_id=1, source_target_pairs={{0,96},{16,112},{32,0},{48,16},{64,32},{80,48},{96,64},{112,80},{1... | collective-permute-start | bytes 368648 | tf_op jit(solution)/shard_map/ppermute | solution.py:283
  90.6 12.6 %collective-permute-start.20 = (bf16[192,1920]{1,0:T(8,128)(2,1)S(1)}, bf16[192,1920]{1,0:T(8,128)(2,1)S(1)}, u32[]{:S(2)}, u32[]{:S(2)}) collective-permute-start(bf16[192,1920]{1,0:T(8,128)(2,1)S(1)} %get-tuple-element.30.near), channel_id=1, source_target_pairs={{0,16},{16,0},{32,48},{48,32},{64,80},{80,64},{96,112},{112,96},{1... | collective-permute-start | bytes 2211848 | tf_op jit(solution)/shard_map/ppermute | solution.py:285
  90.7 9.1 %collective-permute-start.13 = (bf16[64,1920]{1,0:T(8,128)(2,1)S(1)}, bf16[64,1920]{1,0:T(8,128)(2,1)S(1)}, u32[]{:S(2)}, u32[]{:S(2)}) collective-permute-start(bf16[64,1920]{1,0:T(8,128)(2,1)S(1)} %get-tuple-element.27), channel_id=1, source_target_pairs={{0,1},{1,2},{2,3},{3,0},{4,5},{5,6},{6,7},{7,4},{8,9},{9,10},{10,1... | collective-permute-start | bytes 737288 | tf_op jit(solution)/shard_map/ppermute | solution.py:274
  93.9 9.3 %collective-permute-start.14 = (bf16[64,1920]{1,0:T(8,128)(2,1)S(1)}, bf16[64,1920]{1,0:T(8,128)(2,1)S(1)}, u32[]{:S(2)}, u32[]{:S(2)}) collective-permute-start(bf16[64,1920]{1,0:T(8,128)(2,1)S(1)} %get-tuple-element.28), channel_id=1, source_target_pairs={{0,3},{1,0},{2,1},{3,2},{4,7},{5,4},{6,5},{7,6},{8,11},{9,8},{10,9... | collective-permute-start | bytes 737288 | tf_op jit(solution)/shard_map/ppermute | solution.py:275
  93.9 9.3 %collective-permute-start.21 = (bf16[64,1920]{1,0:T(8,128)(2,1)S(1)}, bf16[64,1920]{1,0:T(8,128)(2,1)S(1)}, u32[]{:S(2)}, u32[]{:S(2)}) collective-permute-start(bf16[64,1920]{1,0:T(8,128)(2,1)S(1)} %shard_map.62.near_far), channel_id=1, source_target_pairs={{0,16},{16,0},{32,48},{48,32},{64,80},{80,64},{96,112},{112,96},{1... | collective-permute-start | bytes 737288 | tf_op jit(solution)/shard_map/ppermute | solution.py:289

commit v4 on v2

--- a/solution.py
+++ b/solution.py
@@ -89,14 +89,13 @@
     ).astype(BF16)
 
 
-def halves_kernel(left, right, flipped, low, high, same):
+def halves_kernel(left, right, low, high):
     half = low.shape[0]
     low[...] = left[:half]
     high[...] = right[half:]
-    same[...] = flipped[...]
-
-
-def join_kernel(at_ref, own, left, right, far_a, far_b, flipped, pair, mine, near):
+
+
+def z_join_kernel(at_ref, own, left, right, far_a, far_b, mine):
     z = at_ref[1] >> 2
 
     def put(by, start, ref):
@@ -108,14 +107,15 @@
     put(1, 0, right)
     put(2, 0, far_a)
     put(2, 16, far_b)
+
+
+def pair_join_kernel(at_ref, flipped, pair, near):
     z_lo = at_ref[0] >> 3
     near[pl.ds(pl.multiple_of(z_lo * 32, 32), 32)] = flipped[...]
     near[pl.ds(pl.multiple_of((1 - z_lo) * 32, 32), 32)] = pair[...]
 
 
-def split_kernel(y_left, y_right, near, x_left, x_right, y_low, y_high, x_low, x_high, joined):
-    y_low[...] = y_left[:64]
-    y_high[...] = y_right[64:]
+def split_kernel(near, x_left, x_right, x_low, x_high, joined):
     x_low[...] = x_left[:32]
     x_high[...] = x_right[32:]
     joined[:64] = near[...]
@@ -123,62 +123,93 @@
     joined[128:] = x_right[...]
 
 
-def stack_kernel(one, two, out):
+def stack_kernel(one, two, after, out):
     half = one.shape[0]
     out[:half] = one[...]
     out[half:] = two[...]
 
 
-def turn_kernel(own, left, right, out):
-    for at, ref in enumerate((own, left, right)):
-        out[:, at * 128 : at * 128 + 128] = ref[...].T
+BLOCKS = ((0, 480), (480, 960), (960, 1440), (1440, 1760), (1760, 1920))
 
 
 def last_kernel(
-    at_ref, early, far_a, far_b, near, near_far, other, other_far, out, lhs, rhs
+    at_ref,
+    own,
+    left,
+    right,
+    far_a,
+    far_b,
+    near,
+    near_far,
+    other,
+    other_far,
+    out,
+    lhs,
+    rhs,
+    held,
+    done,
 ):
     row, col = at_ref[0], at_ref[1]
-    rows, columns = out.shape
+    columns = held.shape[1]
+    dims = (((0,), (0,)), ((), ()))
+
+    def sent(at, source=None):
+        first, end = BLOCKS[at]
+        source = held.at[first:end] if source is None else source
+        return pltpu.make_async_copy(source, out.at[first:end], done.at[at])
 
     @pl.when(row <= col)
     def _():
-        @pl.when(pl.program_id(0) == 0)
-        def _():
-            y = col & 3
-            for at, by in enumerate((0, 3, 1)):
-                lane = pl.multiple_of(((y + by) & 3) * 128, 128)
-                lhs[:, pl.ds(lane, 128)] = early[:, at * 128 : at * 128 + 128]
-            lane = pl.multiple_of(((y + 2) & 3) * 128, 128)
-            far = jnp.concatenate([far_a[...], far_b[...]], axis=0)
-            lhs[:, pl.ds(lane, 128)] = far.T
-            x, core = (row >> 1) & 3, row & 1
-            for swap, most, rest in ((0, near, near_far), (1, other, other_far)):
-                for at, by in enumerate((0, 3, 1, 2)):
-                    ref, at = (most, at) if at < 3 else (rest, 0)
-                    y_from = (x + by - (col >> 1)) & 3
-                    for z_lo in range(2):
-                        z_from = z_lo * 2 + (core ^ swap)
-                        first = pl.multiple_of(y_from * 128 + z_from * 32, 32)
-                        rhs[pl.ds(first, 32)] = ref[at * 64 + z_lo * 32 : at * 64 + z_lo * 32 + 32]
-
-        start = pl.multiple_of(pl.program_id(0) * rows, rows)
-        tile = jnp.dot(lhs[pl.ds(start, rows)], rhs[...], preferred_element_type=F32) * (
-            1.0 / FRAMES
-        )
-
-        @pl.when(row < col)
-        def _():
-            out[...] = tile.astype(BF16)
-
-        @pl.when(row == col)
-        def _():
-            down = lax.broadcasted_iota(jnp.int32, tile.shape, 0) + start
-            across = lax.broadcasted_iota(jnp.int32, tile.shape, 1)
-            out[...] = jnp.where(down <= across, tile, 0.0).astype(BF16)
+        y = col & 3
+
+        def put(by, start, ref):
+            first = pl.multiple_of(((y + by) & 3) * 128 + start, 64)
+            lhs[pl.ds(first, ref.shape[0])] = ref[...]
+
+        put(0, 0, own)
+        put(3, 0, left)
+        put(1, 0, right)
+        put(2, 0, far_a)
+        put(2, 64, far_b)
+        x, core = (row >> 1) & 3, row & 1
+        for swap, most, rest in ((0, near, near_far), (1, other, other_far)):
+            for at, by in enumerate((0, 3, 1, 2)):
+                ref, at = (most, at) if at < 3 else (rest, 0)
+                y_from = (x + by - (col >> 1)) & 3
+                for z_lo in range(2):
+                    z_from = z_lo * 2 + (core ^ swap)
+                    first = pl.multiple_of(y_from * 128 + z_from * 32, 32)
+                    rhs[pl.ds(first, 32)] = ref[at * 64 + z_lo * 32 : at * 64 + z_lo * 32 + 32]
+
+    @pl.when(row < col)
+    def _():
+        for at, (first, end) in enumerate(BLOCKS):
+            tile = lax.dot_general(lhs[:, first:end], rhs[...], dims, preferred_element_type=F32)
+            held[first:end] = (tile * (1.0 / FRAMES)).astype(BF16)
+            sent(at).start()
+
+    @pl.when(row == col)
+    def _():
+        for at, (first, end) in enumerate(BLOCKS):
+            low = first // 128 * 128
+            if low:
+                held[first:end, :low] = jnp.zeros((end - first, low), BF16)
+            tile = lax.dot_general(
+                lhs[:, first:end], rhs[:, low:], dims, preferred_element_type=F32
+            ) * (1.0 / FRAMES)
+            down = lax.broadcasted_iota(jnp.int32, tile.shape, 0) + first
+            across = lax.broadcasted_iota(jnp.int32, tile.shape, 1) + low
+            held[first:end, low:] = jnp.where(down <= across, tile, 0.0).astype(BF16)
+            sent(at).start()
 
     @pl.when(row > col)
     def _():
-        out[...] = jnp.zeros_like(out)
+        held[:480] = jnp.zeros((480, columns), BF16)
+        for at, (first, end) in enumerate(BLOCKS):
+            sent(at, held.at[: end - first]).start()
+
+    for at in range(len(BLOCKS)):
+        sent(at).wait()
 
 
 def per_device(residual, interaction, commands, slope_valid, frame_valid):
@@ -229,62 +260,71 @@
         * frame_valid[:, None].astype(F32)
     ).astype(BF16)
 
+    def halves(one, two, flops):
+        half = one.shape[0] // 2
+        return call(
+            halves_kernel,
+            out_shape=(shape(half, rows),) * 2,
+            in_specs=[WHOLE] * 2,
+            out_specs=(WHOLE,) * 2,
+            cost_estimate=pl.CostEstimate(flops=flops, bytes_accessed=983040, transcendentals=0),
+        )(one, two)
+
     left = lax.ppermute(slopes, "col", z_turn(1))
     right = lax.ppermute(slopes, "col", z_turn(-1))
     flipped = lax.ppermute(slopes, ("row", "col"), flip_pairs())
-    low, high, flipped = call(
-        halves_kernel,
-        out_shape=(shape(16, rows), shape(16, rows), shape(32, rows)),
+    low, high = halves(left, right, 8000000000)
+    far_a = lax.ppermute(low, "col", z_turn(1))
+    far_b = lax.ppermute(high, "col", z_turn(-1))
+    mine = call(
+        z_join_kernel,
+        out_shape=shape(128, rows),
+        in_specs=[SCALAR] + [WHOLE] * 5,
+        out_specs=WHOLE,
+    )(at, slopes, left, right, far_a, far_b)
+    left = lax.ppermute(mine, "col", y_turn(1))
+    right = lax.ppermute(mine, "col", y_turn(-1))
+    pair = lax.ppermute(flipped, "row", [(r, r ^ 8) for r in range(16)])
+    near = call(
+        pair_join_kernel,
+        out_shape=shape(64, rows),
+        in_specs=[SCALAR] + [WHOLE] * 2,
+        out_specs=WHOLE,
+    )(at, flipped, pair)
+    x_left = lax.ppermute(near, "row", x_turn(1))
+    x_right = lax.ppermute(near, "row", x_turn(-1))
+    low, high = halves(left, right, 4000000000)
+    far_a = lax.ppermute(low, "col", y_turn(1))
+    far_b = lax.ppermute(high, "col", y_turn(-1))
+    x_low, x_high, near = call(
+        split_kernel,
+        out_shape=(shape(32, rows),) * 2 + (shape(192, rows),),
         in_specs=[WHOLE] * 3,
         out_specs=(WHOLE,) * 3,
-    )(left, right, flipped)
-    far_a = lax.ppermute(low, "col", z_turn(1))
-    far_b = lax.ppermute(high, "col", z_turn(-1))
-    pair = lax.ppermute(flipped, "row", [(r, r ^ 8) for r in range(16)])
-    mine, near = call(
-        join_kernel,
-        out_shape=(shape(128, rows), shape(64, rows)),
-        in_specs=[SCALAR] + [WHOLE] * 7,
-        out_specs=(WHOLE,) * 2,
-    )(at, slopes, left, right, far_a, far_b, flipped, pair)
-    left = lax.ppermute(mine, "col", y_turn(1))
-    right = lax.ppermute(mine, "col", y_turn(-1))
-    x_left = lax.ppermute(near, "row", x_turn(1))
-    x_right = lax.ppermute(near, "row", x_turn(-1))
-    low, high, x_low, x_high, near = call(
-        split_kernel,
-        out_shape=(shape(64, rows),) * 2 + (shape(32, rows),) * 2 + (shape(192, rows),),
-        in_specs=[WHOLE] * 5,
-        out_specs=(WHOLE,) * 5,
-    )(left, right, near, x_left, x_right)
-    far_a = lax.ppermute(low, "col", y_turn(1))
-    far_b = lax.ppermute(high, "col", y_turn(-1))
+    )(near, x_left, x_right)
     x_far_a = lax.ppermute(x_low, "row", x_turn(1))
     x_far_b = lax.ppermute(x_high, "row", x_turn(-1))
     cores = [(r, r ^ 1) for r in range(16)]
     other = lax.ppermute(near, "row", cores)
     near_far = call(
-        stack_kernel, out_shape=shape(64, rows), in_specs=[WHOLE] * 2, out_specs=WHOLE
-    )(x_far_a, x_far_b)
+        stack_kernel, out_shape=shape(64, rows), in_specs=[WHOLE] * 3, out_specs=WHOLE
+    )(x_far_a, x_far_b, low)
     other_far = lax.ppermute(near_far, "row", cores)
-    early = call(
-        turn_kernel,
-        out_shape=shape(rows, 384),
-        in_specs=[WHOLE] * 3,
-        out_specs=WHOLE,
-    )(mine, left, right)
-    steps = 5
     return call(
         last_kernel,
-        grid=(steps,),
         out_shape=shape(rows, rows),
-        in_specs=[SCALAR] + [WHOLE] * 7,
-        out_specs=pl.BlockSpec((rows // steps, rows), lambda i: (i, 0)),
-        scratch_shapes=[pltpu.VMEM((rows, FRAMES), BF16), pltpu.VMEM((FRAMES, rows), BF16)],
+        in_specs=[SCALAR] + [WHOLE] * 9,
+        out_specs=pl.BlockSpec(memory_space=pl.ANY),
+        scratch_shapes=[
+            pltpu.VMEM((FRAMES, rows), BF16),
+            pltpu.VMEM((FRAMES, rows), BF16),
+            pltpu.VMEM((rows, rows), BF16),
+            pltpu.SemaphoreType.DMA((len(BLOCKS),)),
+        ],
         cost_estimate=pl.CostEstimate(
             flops=2 * FRAMES * rows * rows, bytes_accessed=2 * rows * rows, transcendentals=0
         ),
-    )(at, early, far_a, far_b, near, near_far, other, other_far)
+    )(at, mine, left, right, far_a, far_b, near, near_far, other, other_far)
 
 
 def solution(mesh):

time: 110 us -> 111 us (level)
  the two profiles are of different devices: /device:TPU:24 before, /device:TPU:66 now
where the time goes in v4:
time: 111 us
  waiting for transfers between devices  52.4 us (47%)
  starting transfers between devices  43.9 us (40%)
  Pallas kernels  9.66 us (9%)
  local copies, waits for them, and re-layouts  3.62 us (3%)
  other arithmetic  1.24 us (1%)
    ppermute x1, waiting for transfers between devices, per_device(): got_b = lax.ppermute(sent_b, 'col', y_swap(3))  8.44 us
    ppermute x3, starting transfers between devices, per_device(): next_a = lax.ppermute(sent_a, 'col', swap_a)  6.9 us
    ppermute x3, starting transfers between devices, per_device(): next_b = lax.ppermute(sent_b, 'col', swap_b)  6.85 us
    pallas_call x1, Pallas kernels, per_device(): call(last_kernel, out_shape=shape(rows, rows), in_specs=[SCALAR] + [WHOLE...  6.01 us
    ppermute x1, waiting for transfers between devices, per_device(): far_b = lax.ppermute(high, 'col', y_turn(-1))  5.81 us
    ppermute x3, waiting for transfers between devices, per_device(): next_b = lax.ppermute(sent_b, 'col', swap_b)  5.5 us
    ppermute x1, starting transfers between devices, per_device(): pair = lax.ppermute(flipped, 'row', [(r, r ^ 8) for r in range(16)])  5.35 us
    ppermute x3, waiting for transfers between devices, per_device(): next_a = lax.ppermute(sent_a, 'col', swap_a)  4.6 us
  transfers between devices with their start and end apart: 24, of which 17 were waited for; matrix products, arithmetic and copies ran while one was open for 1% of the time, Pallas kernels for 2%

profile of v4, /device:TPU:66, one launch (start us, length us, event | category | flops | bytes accessed | tf_op | source)
XLA Modules:
  0.0 111.1 jit_solution(7939939598530093191)
XLA Ops:
  0.1 1.3 %copy-done = bf16[1920,320]{0,1:T(8,128)(2,1)S(1)} copy-done((bf16[1920,320]{0,1:T(8,128)(2,1)S(1)}, bf16[1920,320]{0,1:T(8,128)(2,1)}, u32[]{:S(2)}) %copy-start) | copy-done | bytes 1228824
  2.3 1.7 %shard_map.55 = (bf16[128,1920]{1,0:T(8,128)(2,1)S(1)}, bf16[128,1920]{1,0:T(8,128)(2,1)S(1)}, bf16[256,320]{1,0:T(8,128)(2,1)S(1)}) custom-call(s32[2]{0:T(128)S(1)} %pad_add_fusion.at_ref, bf16[320,512]{1,0:T(8,128)(2,1)S(1)} %copy-done.2, bf16[320,1920]{1,0:T(8,128)(2,1)S(1)} %bitcast.13), custom_call_target="tpu_custom_call" | custom-call | flops 314572800 | bytes 1600000 | tf_op jit(solution)/shard_map/pallas_call | solution.py:222
  4.0 3.1 %collective-permute-start.3 = (bf16[128,1920]{1,0:T(8,128)(2,1)S(1)}, bf16[128,1920]{1,0:T(8,128)(2,1)S(1)}, u32[]{:S(2)}, u32[]{:S(2)}) collective-permute-start(bf16[128,1920]{1,0:T(8,128)(2,1)S(1)} %get-tuple-element.21), channel_id=1, source_target_pairs={{0,3},{1,2},{2,1},{3,0},{4,7},{5,6},{6,5},{7,4},{8,11},{9,10},{10,... | collective-permute-start | bytes 1474568 | tf_op jit(solution)/shard_map/ppermute | solution.py:232
  7.9 1.3 %copy-done.1 = bf16[1920,320]{0,1:T(8,128)(2,1)S(1)} copy-done((bf16[1920,320]{0,1:T(8,128)(2,1)S(1)}, bf16[1920,320]{0,1:T(8,128)(2,1)}, u32[]{:S(2)}) %copy-start.1) | copy-done | bytes 1228824
  9.9 8.4 %collective-permute-done.3 = bf16[128,1920]{1,0:T(8,128)(2,1)S(1)} collective-permute-done((bf16[128,1920]{1,0:T(8,128)(2,1)S(1)}, bf16[128,1920]{1,0:T(8,128)(2,1)S(1)}, u32[]{:S(2)}, u32[]{:S(2)}) %collective-permute-start.3) | collective-permute-done | bytes 491552 | tf_op jit(solution)/shard_map/ppermute | solution.py:232
  19.9 1.8 %collective-permute-start.1 = (bf16[64,1920]{1,0:T(8,128)(2,1)S(1)}, bf16[64,1920]{1,0:T(8,128)(2,1)S(1)}, u32[]{:S(2)}, u32[]{:S(2)}) collective-permute-start(bf16[64,1920]{1,0:T(8,128)(2,1)S(1)} %get-tuple-element.30), channel_id=1, source_target_pairs={{0,3},{1,2},{2,1},{3,0},{4,7},{5,6},{6,5},{7,4},{8,11},{9,10},{10,... | collective-permute-start | bytes 737288 | tf_op jit(solution)/shard_map/ppermute | solution.py:249
  21.8 3.7 %collective-permute-done.4 = bf16[64,1920]{1,0:T(8,128)(2,1)S(1)} collective-permute-done((bf16[64,1920]{1,0:T(8,128)(2,1)S(1)}, bf16[64,1920]{1,0:T(8,128)(2,1)S(1)}, u32[]{:S(2)}, u32[]{:S(2)}) %collective-permute-start.4) | collective-permute-done | bytes 245792 | tf_op jit(solution)/shard_map/ppermute | solution.py:250
  25.5 4.6 %collective-permute-start.5 = (bf16[32,1920]{1,0:T(8,128)(2,1)S(1)}, bf16[32,1920]{1,0:T(8,128)(2,1)S(1)}, u32[]{:S(2)}, u32[]{:S(2)}) collective-permute-start(bf16[32,1920]{1,0:T(8,128)(2,1)S(1)} %get-tuple-element.36), channel_id=1, source_target_pairs={{0,12},{1,13},{2,14},{3,15},{4,8},{5,9},{6,10},{7,11},{8,4},{9,5},... | collective-permute-start | bytes 368648 | tf_op jit(solution)/shard_map/ppermute | solution.py:250
  30.2 1.6 %collective-permute-start.2 = (bf16[32,1920]{1,0:T(8,128)(2,1)S(1)}, bf16[32,1920]{1,0:T(8,128)(2,1)S(1)}, u32[]{:S(2)}, u32[]{:S(2)}) collective-permute-start(bf16[32,1920]{1,0:T(8,128)(2,1)S(1)} %get-tuple-element.34), channel_id=1, source_target_pairs={{0,4},{1,5},{2,6},{3,7},{4,0},{5,1},{6,2},{7,3},{8,12},{9,13},{10,... | collective-permute-start | bytes 368648 | tf_op jit(solution)/shard_map/ppermute | solution.py:249
  31.7 1.8 %collective-permute-done.5 = bf16[32,1920]{1,0:T(8,128)(2,1)S(1)} collective-permute-done((bf16[32,1920]{1,0:T(8,128)(2,1)S(1)}, bf16[32,1920]{1,0:T(8,128)(2,1)S(1)}, u32[]{:S(2)}, u32[]{:S(2)}) %collective-permute-start.5) | collective-permute-done | bytes 122912 | tf_op jit(solution)/shard_map/ppermute | solution.py:250
  33.5 1.9 %collective-permute-start.7 = (bf16[16,1920]{1,0:T(8,128)(2,1)S(1)}, bf16[16,1920]{1,0:T(8,128)(2,1)S(1)}, u32[]{:S(2)}, u32[]{:S(2)}) collective-permute-start(bf16[16,1920]{1,0:T(8,128)(2,1)S(1)} %get-tuple-element.39), channel_id=1, source_target_pairs={{0,4},{1,5},{2,6},{3,7},{4,0},{5,1},{6,2},{7,3},{8,12},{9,13},{10,... | collective-permute-start | bytes 184328 | tf_op jit(solution)/shard_map/ppermute | solution.py:250
  35.4 1.8 %collective-permute-done.2 = bf16[32,1920]{1,0:T(8,128)(2,1)S(1)} collective-permute-done((bf16[32,1920]{1,0:T(8,128)(2,1)S(1)}, bf16[32,1920]{1,0:T(8,128)(2,1)S(1)}, u32[]{:S(2)}, u32[]{:S(2)}) %collective-permute-start.2) | collective-permute-done | bytes 122912 | tf_op jit(solution)/shard_map/ppermute | solution.py:249
  37.2 3.5 %collective-permute-start.6 = (bf16[16,1920]{1,0:T(8,128)(2,1)S(1)}, bf16[16,1920]{1,0:T(8,128)(2,1)S(1)}, u32[]{:S(2)}, u32[]{:S(2)}) collective-permute-start(bf16[16,1920]{1,0:T(8,128)(2,1)S(1)} %get-tuple-element.37), channel_id=1, source_target_pairs={{0,12},{1,13},{2,14},{3,15},{4,8},{5,9},{6,10},{7,11},{8,4},{9,5},... | collective-permute-start | bytes 184328 | tf_op jit(solution)/shard_map/ppermute | solution.py:249
  40.9 2.8 %collective-permute-done.6 = bf16[16,1920]{1,0:T(8,128)(2,1)S(1)} collective-permute-done((bf16[16,1920]{1,0:T(8,128)(2,1)S(1)}, bf16[16,1920]{1,0:T(8,128)(2,1)S(1)}, u32[]{:S(2)}, u32[]{:S(2)}) %collective-permute-start.6) | collective-permute-done | bytes 61472 | tf_op jit(solution)/shard_map/ppermute | solution.py:249
  43.8 3.8 %collective-permute-start.9 = (bf16[32,1920]{1,0:T(8,128)(2,1)S(1)}, bf16[32,1920]{1,0:T(8,128)(2,1)S(1)}, u32[]{:S(2)}, u32[]{:S(2)}) collective-permute-start(bf16[32,1920]{1,0:T(8,128)(2,1)S(1)} %fusion.2.own), channel_id=1, source_target_pairs={{0,12},{1,13},{2,14},{3,15},{4,0},{5,1},{6,2},{7,3},{8,4},{9,5},{1... | collective-permute-start | bytes 368648 | tf_op jit(solution)/shard_map/ppermute | solution.py:274
  48.0 1.9 %collective-permute-start.16 = (bf16[32,1920]{1,0:T(8,128)(2,1)S(1)}, bf16[32,1920]{1,0:T(8,128)(2,1)S(1)}, u32[]{:S(2)}, u32[]{:S(2)}) collective-permute-start(bf16[32,1920]{1,0:T(8,128)(2,1)S(1)} %fusion.2.own), channel_id=1, source_target_pairs={{0,0},{1,32},{2,64},{3,96},{4,16},{5,48},{6,80},{7,112},{8,128},{9... | collective-permute-start | bytes 368648 | tf_op jit(solution)/shard_map/ppermute | solution.py:275
  50.9 3.1 %collective-permute-done.8.left = bf16[32,1920]{1,0:T(8,128)(2,1)S(1)} collective-permute-done((bf16[32,1920]{1,0:T(8,128)(2,1)S(1)}, bf16[32,1920]{1,0:T(8,128)(2,1)S(1)}, u32[]{:S(2)}, u32[]{:S(2)}) %collective-permute-start.8) | collective-permute-done | bytes 122912 | tf_op jit(solution)/shard_map/ppermute | solution.py:273
  54.1 3.0 %collective-permute-start.10 = (bf16[16,1920]{1,0:T(8,128)(2,1)S(1)}, bf16[16,1920]{1,0:T(8,128)(2,1)S(1)}, u32[]{:S(2)}, u32[]{:S(2)}) collective-permute-start(bf16[16,1920]{1,0:T(8,128)(2,1)S(1)} %get-tuple-element.22), channel_id=1, source_target_pairs={{0,4},{1,5},{2,6},{3,7},{4,8},{5,9},{6,10},{7,11},{8,12},{9,13},{1... | collective-permute-start | bytes 184328 | tf_op jit(solution)/shard_map/ppermute | solution.py:277
  57.4 3.5 %collective-permute-done.10.far_a = bf16[16,1920]{1,0:T(8,128)(2,1)S(1)} collective-permute-done((bf16[16,1920]{1,0:T(8,128)(2,1)S(1)}, bf16[16,1920]{1,0:T(8,128)(2,1)S(1)}, u32[]{:S(2)}, u32[]{:S(2)}) %collective-permute-start.10) | collective-permute-done | bytes 61472 | tf_op jit(solution)/shard_map/ppermute | solution.py:277
  60.9 3.7 %collective-permute-done.11.far_b = bf16[16,1920]{1,0:T(8,128)(2,1)S(1)} collective-permute-done((bf16[16,1920]{1,0:T(8,128)(2,1)S(1)}, bf16[16,1920]{1,0:T(8,128)(2,1)S(1)}, u32[]{:S(2)}, u32[]{:S(2)}) %collective-permute-start.11) | collective-permute-done | bytes 61472 | tf_op jit(solution)/shard_map/ppermute | solution.py:278
  65.2 4.2 %collective-permute-start.13 = (bf16[128,1920]{1,0:T(8,128)(2,1)S(1)}, bf16[128,1920]{1,0:T(8,128)(2,1)S(1)}, u32[]{:S(2)}, u32[]{:S(2)}) collective-permute-start(bf16[128,1920]{1,0:T(8,128)(2,1)S(1)} %shard_map.58.own), channel_id=1, source_target_pairs={{0,3},{1,0},{2,1},{3,2},{4,7},{5,4},{6,5},{7,6},{8,11},{9,8},{10,9... | collective-permute-start | bytes 1474568 | tf_op jit(solution)/shard_map/ppermute | solution.py:286
  69.4 5.3 %collective-permute-start.17 = (bf16[32,1920]{1,0:T(8,128)(2,1)S(1)}, bf16[32,1920]{1,0:T(8,128)(2,1)S(1)}, u32[]{:S(2)}, u32[]{:S(2)}) collective-permute-start(bf16[32,1920]{1,0:T(8,128)(2,1)S(1)} %collective-permute-done.16.flipped), channel_id=1, source_target_pairs={{0,128},{16,144},{32,160},{48,176},{64,192},{80,208},{96,224},{112... | collective-permute-start | bytes 368648 | tf_op jit(solution)/shard_map/ppermute | solution.py:287
  74.8 2.9 %collective-permute-done.17.pair = bf16[32,1920]{1,0:T(8,128)(2,1)S(1)} collective-permute-done((bf16[32,1920]{1,0:T(8,128)(2,1)S(1)}, bf16[32,1920]{1,0:T(8,128)(2,1)S(1)}, u32[]{:S(2)}, u32[]{:S(2)}) %collective-permute-start.17) | collective-permute-done | bytes 122912 | tf_op jit(solution)/shard_map/ppermute | solution.py:287
  78.5 2.0 %collective-permute-start.18 = (bf16[64,1920]{1,0:T(8,128)(2,1)S(1)}, bf16[64,1920]{1,0:T(8,128)(2,1)S(1)}, u32[]{:S(2)}, u32[]{:S(2)}) collective-permute-start(bf16[64,1920]{1,0:T(8,128)(2,1)S(1)} %shard_map.60.near), channel_id=1, source_target_pairs={{0,32},{16,48},{32,64},{48,80},{64,96},{80,112},{96,0},{112,16},{1... | collective-permute-start | bytes 737288 | tf_op jit(solution)/shard_map/ppermute | solution.py:294
  80.5 4.2 %collective-permute-done.19.x_right = bf16[64,1920]{1,0:T(8,128)(2,1)S(1)} collective-permute-done((bf16[64,1920]{1,0:T(8,128)(2,1)S(1)}, bf16[64,1920]{1,0:T(8,128)(2,1)S(1)}, u32[]{:S(2)}, u32[]{:S(2)}) %collective-permute-start.19) | collective-permute-done | bytes 245792 | tf_op jit(solution)/shard_map/ppermute | solution.py:295
  84.9 2.0 %collective-permute-start.20 = (bf16[32,1920]{1,0:T(8,128)(2,1)S(1)}, bf16[32,1920]{1,0:T(8,128)(2,1)S(1)}, u32[]{:S(2)}, u32[]{:S(2)}) collective-permute-start(bf16[32,1920]{1,0:T(8,128)(2,1)S(1)} %get-tuple-element.27), channel_id=1, source_target_pairs={{0,32},{16,48},{32,64},{48,80},{64,96},{80,112},{96,0},{112,16},{1... | collective-permute-start | bytes 368648 | tf_op jit(solution)/shard_map/ppermute | solution.py:305
  87.0 3.6 %collective-permute-done.20.one = bf16[32,1920]{1,0:T(8,128)(2,1)S(1)} collective-permute-done((bf16[32,1920]{1,0:T(8,128)(2,1)S(1)}, bf16[32,1920]{1,0:T(8,128)(2,1)S(1)}, u32[]{:S(2)}, u32[]{:S(2)}) %collective-permute-start.20) | collective-permute-done | bytes 122912 | tf_op jit(solution)/shard_map/ppermute | solution.py:305
  90.6 1.7 %collective-permute-done.21.two = bf16[32,1920]{1,0:T(8,128)(2,1)S(1)} collective-permute-done((bf16[32,1920]{1,0:T(8,128)(2,1)S(1)}, bf16[32,1920]{1,0:T(8,128)(2,1)S(1)}, u32[]{:S(2)}, u32[]{:S(2)}) %collective-permute-start.21) | collective-permute-done | bytes 122912 | tf_op jit(solution)/shard_map/ppermute | solution.py:306
  92.4 3.3 %collective-permute-start.15 = (bf16[64,1920]{1,0:T(8,128)(2,1)S(1)}, bf16[64,1920]{1,0:T(8,128)(2,1)S(1)}, u32[]{:S(2)}, u32[]{:S(2)}) collective-permute-start(bf16[64,1920]{1,0:T(8,128)(2,1)S(1)} %get-tuple-element.25), channel_id=1, source_target_pairs={{0,3},{1,0},{2,1},{3,2},{4,7},{5,4},{6,5},{7,6},{8,11},{9,8},{10,9... | collective-permute-start | bytes 737288 | tf_op jit(solution)/shard_map/ppermute | solution.py:298
  95.7 5.8 %collective-permute-done.15.far_b = bf16[64,1920]{1,0:T(8,128)(2,1)S(1)} collective-permute-done((bf16[64,1920]{1,0:T(8,128)(2,1)S(1)}, bf16[64,1920]{1,0:T(8,128)(2,1)S(1)}, u32[]{:S(2)}, u32[]{:S(2)}) %collective-permute-start.15) | collective-permute-done | bytes 245792 | tf_op jit(solution)/shard_map/ppermute | solution.py:298
  101.5 3.4 %collective-permute-done.14.far_a = bf16[64,1920]{1,0:T(8,128)(2,1)S(1)} collective-permute-done((bf16[64,1920]{1,0:T(8,128)(2,1)S(1)}, bf16[64,1920]{1,0:T(8,128)(2,1)S(1)}, u32[]{:S(2)}, u32[]{:S(2)}) %collective-permute-start.14) | collective-permute-done | bytes 245792 | tf_op jit(solution)/shard_map/ppermute | solution.py:297
  105.0 6.0 %shard_map.63 = bf16[1920,1920]{1,0:T(8,128)(2,1)} custom-call(s32[2]{0:T(128)S(1)} %pad_add_fusion.at_ref, bf16[128,1920]{1,0:T(8,128)(2,1)S(1)} %shard_map.58.own, bf16[128,1920]{1,0:T(8,128)(2,1)S(1)} %collective-permute-done.12.left, bf16[128,1920]{1,0:T(8,128)(2,1)S(1)} %collective-permute-done.13.right, ...), custom_call_target="tpu_custom_call" | custom-call | flops 3774873600 | bytes 7372800 | tf_op jit(solution)/shard_map/pallas_call | solution.py:313
  (46 shorter events, 8.2 us)
Async XLA Ops:
  0.0 40.8 %copy-start.4 = (s32[32]{0:T(128)S(1)}, s32[32]{0:T(128)}, u32[]{:S(2)}) copy-start(s32[32]{0:T(128)} %param.9) | copy-start | bytes 388
  0.1 1.3 %copy-start = (bf16[1920,320]{0,1:T(8,128)(2,1)S(1)}, bf16[1920,320]{0,1:T(8,128)(2,1)}, u32[]{:S(2)}) copy-start(bf16[1920,320]{0,1:T(8,128)(2,1)} %param.6) | copy-start | bytes 3686404
  1.4 1.0 copy-start.2
  2.3 41.3 %copy-start.3 = (bf16[1920,32]{0,1:T(8,128)(2,1)S(1)}, bf16[1920,32]{0,1:T(8,128)(2,1)}, u32[]{:S(2)}) copy-start(bf16[1920,32]{0,1:T(8,128)(2,1)} %param.5) | copy-start | bytes 368644
  4.0 14.3 %collective-permute-start.3 = (bf16[128,1920]{1,0:T(8,128)(2,1)S(1)}, bf16[128,1920]{1,0:T(8,128)(2,1)S(1)}, u32[]{:S(2)}, u32[]{:S(2)}) collective-permute-start(bf16[128,1920]{1,0:T(8,128)(2,1)S(1)} %get-tuple-element.21), channel_id=1, source_target_pairs={{0,3},{1,2},{2,1},{3,0},{4,7},{5,6},{6,5},{7,4},{8,11},{9,10},{10,... | collective-permute-start | bytes 1474568 | tf_op jit(solution)/shard_map/ppermute | solution.py:232
  7.1 12.7 %collective-permute-start = (bf16[128,1920]{1,0:T(8,128)(2,1)S(1)}, bf16[128,1920]{1,0:T(8,128)(2,1)S(1)}, u32[]{:S(2)}, u32[]{:S(2)}) collective-permute-start(bf16[128,1920]{1,0:T(8,128)(2,1)S(1)} %get-tuple-element.19), channel_id=1, source_target_pairs={{0,1},{1,0},{2,3},{3,2},{4,5},{5,4},{6,7},{7,6},{8,9},{9,8},{10,11... | collective-permute-start | bytes 1474568 | tf_op jit(solution)/shard_map/ppermute | solution.py:231
  7.9 1.3 %copy-start.1 = (bf16[1920,320]{0,1:T(8,128)(2,1)S(1)}, bf16[1920,320]{0,1:T(8,128)(2,1)}, u32[]{:S(2)}) copy-start(bf16[1920,320]{0,1:T(8,128)(2,1)} %param.6) | copy-start | bytes 3686404
  18.5 7.0 %collective-permute-start.4 = (bf16[64,1920]{1,0:T(8,128)(2,1)S(1)}, bf16[64,1920]{1,0:T(8,128)(2,1)S(1)}, u32[]{:S(2)}, u32[]{:S(2)}) collective-permute-start(bf16[64,1920]{1,0:T(8,128)(2,1)S(1)} %get-tuple-element.32), channel_id=1, source_target_pairs={{0,1},{1,0},{2,3},{3,2},{4,5},{5,4},{6,7},{7,6},{8,9},{9,8},{10,11... | collective-permute-start | bytes 737288 | tf_op jit(solution)/shard_map/ppermute | solution.py:250
  19.9 10.2 %collective-permute-start.1 = (bf16[64,1920]{1,0:T(8,128)(2,1)S(1)}, bf16[64,1920]{1,0:T(8,128)(2,1)S(1)}, u32[]{:S(2)}, u32[]{:S(2)}) collective-permute-start(bf16[64,1920]{1,0:T(8,128)(2,1)S(1)} %get-tuple-element.30), channel_id=1, source_target_pairs={{0,3},{1,2},{2,1},{3,0},{4,7},{5,6},{6,5},{7,4},{8,11},{9,10},{10,... | collective-permute-start | bytes 737288 | tf_op jit(solution)/shard_map/ppermute | solution.py:249
  25.5 8.0 %collective-permute-start.5 = (bf16[32,1920]{1,0:T(8,128)(2,1)S(1)}, bf16[32,1920]{1,0:T(8,128)(2,1)S(1)}, u32[]{:S(2)}, u32[]{:S(2)}) collective-permute-start(bf16[32,1920]{1,0:T(8,128)(2,1)S(1)} %get-tuple-element.36), channel_id=1, source_target_pairs={{0,12},{1,13},{2,14},{3,15},{4,8},{5,9},{6,10},{7,11},{8,4},{9,5},... | collective-permute-start | bytes 368648 | tf_op jit(solution)/shard_map/ppermute | solution.py:250
  30.2 7.0 %collective-permute-start.2 = (bf16[32,1920]{1,0:T(8,128)(2,1)S(1)}, bf16[32,1920]{1,0:T(8,128)(2,1)S(1)}, u32[]{:S(2)}, u32[]{:S(2)}) collective-permute-start(bf16[32,1920]{1,0:T(8,128)(2,1)S(1)} %get-tuple-element.34), channel_id=1, source_target_pairs={{0,4},{1,5},{2,6},{3,7},{4,0},{5,1},{6,2},{7,3},{8,12},{9,13},{10,... | collective-permute-start | bytes 368648 | tf_op jit(solution)/shard_map/ppermute | solution.py:249
  33.5 7.3 %collective-permute-start.7 = (bf16[16,1920]{1,0:T(8,128)(2,1)S(1)}, bf16[16,1920]{1,0:T(8,128)(2,1)S(1)}, u32[]{:S(2)}, u32[]{:S(2)}) collective-permute-start(bf16[16,1920]{1,0:T(8,128)(2,1)S(1)} %get-tuple-element.39), channel_id=1, source_target_pairs={{0,4},{1,5},{2,6},{3,7},{4,0},{5,1},{6,2},{7,3},{8,12},{9,13},{10,... | collective-permute-start | bytes 184328 | tf_op jit(solution)/shard_map/ppermute | solution.py:250
  37.2 6.4 %collective-permute-start.6 = (bf16[16,1920]{1,0:T(8,128)(2,1)S(1)}, bf16[16,1920]{1,0:T(8,128)(2,1)S(1)}, u32[]{:S(2)}, u32[]{:S(2)}) collective-permute-start(bf16[16,1920]{1,0:T(8,128)(2,1)S(1)} %get-tuple-element.37), channel_id=1, source_target_pairs={{0,12},{1,13},{2,14},{3,15},{4,8},{5,9},{6,10},{7,11},{8,4},{9,5},... | collective-permute-start | bytes 184328 | tf_op jit(solution)/shard_map/ppermute | solution.py:249
  43.8 7.2 %collective-permute-start.9 = (bf16[32,1920]{1,0:T(8,128)(2,1)S(1)}, bf16[32,1920]{1,0:T(8,128)(2,1)S(1)}, u32[]{:S(2)}, u32[]{:S(2)}) collective-permute-start(bf16[32,1920]{1,0:T(8,128)(2,1)S(1)} %fusion.2.own), channel_id=1, source_target_pairs={{0,12},{1,13},{2,14},{3,15},{4,0},{5,1},{6,2},{7,3},{8,4},{9,5},{1... | collective-permute-start | bytes 368648 | tf_op jit(solution)/shard_map/ppermute | solution.py:274
  47.5 6.5 %collective-permute-start.8 = (bf16[32,1920]{1,0:T(8,128)(2,1)S(1)}, bf16[32,1920]{1,0:T(8,128)(2,1)S(1)}, u32[]{:S(2)}, u32[]{:S(2)}) collective-permute-start(bf16[32,1920]{1,0:T(8,128)(2,1)S(1)} %fusion.2.own), channel_id=1, source_target_pairs={{0,4},{1,5},{2,6},{3,7},{4,8},{5,9},{6,10},{7,11},{8,12},{9,13},{1... | collective-permute-start | bytes 368648 | tf_op jit(solution)/shard_map/ppermute | solution.py:273
  48.0 21.4 %collective-permute-start.16 = (bf16[32,1920]{1,0:T(8,128)(2,1)S(1)}, bf16[32,1920]{1,0:T(8,128)(2,1)S(1)}, u32[]{:S(2)}, u32[]{:S(2)}) collective-permute-start(bf16[32,1920]{1,0:T(8,128)(2,1)S(1)} %fusion.2.own), channel_id=1, source_target_pairs={{0,0},{1,32},{2,64},{3,96},{4,16},{5,48},{6,80},{7,112},{8,128},{9... | collective-permute-start | bytes 368648 | tf_op jit(solution)/shard_map/ppermute | solution.py:275
  54.1 6.8 %collective-permute-start.10 = (bf16[16,1920]{1,0:T(8,128)(2,1)S(1)}, bf16[16,1920]{1,0:T(8,128)(2,1)S(1)}, u32[]{:S(2)}, u32[]{:S(2)}) collective-permute-start(bf16[16,1920]{1,0:T(8,128)(2,1)S(1)} %get-tuple-element.22), channel_id=1, source_target_pairs={{0,4},{1,5},{2,6},{3,7},{4,8},{5,9},{6,10},{7,11},{8,12},{9,13},{1... | collective-permute-start | bytes 184328 | tf_op jit(solution)/shard_map/ppermute | solution.py:277
  57.1 7.5 %collective-permute-start.11 = (bf16[16,1920]{1,0:T(8,128)(2,1)S(1)}, bf16[16,1920]{1,0:T(8,128)(2,1)S(1)}, u32[]{:S(2)}, u32[]{:S(2)}) collective-permute-start(bf16[16,1920]{1,0:T(8,128)(2,1)S(1)} %get-tuple-element.23), channel_id=1, source_target_pairs={{0,12},{1,13},{2,14},{3,15},{4,0},{5,1},{6,2},{7,3},{8,4},{9,5},{1... | collective-permute-start | bytes 184328 | tf_op jit(solution)/shard_map/ppermute | solution.py:278
  65.2 21.8 %collective-permute-start.13 = (bf16[128,1920]{1,0:T(8,128)(2,1)S(1)}, bf16[128,1920]{1,0:T(8,128)(2,1)S(1)}, u32[]{:S(2)}, u32[]{:S(2)}) collective-permute-start(bf16[128,1920]{1,0:T(8,128)(2,1)S(1)} %shard_map.58.own), channel_id=1, source_target_pairs={{0,3},{1,0},{2,1},{3,2},{4,7},{5,4},{6,5},{7,6},{8,11},{9,8},{10,9... | collective-permute-start | bytes 1474568 | tf_op jit(solution)/shard_map/ppermute | solution.py:286
  69.4 17.6 %collective-permute-start.12 = (bf16[128,1920]{1,0:T(8,128)(2,1)S(1)}, bf16[128,1920]{1,0:T(8,128)(2,1)S(1)}, u32[]{:S(2)}, u32[]{:S(2)}) collective-permute-start(bf16[128,1920]{1,0:T(8,128)(2,1)S(1)} %shard_map.58.own), channel_id=1, source_target_pairs={{0,1},{1,2},{2,3},{3,0},{4,5},{5,6},{6,7},{7,4},{8,9},{9,10},{10,1... | collective-permute-start | bytes 1474568 | tf_op jit(solution)/shard_map/ppermute | solution.py:285
  69.4 8.2 %collective-permute-start.17 = (bf16[32,1920]{1,0:T(8,128)(2,1)S(1)}, bf16[32,1920]{1,0:T(8,128)(2,1)S(1)}, u32[]{:S(2)}, u32[]{:S(2)}) collective-permute-start(bf16[32,1920]{1,0:T(8,128)(2,1)S(1)} %collective-permute-done.16.flipped), channel_id=1, source_target_pairs={{0,128},{16,144},{32,160},{48,176},{64,192},{80,208},{96,224},{112... | collective-permute-start | bytes 368648 | tf_op jit(solution)/shard_map/ppermute | solution.py:287
  78.2 6.5 %collective-permute-start.19 = (bf16[64,1920]{1,0:T(8,128)(2,1)S(1)}, bf16[64,1920]{1,0:T(8,128)(2,1)S(1)}, u32[]{:S(2)}, u32[]{:S(2)}) collective-permute-start(bf16[64,1920]{1,0:T(8,128)(2,1)S(1)} %shard_map.60.near), channel_id=1, source_target_pairs={{0,96},{16,112},{32,0},{48,16},{64,32},{80,48},{96,64},{112,80},{1... | collective-permute-start | bytes 737288 | tf_op jit(solution)/shard_map/ppermute | solution.py:295
  78.5 6.3 %collective-permute-start.18 = (bf16[64,1920]{1,0:T(8,128)(2,1)S(1)}, bf16[64,1920]{1,0:T(8,128)(2,1)S(1)}, u32[]{:S(2)}, u32[]{:S(2)}) collective-permute-start(bf16[64,1920]{1,0:T(8,128)(2,1)S(1)} %shard_map.60.near), channel_id=1, source_target_pairs={{0,32},{16,48},{32,64},{48,80},{64,96},{80,112},{96,0},{112,16},{1... | collective-permute-start | bytes 737288 | tf_op jit(solution)/shard_map/ppermute | solution.py:294
  84.8 20.2 %collective-permute-start.22 = (bf16[192,1920]{1,0:T(8,128)(2,1)S(1)}, bf16[192,1920]{1,0:T(8,128)(2,1)S(1)}, u32[]{:S(2)}, u32[]{:S(2)}) collective-permute-start(bf16[192,1920]{1,0:T(8,128)(2,1)S(1)} %get-tuple-element.26.near), channel_id=1, source_target_pairs={{0,16},{16,0},{32,48},{48,32},{64,80},{80,64},{96,112},{112,96},{1... | collective-permute-start | bytes 2211848 | tf_op jit(solution)/shard_map/ppermute | solution.py:308
  84.9 5.7 %collective-permute-start.20 = (bf16[32,1920]{1,0:T(8,128)(2,1)S(1)}, bf16[32,1920]{1,0:T(8,128)(2,1)S(1)}, u32[]{:S(2)}, u32[]{:S(2)}) collective-permute-start(bf16[32,1920]{1,0:T(8,128)(2,1)S(1)} %get-tuple-element.27), channel_id=1, source_target_pairs={{0,32},{16,48},{32,64},{48,80},{64,96},{80,112},{96,0},{112,16},{1... | collective-permute-start | bytes 368648 | tf_op jit(solution)/shard_map/ppermute | solution.py:305
  86.9 5.4 %collective-permute-start.21 = (bf16[32,1920]{1,0:T(8,128)(2,1)S(1)}, bf16[32,1920]{1,0:T(8,128)(2,1)S(1)}, u32[]{:S(2)}, u32[]{:S(2)}) collective-permute-start(bf16[32,1920]{1,0:T(8,128)(2,1)S(1)} %get-tuple-element.28), channel_id=1, source_target_pairs={{0,96},{16,112},{32,0},{48,16},{64,32},{80,48},{96,64},{112,80},{1... | collective-permute-start | bytes 368648 | tf_op jit(solution)/shard_map/ppermute | solution.py:306
  92.3 3.4 %collective-permute-start.23 = (bf16[64,1920]{1,0:T(8,128)(2,1)S(1)}, bf16[64,1920]{1,0:T(8,128)(2,1)S(1)}, u32[]{:S(2)}, u32[]{:S(2)}) collective-permute-start(bf16[64,1920]{1,0:T(8,128)(2,1)S(1)} %shard_map.62.near_far), channel_id=1, source_target_pairs={{0,16},{16,0},{32,48},{48,32},{64,80},{80,64},{96,112},{112,96},{1... | collective-permute-start | bytes 737288 | tf_op jit(solution)/shard_map/ppermute | solution.py:312
  92.4 9.1 %collective-permute-start.15 = (bf16[64,1920]{1,0:T(8,128)(2,1)S(1)}, bf16[64,1920]{1,0:T(8,128)(2,1)S(1)}, u32[]{:S(2)}, u32[]{:S(2)}) collective-permute-start(bf16[64,1920]{1,0:T(8,128)(2,1)S(1)} %get-tuple-element.25), channel_id=1, source_target_pairs={{0,3},{1,0},{2,1},{3,2},{4,7},{5,4},{6,5},{7,6},{8,11},{9,8},{10,9... | collective-permute-start | bytes 737288 | tf_op jit(solution)/shard_map/ppermute | solution.py:298
  95.7 9.2 %collective-permute-start.14 = (bf16[64,1920]{1,0:T(8,128)(2,1)S(1)}, bf16[64,1920]{1,0:T(8,128)(2,1)S(1)}, u32[]{:S(2)}, u32[]{:S(2)}) collective-permute-start(bf16[64,1920]{1,0:T(8,128)(2,1)S(1)} %get-tuple-element.24.after), channel_id=1, source_target_pairs={{0,1},{1,2},{2,3},{3,0},{4,5},{5,6},{6,7},{7,4},{8,9},{9,10},{10,1... | collective-permute-start | bytes 737288 | tf_op jit(solution)/shard_map/ppermute | solution.py:297

commit v5 on v4

--- a/solution.py
+++ b/solution.py
@@ -95,7 +95,11 @@
     high[...] = right[half:]
 
 
-def z_join_kernel(at_ref, own, left, right, far_a, far_b, mine):
+def same_kernel(flipped, after, out):
+    out[...] = flipped[...]
+
+
+def join_kernel(at_ref, own, left, right, far_a, far_b, flipped, pair, mine, near):
     z = at_ref[1] >> 2
 
     def put(by, start, ref):
@@ -107,23 +111,19 @@
     put(1, 0, right)
     put(2, 0, far_a)
     put(2, 16, far_b)
-
-
-def pair_join_kernel(at_ref, flipped, pair, near):
     z_lo = at_ref[0] >> 3
     near[pl.ds(pl.multiple_of(z_lo * 32, 32), 32)] = flipped[...]
     near[pl.ds(pl.multiple_of((1 - z_lo) * 32, 32), 32)] = pair[...]
 
 
-def split_kernel(near, x_left, x_right, x_low, x_high, joined):
-    x_low[...] = x_left[:32]
-    x_high[...] = x_right[32:]
-    joined[:64] = near[...]
-    joined[64:128] = x_left[...]
-    joined[128:] = x_right[...]
-
-
-def stack_kernel(one, two, after, out):
+def gather_kernel(near, x_left, x_right, x_far_a, x_far_b, after, out):
+    first = 0
+    for ref in (near, x_left, x_right, x_far_a, x_far_b):
+        out[first : first + ref.shape[0]] = ref[...]
+        first += ref.shape[0]
+
+
+def stack_kernel(one, two, out):
     half = one.shape[0]
     out[:half] = one[...]
     out[half:] = two[...]
@@ -137,12 +137,9 @@
     own,
     left,
     right,
-    far_a,
-    far_b,
+    far,
     near,
-    near_far,
     other,
-    other_far,
     out,
     lhs,
     rhs,
@@ -162,19 +159,11 @@
     def _():
         y = col & 3
 
-        def put(by, start, ref):
-            first = pl.multiple_of(((y + by) & 3) * 128 + start, 64)
-            lhs[pl.ds(first, ref.shape[0])] = ref[...]
-
-        put(0, 0, own)
-        put(3, 0, left)
-        put(1, 0, right)
-        put(2, 0, far_a)
-        put(2, 64, far_b)
+        for by, ref in ((0, own), (3, left), (1, right), (2, far)):
+            lhs[pl.ds(pl.multiple_of(((y + by) & 3) * 128, 128), 128)] = ref[...]
         x, core = (row >> 1) & 3, row & 1
-        for swap, most, rest in ((0, near, near_far), (1, other, other_far)):
+        for swap, ref in ((0, near), (1, other)):
             for at, by in enumerate((0, 3, 1, 2)):
-                ref, at = (most, at) if at < 3 else (rest, 0)
                 y_from = (x + by - (col >> 1)) & 3
                 for z_lo in range(2):
                     z_from = z_lo * 2 + (core ^ swap)
@@ -276,44 +265,41 @@
     low, high = halves(left, right, 8000000000)
     far_a = lax.ppermute(low, "col", z_turn(1))
     far_b = lax.ppermute(high, "col", z_turn(-1))
-    mine = call(
-        z_join_kernel,
-        out_shape=shape(128, rows),
-        in_specs=[SCALAR] + [WHOLE] * 5,
-        out_specs=WHOLE,
-    )(at, slopes, left, right, far_a, far_b)
+    flipped = call(
+        same_kernel, out_shape=shape(32, rows), in_specs=[WHOLE] * 2, out_specs=WHOLE
+    )(flipped, low)
+    pair = lax.ppermute(flipped, "row", [(r, r ^ 8) for r in range(16)])
+    mine, near = call(
+        join_kernel,
+        out_shape=(shape(128, rows), shape(64, rows)),
+        in_specs=[SCALAR] + [WHOLE] * 7,
+        out_specs=(WHOLE,) * 2,
+    )(at, slopes, left, right, far_a, far_b, flipped, pair)
     left = lax.ppermute(mine, "col", y_turn(1))
     right = lax.ppermute(mine, "col", y_turn(-1))
-    pair = lax.ppermute(flipped, "row", [(r, r ^ 8) for r in range(16)])
-    near = call(
-        pair_join_kernel,
-        out_shape=shape(64, rows),
-        in_specs=[SCALAR] + [WHOLE] * 2,
-        out_specs=WHOLE,
-    )(at, flipped, pair)
     x_left = lax.ppermute(near, "row", x_turn(1))
     x_right = lax.ppermute(near, "row", x_turn(-1))
-    low, high = halves(left, right, 4000000000)
+    low, high = halves(left, right, 8000000000)
     far_a = lax.ppermute(low, "col", y_turn(1))
     far_b = lax.ppermute(high, "col", y_turn(-1))
-    x_low, x_high, near = call(
-        split_kernel,
-        out_shape=(shape(32, rows),) * 2 + (shape(192, rows),),
-        in_specs=[WHOLE] * 3,
-        out_specs=(WHOLE,) * 3,
-    )(near, x_left, x_right)
+    far = call(
+        stack_kernel,
+        out_shape=shape(128, rows),
+        in_specs=[WHOLE] * 2,
+        out_specs=WHOLE,
+        cost_estimate=pl.CostEstimate(flops=8000000000, bytes_accessed=983040, transcendentals=0),
+    )(far_a, far_b)
+    x_low, x_high = halves(x_left, x_right, 0)
     x_far_a = lax.ppermute(x_low, "row", x_turn(1))
     x_far_b = lax.ppermute(x_high, "row", x_turn(-1))
-    cores = [(r, r ^ 1) for r in range(16)]
-    other = lax.ppermute(near, "row", cores)
-    near_far = call(
-        stack_kernel, out_shape=shape(64, rows), in_specs=[WHOLE] * 3, out_specs=WHOLE
-    )(x_far_a, x_far_b, low)
-    other_far = lax.ppermute(near_far, "row", cores)
+    near = call(
+        gather_kernel, out_shape=shape(256, rows), in_specs=[WHOLE] * 6, out_specs=WHOLE
+    )(near, x_left, x_right, x_far_a, x_far_b, low)
+    other = lax.ppermute(near, "row", [(r, r ^ 1) for r in range(16)])
     return call(
         last_kernel,
         out_shape=shape(rows, rows),
-        in_specs=[SCALAR] + [WHOLE] * 9,
+        in_specs=[SCALAR] + [WHOLE] * 6,
         out_specs=pl.BlockSpec(memory_space=pl.ANY),
         scratch_shapes=[
             pltpu.VMEM((FRAMES, rows), BF16),
@@ -324,7 +310,7 @@
         cost_estimate=pl.CostEstimate(
             flops=2 * FRAMES * rows * rows, bytes_accessed=2 * rows * rows, transcendentals=0
         ),
-    )(at, mine, left, right, far_a, far_b, near, near_far, other, other_far)
+    )(at, mine, left, right, far, near, other)
 
 
 def solution(mesh):

time: 111 us -> 106 us (0.955)
  the two profiles are of different devices: /device:TPU:66 before, /device:TPU:24 now
where the time goes in v5:
time: 106 us; the launch traced here: 105 us
  waiting for transfers between devices  54.1 us (51%)
  starting transfers between devices  37 us (35%)
  Pallas kernels  9.16 us (9%)
  local copies, waits for them, and re-layouts  3.62 us (3%)
  other arithmetic  1.25 us (1%)
    ppermute x3, waiting for transfers between devices, per_device(): next_a = lax.ppermute(sent_a, 'col', swap_a)  12.6 us
    ppermute x1, waiting for transfers between devices, per_device(): got_b = lax.ppermute(sent_b, 'col', y_swap(3))  9.57 us
    ppermute x3, waiting for transfers between devices, per_device(): next_b = lax.ppermute(sent_b, 'col', swap_b)  7.38 us
    ppermute x3, starting transfers between devices, per_device(): next_b = lax.ppermute(sent_b, 'col', swap_b)  7.11 us
    pallas_call x1, Pallas kernels, per_device(): call(last_kernel, out_shape=shape(rows, rows), in_specs=[SCALAR] + [WHOLE...  6.01 us
    ppermute x1, waiting for transfers between devices, per_device(): x_right = lax.ppermute(near, 'row', x_turn(-1))  5.09 us
    ppermute x1, waiting for transfers between devices, per_device(): far_a = lax.ppermute(low, 'col', z_turn(1))  4.4 us
    ppermute x1, waiting for transfers between devices, per_device(): far_b = lax.ppermute(high, 'col', y_turn(-1))  3.99 us
  transfers between devices with their start and end apart: 23, of which 14 were waited for; matrix products, arithmetic and copies ran while one was open for 1% of the time, Pallas kernels for 1%

profile of v5, /device:TPU:24, one launch (start us, length us, event | category | flops | bytes accessed | tf_op | source)
XLA Modules:
  0.0 105.4 jit_solution(11754546738963007059)
XLA Ops:
  0.1 1.3 %copy-done = bf16[1920,320]{0,1:T(8,128)(2,1)S(1)} copy-done((bf16[1920,320]{0,1:T(8,128)(2,1)S(1)}, bf16[1920,320]{0,1:T(8,128)(2,1)}, u32[]{:S(2)}) %copy-start) | copy-done | bytes 1228824
  1.4 1.0 copy-done.2
  2.3 1.7 %shard_map.55 = (bf16[128,1920]{1,0:T(8,128)(2,1)S(1)}, bf16[128,1920]{1,0:T(8,128)(2,1)S(1)}, bf16[256,320]{1,0:T(8,128)(2,1)S(1)}) custom-call(s32[2]{0:T(128)S(1)} %pad_add_fusion.at_ref, bf16[320,512]{1,0:T(8,128)(2,1)S(1)} %copy-done.2, bf16[320,1920]{1,0:T(8,128)(2,1)S(1)} %bitcast.13), custom_call_target="tpu_custom_call" | custom-call | flops 314572800 | bytes 1600000 | tf_op jit(solution)/shard_map/pallas_call | solution.py:211
  4.0 2.0 %collective-permute-start.3 = (bf16[128,1920]{1,0:T(8,128)(2,1)S(1)}, bf16[128,1920]{1,0:T(8,128)(2,1)S(1)}, u32[]{:S(2)}, u32[]{:S(2)}) collective-permute-start(bf16[128,1920]{1,0:T(8,128)(2,1)S(1)} %get-tuple-element.22), channel_id=1, source_target_pairs={{0,3},{1,2},{2,1},{3,0},{4,7},{5,6},{6,5},{7,4},{8,11},{9,10},{10,... | collective-permute-start | bytes 1474568 | tf_op jit(solution)/shard_map/ppermute | solution.py:221
  6.7 1.3 %copy-done.1 = bf16[1920,320]{0,1:T(8,128)(2,1)S(1)} copy-done((bf16[1920,320]{0,1:T(8,128)(2,1)S(1)}, bf16[1920,320]{0,1:T(8,128)(2,1)}, u32[]{:S(2)}) %copy-start.1) | copy-done | bytes 1228824
  8.0 0.7 shard_map.56
  8.7 9.6 %collective-permute-done.3 = bf16[128,1920]{1,0:T(8,128)(2,1)S(1)} collective-permute-done((bf16[128,1920]{1,0:T(8,128)(2,1)S(1)}, bf16[128,1920]{1,0:T(8,128)(2,1)S(1)}, u32[]{:S(2)}, u32[]{:S(2)}) %collective-permute-start.3) | collective-permute-done | bytes 491552 | tf_op jit(solution)/shard_map/ppermute | solution.py:221
  18.7 2.0 %collective-permute-start.1 = (bf16[64,1920]{1,0:T(8,128)(2,1)S(1)}, bf16[64,1920]{1,0:T(8,128)(2,1)S(1)}, u32[]{:S(2)}, u32[]{:S(2)}) collective-permute-start(bf16[64,1920]{1,0:T(8,128)(2,1)S(1)} %get-tuple-element.32), channel_id=1, source_target_pairs={{0,3},{1,2},{2,1},{3,0},{4,7},{5,6},{6,5},{7,4},{8,11},{9,10},{10,... | collective-permute-start | bytes 737288 | tf_op jit(solution)/shard_map/ppermute | solution.py:238
  20.6 4.7 %collective-permute-done.4 = bf16[64,1920]{1,0:T(8,128)(2,1)S(1)} collective-permute-done((bf16[64,1920]{1,0:T(8,128)(2,1)S(1)}, bf16[64,1920]{1,0:T(8,128)(2,1)S(1)}, u32[]{:S(2)}, u32[]{:S(2)}) %collective-permute-start.4) | collective-permute-done | bytes 245792 | tf_op jit(solution)/shard_map/ppermute | solution.py:239
  25.4 6.4 %collective-permute-start.5 = (bf16[32,1920]{1,0:T(8,128)(2,1)S(1)}, bf16[32,1920]{1,0:T(8,128)(2,1)S(1)}, u32[]{:S(2)}, u32[]{:S(2)}) collective-permute-start(bf16[32,1920]{1,0:T(8,128)(2,1)S(1)} %get-tuple-element.38), channel_id=1, source_target_pairs={{0,12},{1,13},{2,14},{3,15},{4,8},{5,9},{6,10},{7,11},{8,4},{9,5},... | collective-permute-start | bytes 368648 | tf_op jit(solution)/shard_map/ppermute | solution.py:239
  31.9 1.5 %collective-permute-start.2 = (bf16[32,1920]{1,0:T(8,128)(2,1)S(1)}, bf16[32,1920]{1,0:T(8,128)(2,1)S(1)}, u32[]{:S(2)}, u32[]{:S(2)}) collective-permute-start(bf16[32,1920]{1,0:T(8,128)(2,1)S(1)} %get-tuple-element.36), channel_id=1, source_target_pairs={{0,4},{1,5},{2,6},{3,7},{4,0},{5,1},{6,2},{7,3},{8,12},{9,13},{10,... | collective-permute-start | bytes 368648 | tf_op jit(solution)/shard_map/ppermute | solution.py:238
  33.4 2.2 %collective-permute-done.5 = bf16[32,1920]{1,0:T(8,128)(2,1)S(1)} collective-permute-done((bf16[32,1920]{1,0:T(8,128)(2,1)S(1)}, bf16[32,1920]{1,0:T(8,128)(2,1)S(1)}, u32[]{:S(2)}, u32[]{:S(2)}) %collective-permute-start.5) | collective-permute-done | bytes 122912 | tf_op jit(solution)/shard_map/ppermute | solution.py:239
  36.3 5.1 %collective-permute-done.2 = bf16[32,1920]{1,0:T(8,128)(2,1)S(1)} collective-permute-done((bf16[32,1920]{1,0:T(8,128)(2,1)S(1)}, bf16[32,1920]{1,0:T(8,128)(2,1)S(1)}, u32[]{:S(2)}, u32[]{:S(2)}) %collective-permute-start.2) | collective-permute-done | bytes 122912 | tf_op jit(solution)/shard_map/ppermute | solution.py:238
  42.0 7.5 %collective-permute-done.6 = bf16[16,1920]{1,0:T(8,128)(2,1)S(1)} collective-permute-done((bf16[16,1920]{1,0:T(8,128)(2,1)S(1)}, bf16[16,1920]{1,0:T(8,128)(2,1)S(1)}, u32[]{:S(2)}, u32[]{:S(2)}) %collective-permute-start.6) | collective-permute-done | bytes 61472 | tf_op jit(solution)/shard_map/ppermute | solution.py:238
  49.8 2.9 %collective-permute-start.8 = (bf16[32,1920]{1,0:T(8,128)(2,1)S(1)}, bf16[32,1920]{1,0:T(8,128)(2,1)S(1)}, u32[]{:S(2)}, u32[]{:S(2)}) collective-permute-start(bf16[32,1920]{1,0:T(8,128)(2,1)S(1)} %fusion.2.own), channel_id=1, source_target_pairs={{0,4},{1,5},{2,6},{3,7},{4,8},{5,9},{6,10},{7,11},{8,12},{9,13},{1... | collective-permute-start | bytes 368648 | tf_op jit(solution)/shard_map/ppermute | solution.py:262
  52.7 2.4 %collective-permute-start.12 = (bf16[32,1920]{1,0:T(8,128)(2,1)S(1)}, bf16[32,1920]{1,0:T(8,128)(2,1)S(1)}, u32[]{:S(2)}, u32[]{:S(2)}) collective-permute-start(bf16[32,1920]{1,0:T(8,128)(2,1)S(1)} %fusion.2.own), channel_id=1, source_target_pairs={{0,0},{1,32},{2,64},{3,96},{4,16},{5,48},{6,80},{7,112},{8,128},{9... | collective-permute-start | bytes 368648 | tf_op jit(solution)/shard_map/ppermute | solution.py:264
  55.1 1.6 %collective-permute-done.9.right = bf16[32,1920]{1,0:T(8,128)(2,1)S(1)} collective-permute-done((bf16[32,1920]{1,0:T(8,128)(2,1)S(1)}, bf16[32,1920]{1,0:T(8,128)(2,1)S(1)}, u32[]{:S(2)}, u32[]{:S(2)}) %collective-permute-start.9) | collective-permute-done | bytes 122912 | tf_op jit(solution)/shard_map/ppermute | solution.py:263
  56.7 1.4 %collective-permute-done.8.left = bf16[32,1920]{1,0:T(8,128)(2,1)S(1)} collective-permute-done((bf16[32,1920]{1,0:T(8,128)(2,1)S(1)}, bf16[32,1920]{1,0:T(8,128)(2,1)S(1)}, u32[]{:S(2)}, u32[]{:S(2)}) %collective-permute-start.8) | collective-permute-done | bytes 122912 | tf_op jit(solution)/shard_map/ppermute | solution.py:262
  58.1 3.3 %collective-permute-done.12.flipped = bf16[32,1920]{1,0:T(8,128)(2,1)S(1)} collective-permute-done((bf16[32,1920]{1,0:T(8,128)(2,1)S(1)}, bf16[32,1920]{1,0:T(8,128)(2,1)S(1)}, u32[]{:S(2)}, u32[]{:S(2)}) %collective-permute-start.12) | collective-permute-done | bytes 122912 | tf_op jit(solution)/shard_map/ppermute | solution.py:264
  61.5 2.9 %collective-permute-start.13 = (bf16[32,1920]{1,0:T(8,128)(2,1)S(1)}, bf16[32,1920]{1,0:T(8,128)(2,1)S(1)}, u32[]{:S(2)}, u32[]{:S(2)}) collective-permute-start(bf16[32,1920]{1,0:T(8,128)(2,1)S(1)} %shard_map.58.flipped), channel_id=1, source_target_pairs={{0,128},{16,144},{32,160},{48,176},{64,192},{80,208},{96,224},{112... | collective-permute-start | bytes 368648 | tf_op jit(solution)/shard_map/ppermute | solution.py:271
  64.3 3.9 %collective-permute-start.11 = (bf16[16,1920]{1,0:T(8,128)(2,1)S(1)}, bf16[16,1920]{1,0:T(8,128)(2,1)S(1)}, u32[]{:S(2)}, u32[]{:S(2)}) collective-permute-start(bf16[16,1920]{1,0:T(8,128)(2,1)S(1)} %get-tuple-element.24), channel_id=1, source_target_pairs={{0,12},{1,13},{2,14},{3,15},{4,0},{5,1},{6,2},{7,3},{8,4},{9,5},{1... | collective-permute-start | bytes 184328 | tf_op jit(solution)/shard_map/ppermute | solution.py:267
  68.2 2.0 %collective-permute-done.11.far_b = bf16[16,1920]{1,0:T(8,128)(2,1)S(1)} collective-permute-done((bf16[16,1920]{1,0:T(8,128)(2,1)S(1)}, bf16[16,1920]{1,0:T(8,128)(2,1)S(1)}, u32[]{:S(2)}, u32[]{:S(2)}) %collective-permute-start.11) | collective-permute-done | bytes 61472 | tf_op jit(solution)/shard_map/ppermute | solution.py:267
  70.2 4.4 %collective-permute-done.10.far_a = bf16[16,1920]{1,0:T(8,128)(2,1)S(1)} collective-permute-done((bf16[16,1920]{1,0:T(8,128)(2,1)S(1)}, bf16[16,1920]{1,0:T(8,128)(2,1)S(1)}, u32[]{:S(2)}, u32[]{:S(2)}) %collective-permute-start.10) | collective-permute-done | bytes 61472 | tf_op jit(solution)/shard_map/ppermute | solution.py:266
  75.3 3.2 %collective-permute-start.14 = (bf16[128,1920]{1,0:T(8,128)(2,1)S(1)}, bf16[128,1920]{1,0:T(8,128)(2,1)S(1)}, u32[]{:S(2)}, u32[]{:S(2)}) collective-permute-start(bf16[128,1920]{1,0:T(8,128)(2,1)S(1)} %get-tuple-element.25.own), channel_id=1, source_target_pairs={{0,1},{1,2},{2,3},{3,0},{4,5},{5,6},{6,7},{7,4},{8,9},{9,10},{10,1... | collective-permute-start | bytes 1474568 | tf_op jit(solution)/shard_map/ppermute | solution.py:278
  78.5 1.1 %collective-permute-start.19 = (bf16[64,1920]{1,0:T(8,128)(2,1)S(1)}, bf16[64,1920]{1,0:T(8,128)(2,1)S(1)}, u32[]{:S(2)}, u32[]{:S(2)}) collective-permute-start(bf16[64,1920]{1,0:T(8,128)(2,1)S(1)} %get-tuple-element.28.near), channel_id=1, source_target_pairs={{0,96},{16,112},{32,0},{48,16},{64,32},{80,48},{96,64},{112,80},{1... | collective-permute-start | bytes 737288 | tf_op jit(solution)/shard_map/ppermute | solution.py:281
  79.6 0.9 collective-permute-start.18
  80.5 5.1 %collective-permute-done.19.right.x_right = bf16[64,1920]{1,0:T(8,128)(2,1)S(1)} collective-permute-done((bf16[64,1920]{1,0:T(8,128)(2,1)S(1)}, bf16[64,1920]{1,0:T(8,128)(2,1)S(1)}, u32[]{:S(2)}, u32[]{:S(2)}) %collective-permute-start.19) | collective-permute-done | bytes 245792 | tf_op jit(solution)/shard_map/ppermute | solution.py:281
  85.6 2.7 %collective-permute-done.18.left.x_left = bf16[64,1920]{1,0:T(8,128)(2,1)S(1)} collective-permute-done((bf16[64,1920]{1,0:T(8,128)(2,1)S(1)}, bf16[64,1920]{1,0:T(8,128)(2,1)S(1)}, u32[]{:S(2)}, u32[]{:S(2)}) %collective-permute-start.18) | collective-permute-done | bytes 245792 | tf_op jit(solution)/shard_map/ppermute | solution.py:280
  88.5 3.2 %collective-permute-start.21 = (bf16[32,1920]{1,0:T(8,128)(2,1)S(1)}, bf16[32,1920]{1,0:T(8,128)(2,1)S(1)}, u32[]{:S(2)}, u32[]{:S(2)}) collective-permute-start(bf16[32,1920]{1,0:T(8,128)(2,1)S(1)} %get-tuple-element.30), channel_id=1, source_target_pairs={{0,96},{16,112},{32,0},{48,16},{64,32},{80,48},{96,64},{112,80},{1... | collective-permute-start | bytes 368648 | tf_op jit(solution)/shard_map/ppermute | solution.py:294
  91.8 3.2 %collective-permute-start.16 = (bf16[64,1920]{1,0:T(8,128)(2,1)S(1)}, bf16[64,1920]{1,0:T(8,128)(2,1)S(1)}, u32[]{:S(2)}, u32[]{:S(2)}) collective-permute-start(bf16[64,1920]{1,0:T(8,128)(2,1)S(1)} %get-tuple-element.26.after), channel_id=1, source_target_pairs={{0,1},{1,2},{2,3},{3,0},{4,5},{5,6},{6,7},{7,4},{8,9},{9,10},{10,1... | collective-permute-start | bytes 737288 | tf_op jit(solution)/shard_map/ppermute | solution.py:283
  95.2 4.0 %collective-permute-done.17.two = bf16[64,1920]{1,0:T(8,128)(2,1)S(1)} collective-permute-done((bf16[64,1920]{1,0:T(8,128)(2,1)S(1)}, bf16[64,1920]{1,0:T(8,128)(2,1)S(1)}, u32[]{:S(2)}, u32[]{:S(2)}) %collective-permute-start.17) | collective-permute-done | bytes 245792 | tf_op jit(solution)/shard_map/ppermute | solution.py:284
  99.3 6.0 %shard_map.64 = bf16[1920,1920]{1,0:T(8,128)(2,1)} custom-call(s32[2]{0:T(128)S(1)} %pad_add_fusion.at_ref, bf16[128,1920]{1,0:T(8,128)(2,1)S(1)} %get-tuple-element.25.own, bf16[128,1920]{1,0:T(8,128)(2,1)S(1)} %collective-permute-done.14.left, bf16[128,1920]{1,0:T(8,128)(2,1)S(1)} %collective-permute-done.15.right, bf16[128,1920]{1,0:T(8,128)(2,1)S(1)} %shard_map.61.far, ...), custom_call_target="tpu_custom_call" | custom-call | flops 3774873600 | bytes 7372800 | tf_op jit(solution)/shard_map/pallas_call | solution.py:299
  (45 shorter events, 3.8 us)
Async XLA Ops:
  0.0 41.6 %copy-start.4 = (s32[32]{0:T(128)S(1)}, s32[32]{0:T(128)}, u32[]{:S(2)}) copy-start(s32[32]{0:T(128)} %param.9) | copy-start | bytes 388
  0.1 1.3 %copy-start = (bf16[1920,320]{0,1:T(8,128)(2,1)S(1)}, bf16[1920,320]{0,1:T(8,128)(2,1)}, u32[]{:S(2)}) copy-start(bf16[1920,320]{0,1:T(8,128)(2,1)} %param.6) | copy-start | bytes 3686404
  1.4 1.0 copy-start.2
  2.3 47.2 %copy-start.3 = (bf16[1920,32]{0,1:T(8,128)(2,1)S(1)}, bf16[1920,32]{0,1:T(8,128)(2,1)}, u32[]{:S(2)}) copy-start(bf16[1920,32]{0,1:T(8,128)(2,1)} %param.5) | copy-start | bytes 368644
  4.0 14.3 %collective-permute-start.3 = (bf16[128,1920]{1,0:T(8,128)(2,1)S(1)}, bf16[128,1920]{1,0:T(8,128)(2,1)S(1)}, u32[]{:S(2)}, u32[]{:S(2)}) collective-permute-start(bf16[128,1920]{1,0:T(8,128)(2,1)S(1)} %get-tuple-element.22), channel_id=1, source_target_pairs={{0,3},{1,2},{2,1},{3,0},{4,7},{5,6},{6,5},{7,4},{8,11},{9,10},{10,... | collective-permute-start | bytes 1474568 | tf_op jit(solution)/shard_map/ppermute | solution.py:221
  6.1 12.4 %collective-permute-start = (bf16[128,1920]{1,0:T(8,128)(2,1)S(1)}, bf16[128,1920]{1,0:T(8,128)(2,1)S(1)}, u32[]{:S(2)}, u32[]{:S(2)}) collective-permute-start(bf16[128,1920]{1,0:T(8,128)(2,1)S(1)} %get-tuple-element.20), channel_id=1, source_target_pairs={{0,1},{1,0},{2,3},{3,2},{4,5},{5,4},{6,7},{7,6},{8,9},{9,8},{10,11... | collective-permute-start | bytes 1474568 | tf_op jit(solution)/shard_map/ppermute | solution.py:220
  6.7 1.3 %copy-start.1 = (bf16[1920,320]{0,1:T(8,128)(2,1)S(1)}, bf16[1920,320]{0,1:T(8,128)(2,1)}, u32[]{:S(2)}) copy-start(bf16[1920,320]{0,1:T(8,128)(2,1)} %param.6) | copy-start | bytes 3686404
  18.4 6.9 %collective-permute-start.4 = (bf16[64,1920]{1,0:T(8,128)(2,1)S(1)}, bf16[64,1920]{1,0:T(8,128)(2,1)S(1)}, u32[]{:S(2)}, u32[]{:S(2)}) collective-permute-start(bf16[64,1920]{1,0:T(8,128)(2,1)S(1)} %get-tuple-element.34), channel_id=1, source_target_pairs={{0,1},{1,0},{2,3},{3,2},{4,5},{5,4},{6,7},{7,6},{8,9},{9,8},{10,11... | collective-permute-start | bytes 737288 | tf_op jit(solution)/shard_map/ppermute | solution.py:239
  18.7 13.1 %collective-permute-start.1 = (bf16[64,1920]{1,0:T(8,128)(2,1)S(1)}, bf16[64,1920]{1,0:T(8,128)(2,1)S(1)}, u32[]{:S(2)}, u32[]{:S(2)}) collective-permute-start(bf16[64,1920]{1,0:T(8,128)(2,1)S(1)} %get-tuple-element.32), channel_id=1, source_target_pairs={{0,3},{1,2},{2,1},{3,0},{4,7},{5,6},{6,5},{7,4},{8,11},{9,10},{10,... | collective-permute-start | bytes 737288 | tf_op jit(solution)/shard_map/ppermute | solution.py:238
  25.4 10.2 %collective-permute-start.5 = (bf16[32,1920]{1,0:T(8,128)(2,1)S(1)}, bf16[32,1920]{1,0:T(8,128)(2,1)S(1)}, u32[]{:S(2)}, u32[]{:S(2)}) collective-permute-start(bf16[32,1920]{1,0:T(8,128)(2,1)S(1)} %get-tuple-element.38), channel_id=1, source_target_pairs={{0,12},{1,13},{2,14},{3,15},{4,8},{5,9},{6,10},{7,11},{8,4},{9,5},... | collective-permute-start | bytes 368648 | tf_op jit(solution)/shard_map/ppermute | solution.py:239
  31.9 9.5 %collective-permute-start.2 = (bf16[32,1920]{1,0:T(8,128)(2,1)S(1)}, bf16[32,1920]{1,0:T(8,128)(2,1)S(1)}, u32[]{:S(2)}, u32[]{:S(2)}) collective-permute-start(bf16[32,1920]{1,0:T(8,128)(2,1)S(1)} %get-tuple-element.36), channel_id=1, source_target_pairs={{0,4},{1,5},{2,6},{3,7},{4,0},{5,1},{6,2},{7,3},{8,12},{9,13},{10,... | collective-permute-start | bytes 368648 | tf_op jit(solution)/shard_map/ppermute | solution.py:238
  35.7 6.4 %collective-permute-start.7 = (bf16[16,1920]{1,0:T(8,128)(2,1)S(1)}, bf16[16,1920]{1,0:T(8,128)(2,1)S(1)}, u32[]{:S(2)}, u32[]{:S(2)}) collective-permute-start(bf16[16,1920]{1,0:T(8,128)(2,1)S(1)} %get-tuple-element.41), channel_id=1, source_target_pairs={{0,4},{1,5},{2,6},{3,7},{4,0},{5,1},{6,2},{7,3},{8,12},{9,13},{10,... | collective-permute-start | bytes 184328 | tf_op jit(solution)/shard_map/ppermute | solution.py:239
  41.4 8.2 %collective-permute-start.6 = (bf16[16,1920]{1,0:T(8,128)(2,1)S(1)}, bf16[16,1920]{1,0:T(8,128)(2,1)S(1)}, u32[]{:S(2)}, u32[]{:S(2)}) collective-permute-start(bf16[16,1920]{1,0:T(8,128)(2,1)S(1)} %get-tuple-element.39), channel_id=1, source_target_pairs={{0,12},{1,13},{2,14},{3,15},{4,8},{5,9},{6,10},{7,11},{8,4},{9,5},... | collective-permute-start | bytes 184328 | tf_op jit(solution)/shard_map/ppermute | solution.py:238
  49.7 7.1 %collective-permute-start.9 = (bf16[32,1920]{1,0:T(8,128)(2,1)S(1)}, bf16[32,1920]{1,0:T(8,128)(2,1)S(1)}, u32[]{:S(2)}, u32[]{:S(2)}) collective-permute-start(bf16[32,1920]{1,0:T(8,128)(2,1)S(1)} %fusion.2.own), channel_id=1, source_target_pairs={{0,12},{1,13},{2,14},{3,15},{4,0},{5,1},{6,2},{7,3},{8,4},{9,5},{1... | collective-permute-start | bytes 368648 | tf_op jit(solution)/shard_map/ppermute | solution.py:263
  49.8 8.4 %collective-permute-start.8 = (bf16[32,1920]{1,0:T(8,128)(2,1)S(1)}, bf16[32,1920]{1,0:T(8,128)(2,1)S(1)}, u32[]{:S(2)}, u32[]{:S(2)}) collective-permute-start(bf16[32,1920]{1,0:T(8,128)(2,1)S(1)} %fusion.2.own), channel_id=1, source_target_pairs={{0,4},{1,5},{2,6},{3,7},{4,8},{5,9},{6,10},{7,11},{8,12},{9,13},{1... | collective-permute-start | bytes 368648 | tf_op jit(solution)/shard_map/ppermute | solution.py:262
  52.7 8.8 %collective-permute-start.12 = (bf16[32,1920]{1,0:T(8,128)(2,1)S(1)}, bf16[32,1920]{1,0:T(8,128)(2,1)S(1)}, u32[]{:S(2)}, u32[]{:S(2)}) collective-permute-start(bf16[32,1920]{1,0:T(8,128)(2,1)S(1)} %fusion.2.own), channel_id=1, source_target_pairs={{0,0},{1,32},{2,64},{3,96},{4,16},{5,48},{6,80},{7,112},{8,128},{9... | collective-permute-start | bytes 368648 | tf_op jit(solution)/shard_map/ppermute | solution.py:264
  61.5 13.1 %collective-permute-start.13 = (bf16[32,1920]{1,0:T(8,128)(2,1)S(1)}, bf16[32,1920]{1,0:T(8,128)(2,1)S(1)}, u32[]{:S(2)}, u32[]{:S(2)}) collective-permute-start(bf16[32,1920]{1,0:T(8,128)(2,1)S(1)} %shard_map.58.flipped), channel_id=1, source_target_pairs={{0,128},{16,144},{32,160},{48,176},{64,192},{80,208},{96,224},{112... | collective-permute-start | bytes 368648 | tf_op jit(solution)/shard_map/ppermute | solution.py:271
  64.3 5.9 %collective-permute-start.11 = (bf16[16,1920]{1,0:T(8,128)(2,1)S(1)}, bf16[16,1920]{1,0:T(8,128)(2,1)S(1)}, u32[]{:S(2)}, u32[]{:S(2)}) collective-permute-start(bf16[16,1920]{1,0:T(8,128)(2,1)S(1)} %get-tuple-element.24), channel_id=1, source_target_pairs={{0,12},{1,13},{2,14},{3,15},{4,0},{5,1},{6,2},{7,3},{8,4},{9,5},{1... | collective-permute-start | bytes 184328 | tf_op jit(solution)/shard_map/ppermute | solution.py:267
  68.2 6.4 %collective-permute-start.10 = (bf16[16,1920]{1,0:T(8,128)(2,1)S(1)}, bf16[16,1920]{1,0:T(8,128)(2,1)S(1)}, u32[]{:S(2)}, u32[]{:S(2)}) collective-permute-start(bf16[16,1920]{1,0:T(8,128)(2,1)S(1)} %get-tuple-element.23.after), channel_id=1, source_target_pairs={{0,4},{1,5},{2,6},{3,7},{4,8},{5,9},{6,10},{7,11},{8,12},{9,13},{1... | collective-permute-start | bytes 184328 | tf_op jit(solution)/shard_map/ppermute | solution.py:266
  75.2 16.5 %collective-permute-start.15 = (bf16[128,1920]{1,0:T(8,128)(2,1)S(1)}, bf16[128,1920]{1,0:T(8,128)(2,1)S(1)}, u32[]{:S(2)}, u32[]{:S(2)}) collective-permute-start(bf16[128,1920]{1,0:T(8,128)(2,1)S(1)} %get-tuple-element.25.own), channel_id=1, source_target_pairs={{0,3},{1,0},{2,1},{3,2},{4,7},{5,4},{6,5},{7,6},{8,11},{9,8},{10,9... | collective-permute-start | bytes 1474568 | tf_op jit(solution)/shard_map/ppermute | solution.py:279
  75.3 16.4 %collective-permute-start.14 = (bf16[128,1920]{1,0:T(8,128)(2,1)S(1)}, bf16[128,1920]{1,0:T(8,128)(2,1)S(1)}, u32[]{:S(2)}, u32[]{:S(2)}) collective-permute-start(bf16[128,1920]{1,0:T(8,128)(2,1)S(1)} %get-tuple-element.25.own), channel_id=1, source_target_pairs={{0,1},{1,2},{2,3},{3,0},{4,5},{5,6},{6,7},{7,4},{8,9},{9,10},{10,1... | collective-permute-start | bytes 1474568 | tf_op jit(solution)/shard_map/ppermute | solution.py:278
  78.5 7.1 %collective-permute-start.19 = (bf16[64,1920]{1,0:T(8,128)(2,1)S(1)}, bf16[64,1920]{1,0:T(8,128)(2,1)S(1)}, u32[]{:S(2)}, u32[]{:S(2)}) collective-permute-start(bf16[64,1920]{1,0:T(8,128)(2,1)S(1)} %get-tuple-element.28.near), channel_id=1, source_target_pairs={{0,96},{16,112},{32,0},{48,16},{64,32},{80,48},{96,64},{112,80},{1... | collective-permute-start | bytes 737288 | tf_op jit(solution)/shard_map/ppermute | solution.py:281
  79.6 8.7 %collective-permute-start.18 = (bf16[64,1920]{1,0:T(8,128)(2,1)S(1)}, bf16[64,1920]{1,0:T(8,128)(2,1)S(1)}, u32[]{:S(2)}, u32[]{:S(2)}) collective-permute-start(bf16[64,1920]{1,0:T(8,128)(2,1)S(1)} %get-tuple-element.28.near), channel_id=1, source_target_pairs={{0,32},{16,48},{32,64},{48,80},{64,96},{80,112},{96,0},{112,16},{1... | collective-permute-start | bytes 737288 | tf_op jit(solution)/shard_map/ppermute | solution.py:280
  88.4 6.7 %collective-permute-start.20 = (bf16[32,1920]{1,0:T(8,128)(2,1)S(1)}, bf16[32,1920]{1,0:T(8,128)(2,1)S(1)}, u32[]{:S(2)}, u32[]{:S(2)}) collective-permute-start(bf16[32,1920]{1,0:T(8,128)(2,1)S(1)} %get-tuple-element.29), channel_id=1, source_target_pairs={{0,32},{16,48},{32,64},{48,80},{64,96},{80,112},{96,0},{112,16},{1... | collective-permute-start | bytes 368648 | tf_op jit(solution)/shard_map/ppermute | solution.py:293
  88.5 6.6 %collective-permute-start.21 = (bf16[32,1920]{1,0:T(8,128)(2,1)S(1)}, bf16[32,1920]{1,0:T(8,128)(2,1)S(1)}, u32[]{:S(2)}, u32[]{:S(2)}) collective-permute-start(bf16[32,1920]{1,0:T(8,128)(2,1)S(1)} %get-tuple-element.30), channel_id=1, source_target_pairs={{0,96},{16,112},{32,0},{48,16},{64,32},{80,48},{96,64},{112,80},{1... | collective-permute-start | bytes 368648 | tf_op jit(solution)/shard_map/ppermute | solution.py:294
  91.7 7.5 %collective-permute-start.17 = (bf16[64,1920]{1,0:T(8,128)(2,1)S(1)}, bf16[64,1920]{1,0:T(8,128)(2,1)S(1)}, u32[]{:S(2)}, u32[]{:S(2)}) collective-permute-start(bf16[64,1920]{1,0:T(8,128)(2,1)S(1)} %get-tuple-element.27), channel_id=1, source_target_pairs={{0,3},{1,0},{2,1},{3,2},{4,7},{5,4},{6,5},{7,6},{8,11},{9,8},{10,9... | collective-permute-start | bytes 737288 | tf_op jit(solution)/shard_map/ppermute | solution.py:284
  91.8 7.4 %collective-permute-start.16 = (bf16[64,1920]{1,0:T(8,128)(2,1)S(1)}, bf16[64,1920]{1,0:T(8,128)(2,1)S(1)}, u32[]{:S(2)}, u32[]{:S(2)}) collective-permute-start(bf16[64,1920]{1,0:T(8,128)(2,1)S(1)} %get-tuple-element.26.after), channel_id=1, source_target_pairs={{0,1},{1,2},{2,3},{3,0},{4,5},{5,6},{6,7},{7,4},{8,9},{9,10},{10,1... | collective-permute-start | bytes 737288 | tf_op jit(solution)/shard_map/ppermute | solution.py:283
  95.1 4.1 %collective-permute-start.22 = (bf16[256,1920]{1,0:T(8,128)(2,1)S(1)}, bf16[256,1920]{1,0:T(8,128)(2,1)S(1)}, u32[]{:S(2)}, u32[]{:S(2)}) collective-permute-start(bf16[256,1920]{1,0:T(8,128)(2,1)S(1)} %shard_map.63.near), channel_id=1, source_target_pairs={{0,16},{16,0},{32,48},{48,32},{64,80},{80,64},{96,112},{112,96},{1... | collective-permute-start | bytes 2949128 | tf_op jit(solution)/shard_map/ppermute | solution.py:298

commit v6 on v5

--- a/solution.py
+++ b/solution.py
@@ -35,14 +35,15 @@
     return [(r, (r & 9) | ((r + 2 * by) & 6)) for r in range(16)]
 
 
-def flip_pairs():
+def flip_pairs(which):
     pairs = []
     for r in range(16):
         for c in range(16):
             z_hi, y = c >> 2, c & 3
             x = (((r >> 1) & 3) + y) & 3
-            to = (z_hi >> 1) * 8 + x * 2 + (z_hi & 1)
-            pairs.append((r * 16 + c, to * 16 + r))
+            z_lo = (z_hi >> 1) ^ which
+            if r >= 8 or z_lo == 0:
+                pairs.append((r * 16 + c, (z_lo * 8 + x * 2 + (z_hi & 1)) * 16 + r))
     return pairs
 
 
@@ -93,10 +94,6 @@
     half = low.shape[0]
     low[...] = left[:half]
     high[...] = right[half:]
-
-
-def same_kernel(flipped, after, out):
-    out[...] = flipped[...]
 
 
 def join_kernel(at_ref, own, left, right, far_a, far_b, flipped, pair, mine, near):
@@ -261,14 +258,11 @@
 
     left = lax.ppermute(slopes, "col", z_turn(1))
     right = lax.ppermute(slopes, "col", z_turn(-1))
-    flipped = lax.ppermute(slopes, ("row", "col"), flip_pairs())
+    flipped = lax.ppermute(slopes, ("row", "col"), flip_pairs(0))
+    pair = lax.ppermute(slopes, ("row", "col"), flip_pairs(1))
     low, high = halves(left, right, 8000000000)
     far_a = lax.ppermute(low, "col", z_turn(1))
     far_b = lax.ppermute(high, "col", z_turn(-1))
-    flipped = call(
-        same_kernel, out_shape=shape(32, rows), in_specs=[WHOLE] * 2, out_specs=WHOLE
-    )(flipped, low)
-    pair = lax.ppermute(flipped, "row", [(r, r ^ 8) for r in range(16)])
     mine, near = call(
         join_kernel,
         out_shape=(shape(128, rows), shape(64, rows)),

time: 106 us -> 101 us (0.953)
  the two profiles are of different devices: /device:TPU:24 before, /device:TPU:128 now
where the time goes in v6:
time: 101 us
  waiting for transfers between devices  46.9 us (46%)
  starting transfers between devices  39.7 us (39%)
  Pallas kernels  9.16 us (9%)
  local copies, waits for them, and re-layouts  3.62 us (4%)
  other arithmetic  1.25 us (1%)
    ppermute x3, waiting for transfers between devices, per_device(): next_b = lax.ppermute(sent_b, 'col', swap_b)  8.59 us
    ppermute x1, waiting for transfers between devices, per_device(): got_b = lax.ppermute(sent_b, 'col', y_swap(3))  8.43 us
    ppermute x3, waiting for transfers between devices, per_device(): next_a = lax.ppermute(sent_a, 'col', swap_a)  7.04 us
    ppermute x1, starting transfers between devices, per_device(): right = lax.ppermute(mine, 'col', y_turn(-1))  6.95 us
    pallas_call x1, Pallas kernels, per_device(): call(last_kernel, out_shape=shape(rows, rows), in_specs=[SCALAR] + [WHOLE...  6.01 us
    ppermute x1, waiting for transfers between devices, per_device(): x_right = lax.ppermute(near, 'row', x_turn(-1))  6 us
    ppermute x1, starting transfers between devices, per_device(): pair = lax.ppermute(slopes, ('row', 'col'), flip_pairs(1))  5.76 us
    ppermute x1, waiting for transfers between devices, per_device(): flipped = lax.ppermute(slopes, ('row', 'col'), flip_pairs(0))  4.24 us
  transfers between devices with their start and end apart: 23, of which 14 were waited for; matrix products, arithmetic and copies ran while one was open for 1% of the time, Pallas kernels for 1%

profile of v6, /device:TPU:128, one launch (start us, length us, event | category | flops | bytes accessed | tf_op | source)
XLA Modules:
  0.0 101.0 jit_solution(164699112780138143)
XLA Ops:
  0.1 1.3 %copy-done = bf16[1920,320]{0,1:T(8,128)(2,1)S(1)} copy-done((bf16[1920,320]{0,1:T(8,128)(2,1)S(1)}, bf16[1920,320]{0,1:T(8,128)(2,1)}, u32[]{:S(2)}) %copy-start) | copy-done | bytes 1228824
  1.4 1.0 copy-done.2
  2.3 1.7 %shard_map.55 = (bf16[128,1920]{1,0:T(8,128)(2,1)S(1)}, bf16[128,1920]{1,0:T(8,128)(2,1)S(1)}, bf16[256,320]{1,0:T(8,128)(2,1)S(1)}) custom-call(s32[2]{0:T(128)S(1)} %pad_add_fusion.at_ref, bf16[320,512]{1,0:T(8,128)(2,1)S(1)} %copy-done.2, bf16[320,1920]{1,0:T(8,128)(2,1)S(1)} %bitcast.13), custom_call_target="tpu_custom_call" | custom-call | flops 314572800 | bytes 1600000 | tf_op jit(solution)/shard_map/pallas_call | solution.py:208
  4.0 3.1 %collective-permute-start.3 = (bf16[128,1920]{1,0:T(8,128)(2,1)S(1)}, bf16[128,1920]{1,0:T(8,128)(2,1)S(1)}, u32[]{:S(2)}, u32[]{:S(2)}) collective-permute-start(bf16[128,1920]{1,0:T(8,128)(2,1)S(1)} %get-tuple-element.22), channel_id=1, source_target_pairs={{0,3},{1,2},{2,1},{3,0},{4,7},{5,6},{6,5},{7,4},{8,11},{9,10},{10,... | collective-permute-start | bytes 1474568 | tf_op jit(solution)/shard_map/ppermute | solution.py:218
  7.9 1.3 %copy-done.1 = bf16[1920,320]{0,1:T(8,128)(2,1)S(1)} copy-done((bf16[1920,320]{0,1:T(8,128)(2,1)S(1)}, bf16[1920,320]{0,1:T(8,128)(2,1)}, u32[]{:S(2)}) %copy-start.1) | copy-done | bytes 1228824
  9.9 8.4 %collective-permute-done.3 = bf16[128,1920]{1,0:T(8,128)(2,1)S(1)} collective-permute-done((bf16[128,1920]{1,0:T(8,128)(2,1)S(1)}, bf16[128,1920]{1,0:T(8,128)(2,1)S(1)}, u32[]{:S(2)}, u32[]{:S(2)}) %collective-permute-start.3) | collective-permute-done | bytes 491552 | tf_op jit(solution)/shard_map/ppermute | solution.py:218
  18.9 1.0 collective-permute-done
  19.9 1.8 %collective-permute-start.1 = (bf16[64,1920]{1,0:T(8,128)(2,1)S(1)}, bf16[64,1920]{1,0:T(8,128)(2,1)S(1)}, u32[]{:S(2)}, u32[]{:S(2)}) collective-permute-start(bf16[64,1920]{1,0:T(8,128)(2,1)S(1)} %get-tuple-element.32), channel_id=1, source_target_pairs={{0,3},{1,2},{2,1},{3,0},{4,7},{5,6},{6,5},{7,4},{8,11},{9,10},{10,... | collective-permute-start | bytes 737288 | tf_op jit(solution)/shard_map/ppermute | solution.py:235
  21.8 3.7 %collective-permute-done.4 = bf16[64,1920]{1,0:T(8,128)(2,1)S(1)} collective-permute-done((bf16[64,1920]{1,0:T(8,128)(2,1)S(1)}, bf16[64,1920]{1,0:T(8,128)(2,1)S(1)}, u32[]{:S(2)}, u32[]{:S(2)}) %collective-permute-start.4) | collective-permute-done | bytes 245792 | tf_op jit(solution)/shard_map/ppermute | solution.py:236
  25.6 2.1 %collective-permute-done.1 = bf16[64,1920]{1,0:T(8,128)(2,1)S(1)} collective-permute-done((bf16[64,1920]{1,0:T(8,128)(2,1)S(1)}, bf16[64,1920]{1,0:T(8,128)(2,1)S(1)}, u32[]{:S(2)}, u32[]{:S(2)}) %collective-permute-start.1) | collective-permute-done | bytes 245792 | tf_op jit(solution)/shard_map/ppermute | solution.py:235
  27.8 1.6 %collective-permute-start.2 = (bf16[32,1920]{1,0:T(8,128)(2,1)S(1)}, bf16[32,1920]{1,0:T(8,128)(2,1)S(1)}, u32[]{:S(2)}, u32[]{:S(2)}) collective-permute-start(bf16[32,1920]{1,0:T(8,128)(2,1)S(1)} %get-tuple-element.36), channel_id=1, source_target_pairs={{0,4},{1,5},{2,6},{3,7},{4,0},{5,1},{6,2},{7,3},{8,12},{9,13},{10,... | collective-permute-start | bytes 368648 | tf_op jit(solution)/shard_map/ppermute | solution.py:235
  29.4 3.7 %collective-permute-done.5 = bf16[32,1920]{1,0:T(8,128)(2,1)S(1)} collective-permute-done((bf16[32,1920]{1,0:T(8,128)(2,1)S(1)}, bf16[32,1920]{1,0:T(8,128)(2,1)S(1)}, u32[]{:S(2)}, u32[]{:S(2)}) %collective-permute-start.5) | collective-permute-done | bytes 122912 | tf_op jit(solution)/shard_map/ppermute | solution.py:236
  33.1 2.5 %collective-permute-start.7 = (bf16[16,1920]{1,0:T(8,128)(2,1)S(1)}, bf16[16,1920]{1,0:T(8,128)(2,1)S(1)}, u32[]{:S(2)}, u32[]{:S(2)}) collective-permute-start(bf16[16,1920]{1,0:T(8,128)(2,1)S(1)} %get-tuple-element.41), channel_id=1, source_target_pairs={{0,4},{1,5},{2,6},{3,7},{4,0},{5,1},{6,2},{7,3},{8,12},{9,13},{10,... | collective-permute-start | bytes 184328 | tf_op jit(solution)/shard_map/ppermute | solution.py:236
  37.1 1.2 %collective-permute-done.7 = bf16[16,1920]{1,0:T(8,128)(2,1)S(1)} collective-permute-done((bf16[16,1920]{1,0:T(8,128)(2,1)S(1)}, bf16[16,1920]{1,0:T(8,128)(2,1)S(1)}, u32[]{:S(2)}, u32[]{:S(2)}) %collective-permute-start.7) | collective-permute-done | bytes 61472 | tf_op jit(solution)/shard_map/ppermute | solution.py:236
  38.3 4.3 %collective-permute-done.6 = bf16[16,1920]{1,0:T(8,128)(2,1)S(1)} collective-permute-done((bf16[16,1920]{1,0:T(8,128)(2,1)S(1)}, bf16[16,1920]{1,0:T(8,128)(2,1)S(1)}, u32[]{:S(2)}, u32[]{:S(2)}) %collective-permute-start.6) | collective-permute-done | bytes 61472 | tf_op jit(solution)/shard_map/ppermute | solution.py:235
  42.7 0.8 collective-permute-start.9
  43.5 2.2 %collective-permute-start.8 = (bf16[32,1920]{1,0:T(8,128)(2,1)S(1)}, bf16[32,1920]{1,0:T(8,128)(2,1)S(1)}, u32[]{:S(2)}, u32[]{:S(2)}) collective-permute-start(bf16[32,1920]{1,0:T(8,128)(2,1)S(1)} %fusion.2.own), channel_id=1, source_target_pairs={{0,4},{1,5},{2,6},{3,7},{4,8},{5,9},{6,10},{7,11},{8,12},{9,13},{1... | collective-permute-start | bytes 368648 | tf_op jit(solution)/shard_map/ppermute | solution.py:259
  45.7 5.8 %collective-permute-start.13 = (bf16[32,1920]{1,0:T(8,128)(2,1)S(1)}, bf16[32,1920]{1,0:T(8,128)(2,1)S(1)}, u32[]{:S(2)}, u32[]{:S(2)}) collective-permute-start(bf16[32,1920]{1,0:T(8,128)(2,1)S(1)} %fusion.2.own), channel_id=1, source_target_pairs={{8,0},{9,32},{10,64},{11,96},{12,16},{13,48},{14,80},{15,112},{24,... | collective-permute-start | bytes 368648 | tf_op jit(solution)/shard_map/ppermute | solution.py:262
  51.5 1.3 %collective-permute-start.12 = (bf16[32,1920]{1,0:T(8,128)(2,1)S(1)}, bf16[32,1920]{1,0:T(8,128)(2,1)S(1)}, u32[]{:S(2)}, u32[]{:S(2)}) collective-permute-start(bf16[32,1920]{1,0:T(8,128)(2,1)S(1)} %fusion.2.own), channel_id=1, source_target_pairs={{0,0},{1,32},{2,64},{3,96},{4,16},{5,48},{6,80},{7,112},{16,1},{17... | collective-permute-start | bytes 368648 | tf_op jit(solution)/shard_map/ppermute | solution.py:261
  52.9 4.1 %collective-permute-start.11 = (bf16[16,1920]{1,0:T(8,128)(2,1)S(1)}, bf16[16,1920]{1,0:T(8,128)(2,1)S(1)}, u32[]{:S(2)}, u32[]{:S(2)}) collective-permute-start(bf16[16,1920]{1,0:T(8,128)(2,1)S(1)} %get-tuple-element.24), channel_id=1, source_target_pairs={{0,12},{1,13},{2,14},{3,15},{4,0},{5,1},{6,2},{7,3},{8,4},{9,5},{1... | collective-permute-start | bytes 184328 | tf_op jit(solution)/shard_map/ppermute | solution.py:265
  57.0 4.2 %collective-permute-done.12.flipped = bf16[32,1920]{1,0:T(8,128)(2,1)S(1)} collective-permute-done((bf16[32,1920]{1,0:T(8,128)(2,1)S(1)}, bf16[32,1920]{1,0:T(8,128)(2,1)S(1)}, u32[]{:S(2)}, u32[]{:S(2)}) %collective-permute-start.12) | collective-permute-done | bytes 122912 | tf_op jit(solution)/shard_map/ppermute | solution.py:261
  61.9 7.0 %collective-permute-start.15 = (bf16[128,1920]{1,0:T(8,128)(2,1)S(1)}, bf16[128,1920]{1,0:T(8,128)(2,1)S(1)}, u32[]{:S(2)}, u32[]{:S(2)}) collective-permute-start(bf16[128,1920]{1,0:T(8,128)(2,1)S(1)} %get-tuple-element.25.own), channel_id=1, source_target_pairs={{0,3},{1,0},{2,1},{3,2},{4,7},{5,4},{6,5},{7,6},{8,11},{9,8},{10,9... | collective-permute-start | bytes 1474568 | tf_op jit(solution)/shard_map/ppermute | solution.py:273
  68.8 2.6 %collective-permute-start.19 = (bf16[64,1920]{1,0:T(8,128)(2,1)S(1)}, bf16[64,1920]{1,0:T(8,128)(2,1)S(1)}, u32[]{:S(2)}, u32[]{:S(2)}) collective-permute-start(bf16[64,1920]{1,0:T(8,128)(2,1)S(1)} %get-tuple-element.28.near), channel_id=1, source_target_pairs={{0,96},{16,112},{32,0},{48,16},{64,32},{80,48},{96,64},{112,80},{1... | collective-permute-start | bytes 737288 | tf_op jit(solution)/shard_map/ppermute | solution.py:275
  71.5 6.0 %collective-permute-done.19.right.x_right = bf16[64,1920]{1,0:T(8,128)(2,1)S(1)} collective-permute-done((bf16[64,1920]{1,0:T(8,128)(2,1)S(1)}, bf16[64,1920]{1,0:T(8,128)(2,1)S(1)}, u32[]{:S(2)}, u32[]{:S(2)}) %collective-permute-start.19) | collective-permute-done | bytes 245792 | tf_op jit(solution)/shard_map/ppermute | solution.py:275
  77.5 3.4 %collective-permute-done.18.left.x_left = bf16[64,1920]{1,0:T(8,128)(2,1)S(1)} collective-permute-done((bf16[64,1920]{1,0:T(8,128)(2,1)S(1)}, bf16[64,1920]{1,0:T(8,128)(2,1)S(1)}, u32[]{:S(2)}, u32[]{:S(2)}) %collective-permute-start.18) | collective-permute-done | bytes 245792 | tf_op jit(solution)/shard_map/ppermute | solution.py:274
  81.0 3.2 %collective-permute-start.21 = (bf16[32,1920]{1,0:T(8,128)(2,1)S(1)}, bf16[32,1920]{1,0:T(8,128)(2,1)S(1)}, u32[]{:S(2)}, u32[]{:S(2)}) collective-permute-start(bf16[32,1920]{1,0:T(8,128)(2,1)S(1)} %get-tuple-element.30), channel_id=1, source_target_pairs={{0,96},{16,112},{32,0},{48,16},{64,32},{80,48},{96,64},{112,80},{1... | collective-permute-start | bytes 368648 | tf_op jit(solution)/shard_map/ppermute | solution.py:288
  84.2 0.8 collective-permute-start.17
  85.0 1.3 %collective-permute-start.16 = (bf16[64,1920]{1,0:T(8,128)(2,1)S(1)}, bf16[64,1920]{1,0:T(8,128)(2,1)S(1)}, u32[]{:S(2)}, u32[]{:S(2)}) collective-permute-start(bf16[64,1920]{1,0:T(8,128)(2,1)S(1)} %get-tuple-element.26.after), channel_id=1, source_target_pairs={{0,1},{1,2},{2,3},{3,0},{4,5},{5,6},{6,7},{7,4},{8,9},{9,10},{10,1... | collective-permute-start | bytes 737288 | tf_op jit(solution)/shard_map/ppermute | solution.py:277
  86.3 1.8 %collective-permute-done.20.x_far_a = bf16[32,1920]{1,0:T(8,128)(2,1)S(1)} collective-permute-done((bf16[32,1920]{1,0:T(8,128)(2,1)S(1)}, bf16[32,1920]{1,0:T(8,128)(2,1)S(1)}, u32[]{:S(2)}, u32[]{:S(2)}) %collective-permute-start.20) | collective-permute-done | bytes 122912 | tf_op jit(solution)/shard_map/ppermute | solution.py:287
  88.3 4.0 %collective-permute-done.17.two = bf16[64,1920]{1,0:T(8,128)(2,1)S(1)} collective-permute-done((bf16[64,1920]{1,0:T(8,128)(2,1)S(1)}, bf16[64,1920]{1,0:T(8,128)(2,1)S(1)}, u32[]{:S(2)}, u32[]{:S(2)}) %collective-permute-start.17) | collective-permute-done | bytes 245792 | tf_op jit(solution)/shard_map/ppermute | solution.py:278
  92.4 2.4 %collective-permute-done.16.one = bf16[64,1920]{1,0:T(8,128)(2,1)S(1)} collective-permute-done((bf16[64,1920]{1,0:T(8,128)(2,1)S(1)}, bf16[64,1920]{1,0:T(8,128)(2,1)S(1)}, u32[]{:S(2)}, u32[]{:S(2)}) %collective-permute-start.16) | collective-permute-done | bytes 245792 | tf_op jit(solution)/shard_map/ppermute | solution.py:277
  94.8 6.0 %shard_map.63 = bf16[1920,1920]{1,0:T(8,128)(2,1)} custom-call(s32[2]{0:T(128)S(1)} %pad_add_fusion.at_ref, bf16[128,1920]{1,0:T(8,128)(2,1)S(1)} %get-tuple-element.25.own, bf16[128,1920]{1,0:T(8,128)(2,1)S(1)} %collective-permute-done.14.left, bf16[128,1920]{1,0:T(8,128)(2,1)S(1)} %collective-permute-done.15.right, bf16[128,1920]{1,0:T(8,128)(2,1)S(1)} %shard_map.60.far, ...), custom_call_target="tpu_custom_call" | custom-call | flops 3774873600 | bytes 7372800 | tf_op jit(solution)/shard_map/pallas_call | solution.py:293
  (44 shorter events, 5.1 us)
Async XLA Ops:
  0.0 37.1 %copy-start.4 = (s32[32]{0:T(128)S(1)}, s32[32]{0:T(128)}, u32[]{:S(2)}) copy-start(s32[32]{0:T(128)} %param.9) | copy-start | bytes 388
  0.1 1.3 %copy-start = (bf16[1920,320]{0,1:T(8,128)(2,1)S(1)}, bf16[1920,320]{0,1:T(8,128)(2,1)}, u32[]{:S(2)}) copy-start(bf16[1920,320]{0,1:T(8,128)(2,1)} %param.6) | copy-start | bytes 3686404
  1.4 1.0 copy-start.2
  2.3 40.3 %copy-start.3 = (bf16[1920,32]{0,1:T(8,128)(2,1)S(1)}, bf16[1920,32]{0,1:T(8,128)(2,1)}, u32[]{:S(2)}) copy-start(bf16[1920,32]{0,1:T(8,128)(2,1)} %param.5) | copy-start | bytes 368644
  4.0 14.3 %collective-permute-start.3 = (bf16[128,1920]{1,0:T(8,128)(2,1)S(1)}, bf16[128,1920]{1,0:T(8,128)(2,1)S(1)}, u32[]{:S(2)}, u32[]{:S(2)}) collective-permute-start(bf16[128,1920]{1,0:T(8,128)(2,1)S(1)} %get-tuple-element.22), channel_id=1, source_target_pairs={{0,3},{1,2},{2,1},{3,0},{4,7},{5,6},{6,5},{7,4},{8,11},{9,10},{10,... | collective-permute-start | bytes 1474568 | tf_op jit(solution)/shard_map/ppermute | solution.py:218
  7.1 12.7 %collective-permute-start = (bf16[128,1920]{1,0:T(8,128)(2,1)S(1)}, bf16[128,1920]{1,0:T(8,128)(2,1)S(1)}, u32[]{:S(2)}, u32[]{:S(2)}) collective-permute-start(bf16[128,1920]{1,0:T(8,128)(2,1)S(1)} %get-tuple-element.20), channel_id=1, source_target_pairs={{0,1},{1,0},{2,3},{3,2},{4,5},{5,4},{6,7},{7,6},{8,9},{9,8},{10,11... | collective-permute-start | bytes 1474568 | tf_op jit(solution)/shard_map/ppermute | solution.py:217
  7.9 1.3 %copy-start.1 = (bf16[1920,320]{0,1:T(8,128)(2,1)S(1)}, bf16[1920,320]{0,1:T(8,128)(2,1)}, u32[]{:S(2)}) copy-start(bf16[1920,320]{0,1:T(8,128)(2,1)} %param.6) | copy-start | bytes 3686404
  18.5 7.0 %collective-permute-start.4 = (bf16[64,1920]{1,0:T(8,128)(2,1)S(1)}, bf16[64,1920]{1,0:T(8,128)(2,1)S(1)}, u32[]{:S(2)}, u32[]{:S(2)}) collective-permute-start(bf16[64,1920]{1,0:T(8,128)(2,1)S(1)} %get-tuple-element.34), channel_id=1, source_target_pairs={{0,1},{1,0},{2,3},{3,2},{4,5},{5,4},{6,7},{7,6},{8,9},{9,8},{10,11... | collective-permute-start | bytes 737288 | tf_op jit(solution)/shard_map/ppermute | solution.py:236
  19.9 7.8 %collective-permute-start.1 = (bf16[64,1920]{1,0:T(8,128)(2,1)S(1)}, bf16[64,1920]{1,0:T(8,128)(2,1)S(1)}, u32[]{:S(2)}, u32[]{:S(2)}) collective-permute-start(bf16[64,1920]{1,0:T(8,128)(2,1)S(1)} %get-tuple-element.32), channel_id=1, source_target_pairs={{0,3},{1,2},{2,1},{3,0},{4,7},{5,6},{6,5},{7,4},{8,11},{9,10},{10,... | collective-permute-start | bytes 737288 | tf_op jit(solution)/shard_map/ppermute | solution.py:235
  25.5 7.5 %collective-permute-start.5 = (bf16[32,1920]{1,0:T(8,128)(2,1)S(1)}, bf16[32,1920]{1,0:T(8,128)(2,1)S(1)}, u32[]{:S(2)}, u32[]{:S(2)}) collective-permute-start(bf16[32,1920]{1,0:T(8,128)(2,1)S(1)} %get-tuple-element.38), channel_id=1, source_target_pairs={{0,12},{1,13},{2,14},{3,15},{4,8},{5,9},{6,10},{7,11},{8,4},{9,5},... | collective-permute-start | bytes 368648 | tf_op jit(solution)/shard_map/ppermute | solution.py:236
  27.8 8.3 %collective-permute-start.2 = (bf16[32,1920]{1,0:T(8,128)(2,1)S(1)}, bf16[32,1920]{1,0:T(8,128)(2,1)S(1)}, u32[]{:S(2)}, u32[]{:S(2)}) collective-permute-start(bf16[32,1920]{1,0:T(8,128)(2,1)S(1)} %get-tuple-element.36), channel_id=1, source_target_pairs={{0,4},{1,5},{2,6},{3,7},{4,0},{5,1},{6,2},{7,3},{8,12},{9,13},{10,... | collective-permute-start | bytes 368648 | tf_op jit(solution)/shard_map/ppermute | solution.py:235
  33.1 5.2 %collective-permute-start.7 = (bf16[16,1920]{1,0:T(8,128)(2,1)S(1)}, bf16[16,1920]{1,0:T(8,128)(2,1)S(1)}, u32[]{:S(2)}, u32[]{:S(2)}) collective-permute-start(bf16[16,1920]{1,0:T(8,128)(2,1)S(1)} %get-tuple-element.41), channel_id=1, source_target_pairs={{0,4},{1,5},{2,6},{3,7},{4,0},{5,1},{6,2},{7,3},{8,12},{9,13},{10,... | collective-permute-start | bytes 184328 | tf_op jit(solution)/shard_map/ppermute | solution.py:236
  36.2 6.4 %collective-permute-start.6 = (bf16[16,1920]{1,0:T(8,128)(2,1)S(1)}, bf16[16,1920]{1,0:T(8,128)(2,1)S(1)}, u32[]{:S(2)}, u32[]{:S(2)}) collective-permute-start(bf16[16,1920]{1,0:T(8,128)(2,1)S(1)} %get-tuple-element.39), channel_id=1, source_target_pairs={{0,12},{1,13},{2,14},{3,15},{4,8},{5,9},{6,10},{7,11},{8,4},{9,5},... | collective-permute-start | bytes 184328 | tf_op jit(solution)/shard_map/ppermute | solution.py:235
  42.7 10.1 %collective-permute-start.9 = (bf16[32,1920]{1,0:T(8,128)(2,1)S(1)}, bf16[32,1920]{1,0:T(8,128)(2,1)S(1)}, u32[]{:S(2)}, u32[]{:S(2)}) collective-permute-start(bf16[32,1920]{1,0:T(8,128)(2,1)S(1)} %fusion.2.own), channel_id=1, source_target_pairs={{0,12},{1,13},{2,14},{3,15},{4,0},{5,1},{6,2},{7,3},{8,4},{9,5},{1... | collective-permute-start | bytes 368648 | tf_op jit(solution)/shard_map/ppermute | solution.py:260
  43.5 9.3 %collective-permute-start.8 = (bf16[32,1920]{1,0:T(8,128)(2,1)S(1)}, bf16[32,1920]{1,0:T(8,128)(2,1)S(1)}, u32[]{:S(2)}, u32[]{:S(2)}) collective-permute-start(bf16[32,1920]{1,0:T(8,128)(2,1)S(1)} %fusion.2.own), channel_id=1, source_target_pairs={{0,4},{1,5},{2,6},{3,7},{4,8},{5,9},{6,10},{7,11},{8,12},{9,13},{1... | collective-permute-start | bytes 368648 | tf_op jit(solution)/shard_map/ppermute | solution.py:259
  45.7 11.3 %collective-permute-start.13 = (bf16[32,1920]{1,0:T(8,128)(2,1)S(1)}, bf16[32,1920]{1,0:T(8,128)(2,1)S(1)}, u32[]{:S(2)}, u32[]{:S(2)}) collective-permute-start(bf16[32,1920]{1,0:T(8,128)(2,1)S(1)} %fusion.2.own), channel_id=1, source_target_pairs={{8,0},{9,32},{10,64},{11,96},{12,16},{13,48},{14,80},{15,112},{24,... | collective-permute-start | bytes 368648 | tf_op jit(solution)/shard_map/ppermute | solution.py:262
  51.5 9.8 %collective-permute-start.12 = (bf16[32,1920]{1,0:T(8,128)(2,1)S(1)}, bf16[32,1920]{1,0:T(8,128)(2,1)S(1)}, u32[]{:S(2)}, u32[]{:S(2)}) collective-permute-start(bf16[32,1920]{1,0:T(8,128)(2,1)S(1)} %fusion.2.own), channel_id=1, source_target_pairs={{0,0},{1,32},{2,64},{3,96},{4,16},{5,48},{6,80},{7,112},{16,1},{17... | collective-permute-start | bytes 368648 | tf_op jit(solution)/shard_map/ppermute | solution.py:261
  52.8 8.5 %collective-permute-start.10 = (bf16[16,1920]{1,0:T(8,128)(2,1)S(1)}, bf16[16,1920]{1,0:T(8,128)(2,1)S(1)}, u32[]{:S(2)}, u32[]{:S(2)}) collective-permute-start(bf16[16,1920]{1,0:T(8,128)(2,1)S(1)} %get-tuple-element.23), channel_id=1, source_target_pairs={{0,4},{1,5},{2,6},{3,7},{4,8},{5,9},{6,10},{7,11},{8,12},{9,13},{1... | collective-permute-start | bytes 184328 | tf_op jit(solution)/shard_map/ppermute | solution.py:264
  52.9 8.4 %collective-permute-start.11 = (bf16[16,1920]{1,0:T(8,128)(2,1)S(1)}, bf16[16,1920]{1,0:T(8,128)(2,1)S(1)}, u32[]{:S(2)}, u32[]{:S(2)}) collective-permute-start(bf16[16,1920]{1,0:T(8,128)(2,1)S(1)} %get-tuple-element.24), channel_id=1, source_target_pairs={{0,12},{1,13},{2,14},{3,15},{4,0},{5,1},{6,2},{7,3},{8,4},{9,5},{1... | collective-permute-start | bytes 184328 | tf_op jit(solution)/shard_map/ppermute | solution.py:265
  61.9 22.3 %collective-permute-start.15 = (bf16[128,1920]{1,0:T(8,128)(2,1)S(1)}, bf16[128,1920]{1,0:T(8,128)(2,1)S(1)}, u32[]{:S(2)}, u32[]{:S(2)}) collective-permute-start(bf16[128,1920]{1,0:T(8,128)(2,1)S(1)} %get-tuple-element.25.own), channel_id=1, source_target_pairs={{0,3},{1,0},{2,1},{3,2},{4,7},{5,4},{6,5},{7,6},{8,11},{9,8},{10,9... | collective-permute-start | bytes 1474568 | tf_op jit(solution)/shard_map/ppermute | solution.py:273
  68.8 15.3 %collective-permute-start.14 = (bf16[128,1920]{1,0:T(8,128)(2,1)S(1)}, bf16[128,1920]{1,0:T(8,128)(2,1)S(1)}, u32[]{:S(2)}, u32[]{:S(2)}) collective-permute-start(bf16[128,1920]{1,0:T(8,128)(2,1)S(1)} %get-tuple-element.25.own), channel_id=1, source_target_pairs={{0,1},{1,2},{2,3},{3,0},{4,5},{5,6},{6,7},{7,4},{8,9},{9,10},{10,1... | collective-permute-start | bytes 1474568 | tf_op jit(solution)/shard_map/ppermute | solution.py:272
  68.8 8.6 %collective-permute-start.19 = (bf16[64,1920]{1,0:T(8,128)(2,1)S(1)}, bf16[64,1920]{1,0:T(8,128)(2,1)S(1)}, u32[]{:S(2)}, u32[]{:S(2)}) collective-permute-start(bf16[64,1920]{1,0:T(8,128)(2,1)S(1)} %get-tuple-element.28.near), channel_id=1, source_target_pairs={{0,96},{16,112},{32,0},{48,16},{64,32},{80,48},{96,64},{112,80},{1... | collective-permute-start | bytes 737288 | tf_op jit(solution)/shard_map/ppermute | solution.py:275
  71.5 9.4 %collective-permute-start.18 = (bf16[64,1920]{1,0:T(8,128)(2,1)S(1)}, bf16[64,1920]{1,0:T(8,128)(2,1)S(1)}, u32[]{:S(2)}, u32[]{:S(2)}) collective-permute-start(bf16[64,1920]{1,0:T(8,128)(2,1)S(1)} %get-tuple-element.28.near), channel_id=1, source_target_pairs={{0,32},{16,48},{32,64},{48,80},{64,96},{80,112},{96,0},{112,16},{1... | collective-permute-start | bytes 737288 | tf_op jit(solution)/shard_map/ppermute | solution.py:274
  80.9 7.3 %collective-permute-start.20 = (bf16[32,1920]{1,0:T(8,128)(2,1)S(1)}, bf16[32,1920]{1,0:T(8,128)(2,1)S(1)}, u32[]{:S(2)}, u32[]{:S(2)}) collective-permute-start(bf16[32,1920]{1,0:T(8,128)(2,1)S(1)} %get-tuple-element.29), channel_id=1, source_target_pairs={{0,32},{16,48},{32,64},{48,80},{64,96},{80,112},{96,0},{112,16},{1... | collective-permute-start | bytes 368648 | tf_op jit(solution)/shard_map/ppermute | solution.py:287
  81.0 7.2 %collective-permute-start.21 = (bf16[32,1920]{1,0:T(8,128)(2,1)S(1)}, bf16[32,1920]{1,0:T(8,128)(2,1)S(1)}, u32[]{:S(2)}, u32[]{:S(2)}) collective-permute-start(bf16[32,1920]{1,0:T(8,128)(2,1)S(1)} %get-tuple-element.30), channel_id=1, source_target_pairs={{0,96},{16,112},{32,0},{48,16},{64,32},{80,48},{96,64},{112,80},{1... | collective-permute-start | bytes 368648 | tf_op jit(solution)/shard_map/ppermute | solution.py:288
  84.2 8.2 %collective-permute-start.17 = (bf16[64,1920]{1,0:T(8,128)(2,1)S(1)}, bf16[64,1920]{1,0:T(8,128)(2,1)S(1)}, u32[]{:S(2)}, u32[]{:S(2)}) collective-permute-start(bf16[64,1920]{1,0:T(8,128)(2,1)S(1)} %get-tuple-element.27), channel_id=1, source_target_pairs={{0,3},{1,0},{2,1},{3,2},{4,7},{5,4},{6,5},{7,6},{8,11},{9,8},{10,9... | collective-permute-start | bytes 737288 | tf_op jit(solution)/shard_map/ppermute | solution.py:278
  85.0 9.8 %collective-permute-start.16 = (bf16[64,1920]{1,0:T(8,128)(2,1)S(1)}, bf16[64,1920]{1,0:T(8,128)(2,1)S(1)}, u32[]{:S(2)}, u32[]{:S(2)}) collective-permute-start(bf16[64,1920]{1,0:T(8,128)(2,1)S(1)} %get-tuple-element.26.after), channel_id=1, source_target_pairs={{0,1},{1,2},{2,3},{3,0},{4,5},{5,6},{6,7},{7,4},{8,9},{9,10},{10,1... | collective-permute-start | bytes 737288 | tf_op jit(solution)/shard_map/ppermute | solution.py:277
  88.2 6.6 %collective-permute-start.22 = (bf16[256,1920]{1,0:T(8,128)(2,1)S(1)}, bf16[256,1920]{1,0:T(8,128)(2,1)S(1)}, u32[]{:S(2)}, u32[]{:S(2)}) collective-permute-start(bf16[256,1920]{1,0:T(8,128)(2,1)S(1)} %shard_map.62.near), channel_id=1, source_target_pairs={{0,16},{16,0},{32,48},{48,32},{64,80},{80,64},{96,112},{112,96},{1... | collective-permute-start | bytes 2949128 | tf_op jit(solution)/shard_map/ppermute | solution.py:292

commit v7 on v6

--- a/solution.py
+++ b/solution.py
@@ -96,18 +96,10 @@
     high[...] = right[half:]
 
 
-def join_kernel(at_ref, own, left, right, far_a, far_b, flipped, pair, mine, near):
+def join_kernel(at_ref, own, pair, flipped, right, left, far, mine, near):
     z = at_ref[1] >> 2
-
-    def put(by, start, ref):
-        first = pl.multiple_of(((z + by) & 3) * 32 + start, 16)
-        mine[pl.ds(first, ref.shape[0])] = ref[...]
-
-    put(0, 0, own)
-    put(3, 0, left)
-    put(1, 0, right)
-    put(2, 0, far_a)
-    put(2, 16, far_b)
+    for by, ref in ((0, own), (3, left), (1, right), (2, far)):
+        mine[pl.ds(pl.multiple_of(((z + by) & 3) * 32, 32), 32)] = ref[...]
     z_lo = at_ref[0] >> 3
     near[pl.ds(pl.multiple_of(z_lo * 32, 32), 32)] = flipped[...]
     near[pl.ds(pl.multiple_of((1 - z_lo) * 32, 32), 32)] = pair[...]
@@ -256,19 +248,17 @@
             cost_estimate=pl.CostEstimate(flops=flops, bytes_accessed=983040, transcendentals=0),
         )(one, two)
 
+    pair = lax.ppermute(slopes, ("row", "col"), flip_pairs(1))
+    flipped = lax.ppermute(slopes, ("row", "col"), flip_pairs(0))
     left = lax.ppermute(slopes, "col", z_turn(1))
     right = lax.ppermute(slopes, "col", z_turn(-1))
-    flipped = lax.ppermute(slopes, ("row", "col"), flip_pairs(0))
-    pair = lax.ppermute(slopes, ("row", "col"), flip_pairs(1))
-    low, high = halves(left, right, 8000000000)
-    far_a = lax.ppermute(low, "col", z_turn(1))
-    far_b = lax.ppermute(high, "col", z_turn(-1))
+    far = lax.ppermute(slopes, "col", z_turn(2))
     mine, near = call(
         join_kernel,
         out_shape=(shape(128, rows), shape(64, rows)),
-        in_specs=[SCALAR] + [WHOLE] * 7,
+        in_specs=[SCALAR] + [WHOLE] * 6,
         out_specs=(WHOLE,) * 2,
-    )(at, slopes, left, right, far_a, far_b, flipped, pair)
+    )(at, slopes, pair, flipped, right, left, far)
     left = lax.ppermute(mine, "col", y_turn(1))
     right = lax.ppermute(mine, "col", y_turn(-1))
     x_left = lax.ppermute(near, "row", x_turn(1))

time: 101 us -> 106 us (1.050)
  the two profiles are of different devices: /device:TPU:128 before, /device:TPU:24 now
where the time goes in v7:
time: 106 us; the launch traced here: 105 us
  waiting for transfers between devices  55.5 us (52%)
  starting transfers between devices  35.6 us (34%)
  Pallas kernels  9.14 us (9%)
  local copies, waits for them, and re-layouts  3.62 us (3%)
  other arithmetic  1.25 us (1%)
    ppermute x3, waiting for transfers between devices, per_device(): next_a = lax.ppermute(sent_a, 'col', swap_a)  12.4 us
    ppermute x1, waiting for transfers between devices, per_device(): got_b = lax.ppermute(sent_b, 'col', y_swap(3))  9.57 us
    ppermute x1, waiting for transfers between devices, per_device(): pair = lax.ppermute(slopes, ('row', 'col'), flip_pairs(1))  8.75 us
    ppermute x3, waiting for transfers between devices, per_device(): next_b = lax.ppermute(sent_b, 'col', swap_b)  7.38 us
    ppermute x3, starting transfers between devices, per_device(): next_b = lax.ppermute(sent_b, 'col', swap_b)  7.11 us
    pallas_call x1, Pallas kernels, per_device(): call(last_kernel, out_shape=shape(rows, rows), in_specs=[SCALAR] + [WHOLE...  6.01 us
    ppermute x1, waiting for transfers between devices, per_device(): far_b = lax.ppermute(high, 'col', y_turn(-1))  5.26 us
    ppermute x1, starting transfers between devices, per_device(): flipped = lax.ppermute(slopes, ('row', 'col'), flip_pairs(0))  5.04 us
  transfers between devices with their start and end apart: 22, of which 13 were waited for; matrix products, arithmetic and copies ran while one was open for 1% of the time, Pallas kernels for 1%

profile of v7, /device:TPU:24, one launch (start us, length us, event | category | flops | bytes accessed | tf_op | source)
XLA Modules:
  0.0 105.4 jit_solution(9557329721597468867)
XLA Ops:
  0.1 1.3 %copy-done = bf16[1920,320]{0,1:T(8,128)(2,1)S(1)} copy-done((bf16[1920,320]{0,1:T(8,128)(2,1)S(1)}, bf16[1920,320]{0,1:T(8,128)(2,1)}, u32[]{:S(2)}) %copy-start) | copy-done | bytes 1228824
  1.4 1.0 copy-done.2
  2.3 1.7 %shard_map.55 = (bf16[128,1920]{1,0:T(8,128)(2,1)S(1)}, bf16[128,1920]{1,0:T(8,128)(2,1)S(1)}, bf16[256,320]{1,0:T(8,128)(2,1)S(1)}) custom-call(s32[2]{0:T(128)S(1)} %pad_add_fusion.at_ref, bf16[320,512]{1,0:T(8,128)(2,1)S(1)} %copy-done.2, bf16[320,1920]{1,0:T(8,128)(2,1)S(1)} %bitcast.13), custom_call_target="tpu_custom_call" | custom-call | flops 314572800 | bytes 1600000 | tf_op jit(solution)/shard_map/pallas_call | solution.py:200
  4.0 2.0 %collective-permute-start.3 = (bf16[128,1920]{1,0:T(8,128)(2,1)S(1)}, bf16[128,1920]{1,0:T(8,128)(2,1)S(1)}, u32[]{:S(2)}, u32[]{:S(2)}) collective-permute-start(bf16[128,1920]{1,0:T(8,128)(2,1)S(1)} %get-tuple-element.20), channel_id=1, source_target_pairs={{0,3},{1,2},{2,1},{3,0},{4,7},{5,6},{6,5},{7,4},{8,11},{9,10},{10,... | collective-permute-start | bytes 1474568 | tf_op jit(solution)/shard_map/ppermute | solution.py:210
  6.7 1.3 %copy-done.1 = bf16[1920,320]{0,1:T(8,128)(2,1)S(1)} copy-done((bf16[1920,320]{0,1:T(8,128)(2,1)S(1)}, bf16[1920,320]{0,1:T(8,128)(2,1)}, u32[]{:S(2)}) %copy-start.1) | copy-done | bytes 1228824
  8.0 0.7 shard_map.56
  8.7 9.6 %collective-permute-done.3 = bf16[128,1920]{1,0:T(8,128)(2,1)S(1)} collective-permute-done((bf16[128,1920]{1,0:T(8,128)(2,1)S(1)}, bf16[128,1920]{1,0:T(8,128)(2,1)S(1)}, u32[]{:S(2)}, u32[]{:S(2)}) %collective-permute-start.3) | collective-permute-done | bytes 491552 | tf_op jit(solution)/shard_map/ppermute | solution.py:210
  18.7 2.0 %collective-permute-start.1 = (bf16[64,1920]{1,0:T(8,128)(2,1)S(1)}, bf16[64,1920]{1,0:T(8,128)(2,1)S(1)}, u32[]{:S(2)}, u32[]{:S(2)}) collective-permute-start(bf16[64,1920]{1,0:T(8,128)(2,1)S(1)} %get-tuple-element.28), channel_id=1, source_target_pairs={{0,3},{1,2},{2,1},{3,0},{4,7},{5,6},{6,5},{7,4},{8,11},{9,10},{10,... | collective-permute-start | bytes 737288 | tf_op jit(solution)/shard_map/ppermute | solution.py:227
  20.6 4.7 %collective-permute-done.4 = bf16[64,1920]{1,0:T(8,128)(2,1)S(1)} collective-permute-done((bf16[64,1920]{1,0:T(8,128)(2,1)S(1)}, bf16[64,1920]{1,0:T(8,128)(2,1)S(1)}, u32[]{:S(2)}, u32[]{:S(2)}) %collective-permute-start.4) | collective-permute-done | bytes 245792 | tf_op jit(solution)/shard_map/ppermute | solution.py:228
  25.4 6.4 %collective-permute-start.5 = (bf16[32,1920]{1,0:T(8,128)(2,1)S(1)}, bf16[32,1920]{1,0:T(8,128)(2,1)S(1)}, u32[]{:S(2)}, u32[]{:S(2)}) collective-permute-start(bf16[32,1920]{1,0:T(8,128)(2,1)S(1)} %get-tuple-element.34), channel_id=1, source_target_pairs={{0,12},{1,13},{2,14},{3,15},{4,8},{5,9},{6,10},{7,11},{8,4},{9,5},... | collective-permute-start | bytes 368648 | tf_op jit(solution)/shard_map/ppermute | solution.py:228
  31.9 1.5 %collective-permute-start.2 = (bf16[32,1920]{1,0:T(8,128)(2,1)S(1)}, bf16[32,1920]{1,0:T(8,128)(2,1)S(1)}, u32[]{:S(2)}, u32[]{:S(2)}) collective-permute-start(bf16[32,1920]{1,0:T(8,128)(2,1)S(1)} %get-tuple-element.32), channel_id=1, source_target_pairs={{0,4},{1,5},{2,6},{3,7},{4,0},{5,1},{6,2},{7,3},{8,12},{9,13},{10,... | collective-permute-start | bytes 368648 | tf_op jit(solution)/shard_map/ppermute | solution.py:227
  33.4 2.2 %collective-permute-done.5 = bf16[32,1920]{1,0:T(8,128)(2,1)S(1)} collective-permute-done((bf16[32,1920]{1,0:T(8,128)(2,1)S(1)}, bf16[32,1920]{1,0:T(8,128)(2,1)S(1)}, u32[]{:S(2)}, u32[]{:S(2)}) %collective-permute-start.5) | collective-permute-done | bytes 122912 | tf_op jit(solution)/shard_map/ppermute | solution.py:228
  36.3 5.1 %collective-permute-done.2 = bf16[32,1920]{1,0:T(8,128)(2,1)S(1)} collective-permute-done((bf16[32,1920]{1,0:T(8,128)(2,1)S(1)}, bf16[32,1920]{1,0:T(8,128)(2,1)S(1)}, u32[]{:S(2)}, u32[]{:S(2)}) %collective-permute-start.2) | collective-permute-done | bytes 122912 | tf_op jit(solution)/shard_map/ppermute | solution.py:227
  42.0 7.4 %collective-permute-done.6 = bf16[16,1920]{1,0:T(8,128)(2,1)S(1)} collective-permute-done((bf16[16,1920]{1,0:T(8,128)(2,1)S(1)}, bf16[16,1920]{1,0:T(8,128)(2,1)S(1)}, u32[]{:S(2)}, u32[]{:S(2)}) %collective-permute-start.6) | collective-permute-done | bytes 61472 | tf_op jit(solution)/shard_map/ppermute | solution.py:227
  49.6 1.7 %collective-permute-start.11 = (bf16[32,1920]{1,0:T(8,128)(2,1)S(1)}, bf16[32,1920]{1,0:T(8,128)(2,1)S(1)}, u32[]{:S(2)}, u32[]{:S(2)}) collective-permute-start(bf16[32,1920]{1,0:T(8,128)(2,1)S(1)} %fusion.2.own), channel_id=1, source_target_pairs={{0,4},{1,5},{2,6},{3,7},{4,8},{5,9},{6,10},{7,11},{8,12},{9,13},{1... | collective-permute-start | bytes 368648 | tf_op jit(solution)/shard_map/ppermute | solution.py:253
  51.3 2.5 %collective-permute-start.10 = (bf16[32,1920]{1,0:T(8,128)(2,1)S(1)}, bf16[32,1920]{1,0:T(8,128)(2,1)S(1)}, u32[]{:S(2)}, u32[]{:S(2)}) collective-permute-start(bf16[32,1920]{1,0:T(8,128)(2,1)S(1)} %fusion.2.own), channel_id=1, source_target_pairs={{0,12},{1,13},{2,14},{3,15},{4,0},{5,1},{6,2},{7,3},{8,4},{9,5},{1... | collective-permute-start | bytes 368648 | tf_op jit(solution)/shard_map/ppermute | solution.py:254
  53.8 5.0 %collective-permute-start.9 = (bf16[32,1920]{1,0:T(8,128)(2,1)S(1)}, bf16[32,1920]{1,0:T(8,128)(2,1)S(1)}, u32[]{:S(2)}, u32[]{:S(2)}) collective-permute-start(bf16[32,1920]{1,0:T(8,128)(2,1)S(1)} %fusion.2.own), channel_id=1, source_target_pairs={{0,0},{1,32},{2,64},{3,96},{4,16},{5,48},{6,80},{7,112},{16,1},{17... | collective-permute-start | bytes 368648 | tf_op jit(solution)/shard_map/ppermute | solution.py:252
  58.9 1.3 %collective-permute-start.8 = (bf16[32,1920]{1,0:T(8,128)(2,1)S(1)}, bf16[32,1920]{1,0:T(8,128)(2,1)S(1)}, u32[]{:S(2)}, u32[]{:S(2)}) collective-permute-start(bf16[32,1920]{1,0:T(8,128)(2,1)S(1)} %fusion.2.own), channel_id=1, source_target_pairs={{8,0},{9,32},{10,64},{11,96},{12,16},{13,48},{14,80},{15,112},{24,... | collective-permute-start | bytes 368648 | tf_op jit(solution)/shard_map/ppermute | solution.py:251
  60.8 2.9 %collective-permute-done.9.flipped = bf16[32,1920]{1,0:T(8,128)(2,1)S(1)} collective-permute-done((bf16[32,1920]{1,0:T(8,128)(2,1)S(1)}, bf16[32,1920]{1,0:T(8,128)(2,1)S(1)}, u32[]{:S(2)}, u32[]{:S(2)}) %collective-permute-start.9) | collective-permute-done | bytes 122912 | tf_op jit(solution)/shard_map/ppermute | solution.py:252
  63.8 8.8 %collective-permute-done.8.pair = bf16[32,1920]{1,0:T(8,128)(2,1)S(1)} collective-permute-done((bf16[32,1920]{1,0:T(8,128)(2,1)S(1)}, bf16[32,1920]{1,0:T(8,128)(2,1)S(1)}, u32[]{:S(2)}, u32[]{:S(2)}) %collective-permute-start.8) | collective-permute-done | bytes 122912 | tf_op jit(solution)/shard_map/ppermute | solution.py:251
  73.2 2.4 %collective-permute-start.14 = (bf16[128,1920]{1,0:T(8,128)(2,1)S(1)}, bf16[128,1920]{1,0:T(8,128)(2,1)S(1)}, u32[]{:S(2)}, u32[]{:S(2)}) collective-permute-start(bf16[128,1920]{1,0:T(8,128)(2,1)S(1)} %get-tuple-element.21.own), channel_id=1, source_target_pairs={{0,3},{1,0},{2,1},{3,2},{4,7},{5,4},{6,5},{7,6},{8,11},{9,8},{10,9... | collective-permute-start | bytes 1474568 | tf_op jit(solution)/shard_map/ppermute | solution.py:263
  75.6 0.9 collective-permute-start.13
  76.5 0.7 collective-permute-start.18
  77.2 1.3 %collective-permute-start.17 = (bf16[64,1920]{1,0:T(8,128)(2,1)S(1)}, bf16[64,1920]{1,0:T(8,128)(2,1)S(1)}, u32[]{:S(2)}, u32[]{:S(2)}) collective-permute-start(bf16[64,1920]{1,0:T(8,128)(2,1)S(1)} %get-tuple-element.24.near), channel_id=1, source_target_pairs={{0,32},{16,48},{32,64},{48,80},{64,96},{80,112},{96,0},{112,16},{1... | collective-permute-start | bytes 737288 | tf_op jit(solution)/shard_map/ppermute | solution.py:264
  78.5 4.2 %collective-permute-done.18.right.x_right = bf16[64,1920]{1,0:T(8,128)(2,1)S(1)} collective-permute-done((bf16[64,1920]{1,0:T(8,128)(2,1)S(1)}, bf16[64,1920]{1,0:T(8,128)(2,1)S(1)}, u32[]{:S(2)}, u32[]{:S(2)}) %collective-permute-start.18) | collective-permute-done | bytes 245792 | tf_op jit(solution)/shard_map/ppermute | solution.py:265
  82.7 3.9 %collective-permute-done.17.left.x_left = bf16[64,1920]{1,0:T(8,128)(2,1)S(1)} collective-permute-done((bf16[64,1920]{1,0:T(8,128)(2,1)S(1)}, bf16[64,1920]{1,0:T(8,128)(2,1)S(1)}, u32[]{:S(2)}, u32[]{:S(2)}) %collective-permute-start.17) | collective-permute-done | bytes 245792 | tf_op jit(solution)/shard_map/ppermute | solution.py:264
  86.6 0.8 collective-permute-start.19
  87.3 2.7 %collective-permute-start.20 = (bf16[32,1920]{1,0:T(8,128)(2,1)S(1)}, bf16[32,1920]{1,0:T(8,128)(2,1)S(1)}, u32[]{:S(2)}, u32[]{:S(2)}) collective-permute-start(bf16[32,1920]{1,0:T(8,128)(2,1)S(1)} %get-tuple-element.26), channel_id=1, source_target_pairs={{0,96},{16,112},{32,0},{48,16},{64,32},{80,48},{96,64},{112,80},{1... | collective-permute-start | bytes 368648 | tf_op jit(solution)/shard_map/ppermute | solution.py:278
  90.1 0.8 collective-permute-start.16
  90.9 2.5 %collective-permute-start.15 = (bf16[64,1920]{1,0:T(8,128)(2,1)S(1)}, bf16[64,1920]{1,0:T(8,128)(2,1)S(1)}, u32[]{:S(2)}, u32[]{:S(2)}) collective-permute-start(bf16[64,1920]{1,0:T(8,128)(2,1)S(1)} %get-tuple-element.22.after), channel_id=1, source_target_pairs={{0,1},{1,2},{2,3},{3,0},{4,5},{5,6},{6,7},{7,4},{8,9},{9,10},{10,1... | collective-permute-start | bytes 737288 | tf_op jit(solution)/shard_map/ppermute | solution.py:267
  94.0 5.3 %collective-permute-done.16.two = bf16[64,1920]{1,0:T(8,128)(2,1)S(1)} collective-permute-done((bf16[64,1920]{1,0:T(8,128)(2,1)S(1)}, bf16[64,1920]{1,0:T(8,128)(2,1)S(1)}, u32[]{:S(2)}, u32[]{:S(2)}) %collective-permute-start.16) | collective-permute-done | bytes 245792 | tf_op jit(solution)/shard_map/ppermute | solution.py:268
  99.3 6.0 %shard_map.62 = bf16[1920,1920]{1,0:T(8,128)(2,1)} custom-call(s32[2]{0:T(128)S(1)} %pad_add_fusion.at_ref, bf16[128,1920]{1,0:T(8,128)(2,1)S(1)} %get-tuple-element.21.own, bf16[128,1920]{1,0:T(8,128)(2,1)S(1)} %collective-permute-done.13.left, bf16[128,1920]{1,0:T(8,128)(2,1)S(1)} %collective-permute-done.14.right, bf16[128,1920]{1,0:T(8,128)(2,1)S(1)} %shard_map.59.far, ...), custom_call_target="tpu_custom_call" | custom-call | flops 3774873600 | bytes 7372800 | tf_op jit(solution)/shard_map/pallas_call | solution.py:283
  (41 shorter events, 4.6 us)
Async XLA Ops:
  0.0 41.6 %copy-start.4 = (s32[32]{0:T(128)S(1)}, s32[32]{0:T(128)}, u32[]{:S(2)}) copy-start(s32[32]{0:T(128)} %param.9) | copy-start | bytes 388
  0.1 1.3 %copy-start = (bf16[1920,320]{0,1:T(8,128)(2,1)S(1)}, bf16[1920,320]{0,1:T(8,128)(2,1)}, u32[]{:S(2)}) copy-start(bf16[1920,320]{0,1:T(8,128)(2,1)} %param.6) | copy-start | bytes 3686404
  1.4 1.0 copy-start.2
  2.3 47.1 %copy-start.3 = (bf16[1920,32]{0,1:T(8,128)(2,1)S(1)}, bf16[1920,32]{0,1:T(8,128)(2,1)}, u32[]{:S(2)}) copy-start(bf16[1920,32]{0,1:T(8,128)(2,1)} %param.5) | copy-start | bytes 368644
  4.0 14.3 %collective-permute-start.3 = (bf16[128,1920]{1,0:T(8,128)(2,1)S(1)}, bf16[128,1920]{1,0:T(8,128)(2,1)S(1)}, u32[]{:S(2)}, u32[]{:S(2)}) collective-permute-start(bf16[128,1920]{1,0:T(8,128)(2,1)S(1)} %get-tuple-element.20), channel_id=1, source_target_pairs={{0,3},{1,2},{2,1},{3,0},{4,7},{5,6},{6,5},{7,4},{8,11},{9,10},{10,... | collective-permute-start | bytes 1474568 | tf_op jit(solution)/shard_map/ppermute | solution.py:210
  6.1 12.4 %collective-permute-start = (bf16[128,1920]{1,0:T(8,128)(2,1)S(1)}, bf16[128,1920]{1,0:T(8,128)(2,1)S(1)}, u32[]{:S(2)}, u32[]{:S(2)}) collective-permute-start(bf16[128,1920]{1,0:T(8,128)(2,1)S(1)} %get-tuple-element.18), channel_id=1, source_target_pairs={{0,1},{1,0},{2,3},{3,2},{4,5},{5,4},{6,7},{7,6},{8,9},{9,8},{10,11... | collective-permute-start | bytes 1474568 | tf_op jit(solution)/shard_map/ppermute | solution.py:209
  6.7 1.3 %copy-start.1 = (bf16[1920,320]{0,1:T(8,128)(2,1)S(1)}, bf16[1920,320]{0,1:T(8,128)(2,1)}, u32[]{:S(2)}) copy-start(bf16[1920,320]{0,1:T(8,128)(2,1)} %param.6) | copy-start | bytes 3686404
  18.4 6.9 %collective-permute-start.4 = (bf16[64,1920]{1,0:T(8,128)(2,1)S(1)}, bf16[64,1920]{1,0:T(8,128)(2,1)S(1)}, u32[]{:S(2)}, u32[]{:S(2)}) collective-permute-start(bf16[64,1920]{1,0:T(8,128)(2,1)S(1)} %get-tuple-element.30), channel_id=1, source_target_pairs={{0,1},{1,0},{2,3},{3,2},{4,5},{5,4},{6,7},{7,6},{8,9},{9,8},{10,11... | collective-permute-start | bytes 737288 | tf_op jit(solution)/shard_map/ppermute | solution.py:228
  18.7 13.1 %collective-permute-start.1 = (bf16[64,1920]{1,0:T(8,128)(2,1)S(1)}, bf16[64,1920]{1,0:T(8,128)(2,1)S(1)}, u32[]{:S(2)}, u32[]{:S(2)}) collective-permute-start(bf16[64,1920]{1,0:T(8,128)(2,1)S(1)} %get-tuple-element.28), channel_id=1, source_target_pairs={{0,3},{1,2},{2,1},{3,0},{4,7},{5,6},{6,5},{7,4},{8,11},{9,10},{10,... | collective-permute-start | bytes 737288 | tf_op jit(solution)/shard_map/ppermute | solution.py:227
  25.4 10.2 %collective-permute-start.5 = (bf16[32,1920]{1,0:T(8,128)(2,1)S(1)}, bf16[32,1920]{1,0:T(8,128)(2,1)S(1)}, u32[]{:S(2)}, u32[]{:S(2)}) collective-permute-start(bf16[32,1920]{1,0:T(8,128)(2,1)S(1)} %get-tuple-element.34), channel_id=1, source_target_pairs={{0,12},{1,13},{2,14},{3,15},{4,8},{5,9},{6,10},{7,11},{8,4},{9,5},... | collective-permute-start | bytes 368648 | tf_op jit(solution)/shard_map/ppermute | solution.py:228
  31.9 9.5 %collective-permute-start.2 = (bf16[32,1920]{1,0:T(8,128)(2,1)S(1)}, bf16[32,1920]{1,0:T(8,128)(2,1)S(1)}, u32[]{:S(2)}, u32[]{:S(2)}) collective-permute-start(bf16[32,1920]{1,0:T(8,128)(2,1)S(1)} %get-tuple-element.32), channel_id=1, source_target_pairs={{0,4},{1,5},{2,6},{3,7},{4,0},{5,1},{6,2},{7,3},{8,12},{9,13},{10,... | collective-permute-start | bytes 368648 | tf_op jit(solution)/shard_map/ppermute | solution.py:227
  35.7 6.4 %collective-permute-start.7 = (bf16[16,1920]{1,0:T(8,128)(2,1)S(1)}, bf16[16,1920]{1,0:T(8,128)(2,1)S(1)}, u32[]{:S(2)}, u32[]{:S(2)}) collective-permute-start(bf16[16,1920]{1,0:T(8,128)(2,1)S(1)} %get-tuple-element.37), channel_id=1, source_target_pairs={{0,4},{1,5},{2,6},{3,7},{4,0},{5,1},{6,2},{7,3},{8,12},{9,13},{10,... | collective-permute-start | bytes 184328 | tf_op jit(solution)/shard_map/ppermute | solution.py:228
  41.4 8.0 %collective-permute-start.6 = (bf16[16,1920]{1,0:T(8,128)(2,1)S(1)}, bf16[16,1920]{1,0:T(8,128)(2,1)S(1)}, u32[]{:S(2)}, u32[]{:S(2)}) collective-permute-start(bf16[16,1920]{1,0:T(8,128)(2,1)S(1)} %get-tuple-element.35), channel_id=1, source_target_pairs={{0,12},{1,13},{2,14},{3,15},{4,8},{5,9},{6,10},{7,11},{8,4},{9,5},... | collective-permute-start | bytes 184328 | tf_op jit(solution)/shard_map/ppermute | solution.py:227
  49.5 10.7 %collective-permute-start.12 = (bf16[32,1920]{1,0:T(8,128)(2,1)S(1)}, bf16[32,1920]{1,0:T(8,128)(2,1)S(1)}, u32[]{:S(2)}, u32[]{:S(2)}) collective-permute-start(bf16[32,1920]{1,0:T(8,128)(2,1)S(1)} %fusion.2.own), channel_id=1, source_target_pairs={{0,8},{1,9},{2,10},{3,11},{4,12},{5,13},{6,14},{7,15},{8,0},{9,1},... | collective-permute-start | bytes 368648 | tf_op jit(solution)/shard_map/ppermute | solution.py:255
  49.6 10.6 %collective-permute-start.11 = (bf16[32,1920]{1,0:T(8,128)(2,1)S(1)}, bf16[32,1920]{1,0:T(8,128)(2,1)S(1)}, u32[]{:S(2)}, u32[]{:S(2)}) collective-permute-start(bf16[32,1920]{1,0:T(8,128)(2,1)S(1)} %fusion.2.own), channel_id=1, source_target_pairs={{0,4},{1,5},{2,6},{3,7},{4,8},{5,9},{6,10},{7,11},{8,12},{9,13},{1... | collective-permute-start | bytes 368648 | tf_op jit(solution)/shard_map/ppermute | solution.py:253
  51.3 9.5 %collective-permute-start.10 = (bf16[32,1920]{1,0:T(8,128)(2,1)S(1)}, bf16[32,1920]{1,0:T(8,128)(2,1)S(1)}, u32[]{:S(2)}, u32[]{:S(2)}) collective-permute-start(bf16[32,1920]{1,0:T(8,128)(2,1)S(1)} %fusion.2.own), channel_id=1, source_target_pairs={{0,12},{1,13},{2,14},{3,15},{4,0},{5,1},{6,2},{7,3},{8,4},{9,5},{1... | collective-permute-start | bytes 368648 | tf_op jit(solution)/shard_map/ppermute | solution.py:254
  53.8 10.0 %collective-permute-start.9 = (bf16[32,1920]{1,0:T(8,128)(2,1)S(1)}, bf16[32,1920]{1,0:T(8,128)(2,1)S(1)}, u32[]{:S(2)}, u32[]{:S(2)}) collective-permute-start(bf16[32,1920]{1,0:T(8,128)(2,1)S(1)} %fusion.2.own), channel_id=1, source_target_pairs={{0,0},{1,32},{2,64},{3,96},{4,16},{5,48},{6,80},{7,112},{16,1},{17... | collective-permute-start | bytes 368648 | tf_op jit(solution)/shard_map/ppermute | solution.py:252
  58.9 13.7 %collective-permute-start.8 = (bf16[32,1920]{1,0:T(8,128)(2,1)S(1)}, bf16[32,1920]{1,0:T(8,128)(2,1)S(1)}, u32[]{:S(2)}, u32[]{:S(2)}) collective-permute-start(bf16[32,1920]{1,0:T(8,128)(2,1)S(1)} %fusion.2.own), channel_id=1, source_target_pairs={{8,0},{9,32},{10,64},{11,96},{12,16},{13,48},{14,80},{15,112},{24,... | collective-permute-start | bytes 368648 | tf_op jit(solution)/shard_map/ppermute | solution.py:251
  73.2 16.9 %collective-permute-start.14 = (bf16[128,1920]{1,0:T(8,128)(2,1)S(1)}, bf16[128,1920]{1,0:T(8,128)(2,1)S(1)}, u32[]{:S(2)}, u32[]{:S(2)}) collective-permute-start(bf16[128,1920]{1,0:T(8,128)(2,1)S(1)} %get-tuple-element.21.own), channel_id=1, source_target_pairs={{0,3},{1,0},{2,1},{3,2},{4,7},{5,4},{6,5},{7,6},{8,11},{9,8},{10,9... | collective-permute-start | bytes 1474568 | tf_op jit(solution)/shard_map/ppermute | solution.py:263
  75.6 14.5 %collective-permute-start.13 = (bf16[128,1920]{1,0:T(8,128)(2,1)S(1)}, bf16[128,1920]{1,0:T(8,128)(2,1)S(1)}, u32[]{:S(2)}, u32[]{:S(2)}) collective-permute-start(bf16[128,1920]{1,0:T(8,128)(2,1)S(1)} %get-tuple-element.21.own), channel_id=1, source_target_pairs={{0,1},{1,2},{2,3},{3,0},{4,5},{5,6},{6,7},{7,4},{8,9},{9,10},{10,1... | collective-permute-start | bytes 1474568 | tf_op jit(solution)/shard_map/ppermute | solution.py:262
  76.5 6.2 %collective-permute-start.18 = (bf16[64,1920]{1,0:T(8,128)(2,1)S(1)}, bf16[64,1920]{1,0:T(8,128)(2,1)S(1)}, u32[]{:S(2)}, u32[]{:S(2)}) collective-permute-start(bf16[64,1920]{1,0:T(8,128)(2,1)S(1)} %get-tuple-element.24.near), channel_id=1, source_target_pairs={{0,96},{16,112},{32,0},{48,16},{64,32},{80,48},{96,64},{112,80},{1... | collective-permute-start | bytes 737288 | tf_op jit(solution)/shard_map/ppermute | solution.py:265
  77.2 9.3 %collective-permute-start.17 = (bf16[64,1920]{1,0:T(8,128)(2,1)S(1)}, bf16[64,1920]{1,0:T(8,128)(2,1)S(1)}, u32[]{:S(2)}, u32[]{:S(2)}) collective-permute-start(bf16[64,1920]{1,0:T(8,128)(2,1)S(1)} %get-tuple-element.24.near), channel_id=1, source_target_pairs={{0,32},{16,48},{32,64},{48,80},{64,96},{80,112},{96,0},{112,16},{1... | collective-permute-start | bytes 737288 | tf_op jit(solution)/shard_map/ppermute | solution.py:264
  86.6 7.2 %collective-permute-start.19 = (bf16[32,1920]{1,0:T(8,128)(2,1)S(1)}, bf16[32,1920]{1,0:T(8,128)(2,1)S(1)}, u32[]{:S(2)}, u32[]{:S(2)}) collective-permute-start(bf16[32,1920]{1,0:T(8,128)(2,1)S(1)} %get-tuple-element.25), channel_id=1, source_target_pairs={{0,32},{16,48},{32,64},{48,80},{64,96},{80,112},{96,0},{112,16},{1... | collective-permute-start | bytes 368648 | tf_op jit(solution)/shard_map/ppermute | solution.py:277
  87.3 6.5 %collective-permute-start.20 = (bf16[32,1920]{1,0:T(8,128)(2,1)S(1)}, bf16[32,1920]{1,0:T(8,128)(2,1)S(1)}, u32[]{:S(2)}, u32[]{:S(2)}) collective-permute-start(bf16[32,1920]{1,0:T(8,128)(2,1)S(1)} %get-tuple-element.26), channel_id=1, source_target_pairs={{0,96},{16,112},{32,0},{48,16},{64,32},{80,48},{96,64},{112,80},{1... | collective-permute-start | bytes 368648 | tf_op jit(solution)/shard_map/ppermute | solution.py:278
  90.1 9.1 %collective-permute-start.16 = (bf16[64,1920]{1,0:T(8,128)(2,1)S(1)}, bf16[64,1920]{1,0:T(8,128)(2,1)S(1)}, u32[]{:S(2)}, u32[]{:S(2)}) collective-permute-start(bf16[64,1920]{1,0:T(8,128)(2,1)S(1)} %get-tuple-element.23), channel_id=1, source_target_pairs={{0,3},{1,0},{2,1},{3,2},{4,7},{5,4},{6,5},{7,6},{8,11},{9,8},{10,9... | collective-permute-start | bytes 737288 | tf_op jit(solution)/shard_map/ppermute | solution.py:268
  90.9 8.3 %collective-permute-start.15 = (bf16[64,1920]{1,0:T(8,128)(2,1)S(1)}, bf16[64,1920]{1,0:T(8,128)(2,1)S(1)}, u32[]{:S(2)}, u32[]{:S(2)}) collective-permute-start(bf16[64,1920]{1,0:T(8,128)(2,1)S(1)} %get-tuple-element.22.after), channel_id=1, source_target_pairs={{0,1},{1,2},{2,3},{3,0},{4,5},{5,6},{6,7},{7,4},{8,9},{9,10},{10,1... | collective-permute-start | bytes 737288 | tf_op jit(solution)/shard_map/ppermute | solution.py:267
  93.9 5.4 %collective-permute-start.21 = (bf16[256,1920]{1,0:T(8,128)(2,1)S(1)}, bf16[256,1920]{1,0:T(8,128)(2,1)S(1)}, u32[]{:S(2)}, u32[]{:S(2)}) collective-permute-start(bf16[256,1920]{1,0:T(8,128)(2,1)S(1)} %shard_map.61.near), channel_id=1, source_target_pairs={{0,16},{16,0},{32,48},{48,32},{64,80},{80,64},{96,112},{112,96},{1... | collective-permute-start | bytes 2949128 | tf_op jit(solution)/shard_map/ppermute | solution.py:282

commit v8 on v5

--- a/solution.py
+++ b/solution.py
@@ -95,11 +95,7 @@
     high[...] = right[half:]
 
 
-def same_kernel(flipped, after, out):
-    out[...] = flipped[...]
-
-
-def join_kernel(at_ref, own, left, right, far_a, far_b, flipped, pair, mine, near):
+def z_join_kernel(at_ref, own, left, right, far_a, far_b, mine):
     z = at_ref[1] >> 2
 
     def put(by, start, ref):
@@ -111,6 +107,9 @@
     put(1, 0, right)
     put(2, 0, far_a)
     put(2, 16, far_b)
+
+
+def pair_join_kernel(at_ref, flipped, pair, near):
     z_lo = at_ref[0] >> 3
     near[pl.ds(pl.multiple_of(z_lo * 32, 32), 32)] = flipped[...]
     near[pl.ds(pl.multiple_of((1 - z_lo) * 32, 32), 32)] = pair[...]
@@ -265,21 +264,25 @@
     low, high = halves(left, right, 8000000000)
     far_a = lax.ppermute(low, "col", z_turn(1))
     far_b = lax.ppermute(high, "col", z_turn(-1))
-    flipped = call(
-        same_kernel, out_shape=shape(32, rows), in_specs=[WHOLE] * 2, out_specs=WHOLE
-    )(flipped, low)
-    pair = lax.ppermute(flipped, "row", [(r, r ^ 8) for r in range(16)])
-    mine, near = call(
-        join_kernel,
-        out_shape=(shape(128, rows), shape(64, rows)),
-        in_specs=[SCALAR] + [WHOLE] * 7,
-        out_specs=(WHOLE,) * 2,
-    )(at, slopes, left, right, far_a, far_b, flipped, pair)
+    mine = call(
+        z_join_kernel,
+        out_shape=shape(128, rows),
+        in_specs=[SCALAR] + [WHOLE] * 5,
+        out_specs=WHOLE,
+    )(at, slopes, left, right, far_a, far_b)
     left = lax.ppermute(mine, "col", y_turn(1))
     right = lax.ppermute(mine, "col", y_turn(-1))
+    pair = lax.ppermute(flipped, "row", [(r, r ^ 8) for r in range(16)])
+    near = call(
+        pair_join_kernel,
+        out_shape=shape(64, rows),
+        in_specs=[SCALAR] + [WHOLE] * 2,
+        out_specs=WHOLE,
+        cost_estimate=pl.CostEstimate(flops=4000000000, bytes_accessed=491520, transcendentals=0),
+    )(at, flipped, pair)
     x_left = lax.ppermute(near, "row", x_turn(1))
     x_right = lax.ppermute(near, "row", x_turn(-1))
-    low, high = halves(left, right, 8000000000)
+    low, high = halves(left, right, 16000000000)
     far_a = lax.ppermute(low, "col", y_turn(1))
     far_b = lax.ppermute(high, "col", y_turn(-1))
     far = call(
@@ -287,7 +290,7 @@
         out_shape=shape(128, rows),
         in_specs=[WHOLE] * 2,
         out_specs=WHOLE,
-        cost_estimate=pl.CostEstimate(flops=8000000000, bytes_accessed=983040, transcendentals=0),
+        cost_estimate=pl.CostEstimate(flops=16000000000, bytes_accessed=983040, transcendentals=0),
     )(far_a, far_b)
     x_low, x_high = halves(x_left, x_right, 0)
     x_far_a = lax.ppermute(x_low, "row", x_turn(1))

time: 106 us -> 101 us (0.953)
  waiting for transfers between devices: 54.1 us -> 48.5 us
    ppermute x1, waiting for transfers between devices: 0.01 us -> 5.84 us  [per_device(): right = lax.ppermute(mine, 'col', y_turn(-1))]
    ppermute x1, waiting for transfers between devices: 5.09 us -> 0.01 us  [per_device(): x_right = lax.ppermute(near, 'row', x_turn(-1))]
    ppermute x1, waiting for transfers between devices: 4.4 us -> 0.4 us  [per_device(): far_a = lax.ppermute(low, 'col', z_turn(1))]
    ppermute x1, waiting for transfers between devices: 3.99 us -> 0.01 us  [per_device(): far_b = lax.ppermute(high, 'col', y_turn(-1))]
    ppermute x1, waiting for transfers between devices: 3.29 us -> 0.01 us  [per_device(): flipped = lax.ppermute(slopes, ('row', 'col'), flip_pairs())]
    ppermute x1, waiting for transfers between devices: 0.01 us -> 2.85 us  [per_device(): x_far_a = lax.ppermute(x_low, 'row', x_turn(1))]
    ppermute x1, waiting for transfers between devices: 2.72 us -> 0.01 us  [per_device(): x_left = lax.ppermute(near, 'row', x_turn(1))]
    ppermute x1, starting transfers between devices: 0.01 us -> 2.62 us  [per_device(): far_a = lax.ppermute(low, 'col', z_turn(1))]
  transfers between devices with their start and end apart: 23 -> 23, of which waited for: 14 -> 14; matrix products, arithmetic and copies ran while one was open for 1% -> 1% of each run, Pallas kernels for 1% -> 2%
where the time goes in v8:
time: 101 us; the launch traced here: 100 us
  waiting for transfers between devices  48.5 us (48%)
  starting transfers between devices  36.7 us (36%)
  Pallas kernels  9.7 us (10%)
  local copies, waits for them, and re-layouts  3.62 us (4%)
  other arithmetic  1.24 us (1%)
    ppermute x3, waiting for transfers between devices, per_device(): next_a = lax.ppermute(sent_a, 'col', swap_a)  12.6 us
    ppermute x1, waiting for transfers between devices, per_device(): got_b = lax.ppermute(sent_b, 'col', y_swap(3))  9.57 us
    ppermute x3, waiting for transfers between devices, per_device(): next_b = lax.ppermute(sent_b, 'col', swap_b)  7.39 us
    ppermute x3, starting transfers between devices, per_device(): next_b = lax.ppermute(sent_b, 'col', swap_b)  7.11 us
    pallas_call x1, Pallas kernels, per_device(): call(last_kernel, out_shape=shape(rows, rows), in_specs=[SCALAR] + [WHOLE...  6 us
    ppermute x1, waiting for transfers between devices, per_device(): right = lax.ppermute(mine, 'col', y_turn(-1))  5.84 us
    ppermute x3, starting transfers between devices, per_device(): next_a = lax.ppermute(sent_a, 'col', swap_a)  3.59 us
    unnamed x10, local copies, waits for them, and re-layouts  3.55 us
  transfers between devices with their start and end apart: 23, of which 14 were waited for; matrix products, arithmetic and copies ran while one was open for 1% of the time, Pallas kernels for 2%

profile of v8, /device:TPU:24, one launch (start us, length us, event | category | flops | bytes accessed | tf_op | source)
XLA Modules:
  0.0 100.0 jit_solution(15551054456217708812)
XLA Ops:
  0.1 1.3 %copy-done = bf16[1920,320]{0,1:T(8,128)(2,1)S(1)} copy-done((bf16[1920,320]{0,1:T(8,128)(2,1)S(1)}, bf16[1920,320]{0,1:T(8,128)(2,1)}, u32[]{:S(2)}) %copy-start) | copy-done | bytes 1228824
  1.4 1.0 copy-done.2
  2.3 1.7 %shard_map.55 = (bf16[128,1920]{1,0:T(8,128)(2,1)S(1)}, bf16[128,1920]{1,0:T(8,128)(2,1)S(1)}, bf16[256,320]{1,0:T(8,128)(2,1)S(1)}) custom-call(s32[2]{0:T(128)S(1)} %pad_add_fusion.at_ref, bf16[320,512]{1,0:T(8,128)(2,1)S(1)} %copy-done.2, bf16[320,1920]{1,0:T(8,128)(2,1)S(1)} %bitcast.13), custom_call_target="tpu_custom_call" | custom-call | flops 314572800 | bytes 1600000 | tf_op jit(solution)/shard_map/pallas_call | solution.py:210
  4.0 2.0 %collective-permute-start.3 = (bf16[128,1920]{1,0:T(8,128)(2,1)S(1)}, bf16[128,1920]{1,0:T(8,128)(2,1)S(1)}, u32[]{:S(2)}, u32[]{:S(2)}) collective-permute-start(bf16[128,1920]{1,0:T(8,128)(2,1)S(1)} %get-tuple-element.20), channel_id=1, source_target_pairs={{0,3},{1,2},{2,1},{3,0},{4,7},{5,6},{6,5},{7,4},{8,11},{9,10},{10,... | collective-permute-start | bytes 1474568 | tf_op jit(solution)/shard_map/ppermute | solution.py:220
  6.7 1.3 %copy-done.1 = bf16[1920,320]{0,1:T(8,128)(2,1)S(1)} copy-done((bf16[1920,320]{0,1:T(8,128)(2,1)S(1)}, bf16[1920,320]{0,1:T(8,128)(2,1)}, u32[]{:S(2)}) %copy-start.1) | copy-done | bytes 1228824
  8.0 0.7 shard_map.56
  8.7 9.6 %collective-permute-done.3 = bf16[128,1920]{1,0:T(8,128)(2,1)S(1)} collective-permute-done((bf16[128,1920]{1,0:T(8,128)(2,1)S(1)}, bf16[128,1920]{1,0:T(8,128)(2,1)S(1)}, u32[]{:S(2)}, u32[]{:S(2)}) %collective-permute-start.3) | collective-permute-done | bytes 491552 | tf_op jit(solution)/shard_map/ppermute | solution.py:220
  18.7 2.0 %collective-permute-start.1 = (bf16[64,1920]{1,0:T(8,128)(2,1)S(1)}, bf16[64,1920]{1,0:T(8,128)(2,1)S(1)}, u32[]{:S(2)}, u32[]{:S(2)}) collective-permute-start(bf16[64,1920]{1,0:T(8,128)(2,1)S(1)} %get-tuple-element.28), channel_id=1, source_target_pairs={{0,3},{1,2},{2,1},{3,0},{4,7},{5,6},{6,5},{7,4},{8,11},{9,10},{10,... | collective-permute-start | bytes 737288 | tf_op jit(solution)/shard_map/ppermute | solution.py:237
  20.6 4.7 %collective-permute-done.4 = bf16[64,1920]{1,0:T(8,128)(2,1)S(1)} collective-permute-done((bf16[64,1920]{1,0:T(8,128)(2,1)S(1)}, bf16[64,1920]{1,0:T(8,128)(2,1)S(1)}, u32[]{:S(2)}, u32[]{:S(2)}) %collective-permute-start.4) | collective-permute-done | bytes 245792 | tf_op jit(solution)/shard_map/ppermute | solution.py:238
  25.4 6.4 %collective-permute-start.5 = (bf16[32,1920]{1,0:T(8,128)(2,1)S(1)}, bf16[32,1920]{1,0:T(8,128)(2,1)S(1)}, u32[]{:S(2)}, u32[]{:S(2)}) collective-permute-start(bf16[32,1920]{1,0:T(8,128)(2,1)S(1)} %get-tuple-element.34), channel_id=1, source_target_pairs={{0,12},{1,13},{2,14},{3,15},{4,8},{5,9},{6,10},{7,11},{8,4},{9,5},... | collective-permute-start | bytes 368648 | tf_op jit(solution)/shard_map/ppermute | solution.py:238
  31.8 1.5 %collective-permute-start.2 = (bf16[32,1920]{1,0:T(8,128)(2,1)S(1)}, bf16[32,1920]{1,0:T(8,128)(2,1)S(1)}, u32[]{:S(2)}, u32[]{:S(2)}) collective-permute-start(bf16[32,1920]{1,0:T(8,128)(2,1)S(1)} %get-tuple-element.32), channel_id=1, source_target_pairs={{0,4},{1,5},{2,6},{3,7},{4,0},{5,1},{6,2},{7,3},{8,12},{9,13},{10,... | collective-permute-start | bytes 368648 | tf_op jit(solution)/shard_map/ppermute | solution.py:237
  33.4 2.2 %collective-permute-done.5 = bf16[32,1920]{1,0:T(8,128)(2,1)S(1)} collective-permute-done((bf16[32,1920]{1,0:T(8,128)(2,1)S(1)}, bf16[32,1920]{1,0:T(8,128)(2,1)S(1)}, u32[]{:S(2)}, u32[]{:S(2)}) %collective-permute-start.5) | collective-permute-done | bytes 122912 | tf_op jit(solution)/shard_map/ppermute | solution.py:238
  36.3 5.1 %collective-permute-done.2 = bf16[32,1920]{1,0:T(8,128)(2,1)S(1)} collective-permute-done((bf16[32,1920]{1,0:T(8,128)(2,1)S(1)}, bf16[32,1920]{1,0:T(8,128)(2,1)S(1)}, u32[]{:S(2)}, u32[]{:S(2)}) %collective-permute-start.2) | collective-permute-done | bytes 122912 | tf_op jit(solution)/shard_map/ppermute | solution.py:237
  42.0 7.5 %collective-permute-done.6 = bf16[16,1920]{1,0:T(8,128)(2,1)S(1)} collective-permute-done((bf16[16,1920]{1,0:T(8,128)(2,1)S(1)}, bf16[16,1920]{1,0:T(8,128)(2,1)S(1)}, u32[]{:S(2)}, u32[]{:S(2)}) %collective-permute-start.6) | collective-permute-done | bytes 61472 | tf_op jit(solution)/shard_map/ppermute | solution.py:237
  49.8 2.9 %collective-permute-start.8 = (bf16[32,1920]{1,0:T(8,128)(2,1)S(1)}, bf16[32,1920]{1,0:T(8,128)(2,1)S(1)}, u32[]{:S(2)}, u32[]{:S(2)}) collective-permute-start(bf16[32,1920]{1,0:T(8,128)(2,1)S(1)} %fusion.2.own), channel_id=1, source_target_pairs={{0,4},{1,5},{2,6},{3,7},{4,8},{5,9},{6,10},{7,11},{8,12},{9,13},{1... | collective-permute-start | bytes 368648 | tf_op jit(solution)/shard_map/ppermute | solution.py:261
  52.7 2.4 %collective-permute-start.16 = (bf16[32,1920]{1,0:T(8,128)(2,1)S(1)}, bf16[32,1920]{1,0:T(8,128)(2,1)S(1)}, u32[]{:S(2)}, u32[]{:S(2)}) collective-permute-start(bf16[32,1920]{1,0:T(8,128)(2,1)S(1)} %fusion.2.own), channel_id=1, source_target_pairs={{0,0},{1,32},{2,64},{3,96},{4,16},{5,48},{6,80},{7,112},{8,128},{9... | collective-permute-start | bytes 368648 | tf_op jit(solution)/shard_map/ppermute | solution.py:263
  55.1 1.6 %collective-permute-done.9.right = bf16[32,1920]{1,0:T(8,128)(2,1)S(1)} collective-permute-done((bf16[32,1920]{1,0:T(8,128)(2,1)S(1)}, bf16[32,1920]{1,0:T(8,128)(2,1)S(1)}, u32[]{:S(2)}, u32[]{:S(2)}) %collective-permute-start.9) | collective-permute-done | bytes 122912 | tf_op jit(solution)/shard_map/ppermute | solution.py:262
  56.7 1.4 %collective-permute-done.8.left = bf16[32,1920]{1,0:T(8,128)(2,1)S(1)} collective-permute-done((bf16[32,1920]{1,0:T(8,128)(2,1)S(1)}, bf16[32,1920]{1,0:T(8,128)(2,1)S(1)}, u32[]{:S(2)}, u32[]{:S(2)}) %collective-permute-start.8) | collective-permute-done | bytes 122912 | tf_op jit(solution)/shard_map/ppermute | solution.py:261
  58.2 2.6 %collective-permute-start.10 = (bf16[16,1920]{1,0:T(8,128)(2,1)S(1)}, bf16[16,1920]{1,0:T(8,128)(2,1)S(1)}, u32[]{:S(2)}, u32[]{:S(2)}) collective-permute-start(bf16[16,1920]{1,0:T(8,128)(2,1)S(1)} %get-tuple-element.21), channel_id=1, source_target_pairs={{0,4},{1,5},{2,6},{3,7},{4,8},{5,9},{6,10},{7,11},{8,12},{9,13},{1... | collective-permute-start | bytes 184328 | tf_op jit(solution)/shard_map/ppermute | solution.py:265
  60.8 1.6 %collective-permute-start.11 = (bf16[16,1920]{1,0:T(8,128)(2,1)S(1)}, bf16[16,1920]{1,0:T(8,128)(2,1)S(1)}, u32[]{:S(2)}, u32[]{:S(2)}) collective-permute-start(bf16[16,1920]{1,0:T(8,128)(2,1)S(1)} %get-tuple-element.22), channel_id=1, source_target_pairs={{0,12},{1,13},{2,14},{3,15},{4,0},{5,1},{6,2},{7,3},{8,4},{9,5},{1... | collective-permute-start | bytes 184328 | tf_op jit(solution)/shard_map/ppermute | solution.py:266
  62.4 2.0 %collective-permute-start.17 = (bf16[32,1920]{1,0:T(8,128)(2,1)S(1)}, bf16[32,1920]{1,0:T(8,128)(2,1)S(1)}, u32[]{:S(2)}, u32[]{:S(2)}) collective-permute-start(bf16[32,1920]{1,0:T(8,128)(2,1)S(1)} %collective-permute-done.16.flipped), channel_id=1, source_target_pairs={{0,128},{16,144},{32,160},{48,176},{64,192},{80,208},{96,224},{112... | collective-permute-start | bytes 368648 | tf_op jit(solution)/shard_map/ppermute | solution.py:275
  64.7 1.8 %collective-permute-done.11.far_b = bf16[16,1920]{1,0:T(8,128)(2,1)S(1)} collective-permute-done((bf16[16,1920]{1,0:T(8,128)(2,1)S(1)}, bf16[16,1920]{1,0:T(8,128)(2,1)S(1)}, u32[]{:S(2)}, u32[]{:S(2)}) %collective-permute-start.11) | collective-permute-done | bytes 61472 | tf_op jit(solution)/shard_map/ppermute | solution.py:266
  67.2 3.2 %collective-permute-start.12 = (bf16[128,1920]{1,0:T(8,128)(2,1)S(1)}, bf16[128,1920]{1,0:T(8,128)(2,1)S(1)}, u32[]{:S(2)}, u32[]{:S(2)}) collective-permute-start(bf16[128,1920]{1,0:T(8,128)(2,1)S(1)} %shard_map.58.own), channel_id=1, source_target_pairs={{0,1},{1,2},{2,3},{3,0},{4,5},{5,6},{6,7},{7,4},{8,9},{9,10},{10,1... | collective-permute-start | bytes 1474568 | tf_op jit(solution)/shard_map/ppermute | solution.py:273
  71.0 2.2 %collective-permute-start.19 = (bf16[64,1920]{1,0:T(8,128)(2,1)S(1)}, bf16[64,1920]{1,0:T(8,128)(2,1)S(1)}, u32[]{:S(2)}, u32[]{:S(2)}) collective-permute-start(bf16[64,1920]{1,0:T(8,128)(2,1)S(1)} %shard_map.61.near), channel_id=1, source_target_pairs={{0,96},{16,112},{32,0},{48,16},{64,32},{80,48},{96,64},{112,80},{1... | collective-permute-start | bytes 737288 | tf_op jit(solution)/shard_map/ppermute | solution.py:284
  73.3 5.8 %collective-permute-done.13.right = bf16[128,1920]{1,0:T(8,128)(2,1)S(1)} collective-permute-done((bf16[128,1920]{1,0:T(8,128)(2,1)S(1)}, bf16[128,1920]{1,0:T(8,128)(2,1)S(1)}, u32[]{:S(2)}, u32[]{:S(2)}) %collective-permute-start.13) | collective-permute-done | bytes 491552 | tf_op jit(solution)/shard_map/ppermute | solution.py:274
  79.3 3.2 %collective-permute-start.14 = (bf16[64,1920]{1,0:T(8,128)(2,1)S(1)}, bf16[64,1920]{1,0:T(8,128)(2,1)S(1)}, u32[]{:S(2)}, u32[]{:S(2)}) collective-permute-start(bf16[64,1920]{1,0:T(8,128)(2,1)S(1)} %get-tuple-element.23.after), channel_id=1, source_target_pairs={{0,1},{1,2},{2,3},{3,0},{4,5},{5,6},{6,7},{7,4},{8,9},{9,10},{10,1... | collective-permute-start | bytes 737288 | tf_op jit(solution)/shard_map/ppermute | solution.py:286
  82.5 2.3 %collective-permute-start.20 = (bf16[32,1920]{1,0:T(8,128)(2,1)S(1)}, bf16[32,1920]{1,0:T(8,128)(2,1)S(1)}, u32[]{:S(2)}, u32[]{:S(2)}) collective-permute-start(bf16[32,1920]{1,0:T(8,128)(2,1)S(1)} %get-tuple-element.25), channel_id=1, source_target_pairs={{0,32},{16,48},{32,64},{48,80},{64,96},{80,112},{96,0},{112,16},{1... | collective-permute-start | bytes 368648 | tf_op jit(solution)/shard_map/ppermute | solution.py:296
  84.8 1.0 %collective-permute-start.21 = (bf16[32,1920]{1,0:T(8,128)(2,1)S(1)}, bf16[32,1920]{1,0:T(8,128)(2,1)S(1)}, u32[]{:S(2)}, u32[]{:S(2)}) collective-permute-start(bf16[32,1920]{1,0:T(8,128)(2,1)S(1)} %get-tuple-element.26), channel_id=1, source_target_pairs={{0,96},{16,112},{32,0},{48,16},{64,32},{80,48},{96,64},{112,80},{1... | collective-permute-start | bytes 368648 | tf_op jit(solution)/shard_map/ppermute | solution.py:297
  85.8 2.9 %collective-permute-done.20.x_far_a = bf16[32,1920]{1,0:T(8,128)(2,1)S(1)} collective-permute-done((bf16[32,1920]{1,0:T(8,128)(2,1)S(1)}, bf16[32,1920]{1,0:T(8,128)(2,1)S(1)}, u32[]{:S(2)}, u32[]{:S(2)}) %collective-permute-start.20) | collective-permute-done | bytes 122912 | tf_op jit(solution)/shard_map/ppermute | solution.py:296
  88.7 2.5 %collective-permute-done.21.x_far_b = bf16[32,1920]{1,0:T(8,128)(2,1)S(1)} collective-permute-done((bf16[32,1920]{1,0:T(8,128)(2,1)S(1)}, bf16[32,1920]{1,0:T(8,128)(2,1)S(1)}, u32[]{:S(2)}, u32[]{:S(2)}) %collective-permute-start.21) | collective-permute-done | bytes 122912 | tf_op jit(solution)/shard_map/ppermute | solution.py:297
  91.4 2.5 %collective-permute-done.22.other = bf16[256,1920]{1,0:T(8,128)(2,1)S(1)} collective-permute-done((bf16[256,1920]{1,0:T(8,128)(2,1)S(1)}, bf16[256,1920]{1,0:T(8,128)(2,1)S(1)}, u32[]{:S(2)}, u32[]{:S(2)}) %collective-permute-start.22) | collective-permute-done | bytes 983072 | tf_op jit(solution)/shard_map/ppermute | solution.py:301
  93.9 6.0 %shard_map.64 = bf16[1920,1920]{1,0:T(8,128)(2,1)} custom-call(s32[2]{0:T(128)S(1)} %pad_add_fusion.at_ref, bf16[128,1920]{1,0:T(8,128)(2,1)S(1)} %shard_map.58.own, bf16[128,1920]{1,0:T(8,128)(2,1)S(1)} %collective-permute-done.12.left, bf16[128,1920]{1,0:T(8,128)(2,1)S(1)} %collective-permute-done.13.right, bf16[128,1920]{1,0:T(8,128)(2,1)S(1)} %shard_map.60.far, ...), custom_call_target="tpu_custom_call" | custom-call | flops 3774873600 | bytes 7372800 | tf_op jit(solution)/shard_map/pallas_call | solution.py:302
  (45 shorter events, 4.7 us)
Async XLA Ops:
  0.0 41.6 %copy-start.4 = (s32[32]{0:T(128)S(1)}, s32[32]{0:T(128)}, u32[]{:S(2)}) copy-start(s32[32]{0:T(128)} %param.9) | copy-start | bytes 388
  0.1 1.3 %copy-start = (bf16[1920,320]{0,1:T(8,128)(2,1)S(1)}, bf16[1920,320]{0,1:T(8,128)(2,1)}, u32[]{:S(2)}) copy-start(bf16[1920,320]{0,1:T(8,128)(2,1)} %param.6) | copy-start | bytes 3686404
  1.4 1.0 copy-start.2
  2.3 47.2 %copy-start.3 = (bf16[1920,32]{0,1:T(8,128)(2,1)S(1)}, bf16[1920,32]{0,1:T(8,128)(2,1)}, u32[]{:S(2)}) copy-start(bf16[1920,32]{0,1:T(8,128)(2,1)} %param.5) | copy-start | bytes 368644
  4.0 14.3 %collective-permute-start.3 = (bf16[128,1920]{1,0:T(8,128)(2,1)S(1)}, bf16[128,1920]{1,0:T(8,128)(2,1)S(1)}, u32[]{:S(2)}, u32[]{:S(2)}) collective-permute-start(bf16[128,1920]{1,0:T(8,128)(2,1)S(1)} %get-tuple-element.20), channel_id=1, source_target_pairs={{0,3},{1,2},{2,1},{3,0},{4,7},{5,6},{6,5},{7,4},{8,11},{9,10},{10,... | collective-permute-start | bytes 1474568 | tf_op jit(solution)/shard_map/ppermute | solution.py:220
  6.1 12.4 %collective-permute-start = (bf16[128,1920]{1,0:T(8,128)(2,1)S(1)}, bf16[128,1920]{1,0:T(8,128)(2,1)S(1)}, u32[]{:S(2)}, u32[]{:S(2)}) collective-permute-start(bf16[128,1920]{1,0:T(8,128)(2,1)S(1)} %get-tuple-element.18), channel_id=1, source_target_pairs={{0,1},{1,0},{2,3},{3,2},{4,5},{5,4},{6,7},{7,6},{8,9},{9,8},{10,11... | collective-permute-start | bytes 1474568 | tf_op jit(solution)/shard_map/ppermute | solution.py:219
  6.7 1.3 %copy-start.1 = (bf16[1920,320]{0,1:T(8,128)(2,1)S(1)}, bf16[1920,320]{0,1:T(8,128)(2,1)}, u32[]{:S(2)}) copy-start(bf16[1920,320]{0,1:T(8,128)(2,1)} %param.6) | copy-start | bytes 3686404
  18.4 6.9 %collective-permute-start.4 = (bf16[64,1920]{1,0:T(8,128)(2,1)S(1)}, bf16[64,1920]{1,0:T(8,128)(2,1)S(1)}, u32[]{:S(2)}, u32[]{:S(2)}) collective-permute-start(bf16[64,1920]{1,0:T(8,128)(2,1)S(1)} %get-tuple-element.30), channel_id=1, source_target_pairs={{0,1},{1,0},{2,3},{3,2},{4,5},{5,4},{6,7},{7,6},{8,9},{9,8},{10,11... | collective-permute-start | bytes 737288 | tf_op jit(solution)/shard_map/ppermute | solution.py:238
  18.7 13.1 %collective-permute-start.1 = (bf16[64,1920]{1,0:T(8,128)(2,1)S(1)}, bf16[64,1920]{1,0:T(8,128)(2,1)S(1)}, u32[]{:S(2)}, u32[]{:S(2)}) collective-permute-start(bf16[64,1920]{1,0:T(8,128)(2,1)S(1)} %get-tuple-element.28), channel_id=1, source_target_pairs={{0,3},{1,2},{2,1},{3,0},{4,7},{5,6},{6,5},{7,4},{8,11},{9,10},{10,... | collective-permute-start | bytes 737288 | tf_op jit(solution)/shard_map/ppermute | solution.py:237
  25.4 10.2 %collective-permute-start.5 = (bf16[32,1920]{1,0:T(8,128)(2,1)S(1)}, bf16[32,1920]{1,0:T(8,128)(2,1)S(1)}, u32[]{:S(2)}, u32[]{:S(2)}) collective-permute-start(bf16[32,1920]{1,0:T(8,128)(2,1)S(1)} %get-tuple-element.34), channel_id=1, source_target_pairs={{0,12},{1,13},{2,14},{3,15},{4,8},{5,9},{6,10},{7,11},{8,4},{9,5},... | collective-permute-start | bytes 368648 | tf_op jit(solution)/shard_map/ppermute | solution.py:238
  31.8 9.5 %collective-permute-start.2 = (bf16[32,1920]{1,0:T(8,128)(2,1)S(1)}, bf16[32,1920]{1,0:T(8,128)(2,1)S(1)}, u32[]{:S(2)}, u32[]{:S(2)}) collective-permute-start(bf16[32,1920]{1,0:T(8,128)(2,1)S(1)} %get-tuple-element.32), channel_id=1, source_target_pairs={{0,4},{1,5},{2,6},{3,7},{4,0},{5,1},{6,2},{7,3},{8,12},{9,13},{10,... | collective-permute-start | bytes 368648 | tf_op jit(solution)/shard_map/ppermute | solution.py:237
  35.7 6.4 %collective-permute-start.7 = (bf16[16,1920]{1,0:T(8,128)(2,1)S(1)}, bf16[16,1920]{1,0:T(8,128)(2,1)S(1)}, u32[]{:S(2)}, u32[]{:S(2)}) collective-permute-start(bf16[16,1920]{1,0:T(8,128)(2,1)S(1)} %get-tuple-element.37), channel_id=1, source_target_pairs={{0,4},{1,5},{2,6},{3,7},{4,0},{5,1},{6,2},{7,3},{8,12},{9,13},{10,... | collective-permute-start | bytes 184328 | tf_op jit(solution)/shard_map/ppermute | solution.py:238
  41.4 8.2 %collective-permute-start.6 = (bf16[16,1920]{1,0:T(8,128)(2,1)S(1)}, bf16[16,1920]{1,0:T(8,128)(2,1)S(1)}, u32[]{:S(2)}, u32[]{:S(2)}) collective-permute-start(bf16[16,1920]{1,0:T(8,128)(2,1)S(1)} %get-tuple-element.35), channel_id=1, source_target_pairs={{0,12},{1,13},{2,14},{3,15},{4,8},{5,9},{6,10},{7,11},{8,4},{9,5},... | collective-permute-start | bytes 184328 | tf_op jit(solution)/shard_map/ppermute | solution.py:237
  49.7 7.1 %collective-permute-start.9 = (bf16[32,1920]{1,0:T(8,128)(2,1)S(1)}, bf16[32,1920]{1,0:T(8,128)(2,1)S(1)}, u32[]{:S(2)}, u32[]{:S(2)}) collective-permute-start(bf16[32,1920]{1,0:T(8,128)(2,1)S(1)} %fusion.2.own), channel_id=1, source_target_pairs={{0,12},{1,13},{2,14},{3,15},{4,0},{5,1},{6,2},{7,3},{8,4},{9,5},{1... | collective-permute-start | bytes 368648 | tf_op jit(solution)/shard_map/ppermute | solution.py:262
  49.8 8.4 %collective-permute-start.8 = (bf16[32,1920]{1,0:T(8,128)(2,1)S(1)}, bf16[32,1920]{1,0:T(8,128)(2,1)S(1)}, u32[]{:S(2)}, u32[]{:S(2)}) collective-permute-start(bf16[32,1920]{1,0:T(8,128)(2,1)S(1)} %fusion.2.own), channel_id=1, source_target_pairs={{0,4},{1,5},{2,6},{3,7},{4,8},{5,9},{6,10},{7,11},{8,12},{9,13},{1... | collective-permute-start | bytes 368648 | tf_op jit(solution)/shard_map/ppermute | solution.py:261
  52.7 9.7 %collective-permute-start.16 = (bf16[32,1920]{1,0:T(8,128)(2,1)S(1)}, bf16[32,1920]{1,0:T(8,128)(2,1)S(1)}, u32[]{:S(2)}, u32[]{:S(2)}) collective-permute-start(bf16[32,1920]{1,0:T(8,128)(2,1)S(1)} %fusion.2.own), channel_id=1, source_target_pairs={{0,0},{1,32},{2,64},{3,96},{4,16},{5,48},{6,80},{7,112},{8,128},{9... | collective-permute-start | bytes 368648 | tf_op jit(solution)/shard_map/ppermute | solution.py:263
  58.2 6.6 %collective-permute-start.10 = (bf16[16,1920]{1,0:T(8,128)(2,1)S(1)}, bf16[16,1920]{1,0:T(8,128)(2,1)S(1)}, u32[]{:S(2)}, u32[]{:S(2)}) collective-permute-start(bf16[16,1920]{1,0:T(8,128)(2,1)S(1)} %get-tuple-element.21), channel_id=1, source_target_pairs={{0,4},{1,5},{2,6},{3,7},{4,8},{5,9},{6,10},{7,11},{8,12},{9,13},{1... | collective-permute-start | bytes 184328 | tf_op jit(solution)/shard_map/ppermute | solution.py:265
  60.8 5.7 %collective-permute-start.11 = (bf16[16,1920]{1,0:T(8,128)(2,1)S(1)}, bf16[16,1920]{1,0:T(8,128)(2,1)S(1)}, u32[]{:S(2)}, u32[]{:S(2)}) collective-permute-start(bf16[16,1920]{1,0:T(8,128)(2,1)S(1)} %get-tuple-element.22), channel_id=1, source_target_pairs={{0,12},{1,13},{2,14},{3,15},{4,0},{5,1},{6,2},{7,3},{8,4},{9,5},{1... | collective-permute-start | bytes 184328 | tf_op jit(solution)/shard_map/ppermute | solution.py:266
  62.4 8.1 %collective-permute-start.17 = (bf16[32,1920]{1,0:T(8,128)(2,1)S(1)}, bf16[32,1920]{1,0:T(8,128)(2,1)S(1)}, u32[]{:S(2)}, u32[]{:S(2)}) collective-permute-start(bf16[32,1920]{1,0:T(8,128)(2,1)S(1)} %collective-permute-done.16.flipped), channel_id=1, source_target_pairs={{0,128},{16,144},{32,160},{48,176},{64,192},{80,208},{96,224},{112... | collective-permute-start | bytes 368648 | tf_op jit(solution)/shard_map/ppermute | solution.py:275
  67.1 12.0 %collective-permute-start.13 = (bf16[128,1920]{1,0:T(8,128)(2,1)S(1)}, bf16[128,1920]{1,0:T(8,128)(2,1)S(1)}, u32[]{:S(2)}, u32[]{:S(2)}) collective-permute-start(bf16[128,1920]{1,0:T(8,128)(2,1)S(1)} %shard_map.58.own), channel_id=1, source_target_pairs={{0,3},{1,0},{2,1},{3,2},{4,7},{5,4},{6,5},{7,6},{8,11},{9,8},{10,9... | collective-permute-start | bytes 1474568 | tf_op jit(solution)/shard_map/ppermute | solution.py:274
  67.2 11.9 %collective-permute-start.12 = (bf16[128,1920]{1,0:T(8,128)(2,1)S(1)}, bf16[128,1920]{1,0:T(8,128)(2,1)S(1)}, u32[]{:S(2)}, u32[]{:S(2)}) collective-permute-start(bf16[128,1920]{1,0:T(8,128)(2,1)S(1)} %shard_map.58.own), channel_id=1, source_target_pairs={{0,1},{1,2},{2,3},{3,0},{4,5},{5,6},{6,7},{7,4},{8,9},{9,10},{10,1... | collective-permute-start | bytes 1474568 | tf_op jit(solution)/shard_map/ppermute | solution.py:273
  71.0 11.5 %collective-permute-start.19 = (bf16[64,1920]{1,0:T(8,128)(2,1)S(1)}, bf16[64,1920]{1,0:T(8,128)(2,1)S(1)}, u32[]{:S(2)}, u32[]{:S(2)}) collective-permute-start(bf16[64,1920]{1,0:T(8,128)(2,1)S(1)} %shard_map.61.near), channel_id=1, source_target_pairs={{0,96},{16,112},{32,0},{48,16},{64,32},{80,48},{96,64},{112,80},{1... | collective-permute-start | bytes 737288 | tf_op jit(solution)/shard_map/ppermute | solution.py:284
  73.2 9.3 %collective-permute-start.18 = (bf16[64,1920]{1,0:T(8,128)(2,1)S(1)}, bf16[64,1920]{1,0:T(8,128)(2,1)S(1)}, u32[]{:S(2)}, u32[]{:S(2)}) collective-permute-start(bf16[64,1920]{1,0:T(8,128)(2,1)S(1)} %shard_map.61.near), channel_id=1, source_target_pairs={{0,32},{16,48},{32,64},{48,80},{64,96},{80,112},{96,0},{112,16},{1... | collective-permute-start | bytes 737288 | tf_op jit(solution)/shard_map/ppermute | solution.py:283
  79.2 12.2 %collective-permute-start.15 = (bf16[64,1920]{1,0:T(8,128)(2,1)S(1)}, bf16[64,1920]{1,0:T(8,128)(2,1)S(1)}, u32[]{:S(2)}, u32[]{:S(2)}) collective-permute-start(bf16[64,1920]{1,0:T(8,128)(2,1)S(1)} %get-tuple-element.24), channel_id=1, source_target_pairs={{0,3},{1,0},{2,1},{3,2},{4,7},{5,4},{6,5},{7,6},{8,11},{9,8},{10,9... | collective-permute-start | bytes 737288 | tf_op jit(solution)/shard_map/ppermute | solution.py:287
  79.3 12.1 %collective-permute-start.14 = (bf16[64,1920]{1,0:T(8,128)(2,1)S(1)}, bf16[64,1920]{1,0:T(8,128)(2,1)S(1)}, u32[]{:S(2)}, u32[]{:S(2)}) collective-permute-start(bf16[64,1920]{1,0:T(8,128)(2,1)S(1)} %get-tuple-element.23.after), channel_id=1, source_target_pairs={{0,1},{1,2},{2,3},{3,0},{4,5},{5,6},{6,7},{7,4},{8,9},{9,10},{10,1... | collective-permute-start | bytes 737288 | tf_op jit(solution)/shard_map/ppermute | solution.py:286
  82.5 6.2 %collective-permute-start.20 = (bf16[32,1920]{1,0:T(8,128)(2,1)S(1)}, bf16[32,1920]{1,0:T(8,128)(2,1)S(1)}, u32[]{:S(2)}, u32[]{:S(2)}) collective-permute-start(bf16[32,1920]{1,0:T(8,128)(2,1)S(1)} %get-tuple-element.25), channel_id=1, source_target_pairs={{0,32},{16,48},{32,64},{48,80},{64,96},{80,112},{96,0},{112,16},{1... | collective-permute-start | bytes 368648 | tf_op jit(solution)/shard_map/ppermute | solution.py:296
  84.8 6.4 %collective-permute-start.21 = (bf16[32,1920]{1,0:T(8,128)(2,1)S(1)}, bf16[32,1920]{1,0:T(8,128)(2,1)S(1)}, u32[]{:S(2)}, u32[]{:S(2)}) collective-permute-start(bf16[32,1920]{1,0:T(8,128)(2,1)S(1)} %get-tuple-element.26), channel_id=1, source_target_pairs={{0,96},{16,112},{32,0},{48,16},{64,32},{80,48},{96,64},{112,80},{1... | collective-permute-start | bytes 368648 | tf_op jit(solution)/shard_map/ppermute | solution.py:297
  91.2 2.7 %collective-permute-start.22 = (bf16[256,1920]{1,0:T(8,128)(2,1)S(1)}, bf16[256,1920]{1,0:T(8,128)(2,1)S(1)}, u32[]{:S(2)}, u32[]{:S(2)}) collective-permute-start(bf16[256,1920]{1,0:T(8,128)(2,1)S(1)} %shard_map.63.near), channel_id=1, source_target_pairs={{0,16},{16,0},{32,48},{48,32},{64,80},{80,64},{96,112},{112,96},{1... | collective-permute-start | bytes 2949128 | tf_op jit(solution)/shard_map/ppermute | solution.py:301

commit v9 on v8

--- a/solution.py
+++ b/solution.py
@@ -278,11 +278,11 @@
         out_shape=shape(64, rows),
         in_specs=[SCALAR] + [WHOLE] * 2,
         out_specs=WHOLE,
-        cost_estimate=pl.CostEstimate(flops=4000000000, bytes_accessed=491520, transcendentals=0),
+        cost_estimate=pl.CostEstimate(flops=1600000000, bytes_accessed=491520, transcendentals=0),
     )(at, flipped, pair)
     x_left = lax.ppermute(near, "row", x_turn(1))
     x_right = lax.ppermute(near, "row", x_turn(-1))
-    low, high = halves(left, right, 16000000000)
+    low, high = halves(left, right, 8000000000)
     far_a = lax.ppermute(low, "col", y_turn(1))
     far_b = lax.ppermute(high, "col", y_turn(-1))
     far = call(
@@ -290,7 +290,7 @@
         out_shape=shape(128, rows),
         in_specs=[WHOLE] * 2,
         out_specs=WHOLE,
-        cost_estimate=pl.CostEstimate(flops=16000000000, bytes_accessed=983040, transcendentals=0),
+        cost_estimate=pl.CostEstimate(flops=8000000000, bytes_accessed=983040, transcendentals=0),
     )(far_a, far_b)
     x_low, x_high = halves(x_left, x_right, 0)
     x_far_a = lax.ppermute(x_low, "row", x_turn(1))

time: 101 us -> 100 us (0.990)
    ppermute x1, waiting for transfers between devices: 5.84 us -> 0.01 us  [per_device(): right = lax.ppermute(mine, 'col', y_turn(-1))]
    ppermute x1, waiting for transfers between devices: 0.01 us -> 4.79 us  [per_device(): x_left = lax.ppermute(near, 'row', x_turn(1))]
    ppermute x1, waiting for transfers between devices: 0.01 us -> 4.17 us  [per_device(): x_right = lax.ppermute(near, 'row', x_turn(-1))]
    ppermute x1, waiting for transfers between devices: 0.01 us -> 3.99 us  [per_device(): far_b = lax.ppermute(high, 'col', y_turn(-1))]
    ppermute x1, waiting for transfers between devices: 2.85 us -> 0.01 us  [per_device(): x_far_a = lax.ppermute(x_low, 'row', x_turn(1))]
    ppermute x1, waiting for transfers between devices: 2.49 us -> 0.01 us  [per_device(): other = lax.ppermute(near, 'row', [(r, r ^ 1) for r in range(16)])]
    ppermute x1, waiting for transfers between devices: 2.48 us -> 0.01 us  [per_device(): x_far_b = lax.ppermute(x_high, 'row', x_turn(-1))]
    ppermute x1, starting transfers between devices: 2.27 us -> 0.08 us  [per_device(): x_far_a = lax.ppermute(x_low, 'row', x_turn(1))]
  transfers between devices with their start and end apart: 23 -> 23, of which waited for: 14 -> 13; matrix products, arithmetic and copies ran while one was open for 1% -> 1% of each run, Pallas kernels for 2% -> 2%
where the time goes in v9:
time: 100 us; the launch traced here: 99.3 us
  waiting for transfers between devices  47.8 us (48%)
  starting transfers between devices  36.7 us (37%)
  Pallas kernels  9.7 us (10%)
  local copies, waits for them, and re-layouts  3.62 us (4%)
  other arithmetic  1.24 us (1%)
    ppermute x3, waiting for transfers between devices, per_device(): next_a = lax.ppermute(sent_a, 'col', swap_a)  12.6 us
    ppermute x1, waiting for transfers between devices, per_device(): got_b = lax.ppermute(sent_b, 'col', y_swap(3))  9.57 us
    ppermute x3, waiting for transfers between devices, per_device(): next_b = lax.ppermute(sent_b, 'col', swap_b)  7.39 us
    ppermute x3, starting transfers between devices, per_device(): next_b = lax.ppermute(sent_b, 'col', swap_b)  7.11 us
    pallas_call x1, Pallas kernels, per_device(): call(last_kernel, out_shape=shape(rows, rows), in_specs=[SCALAR] + [WHOLE...  6.01 us
    ppermute x1, waiting for transfers between devices, per_device(): x_left = lax.ppermute(near, 'row', x_turn(1))  4.79 us
    ppermute x1, waiting for transfers between devices, per_device(): x_right = lax.ppermute(near, 'row', x_turn(-1))  4.17 us
    ppermute x1, waiting for transfers between devices, per_device(): far_b = lax.ppermute(high, 'col', y_turn(-1))  3.99 us
  transfers between devices with their start and end apart: 23, of which 13 were waited for; matrix products, arithmetic and copies ran while one was open for 1% of the time, Pallas kernels for 2%

profile of v9, /device:TPU:24, one launch (start us, length us, event | category | flops | bytes accessed | tf_op | source)
XLA Modules:
  0.0 99.3 jit_solution(5583949922247210482)
XLA Ops:
  0.1 1.3 %copy-done = bf16[1920,320]{0,1:T(8,128)(2,1)S(1)} copy-done((bf16[1920,320]{0,1:T(8,128)(2,1)S(1)}, bf16[1920,320]{0,1:T(8,128)(2,1)}, u32[]{:S(2)}) %copy-start) | copy-done | bytes 1228824
  1.4 1.0 copy-done.2
  2.3 1.7 %shard_map.55 = (bf16[128,1920]{1,0:T(8,128)(2,1)S(1)}, bf16[128,1920]{1,0:T(8,128)(2,1)S(1)}, bf16[256,320]{1,0:T(8,128)(2,1)S(1)}) custom-call(s32[2]{0:T(128)S(1)} %pad_add_fusion.at_ref, bf16[320,512]{1,0:T(8,128)(2,1)S(1)} %copy-done.2, bf16[320,1920]{1,0:T(8,128)(2,1)S(1)} %bitcast.13), custom_call_target="tpu_custom_call" | custom-call | flops 314572800 | bytes 1600000 | tf_op jit(solution)/shard_map/pallas_call | solution.py:210
  4.0 2.0 %collective-permute-start.3 = (bf16[128,1920]{1,0:T(8,128)(2,1)S(1)}, bf16[128,1920]{1,0:T(8,128)(2,1)S(1)}, u32[]{:S(2)}, u32[]{:S(2)}) collective-permute-start(bf16[128,1920]{1,0:T(8,128)(2,1)S(1)} %get-tuple-element.20), channel_id=1, source_target_pairs={{0,3},{1,2},{2,1},{3,0},{4,7},{5,6},{6,5},{7,4},{8,11},{9,10},{10,... | collective-permute-start | bytes 1474568 | tf_op jit(solution)/shard_map/ppermute | solution.py:220
  6.1 0.7 convert_element_type.179
  6.7 1.3 %copy-done.1 = bf16[1920,320]{0,1:T(8,128)(2,1)S(1)} copy-done((bf16[1920,320]{0,1:T(8,128)(2,1)S(1)}, bf16[1920,320]{0,1:T(8,128)(2,1)}, u32[]{:S(2)}) %copy-start.1) | copy-done | bytes 1228824
  8.0 0.7 shard_map.56
  8.7 9.6 %collective-permute-done.3 = bf16[128,1920]{1,0:T(8,128)(2,1)S(1)} collective-permute-done((bf16[128,1920]{1,0:T(8,128)(2,1)S(1)}, bf16[128,1920]{1,0:T(8,128)(2,1)S(1)}, u32[]{:S(2)}, u32[]{:S(2)}) %collective-permute-start.3) | collective-permute-done | bytes 491552 | tf_op jit(solution)/shard_map/ppermute | solution.py:220
  18.7 2.0 %collective-permute-start.1 = (bf16[64,1920]{1,0:T(8,128)(2,1)S(1)}, bf16[64,1920]{1,0:T(8,128)(2,1)S(1)}, u32[]{:S(2)}, u32[]{:S(2)}) collective-permute-start(bf16[64,1920]{1,0:T(8,128)(2,1)S(1)} %get-tuple-element.28), channel_id=1, source_target_pairs={{0,3},{1,2},{2,1},{3,0},{4,7},{5,6},{6,5},{7,4},{8,11},{9,10},{10,... | collective-permute-start | bytes 737288 | tf_op jit(solution)/shard_map/ppermute | solution.py:237
  20.6 4.7 %collective-permute-done.4 = bf16[64,1920]{1,0:T(8,128)(2,1)S(1)} collective-permute-done((bf16[64,1920]{1,0:T(8,128)(2,1)S(1)}, bf16[64,1920]{1,0:T(8,128)(2,1)S(1)}, u32[]{:S(2)}, u32[]{:S(2)}) %collective-permute-start.4) | collective-permute-done | bytes 245792 | tf_op jit(solution)/shard_map/ppermute | solution.py:238
  25.4 6.4 %collective-permute-start.5 = (bf16[32,1920]{1,0:T(8,128)(2,1)S(1)}, bf16[32,1920]{1,0:T(8,128)(2,1)S(1)}, u32[]{:S(2)}, u32[]{:S(2)}) collective-permute-start(bf16[32,1920]{1,0:T(8,128)(2,1)S(1)} %get-tuple-element.34), channel_id=1, source_target_pairs={{0,12},{1,13},{2,14},{3,15},{4,8},{5,9},{6,10},{7,11},{8,4},{9,5},... | collective-permute-start | bytes 368648 | tf_op jit(solution)/shard_map/ppermute | solution.py:238
  31.8 1.5 %collective-permute-start.2 = (bf16[32,1920]{1,0:T(8,128)(2,1)S(1)}, bf16[32,1920]{1,0:T(8,128)(2,1)S(1)}, u32[]{:S(2)}, u32[]{:S(2)}) collective-permute-start(bf16[32,1920]{1,0:T(8,128)(2,1)S(1)} %get-tuple-element.32), channel_id=1, source_target_pairs={{0,4},{1,5},{2,6},{3,7},{4,0},{5,1},{6,2},{7,3},{8,12},{9,13},{10,... | collective-permute-start | bytes 368648 | tf_op jit(solution)/shard_map/ppermute | solution.py:237
  33.4 2.2 %collective-permute-done.5 = bf16[32,1920]{1,0:T(8,128)(2,1)S(1)} collective-permute-done((bf16[32,1920]{1,0:T(8,128)(2,1)S(1)}, bf16[32,1920]{1,0:T(8,128)(2,1)S(1)}, u32[]{:S(2)}, u32[]{:S(2)}) %collective-permute-start.5) | collective-permute-done | bytes 122912 | tf_op jit(solution)/shard_map/ppermute | solution.py:238
  35.7 0.6 collective-permute-start.7
  36.3 5.1 %collective-permute-done.2 = bf16[32,1920]{1,0:T(8,128)(2,1)S(1)} collective-permute-done((bf16[32,1920]{1,0:T(8,128)(2,1)S(1)}, bf16[32,1920]{1,0:T(8,128)(2,1)S(1)}, u32[]{:S(2)}, u32[]{:S(2)}) %collective-permute-start.2) | collective-permute-done | bytes 122912 | tf_op jit(solution)/shard_map/ppermute | solution.py:237
  42.0 7.5 %collective-permute-done.6 = bf16[16,1920]{1,0:T(8,128)(2,1)S(1)} collective-permute-done((bf16[16,1920]{1,0:T(8,128)(2,1)S(1)}, bf16[16,1920]{1,0:T(8,128)(2,1)S(1)}, u32[]{:S(2)}, u32[]{:S(2)}) %collective-permute-start.6) | collective-permute-done | bytes 61472 | tf_op jit(solution)/shard_map/ppermute | solution.py:237
  49.8 2.9 %collective-permute-start.8 = (bf16[32,1920]{1,0:T(8,128)(2,1)S(1)}, bf16[32,1920]{1,0:T(8,128)(2,1)S(1)}, u32[]{:S(2)}, u32[]{:S(2)}) collective-permute-start(bf16[32,1920]{1,0:T(8,128)(2,1)S(1)} %fusion.2.own), channel_id=1, source_target_pairs={{0,4},{1,5},{2,6},{3,7},{4,8},{5,9},{6,10},{7,11},{8,12},{9,13},{1... | collective-permute-start | bytes 368648 | tf_op jit(solution)/shard_map/ppermute | solution.py:261
  52.7 2.4 %collective-permute-start.16 = (bf16[32,1920]{1,0:T(8,128)(2,1)S(1)}, bf16[32,1920]{1,0:T(8,128)(2,1)S(1)}, u32[]{:S(2)}, u32[]{:S(2)}) collective-permute-start(bf16[32,1920]{1,0:T(8,128)(2,1)S(1)} %fusion.2.own), channel_id=1, source_target_pairs={{0,0},{1,32},{2,64},{3,96},{4,16},{5,48},{6,80},{7,112},{8,128},{9... | collective-permute-start | bytes 368648 | tf_op jit(solution)/shard_map/ppermute | solution.py:263
  55.1 1.6 %collective-permute-done.9.right = bf16[32,1920]{1,0:T(8,128)(2,1)S(1)} collective-permute-done((bf16[32,1920]{1,0:T(8,128)(2,1)S(1)}, bf16[32,1920]{1,0:T(8,128)(2,1)S(1)}, u32[]{:S(2)}, u32[]{:S(2)}) %collective-permute-start.9) | collective-permute-done | bytes 122912 | tf_op jit(solution)/shard_map/ppermute | solution.py:262
  56.7 1.4 %collective-permute-done.8.left = bf16[32,1920]{1,0:T(8,128)(2,1)S(1)} collective-permute-done((bf16[32,1920]{1,0:T(8,128)(2,1)S(1)}, bf16[32,1920]{1,0:T(8,128)(2,1)S(1)}, u32[]{:S(2)}, u32[]{:S(2)}) %collective-permute-start.8) | collective-permute-done | bytes 122912 | tf_op jit(solution)/shard_map/ppermute | solution.py:261
  58.2 2.6 %collective-permute-start.10 = (bf16[16,1920]{1,0:T(8,128)(2,1)S(1)}, bf16[16,1920]{1,0:T(8,128)(2,1)S(1)}, u32[]{:S(2)}, u32[]{:S(2)}) collective-permute-start(bf16[16,1920]{1,0:T(8,128)(2,1)S(1)} %get-tuple-element.21), channel_id=1, source_target_pairs={{0,4},{1,5},{2,6},{3,7},{4,8},{5,9},{6,10},{7,11},{8,12},{9,13},{1... | collective-permute-start | bytes 184328 | tf_op jit(solution)/shard_map/ppermute | solution.py:265
  60.8 1.6 %collective-permute-start.11 = (bf16[16,1920]{1,0:T(8,128)(2,1)S(1)}, bf16[16,1920]{1,0:T(8,128)(2,1)S(1)}, u32[]{:S(2)}, u32[]{:S(2)}) collective-permute-start(bf16[16,1920]{1,0:T(8,128)(2,1)S(1)} %get-tuple-element.22), channel_id=1, source_target_pairs={{0,12},{1,13},{2,14},{3,15},{4,0},{5,1},{6,2},{7,3},{8,4},{9,5},{1... | collective-permute-start | bytes 184328 | tf_op jit(solution)/shard_map/ppermute | solution.py:266
  62.4 2.0 %collective-permute-start.17 = (bf16[32,1920]{1,0:T(8,128)(2,1)S(1)}, bf16[32,1920]{1,0:T(8,128)(2,1)S(1)}, u32[]{:S(2)}, u32[]{:S(2)}) collective-permute-start(bf16[32,1920]{1,0:T(8,128)(2,1)S(1)} %collective-permute-done.16.flipped), channel_id=1, source_target_pairs={{0,128},{16,144},{32,160},{48,176},{64,192},{80,208},{96,224},{112... | collective-permute-start | bytes 368648 | tf_op jit(solution)/shard_map/ppermute | solution.py:275
  64.7 1.8 %collective-permute-done.11.far_b = bf16[16,1920]{1,0:T(8,128)(2,1)S(1)} collective-permute-done((bf16[16,1920]{1,0:T(8,128)(2,1)S(1)}, bf16[16,1920]{1,0:T(8,128)(2,1)S(1)}, u32[]{:S(2)}, u32[]{:S(2)}) %collective-permute-start.11) | collective-permute-done | bytes 61472 | tf_op jit(solution)/shard_map/ppermute | solution.py:266
  67.2 3.2 %collective-permute-start.12 = (bf16[128,1920]{1,0:T(8,128)(2,1)S(1)}, bf16[128,1920]{1,0:T(8,128)(2,1)S(1)}, u32[]{:S(2)}, u32[]{:S(2)}) collective-permute-start(bf16[128,1920]{1,0:T(8,128)(2,1)S(1)} %shard_map.58.own), channel_id=1, source_target_pairs={{0,1},{1,2},{2,3},{3,0},{4,5},{5,6},{6,7},{7,4},{8,9},{9,10},{10,1... | collective-permute-start | bytes 1474568 | tf_op jit(solution)/shard_map/ppermute | solution.py:273
  71.0 2.2 %collective-permute-start.19 = (bf16[64,1920]{1,0:T(8,128)(2,1)S(1)}, bf16[64,1920]{1,0:T(8,128)(2,1)S(1)}, u32[]{:S(2)}, u32[]{:S(2)}) collective-permute-start(bf16[64,1920]{1,0:T(8,128)(2,1)S(1)} %shard_map.61.near), channel_id=1, source_target_pairs={{0,96},{16,112},{32,0},{48,16},{64,32},{80,48},{96,64},{112,80},{1... | collective-permute-start | bytes 737288 | tf_op jit(solution)/shard_map/ppermute | solution.py:284
  73.3 4.2 %collective-permute-done.19.right.x_right = bf16[64,1920]{1,0:T(8,128)(2,1)S(1)} collective-permute-done((bf16[64,1920]{1,0:T(8,128)(2,1)S(1)}, bf16[64,1920]{1,0:T(8,128)(2,1)S(1)}, u32[]{:S(2)}, u32[]{:S(2)}) %collective-permute-start.19) | collective-permute-done | bytes 245792 | tf_op jit(solution)/shard_map/ppermute | solution.py:284
  77.4 4.8 %collective-permute-done.18.left.x_left = bf16[64,1920]{1,0:T(8,128)(2,1)S(1)} collective-permute-done((bf16[64,1920]{1,0:T(8,128)(2,1)S(1)}, bf16[64,1920]{1,0:T(8,128)(2,1)S(1)}, u32[]{:S(2)}, u32[]{:S(2)}) %collective-permute-start.18) | collective-permute-done | bytes 245792 | tf_op jit(solution)/shard_map/ppermute | solution.py:283
  82.3 3.2 %collective-permute-start.21 = (bf16[32,1920]{1,0:T(8,128)(2,1)S(1)}, bf16[32,1920]{1,0:T(8,128)(2,1)S(1)}, u32[]{:S(2)}, u32[]{:S(2)}) collective-permute-start(bf16[32,1920]{1,0:T(8,128)(2,1)S(1)} %get-tuple-element.26), channel_id=1, source_target_pairs={{0,96},{16,112},{32,0},{48,16},{64,32},{80,48},{96,64},{112,80},{1... | collective-permute-start | bytes 368648 | tf_op jit(solution)/shard_map/ppermute | solution.py:297
  85.7 3.2 %collective-permute-start.14 = (bf16[64,1920]{1,0:T(8,128)(2,1)S(1)}, bf16[64,1920]{1,0:T(8,128)(2,1)S(1)}, u32[]{:S(2)}, u32[]{:S(2)}) collective-permute-start(bf16[64,1920]{1,0:T(8,128)(2,1)S(1)} %get-tuple-element.23.after), channel_id=1, source_target_pairs={{0,1},{1,2},{2,3},{3,0},{4,5},{5,6},{6,7},{7,4},{8,9},{9,10},{10,1... | collective-permute-start | bytes 737288 | tf_op jit(solution)/shard_map/ppermute | solution.py:286
  89.1 4.0 %collective-permute-done.15.two = bf16[64,1920]{1,0:T(8,128)(2,1)S(1)} collective-permute-done((bf16[64,1920]{1,0:T(8,128)(2,1)S(1)}, bf16[64,1920]{1,0:T(8,128)(2,1)S(1)}, u32[]{:S(2)}, u32[]{:S(2)}) %collective-permute-start.15) | collective-permute-done | bytes 245792 | tf_op jit(solution)/shard_map/ppermute | solution.py:287
  93.2 6.0 %shard_map.64 = bf16[1920,1920]{1,0:T(8,128)(2,1)} custom-call(s32[2]{0:T(128)S(1)} %pad_add_fusion.at_ref, bf16[128,1920]{1,0:T(8,128)(2,1)S(1)} %shard_map.58.own, bf16[128,1920]{1,0:T(8,128)(2,1)S(1)} %collective-permute-done.12.left, bf16[128,1920]{1,0:T(8,128)(2,1)S(1)} %collective-permute-done.13.right, bf16[128,1920]{1,0:T(8,128)(2,1)S(1)} %shard_map.60.far, ...), custom_call_target="tpu_custom_call" | custom-call | flops 3774873600 | bytes 7372800 | tf_op jit(solution)/shard_map/pallas_call | solution.py:302
  (45 shorter events, 3.5 us)
Async XLA Ops:
  0.0 41.6 %copy-start.4 = (s32[32]{0:T(128)S(1)}, s32[32]{0:T(128)}, u32[]{:S(2)}) copy-start(s32[32]{0:T(128)} %param.9) | copy-start | bytes 388
  0.1 1.3 %copy-start = (bf16[1920,320]{0,1:T(8,128)(2,1)S(1)}, bf16[1920,320]{0,1:T(8,128)(2,1)}, u32[]{:S(2)}) copy-start(bf16[1920,320]{0,1:T(8,128)(2,1)} %param.6) | copy-start | bytes 3686404
  1.4 1.0 copy-start.2
  2.3 47.2 %copy-start.3 = (bf16[1920,32]{0,1:T(8,128)(2,1)S(1)}, bf16[1920,32]{0,1:T(8,128)(2,1)}, u32[]{:S(2)}) copy-start(bf16[1920,32]{0,1:T(8,128)(2,1)} %param.5) | copy-start | bytes 368644
  4.0 14.3 %collective-permute-start.3 = (bf16[128,1920]{1,0:T(8,128)(2,1)S(1)}, bf16[128,1920]{1,0:T(8,128)(2,1)S(1)}, u32[]{:S(2)}, u32[]{:S(2)}) collective-permute-start(bf16[128,1920]{1,0:T(8,128)(2,1)S(1)} %get-tuple-element.20), channel_id=1, source_target_pairs={{0,3},{1,2},{2,1},{3,0},{4,7},{5,6},{6,5},{7,4},{8,11},{9,10},{10,... | collective-permute-start | bytes 1474568 | tf_op jit(solution)/shard_map/ppermute | solution.py:220
  6.1 12.4 %collective-permute-start = (bf16[128,1920]{1,0:T(8,128)(2,1)S(1)}, bf16[128,1920]{1,0:T(8,128)(2,1)S(1)}, u32[]{:S(2)}, u32[]{:S(2)}) collective-permute-start(bf16[128,1920]{1,0:T(8,128)(2,1)S(1)} %get-tuple-element.18), channel_id=1, source_target_pairs={{0,1},{1,0},{2,3},{3,2},{4,5},{5,4},{6,7},{7,6},{8,9},{9,8},{10,11... | collective-permute-start | bytes 1474568 | tf_op jit(solution)/shard_map/ppermute | solution.py:219
  6.7 1.3 %copy-start.1 = (bf16[1920,320]{0,1:T(8,128)(2,1)S(1)}, bf16[1920,320]{0,1:T(8,128)(2,1)}, u32[]{:S(2)}) copy-start(bf16[1920,320]{0,1:T(8,128)(2,1)} %param.6) | copy-start | bytes 3686404
  18.4 6.9 %collective-permute-start.4 = (bf16[64,1920]{1,0:T(8,128)(2,1)S(1)}, bf16[64,1920]{1,0:T(8,128)(2,1)S(1)}, u32[]{:S(2)}, u32[]{:S(2)}) collective-permute-start(bf16[64,1920]{1,0:T(8,128)(2,1)S(1)} %get-tuple-element.30), channel_id=1, source_target_pairs={{0,1},{1,0},{2,3},{3,2},{4,5},{5,4},{6,7},{7,6},{8,9},{9,8},{10,11... | collective-permute-start | bytes 737288 | tf_op jit(solution)/shard_map/ppermute | solution.py:238
  18.7 13.1 %collective-permute-start.1 = (bf16[64,1920]{1,0:T(8,128)(2,1)S(1)}, bf16[64,1920]{1,0:T(8,128)(2,1)S(1)}, u32[]{:S(2)}, u32[]{:S(2)}) collective-permute-start(bf16[64,1920]{1,0:T(8,128)(2,1)S(1)} %get-tuple-element.28), channel_id=1, source_target_pairs={{0,3},{1,2},{2,1},{3,0},{4,7},{5,6},{6,5},{7,4},{8,11},{9,10},{10,... | collective-permute-start | bytes 737288 | tf_op jit(solution)/shard_map/ppermute | solution.py:237
  25.4 10.2 %collective-permute-start.5 = (bf16[32,1920]{1,0:T(8,128)(2,1)S(1)}, bf16[32,1920]{1,0:T(8,128)(2,1)S(1)}, u32[]{:S(2)}, u32[]{:S(2)}) collective-permute-start(bf16[32,1920]{1,0:T(8,128)(2,1)S(1)} %get-tuple-element.34), channel_id=1, source_target_pairs={{0,12},{1,13},{2,14},{3,15},{4,8},{5,9},{6,10},{7,11},{8,4},{9,5},... | collective-permute-start | bytes 368648 | tf_op jit(solution)/shard_map/ppermute | solution.py:238
  31.8 9.5 %collective-permute-start.2 = (bf16[32,1920]{1,0:T(8,128)(2,1)S(1)}, bf16[32,1920]{1,0:T(8,128)(2,1)S(1)}, u32[]{:S(2)}, u32[]{:S(2)}) collective-permute-start(bf16[32,1920]{1,0:T(8,128)(2,1)S(1)} %get-tuple-element.32), channel_id=1, source_target_pairs={{0,4},{1,5},{2,6},{3,7},{4,0},{5,1},{6,2},{7,3},{8,12},{9,13},{10,... | collective-permute-start | bytes 368648 | tf_op jit(solution)/shard_map/ppermute | solution.py:237
  35.7 6.4 %collective-permute-start.7 = (bf16[16,1920]{1,0:T(8,128)(2,1)S(1)}, bf16[16,1920]{1,0:T(8,128)(2,1)S(1)}, u32[]{:S(2)}, u32[]{:S(2)}) collective-permute-start(bf16[16,1920]{1,0:T(8,128)(2,1)S(1)} %get-tuple-element.37), channel_id=1, source_target_pairs={{0,4},{1,5},{2,6},{3,7},{4,0},{5,1},{6,2},{7,3},{8,12},{9,13},{10,... | collective-permute-start | bytes 184328 | tf_op jit(solution)/shard_map/ppermute | solution.py:238
  41.4 8.2 %collective-permute-start.6 = (bf16[16,1920]{1,0:T(8,128)(2,1)S(1)}, bf16[16,1920]{1,0:T(8,128)(2,1)S(1)}, u32[]{:S(2)}, u32[]{:S(2)}) collective-permute-start(bf16[16,1920]{1,0:T(8,128)(2,1)S(1)} %get-tuple-element.35), channel_id=1, source_target_pairs={{0,12},{1,13},{2,14},{3,15},{4,8},{5,9},{6,10},{7,11},{8,4},{9,5},... | collective-permute-start | bytes 184328 | tf_op jit(solution)/shard_map/ppermute | solution.py:237
  49.7 7.1 %collective-permute-start.9 = (bf16[32,1920]{1,0:T(8,128)(2,1)S(1)}, bf16[32,1920]{1,0:T(8,128)(2,1)S(1)}, u32[]{:S(2)}, u32[]{:S(2)}) collective-permute-start(bf16[32,1920]{1,0:T(8,128)(2,1)S(1)} %fusion.2.own), channel_id=1, source_target_pairs={{0,12},{1,13},{2,14},{3,15},{4,0},{5,1},{6,2},{7,3},{8,4},{9,5},{1... | collective-permute-start | bytes 368648 | tf_op jit(solution)/shard_map/ppermute | solution.py:262
  49.8 8.4 %collective-permute-start.8 = (bf16[32,1920]{1,0:T(8,128)(2,1)S(1)}, bf16[32,1920]{1,0:T(8,128)(2,1)S(1)}, u32[]{:S(2)}, u32[]{:S(2)}) collective-permute-start(bf16[32,1920]{1,0:T(8,128)(2,1)S(1)} %fusion.2.own), channel_id=1, source_target_pairs={{0,4},{1,5},{2,6},{3,7},{4,8},{5,9},{6,10},{7,11},{8,12},{9,13},{1... | collective-permute-start | bytes 368648 | tf_op jit(solution)/shard_map/ppermute | solution.py:261
  52.7 9.7 %collective-permute-start.16 = (bf16[32,1920]{1,0:T(8,128)(2,1)S(1)}, bf16[32,1920]{1,0:T(8,128)(2,1)S(1)}, u32[]{:S(2)}, u32[]{:S(2)}) collective-permute-start(bf16[32,1920]{1,0:T(8,128)(2,1)S(1)} %fusion.2.own), channel_id=1, source_target_pairs={{0,0},{1,32},{2,64},{3,96},{4,16},{5,48},{6,80},{7,112},{8,128},{9... | collective-permute-start | bytes 368648 | tf_op jit(solution)/shard_map/ppermute | solution.py:263
  58.2 6.6 %collective-permute-start.10 = (bf16[16,1920]{1,0:T(8,128)(2,1)S(1)}, bf16[16,1920]{1,0:T(8,128)(2,1)S(1)}, u32[]{:S(2)}, u32[]{:S(2)}) collective-permute-start(bf16[16,1920]{1,0:T(8,128)(2,1)S(1)} %get-tuple-element.21), channel_id=1, source_target_pairs={{0,4},{1,5},{2,6},{3,7},{4,8},{5,9},{6,10},{7,11},{8,12},{9,13},{1... | collective-permute-start | bytes 184328 | tf_op jit(solution)/shard_map/ppermute | solution.py:265
  60.8 5.7 %collective-permute-start.11 = (bf16[16,1920]{1,0:T(8,128)(2,1)S(1)}, bf16[16,1920]{1,0:T(8,128)(2,1)S(1)}, u32[]{:S(2)}, u32[]{:S(2)}) collective-permute-start(bf16[16,1920]{1,0:T(8,128)(2,1)S(1)} %get-tuple-element.22), channel_id=1, source_target_pairs={{0,12},{1,13},{2,14},{3,15},{4,0},{5,1},{6,2},{7,3},{8,4},{9,5},{1... | collective-permute-start | bytes 184328 | tf_op jit(solution)/shard_map/ppermute | solution.py:266
  62.4 8.1 %collective-permute-start.17 = (bf16[32,1920]{1,0:T(8,128)(2,1)S(1)}, bf16[32,1920]{1,0:T(8,128)(2,1)S(1)}, u32[]{:S(2)}, u32[]{:S(2)}) collective-permute-start(bf16[32,1920]{1,0:T(8,128)(2,1)S(1)} %collective-permute-done.16.flipped), channel_id=1, source_target_pairs={{0,128},{16,144},{32,160},{48,176},{64,192},{80,208},{96,224},{112... | collective-permute-start | bytes 368648 | tf_op jit(solution)/shard_map/ppermute | solution.py:275
  67.1 18.5 %collective-permute-start.13 = (bf16[128,1920]{1,0:T(8,128)(2,1)S(1)}, bf16[128,1920]{1,0:T(8,128)(2,1)S(1)}, u32[]{:S(2)}, u32[]{:S(2)}) collective-permute-start(bf16[128,1920]{1,0:T(8,128)(2,1)S(1)} %shard_map.58.own), channel_id=1, source_target_pairs={{0,3},{1,0},{2,1},{3,2},{4,7},{5,4},{6,5},{7,6},{8,11},{9,8},{10,9... | collective-permute-start | bytes 1474568 | tf_op jit(solution)/shard_map/ppermute | solution.py:274
  67.2 18.4 %collective-permute-start.12 = (bf16[128,1920]{1,0:T(8,128)(2,1)S(1)}, bf16[128,1920]{1,0:T(8,128)(2,1)S(1)}, u32[]{:S(2)}, u32[]{:S(2)}) collective-permute-start(bf16[128,1920]{1,0:T(8,128)(2,1)S(1)} %shard_map.58.own), channel_id=1, source_target_pairs={{0,1},{1,2},{2,3},{3,0},{4,5},{5,6},{6,7},{7,4},{8,9},{9,10},{10,1... | collective-permute-start | bytes 1474568 | tf_op jit(solution)/shard_map/ppermute | solution.py:273
  71.0 6.5 %collective-permute-start.19 = (bf16[64,1920]{1,0:T(8,128)(2,1)S(1)}, bf16[64,1920]{1,0:T(8,128)(2,1)S(1)}, u32[]{:S(2)}, u32[]{:S(2)}) collective-permute-start(bf16[64,1920]{1,0:T(8,128)(2,1)S(1)} %shard_map.61.near), channel_id=1, source_target_pairs={{0,96},{16,112},{32,0},{48,16},{64,32},{80,48},{96,64},{112,80},{1... | collective-permute-start | bytes 737288 | tf_op jit(solution)/shard_map/ppermute | solution.py:284
  73.2 9.0 %collective-permute-start.18 = (bf16[64,1920]{1,0:T(8,128)(2,1)S(1)}, bf16[64,1920]{1,0:T(8,128)(2,1)S(1)}, u32[]{:S(2)}, u32[]{:S(2)}) collective-permute-start(bf16[64,1920]{1,0:T(8,128)(2,1)S(1)} %shard_map.61.near), channel_id=1, source_target_pairs={{0,32},{16,48},{32,64},{48,80},{64,96},{80,112},{96,0},{112,16},{1... | collective-permute-start | bytes 737288 | tf_op jit(solution)/shard_map/ppermute | solution.py:283
  82.3 6.7 %collective-permute-start.20 = (bf16[32,1920]{1,0:T(8,128)(2,1)S(1)}, bf16[32,1920]{1,0:T(8,128)(2,1)S(1)}, u32[]{:S(2)}, u32[]{:S(2)}) collective-permute-start(bf16[32,1920]{1,0:T(8,128)(2,1)S(1)} %get-tuple-element.25), channel_id=1, source_target_pairs={{0,32},{16,48},{32,64},{48,80},{64,96},{80,112},{96,0},{112,16},{1... | collective-permute-start | bytes 368648 | tf_op jit(solution)/shard_map/ppermute | solution.py:296
  82.3 6.6 %collective-permute-start.21 = (bf16[32,1920]{1,0:T(8,128)(2,1)S(1)}, bf16[32,1920]{1,0:T(8,128)(2,1)S(1)}, u32[]{:S(2)}, u32[]{:S(2)}) collective-permute-start(bf16[32,1920]{1,0:T(8,128)(2,1)S(1)} %get-tuple-element.26), channel_id=1, source_target_pairs={{0,96},{16,112},{32,0},{48,16},{64,32},{80,48},{96,64},{112,80},{1... | collective-permute-start | bytes 368648 | tf_op jit(solution)/shard_map/ppermute | solution.py:297
  85.6 7.5 %collective-permute-start.15 = (bf16[64,1920]{1,0:T(8,128)(2,1)S(1)}, bf16[64,1920]{1,0:T(8,128)(2,1)S(1)}, u32[]{:S(2)}, u32[]{:S(2)}) collective-permute-start(bf16[64,1920]{1,0:T(8,128)(2,1)S(1)} %get-tuple-element.24), channel_id=1, source_target_pairs={{0,3},{1,0},{2,1},{3,2},{4,7},{5,4},{6,5},{7,6},{8,11},{9,8},{10,9... | collective-permute-start | bytes 737288 | tf_op jit(solution)/shard_map/ppermute | solution.py:287
  85.7 7.4 %collective-permute-start.14 = (bf16[64,1920]{1,0:T(8,128)(2,1)S(1)}, bf16[64,1920]{1,0:T(8,128)(2,1)S(1)}, u32[]{:S(2)}, u32[]{:S(2)}) collective-permute-start(bf16[64,1920]{1,0:T(8,128)(2,1)S(1)} %get-tuple-element.23.after), channel_id=1, source_target_pairs={{0,1},{1,2},{2,3},{3,0},{4,5},{5,6},{6,7},{7,4},{8,9},{9,10},{10,1... | collective-permute-start | bytes 737288 | tf_op jit(solution)/shard_map/ppermute | solution.py:286
  89.0 4.1 %collective-permute-start.22 = (bf16[256,1920]{1,0:T(8,128)(2,1)S(1)}, bf16[256,1920]{1,0:T(8,128)(2,1)S(1)}, u32[]{:S(2)}, u32[]{:S(2)}) collective-permute-start(bf16[256,1920]{1,0:T(8,128)(2,1)S(1)} %shard_map.63.near), channel_id=1, source_target_pairs={{0,16},{16,0},{32,48},{48,32},{64,80},{80,64},{96,112},{112,96},{1... | collective-permute-start | bytes 2949128 | tf_op jit(solution)/shard_map/ppermute | solution.py:301

commit v10 on v9

--- a/solution.py
+++ b/solution.py
@@ -95,18 +95,10 @@
     high[...] = right[half:]
 
 
-def z_join_kernel(at_ref, own, left, right, far_a, far_b, mine):
+def z_join_kernel(at_ref, own, right, left, far, mine):
     z = at_ref[1] >> 2
-
-    def put(by, start, ref):
-        first = pl.multiple_of(((z + by) & 3) * 32 + start, 16)
-        mine[pl.ds(first, ref.shape[0])] = ref[...]
-
-    put(0, 0, own)
-    put(3, 0, left)
-    put(1, 0, right)
-    put(2, 0, far_a)
-    put(2, 16, far_b)
+    for by, ref in ((0, own), (3, left), (1, right), (2, far)):
+        mine[pl.ds(pl.multiple_of(((z + by) & 3) * 32, 32), 32)] = ref[...]
 
 
 def pair_join_kernel(at_ref, flipped, pair, near):
@@ -261,15 +253,14 @@
     left = lax.ppermute(slopes, "col", z_turn(1))
     right = lax.ppermute(slopes, "col", z_turn(-1))
     flipped = lax.ppermute(slopes, ("row", "col"), flip_pairs())
-    low, high = halves(left, right, 8000000000)
-    far_a = lax.ppermute(low, "col", z_turn(1))
-    far_b = lax.ppermute(high, "col", z_turn(-1))
+    far = lax.ppermute(slopes, "col", z_turn(2))
     mine = call(
         z_join_kernel,
         out_shape=shape(128, rows),
-        in_specs=[SCALAR] + [WHOLE] * 5,
+        in_specs=[SCALAR] + [WHOLE] * 4,
         out_specs=WHOLE,
-    )(at, slopes, left, right, far_a, far_b)
+        cost_estimate=pl.CostEstimate(flops=4000000000, bytes_accessed=983040, transcendentals=0),
+    )(at, slopes, right, left, far)
     left = lax.ppermute(mine, "col", y_turn(1))
     right = lax.ppermute(mine, "col", y_turn(-1))
     pair = lax.ppermute(flipped, "row", [(r, r ^ 8) for r in range(16)])
@@ -278,7 +269,7 @@
         out_shape=shape(64, rows),
         in_specs=[SCALAR] + [WHOLE] * 2,
         out_specs=WHOLE,
-        cost_estimate=pl.CostEstimate(flops=1600000000, bytes_accessed=491520, transcendentals=0),
+        cost_estimate=pl.CostEstimate(flops=0, bytes_accessed=491520, transcendentals=0),
     )(at, flipped, pair)
     x_left = lax.ppermute(near, "row", x_turn(1))
     x_right = lax.ppermute(near, "row", x_turn(-1))

time: 100 us -> 103 us (1.030)
  the two profiles are of different devices: /device:TPU:24 before, /device:TPU:64 now
where the time goes in v10:
time: 103 us
  waiting for transfers between devices  46.5 us (45%)
  starting transfers between devices  41.5 us (40%)
  Pallas kernels  9.69 us (9%)
  local copies, waits for them, and re-layouts  3.62 us (4%)
  other arithmetic  1.25 us (1%)
    ppermute x1, waiting for transfers between devices, per_device(): got_b = lax.ppermute(sent_b, 'col', y_swap(3))  8.43 us
    ppermute x3, starting transfers between devices, per_device(): next_a = lax.ppermute(sent_a, 'col', swap_a)  6.88 us
    ppermute x3, starting transfers between devices, per_device(): next_b = lax.ppermute(sent_b, 'col', swap_b)  6.87 us
    pallas_call x1, Pallas kernels, per_device(): call(last_kernel, out_shape=shape(rows, rows), in_specs=[SCALAR] + [WHOLE...  6.01 us
    ppermute x3, waiting for transfers between devices, per_device(): next_b = lax.ppermute(sent_b, 'col', swap_b)  5.48 us
    ppermute x1, waiting for transfers between devices, per_device(): x_left = lax.ppermute(near, 'row', x_turn(1))  4.88 us
    ppermute x1, waiting for transfers between devices, per_device(): left = lax.ppermute(slopes, 'col', z_turn(1))  4.65 us
    ppermute x3, waiting for transfers between devices, per_device(): next_a = lax.ppermute(sent_a, 'col', swap_a)  4.59 us
  transfers between devices with their start and end apart: 22, of which 15 were waited for; matrix products, arithmetic and copies ran while one was open for 1% of the time, Pallas kernels for 2%

profile of v10, /device:TPU:64, one launch (start us, length us, event | category | flops | bytes accessed | tf_op | source)
XLA Modules:
  0.0 102.9 jit_solution(12654809231863633342)
XLA Ops:
  0.1 1.3 %copy-done = bf16[1920,320]{0,1:T(8,128)(2,1)S(1)} copy-done((bf16[1920,320]{0,1:T(8,128)(2,1)S(1)}, bf16[1920,320]{0,1:T(8,128)(2,1)}, u32[]{:S(2)}) %copy-start) | copy-done | bytes 1228824
  1.4 1.0 copy-done.2
  2.3 1.7 %shard_map.55 = (bf16[128,1920]{1,0:T(8,128)(2,1)S(1)}, bf16[128,1920]{1,0:T(8,128)(2,1)S(1)}, bf16[256,320]{1,0:T(8,128)(2,1)S(1)}) custom-call(s32[2]{0:T(128)S(1)} %pad_add_fusion.at_ref, bf16[320,512]{1,0:T(8,128)(2,1)S(1)} %copy-done.2, bf16[320,1920]{1,0:T(8,128)(2,1)S(1)} %bitcast.13), custom_call_target="tpu_custom_call" | custom-call | flops 314572800 | bytes 1600000 | tf_op jit(solution)/shard_map/pallas_call | solution.py:202
  4.0 3.1 %collective-permute-start.3 = (bf16[128,1920]{1,0:T(8,128)(2,1)S(1)}, bf16[128,1920]{1,0:T(8,128)(2,1)S(1)}, u32[]{:S(2)}, u32[]{:S(2)}) collective-permute-start(bf16[128,1920]{1,0:T(8,128)(2,1)S(1)} %get-tuple-element.18), channel_id=1, source_target_pairs={{0,3},{1,2},{2,1},{3,0},{4,7},{5,6},{6,5},{7,4},{8,11},{9,10},{10,... | collective-permute-start | bytes 1474568 | tf_op jit(solution)/shard_map/ppermute | solution.py:212
  7.9 1.3 %copy-done.1 = bf16[1920,320]{0,1:T(8,128)(2,1)S(1)} copy-done((bf16[1920,320]{0,1:T(8,128)(2,1)S(1)}, bf16[1920,320]{0,1:T(8,128)(2,1)}, u32[]{:S(2)}) %copy-start.1) | copy-done | bytes 1228824
  9.9 8.4 %collective-permute-done.3 = bf16[128,1920]{1,0:T(8,128)(2,1)S(1)} collective-permute-done((bf16[128,1920]{1,0:T(8,128)(2,1)S(1)}, bf16[128,1920]{1,0:T(8,128)(2,1)S(1)}, u32[]{:S(2)}, u32[]{:S(2)}) %collective-permute-start.3) | collective-permute-done | bytes 491552 | tf_op jit(solution)/shard_map/ppermute | solution.py:212
  18.9 0.9 collective-permute-done
  19.9 1.8 %collective-permute-start.1 = (bf16[64,1920]{1,0:T(8,128)(2,1)S(1)}, bf16[64,1920]{1,0:T(8,128)(2,1)S(1)}, u32[]{:S(2)}, u32[]{:S(2)}) collective-permute-start(bf16[64,1920]{1,0:T(8,128)(2,1)S(1)} %get-tuple-element.24), channel_id=1, source_target_pairs={{0,3},{1,2},{2,1},{3,0},{4,7},{5,6},{6,5},{7,4},{8,11},{9,10},{10,... | collective-permute-start | bytes 737288 | tf_op jit(solution)/shard_map/ppermute | solution.py:229
  21.8 3.7 %collective-permute-done.4 = bf16[64,1920]{1,0:T(8,128)(2,1)S(1)} collective-permute-done((bf16[64,1920]{1,0:T(8,128)(2,1)S(1)}, bf16[64,1920]{1,0:T(8,128)(2,1)S(1)}, u32[]{:S(2)}, u32[]{:S(2)}) %collective-permute-start.4) | collective-permute-done | bytes 245792 | tf_op jit(solution)/shard_map/ppermute | solution.py:230
  25.5 4.6 %collective-permute-start.5 = (bf16[32,1920]{1,0:T(8,128)(2,1)S(1)}, bf16[32,1920]{1,0:T(8,128)(2,1)S(1)}, u32[]{:S(2)}, u32[]{:S(2)}) collective-permute-start(bf16[32,1920]{1,0:T(8,128)(2,1)S(1)} %get-tuple-element.30), channel_id=1, source_target_pairs={{0,12},{1,13},{2,14},{3,15},{4,8},{5,9},{6,10},{7,11},{8,4},{9,5},... | collective-permute-start | bytes 368648 | tf_op jit(solution)/shard_map/ppermute | solution.py:230
  30.2 1.6 %collective-permute-start.2 = (bf16[32,1920]{1,0:T(8,128)(2,1)S(1)}, bf16[32,1920]{1,0:T(8,128)(2,1)S(1)}, u32[]{:S(2)}, u32[]{:S(2)}) collective-permute-start(bf16[32,1920]{1,0:T(8,128)(2,1)S(1)} %get-tuple-element.28), channel_id=1, source_target_pairs={{0,4},{1,5},{2,6},{3,7},{4,0},{5,1},{6,2},{7,3},{8,12},{9,13},{10,... | collective-permute-start | bytes 368648 | tf_op jit(solution)/shard_map/ppermute | solution.py:229
  31.7 1.8 %collective-permute-done.5 = bf16[32,1920]{1,0:T(8,128)(2,1)S(1)} collective-permute-done((bf16[32,1920]{1,0:T(8,128)(2,1)S(1)}, bf16[32,1920]{1,0:T(8,128)(2,1)S(1)}, u32[]{:S(2)}, u32[]{:S(2)}) %collective-permute-start.5) | collective-permute-done | bytes 122912 | tf_op jit(solution)/shard_map/ppermute | solution.py:230
  33.5 1.9 %collective-permute-start.7 = (bf16[16,1920]{1,0:T(8,128)(2,1)S(1)}, bf16[16,1920]{1,0:T(8,128)(2,1)S(1)}, u32[]{:S(2)}, u32[]{:S(2)}) collective-permute-start(bf16[16,1920]{1,0:T(8,128)(2,1)S(1)} %get-tuple-element.33), channel_id=1, source_target_pairs={{0,4},{1,5},{2,6},{3,7},{4,0},{5,1},{6,2},{7,3},{8,12},{9,13},{10,... | collective-permute-start | bytes 184328 | tf_op jit(solution)/shard_map/ppermute | solution.py:230
  35.4 1.8 %collective-permute-done.2 = bf16[32,1920]{1,0:T(8,128)(2,1)S(1)} collective-permute-done((bf16[32,1920]{1,0:T(8,128)(2,1)S(1)}, bf16[32,1920]{1,0:T(8,128)(2,1)S(1)}, u32[]{:S(2)}, u32[]{:S(2)}) %collective-permute-start.2) | collective-permute-done | bytes 122912 | tf_op jit(solution)/shard_map/ppermute | solution.py:229
  37.2 3.5 %collective-permute-start.6 = (bf16[16,1920]{1,0:T(8,128)(2,1)S(1)}, bf16[16,1920]{1,0:T(8,128)(2,1)S(1)}, u32[]{:S(2)}, u32[]{:S(2)}) collective-permute-start(bf16[16,1920]{1,0:T(8,128)(2,1)S(1)} %get-tuple-element.31), channel_id=1, source_target_pairs={{0,12},{1,13},{2,14},{3,15},{4,8},{5,9},{6,10},{7,11},{8,4},{9,5},... | collective-permute-start | bytes 184328 | tf_op jit(solution)/shard_map/ppermute | solution.py:229
  40.8 2.8 %collective-permute-done.6 = bf16[16,1920]{1,0:T(8,128)(2,1)S(1)} collective-permute-done((bf16[16,1920]{1,0:T(8,128)(2,1)S(1)}, bf16[16,1920]{1,0:T(8,128)(2,1)S(1)}, u32[]{:S(2)}, u32[]{:S(2)}) %collective-permute-start.6) | collective-permute-done | bytes 61472 | tf_op jit(solution)/shard_map/ppermute | solution.py:229
  43.8 3.0 %collective-permute-start.10 = (bf16[32,1920]{1,0:T(8,128)(2,1)S(1)}, bf16[32,1920]{1,0:T(8,128)(2,1)S(1)}, u32[]{:S(2)}, u32[]{:S(2)}) collective-permute-start(bf16[32,1920]{1,0:T(8,128)(2,1)S(1)} %fusion.2.own), channel_id=1, source_target_pairs={{0,8},{1,9},{2,10},{3,11},{4,12},{5,13},{6,14},{7,15},{8,0},{9,1},... | collective-permute-start | bytes 368648 | tf_op jit(solution)/shard_map/ppermute | solution.py:256
  46.7 4.1 %collective-permute-start.9 = (bf16[32,1920]{1,0:T(8,128)(2,1)S(1)}, bf16[32,1920]{1,0:T(8,128)(2,1)S(1)}, u32[]{:S(2)}, u32[]{:S(2)}) collective-permute-start(bf16[32,1920]{1,0:T(8,128)(2,1)S(1)} %fusion.2.own), channel_id=1, source_target_pairs={{0,4},{1,5},{2,6},{3,7},{4,8},{5,9},{6,10},{7,11},{8,12},{9,13},{1... | collective-permute-start | bytes 368648 | tf_op jit(solution)/shard_map/ppermute | solution.py:253
  50.9 1.9 %collective-permute-start.15 = (bf16[32,1920]{1,0:T(8,128)(2,1)S(1)}, bf16[32,1920]{1,0:T(8,128)(2,1)S(1)}, u32[]{:S(2)}, u32[]{:S(2)}) collective-permute-start(bf16[32,1920]{1,0:T(8,128)(2,1)S(1)} %fusion.2.own), channel_id=1, source_target_pairs={{0,0},{1,32},{2,64},{3,96},{4,16},{5,48},{6,80},{7,112},{8,128},{9... | collective-permute-start | bytes 368648 | tf_op jit(solution)/shard_map/ppermute | solution.py:255
  53.7 4.7 %collective-permute-done.9.left = bf16[32,1920]{1,0:T(8,128)(2,1)S(1)} collective-permute-done((bf16[32,1920]{1,0:T(8,128)(2,1)S(1)}, bf16[32,1920]{1,0:T(8,128)(2,1)S(1)}, u32[]{:S(2)}, u32[]{:S(2)}) %collective-permute-start.9) | collective-permute-done | bytes 122912 | tf_op jit(solution)/shard_map/ppermute | solution.py:253
  58.3 2.8 %collective-permute-done.8.right = bf16[32,1920]{1,0:T(8,128)(2,1)S(1)} collective-permute-done((bf16[32,1920]{1,0:T(8,128)(2,1)S(1)}, bf16[32,1920]{1,0:T(8,128)(2,1)S(1)}, u32[]{:S(2)}, u32[]{:S(2)}) %collective-permute-start.8) | collective-permute-done | bytes 122912 | tf_op jit(solution)/shard_map/ppermute | solution.py:254
  61.7 3.4 %collective-permute-start.12 = (bf16[128,1920]{1,0:T(8,128)(2,1)S(1)}, bf16[128,1920]{1,0:T(8,128)(2,1)S(1)}, u32[]{:S(2)}, u32[]{:S(2)}) collective-permute-start(bf16[128,1920]{1,0:T(8,128)(2,1)S(1)} %shard_map.57.own), channel_id=1, source_target_pairs={{0,3},{1,0},{2,1},{3,2},{4,7},{5,4},{6,5},{7,6},{8,11},{9,8},{10,9... | collective-permute-start | bytes 1474568 | tf_op jit(solution)/shard_map/ppermute | solution.py:265
  65.1 3.5 %collective-permute-start.16 = (bf16[32,1920]{1,0:T(8,128)(2,1)S(1)}, bf16[32,1920]{1,0:T(8,128)(2,1)S(1)}, u32[]{:S(2)}, u32[]{:S(2)}) collective-permute-start(bf16[32,1920]{1,0:T(8,128)(2,1)S(1)} %collective-permute-done.15.flipped), channel_id=1, source_target_pairs={{0,128},{16,144},{32,160},{48,176},{64,192},{80,208},{96,224},{112... | collective-permute-start | bytes 368648 | tf_op jit(solution)/shard_map/ppermute | solution.py:266
  68.6 2.9 %collective-permute-done.16.pair = bf16[32,1920]{1,0:T(8,128)(2,1)S(1)} collective-permute-done((bf16[32,1920]{1,0:T(8,128)(2,1)S(1)}, bf16[32,1920]{1,0:T(8,128)(2,1)S(1)}, u32[]{:S(2)}, u32[]{:S(2)}) %collective-permute-start.16) | collective-permute-done | bytes 122912 | tf_op jit(solution)/shard_map/ppermute | solution.py:266
  72.1 3.1 %collective-permute-start.18 = (bf16[64,1920]{1,0:T(8,128)(2,1)S(1)}, bf16[64,1920]{1,0:T(8,128)(2,1)S(1)}, u32[]{:S(2)}, u32[]{:S(2)}) collective-permute-start(bf16[64,1920]{1,0:T(8,128)(2,1)S(1)} %shard_map.60.near), channel_id=1, source_target_pairs={{0,96},{16,112},{32,0},{48,16},{64,32},{80,48},{96,64},{112,80},{1... | collective-permute-start | bytes 737288 | tf_op jit(solution)/shard_map/ppermute | solution.py:275
  75.1 3.7 %collective-permute-done.18.right.x_right = bf16[64,1920]{1,0:T(8,128)(2,1)S(1)} collective-permute-done((bf16[64,1920]{1,0:T(8,128)(2,1)S(1)}, bf16[64,1920]{1,0:T(8,128)(2,1)S(1)}, u32[]{:S(2)}, u32[]{:S(2)}) %collective-permute-start.18) | collective-permute-done | bytes 245792 | tf_op jit(solution)/shard_map/ppermute | solution.py:275
  78.9 4.9 %collective-permute-done.17.left.x_left = bf16[64,1920]{1,0:T(8,128)(2,1)S(1)} collective-permute-done((bf16[64,1920]{1,0:T(8,128)(2,1)S(1)}, bf16[64,1920]{1,0:T(8,128)(2,1)S(1)}, u32[]{:S(2)}, u32[]{:S(2)}) %collective-permute-start.17) | collective-permute-done | bytes 245792 | tf_op jit(solution)/shard_map/ppermute | solution.py:274
  83.8 3.2 %collective-permute-start.20 = (bf16[32,1920]{1,0:T(8,128)(2,1)S(1)}, bf16[32,1920]{1,0:T(8,128)(2,1)S(1)}, u32[]{:S(2)}, u32[]{:S(2)}) collective-permute-start(bf16[32,1920]{1,0:T(8,128)(2,1)S(1)} %get-tuple-element.22), channel_id=1, source_target_pairs={{0,96},{16,112},{32,0},{48,16},{64,32},{80,48},{96,64},{112,80},{1... | collective-permute-start | bytes 368648 | tf_op jit(solution)/shard_map/ppermute | solution.py:288
  87.1 2.1 %collective-permute-start.14 = (bf16[64,1920]{1,0:T(8,128)(2,1)S(1)}, bf16[64,1920]{1,0:T(8,128)(2,1)S(1)}, u32[]{:S(2)}, u32[]{:S(2)}) collective-permute-start(bf16[64,1920]{1,0:T(8,128)(2,1)S(1)} %get-tuple-element.20), channel_id=1, source_target_pairs={{0,3},{1,0},{2,1},{3,2},{4,7},{5,4},{6,5},{7,6},{8,11},{9,8},{10,9... | collective-permute-start | bytes 737288 | tf_op jit(solution)/shard_map/ppermute | solution.py:278
  90.1 3.3 %collective-permute-done.14.two = bf16[64,1920]{1,0:T(8,128)(2,1)S(1)} collective-permute-done((bf16[64,1920]{1,0:T(8,128)(2,1)S(1)}, bf16[64,1920]{1,0:T(8,128)(2,1)S(1)}, u32[]{:S(2)}, u32[]{:S(2)}) %collective-permute-start.14) | collective-permute-done | bytes 245792 | tf_op jit(solution)/shard_map/ppermute | solution.py:278
  93.4 3.2 %collective-permute-done.13.one = bf16[64,1920]{1,0:T(8,128)(2,1)S(1)} collective-permute-done((bf16[64,1920]{1,0:T(8,128)(2,1)S(1)}, bf16[64,1920]{1,0:T(8,128)(2,1)S(1)}, u32[]{:S(2)}, u32[]{:S(2)}) %collective-permute-start.13) | collective-permute-done | bytes 245792 | tf_op jit(solution)/shard_map/ppermute | solution.py:277
  96.7 6.0 %shard_map.63 = bf16[1920,1920]{1,0:T(8,128)(2,1)} custom-call(s32[2]{0:T(128)S(1)} %pad_add_fusion.at_ref, bf16[128,1920]{1,0:T(8,128)(2,1)S(1)} %shard_map.57.own, bf16[128,1920]{1,0:T(8,128)(2,1)S(1)} %collective-permute-done.11.left, bf16[128,1920]{1,0:T(8,128)(2,1)S(1)} %collective-permute-done.12.right, bf16[128,1920]{1,0:T(8,128)(2,1)S(1)} %shard_map.59.far, ...), custom_call_target="tpu_custom_call" | custom-call | flops 3774873600 | bytes 7372800 | tf_op jit(solution)/shard_map/pallas_call | solution.py:293
  (42 shorter events, 5.7 us)
Async XLA Ops:
  0.0 40.8 %copy-start.4 = (s32[32]{0:T(128)S(1)}, s32[32]{0:T(128)}, u32[]{:S(2)}) copy-start(s32[32]{0:T(128)} %param.9) | copy-start | bytes 388
  0.1 1.3 %copy-start = (bf16[1920,320]{0,1:T(8,128)(2,1)S(1)}, bf16[1920,320]{0,1:T(8,128)(2,1)}, u32[]{:S(2)}) copy-start(bf16[1920,320]{0,1:T(8,128)(2,1)} %param.6) | copy-start | bytes 3686404
  1.4 1.0 copy-start.2
  2.3 41.3 %copy-start.3 = (bf16[1920,32]{0,1:T(8,128)(2,1)S(1)}, bf16[1920,32]{0,1:T(8,128)(2,1)}, u32[]{:S(2)}) copy-start(bf16[1920,32]{0,1:T(8,128)(2,1)} %param.5) | copy-start | bytes 368644
  4.0 14.3 %collective-permute-start.3 = (bf16[128,1920]{1,0:T(8,128)(2,1)S(1)}, bf16[128,1920]{1,0:T(8,128)(2,1)S(1)}, u32[]{:S(2)}, u32[]{:S(2)}) collective-permute-start(bf16[128,1920]{1,0:T(8,128)(2,1)S(1)} %get-tuple-element.18), channel_id=1, source_target_pairs={{0,3},{1,2},{2,1},{3,0},{4,7},{5,6},{6,5},{7,4},{8,11},{9,10},{10,... | collective-permute-start | bytes 1474568 | tf_op jit(solution)/shard_map/ppermute | solution.py:212
  7.1 12.7 %collective-permute-start = (bf16[128,1920]{1,0:T(8,128)(2,1)S(1)}, bf16[128,1920]{1,0:T(8,128)(2,1)S(1)}, u32[]{:S(2)}, u32[]{:S(2)}) collective-permute-start(bf16[128,1920]{1,0:T(8,128)(2,1)S(1)} %get-tuple-element.16), channel_id=1, source_target_pairs={{0,1},{1,0},{2,3},{3,2},{4,5},{5,4},{6,7},{7,6},{8,9},{9,8},{10,11... | collective-permute-start | bytes 1474568 | tf_op jit(solution)/shard_map/ppermute | solution.py:211
  7.9 1.3 %copy-start.1 = (bf16[1920,320]{0,1:T(8,128)(2,1)S(1)}, bf16[1920,320]{0,1:T(8,128)(2,1)}, u32[]{:S(2)}) copy-start(bf16[1920,320]{0,1:T(8,128)(2,1)} %param.6) | copy-start | bytes 3686404
  18.5 7.0 %collective-permute-start.4 = (bf16[64,1920]{1,0:T(8,128)(2,1)S(1)}, bf16[64,1920]{1,0:T(8,128)(2,1)S(1)}, u32[]{:S(2)}, u32[]{:S(2)}) collective-permute-start(bf16[64,1920]{1,0:T(8,128)(2,1)S(1)} %get-tuple-element.26), channel_id=1, source_target_pairs={{0,1},{1,0},{2,3},{3,2},{4,5},{5,4},{6,7},{7,6},{8,9},{9,8},{10,11... | collective-permute-start | bytes 737288 | tf_op jit(solution)/shard_map/ppermute | solution.py:230
  19.9 10.2 %collective-permute-start.1 = (bf16[64,1920]{1,0:T(8,128)(2,1)S(1)}, bf16[64,1920]{1,0:T(8,128)(2,1)S(1)}, u32[]{:S(2)}, u32[]{:S(2)}) collective-permute-start(bf16[64,1920]{1,0:T(8,128)(2,1)S(1)} %get-tuple-element.24), channel_id=1, source_target_pairs={{0,3},{1,2},{2,1},{3,0},{4,7},{5,6},{6,5},{7,4},{8,11},{9,10},{10,... | collective-permute-start | bytes 737288 | tf_op jit(solution)/shard_map/ppermute | solution.py:229
  25.5 8.0 %collective-permute-start.5 = (bf16[32,1920]{1,0:T(8,128)(2,1)S(1)}, bf16[32,1920]{1,0:T(8,128)(2,1)S(1)}, u32[]{:S(2)}, u32[]{:S(2)}) collective-permute-start(bf16[32,1920]{1,0:T(8,128)(2,1)S(1)} %get-tuple-element.30), channel_id=1, source_target_pairs={{0,12},{1,13},{2,14},{3,15},{4,8},{5,9},{6,10},{7,11},{8,4},{9,5},... | collective-permute-start | bytes 368648 | tf_op jit(solution)/shard_map/ppermute | solution.py:230
  30.2 7.0 %collective-permute-start.2 = (bf16[32,1920]{1,0:T(8,128)(2,1)S(1)}, bf16[32,1920]{1,0:T(8,128)(2,1)S(1)}, u32[]{:S(2)}, u32[]{:S(2)}) collective-permute-start(bf16[32,1920]{1,0:T(8,128)(2,1)S(1)} %get-tuple-element.28), channel_id=1, source_target_pairs={{0,4},{1,5},{2,6},{3,7},{4,0},{5,1},{6,2},{7,3},{8,12},{9,13},{10,... | collective-permute-start | bytes 368648 | tf_op jit(solution)/shard_map/ppermute | solution.py:229
  33.5 7.3 %collective-permute-start.7 = (bf16[16,1920]{1,0:T(8,128)(2,1)S(1)}, bf16[16,1920]{1,0:T(8,128)(2,1)S(1)}, u32[]{:S(2)}, u32[]{:S(2)}) collective-permute-start(bf16[16,1920]{1,0:T(8,128)(2,1)S(1)} %get-tuple-element.33), channel_id=1, source_target_pairs={{0,4},{1,5},{2,6},{3,7},{4,0},{5,1},{6,2},{7,3},{8,12},{9,13},{10,... | collective-permute-start | bytes 184328 | tf_op jit(solution)/shard_map/ppermute | solution.py:230
  37.2 6.4 %collective-permute-start.6 = (bf16[16,1920]{1,0:T(8,128)(2,1)S(1)}, bf16[16,1920]{1,0:T(8,128)(2,1)S(1)}, u32[]{:S(2)}, u32[]{:S(2)}) collective-permute-start(bf16[16,1920]{1,0:T(8,128)(2,1)S(1)} %get-tuple-element.31), channel_id=1, source_target_pairs={{0,12},{1,13},{2,14},{3,15},{4,8},{5,9},{6,10},{7,11},{8,4},{9,5},... | collective-permute-start | bytes 184328 | tf_op jit(solution)/shard_map/ppermute | solution.py:229
  43.8 9.9 %collective-permute-start.10 = (bf16[32,1920]{1,0:T(8,128)(2,1)S(1)}, bf16[32,1920]{1,0:T(8,128)(2,1)S(1)}, u32[]{:S(2)}, u32[]{:S(2)}) collective-permute-start(bf16[32,1920]{1,0:T(8,128)(2,1)S(1)} %fusion.2.own), channel_id=1, source_target_pairs={{0,8},{1,9},{2,10},{3,11},{4,12},{5,13},{6,14},{7,15},{8,0},{9,1},... | collective-permute-start | bytes 368648 | tf_op jit(solution)/shard_map/ppermute | solution.py:256
  46.7 11.6 %collective-permute-start.9 = (bf16[32,1920]{1,0:T(8,128)(2,1)S(1)}, bf16[32,1920]{1,0:T(8,128)(2,1)S(1)}, u32[]{:S(2)}, u32[]{:S(2)}) collective-permute-start(bf16[32,1920]{1,0:T(8,128)(2,1)S(1)} %fusion.2.own), channel_id=1, source_target_pairs={{0,4},{1,5},{2,6},{3,7},{4,8},{5,9},{6,10},{7,11},{8,12},{9,13},{1... | collective-permute-start | bytes 368648 | tf_op jit(solution)/shard_map/ppermute | solution.py:253
  50.9 10.3 %collective-permute-start.8 = (bf16[32,1920]{1,0:T(8,128)(2,1)S(1)}, bf16[32,1920]{1,0:T(8,128)(2,1)S(1)}, u32[]{:S(2)}, u32[]{:S(2)}) collective-permute-start(bf16[32,1920]{1,0:T(8,128)(2,1)S(1)} %fusion.2.own), channel_id=1, source_target_pairs={{0,12},{1,13},{2,14},{3,15},{4,0},{5,1},{6,2},{7,3},{8,4},{9,5},{1... | collective-permute-start | bytes 368648 | tf_op jit(solution)/shard_map/ppermute | solution.py:254
  50.9 14.2 %collective-permute-start.15 = (bf16[32,1920]{1,0:T(8,128)(2,1)S(1)}, bf16[32,1920]{1,0:T(8,128)(2,1)S(1)}, u32[]{:S(2)}, u32[]{:S(2)}) collective-permute-start(bf16[32,1920]{1,0:T(8,128)(2,1)S(1)} %fusion.2.own), channel_id=1, source_target_pairs={{0,0},{1,32},{2,64},{3,96},{4,16},{5,48},{6,80},{7,112},{8,128},{9... | collective-permute-start | bytes 368648 | tf_op jit(solution)/shard_map/ppermute | solution.py:255
  61.7 25.3 %collective-permute-start.12 = (bf16[128,1920]{1,0:T(8,128)(2,1)S(1)}, bf16[128,1920]{1,0:T(8,128)(2,1)S(1)}, u32[]{:S(2)}, u32[]{:S(2)}) collective-permute-start(bf16[128,1920]{1,0:T(8,128)(2,1)S(1)} %shard_map.57.own), channel_id=1, source_target_pairs={{0,3},{1,0},{2,1},{3,2},{4,7},{5,4},{6,5},{7,6},{8,11},{9,8},{10,9... | collective-permute-start | bytes 1474568 | tf_op jit(solution)/shard_map/ppermute | solution.py:265
  65.1 22.0 %collective-permute-start.11 = (bf16[128,1920]{1,0:T(8,128)(2,1)S(1)}, bf16[128,1920]{1,0:T(8,128)(2,1)S(1)}, u32[]{:S(2)}, u32[]{:S(2)}) collective-permute-start(bf16[128,1920]{1,0:T(8,128)(2,1)S(1)} %shard_map.57.own), channel_id=1, source_target_pairs={{0,1},{1,2},{2,3},{3,0},{4,5},{5,6},{6,7},{7,4},{8,9},{9,10},{10,1... | collective-permute-start | bytes 1474568 | tf_op jit(solution)/shard_map/ppermute | solution.py:264
  65.1 6.4 %collective-permute-start.16 = (bf16[32,1920]{1,0:T(8,128)(2,1)S(1)}, bf16[32,1920]{1,0:T(8,128)(2,1)S(1)}, u32[]{:S(2)}, u32[]{:S(2)}) collective-permute-start(bf16[32,1920]{1,0:T(8,128)(2,1)S(1)} %collective-permute-done.15.flipped), channel_id=1, source_target_pairs={{0,128},{16,144},{32,160},{48,176},{64,192},{80,208},{96,224},{112... | collective-permute-start | bytes 368648 | tf_op jit(solution)/shard_map/ppermute | solution.py:266
  72.1 6.8 %collective-permute-start.18 = (bf16[64,1920]{1,0:T(8,128)(2,1)S(1)}, bf16[64,1920]{1,0:T(8,128)(2,1)S(1)}, u32[]{:S(2)}, u32[]{:S(2)}) collective-permute-start(bf16[64,1920]{1,0:T(8,128)(2,1)S(1)} %shard_map.60.near), channel_id=1, source_target_pairs={{0,96},{16,112},{32,0},{48,16},{64,32},{80,48},{96,64},{112,80},{1... | collective-permute-start | bytes 737288 | tf_op jit(solution)/shard_map/ppermute | solution.py:275
  75.1 8.6 %collective-permute-start.17 = (bf16[64,1920]{1,0:T(8,128)(2,1)S(1)}, bf16[64,1920]{1,0:T(8,128)(2,1)S(1)}, u32[]{:S(2)}, u32[]{:S(2)}) collective-permute-start(bf16[64,1920]{1,0:T(8,128)(2,1)S(1)} %shard_map.60.near), channel_id=1, source_target_pairs={{0,32},{16,48},{32,64},{48,80},{64,96},{80,112},{96,0},{112,16},{1... | collective-permute-start | bytes 737288 | tf_op jit(solution)/shard_map/ppermute | solution.py:274
  83.8 6.2 %collective-permute-start.19 = (bf16[32,1920]{1,0:T(8,128)(2,1)S(1)}, bf16[32,1920]{1,0:T(8,128)(2,1)S(1)}, u32[]{:S(2)}, u32[]{:S(2)}) collective-permute-start(bf16[32,1920]{1,0:T(8,128)(2,1)S(1)} %get-tuple-element.21), channel_id=1, source_target_pairs={{0,32},{16,48},{32,64},{48,80},{64,96},{80,112},{96,0},{112,16},{1... | collective-permute-start | bytes 368648 | tf_op jit(solution)/shard_map/ppermute | solution.py:287
  83.8 6.1 %collective-permute-start.20 = (bf16[32,1920]{1,0:T(8,128)(2,1)S(1)}, bf16[32,1920]{1,0:T(8,128)(2,1)S(1)}, u32[]{:S(2)}, u32[]{:S(2)}) collective-permute-start(bf16[32,1920]{1,0:T(8,128)(2,1)S(1)} %get-tuple-element.22), channel_id=1, source_target_pairs={{0,96},{16,112},{32,0},{48,16},{64,32},{80,48},{96,64},{112,80},{1... | collective-permute-start | bytes 368648 | tf_op jit(solution)/shard_map/ppermute | solution.py:288
  87.1 6.3 %collective-permute-start.14 = (bf16[64,1920]{1,0:T(8,128)(2,1)S(1)}, bf16[64,1920]{1,0:T(8,128)(2,1)S(1)}, u32[]{:S(2)}, u32[]{:S(2)}) collective-permute-start(bf16[64,1920]{1,0:T(8,128)(2,1)S(1)} %get-tuple-element.20), channel_id=1, source_target_pairs={{0,3},{1,0},{2,1},{3,2},{4,7},{5,4},{6,5},{7,6},{8,11},{9,8},{10,9... | collective-permute-start | bytes 737288 | tf_op jit(solution)/shard_map/ppermute | solution.py:278
  89.2 7.4 %collective-permute-start.13 = (bf16[64,1920]{1,0:T(8,128)(2,1)S(1)}, bf16[64,1920]{1,0:T(8,128)(2,1)S(1)}, u32[]{:S(2)}, u32[]{:S(2)}) collective-permute-start(bf16[64,1920]{1,0:T(8,128)(2,1)S(1)} %get-tuple-element.19.after), channel_id=1, source_target_pairs={{0,1},{1,2},{2,3},{3,0},{4,5},{5,6},{6,7},{7,4},{8,9},{9,10},{10,1... | collective-permute-start | bytes 737288 | tf_op jit(solution)/shard_map/ppermute | solution.py:277
  90.0 6.7 %collective-permute-start.21 = (bf16[256,1920]{1,0:T(8,128)(2,1)S(1)}, bf16[256,1920]{1,0:T(8,128)(2,1)S(1)}, u32[]{:S(2)}, u32[]{:S(2)}) collective-permute-start(bf16[256,1920]{1,0:T(8,128)(2,1)S(1)} %shard_map.62.near), channel_id=1, source_target_pairs={{0,16},{16,0},{32,48},{48,32},{64,80},{80,64},{96,112},{112,96},{1... | collective-permute-start | bytes 2949128 | tf_op jit(solution)/shard_map/ppermute | solution.py:292

commit v11 on v10

--- a/solution.py
+++ b/solution.py
@@ -269,11 +269,11 @@
         out_shape=shape(64, rows),
         in_specs=[SCALAR] + [WHOLE] * 2,
         out_specs=WHOLE,
-        cost_estimate=pl.CostEstimate(flops=0, bytes_accessed=491520, transcendentals=0),
+        cost_estimate=pl.CostEstimate(flops=3000000000, bytes_accessed=491520, transcendentals=0),
     )(at, flipped, pair)
     x_left = lax.ppermute(near, "row", x_turn(1))
     x_right = lax.ppermute(near, "row", x_turn(-1))
-    low, high = halves(left, right, 8000000000)
+    low, high = halves(left, right, 16000000000)
     far_a = lax.ppermute(low, "col", y_turn(1))
     far_b = lax.ppermute(high, "col", y_turn(-1))
     far = call(
@@ -281,7 +281,7 @@
         out_shape=shape(128, rows),
         in_specs=[WHOLE] * 2,
         out_specs=WHOLE,
-        cost_estimate=pl.CostEstimate(flops=8000000000, bytes_accessed=983040, transcendentals=0),
+        cost_estimate=pl.CostEstimate(flops=30000000000, bytes_accessed=983040, transcendentals=0),
     )(far_a, far_b)
     x_low, x_high = halves(x_left, x_right, 0)
     x_far_a = lax.ppermute(x_low, "row", x_turn(1))

time: 103 us -> 99.3 us (0.964)
  the two profiles are of different devices: /device:TPU:64 before, /device:TPU:24 now
where the time goes in v11:
time: 99.3 us; the launch traced here: 98.5 us
  waiting for transfers between devices  45 us (45%)
  starting transfers between devices  38.6 us (39%)
  Pallas kernels  9.69 us (10%)
  local copies, waits for them, and re-layouts  3.62 us (4%)
  other arithmetic  1.25 us (1%)
    ppermute x3, waiting for transfers between devices, per_device(): next_a = lax.ppermute(sent_a, 'col', swap_a)  12.4 us
    ppermute x1, waiting for transfers between devices, per_device(): got_b = lax.ppermute(sent_b, 'col', y_swap(3))  9.57 us
    ppermute x3, waiting for transfers between devices, per_device(): next_b = lax.ppermute(sent_b, 'col', swap_b)  7.38 us
    ppermute x3, starting transfers between devices, per_device(): next_b = lax.ppermute(sent_b, 'col', swap_b)  7.11 us
    pallas_call x1, Pallas kernels, per_device(): call(last_kernel, out_shape=shape(rows, rows), in_specs=[SCALAR] + [WHOLE...  6 us
    ppermute x1, starting transfers between devices, per_device(): flipped = lax.ppermute(slopes, ('row', 'col'), flip_pairs())  5.04 us
    ppermute x1, waiting for transfers between devices, per_device(): x_left = lax.ppermute(near, 'row', x_turn(1))  5.01 us
    ppermute x1, starting transfers between devices, per_device(): x_right = lax.ppermute(near, 'row', x_turn(-1))  3.96 us
  transfers between devices with their start and end apart: 22, of which 13 were waited for; matrix products, arithmetic and copies ran while one was open for 1% of the time, Pallas kernels for 2%

profile of v11, /device:TPU:24, one launch (start us, length us, event | category | flops | bytes accessed | tf_op | source)
XLA Modules:
  0.0 98.5 jit_solution(17292524849052717243)
XLA Ops:
  0.1 1.3 %copy-done = bf16[1920,320]{0,1:T(8,128)(2,1)S(1)} copy-done((bf16[1920,320]{0,1:T(8,128)(2,1)S(1)}, bf16[1920,320]{0,1:T(8,128)(2,1)}, u32[]{:S(2)}) %copy-start) | copy-done | bytes 1228824
  1.4 1.0 copy-done.2
  2.3 1.7 %shard_map.55 = (bf16[128,1920]{1,0:T(8,128)(2,1)S(1)}, bf16[128,1920]{1,0:T(8,128)(2,1)S(1)}, bf16[256,320]{1,0:T(8,128)(2,1)S(1)}) custom-call(s32[2]{0:T(128)S(1)} %pad_add_fusion.at_ref, bf16[320,512]{1,0:T(8,128)(2,1)S(1)} %copy-done.2, bf16[320,1920]{1,0:T(8,128)(2,1)S(1)} %bitcast.13), custom_call_target="tpu_custom_call" | custom-call | flops 314572800 | bytes 1600000 | tf_op jit(solution)/shard_map/pallas_call | solution.py:202
  4.0 2.0 %collective-permute-start.3 = (bf16[128,1920]{1,0:T(8,128)(2,1)S(1)}, bf16[128,1920]{1,0:T(8,128)(2,1)S(1)}, u32[]{:S(2)}, u32[]{:S(2)}) collective-permute-start(bf16[128,1920]{1,0:T(8,128)(2,1)S(1)} %get-tuple-element.18), channel_id=1, source_target_pairs={{0,3},{1,2},{2,1},{3,0},{4,7},{5,6},{6,5},{7,4},{8,11},{9,10},{10,... | collective-permute-start | bytes 1474568 | tf_op jit(solution)/shard_map/ppermute | solution.py:212
  6.1 0.7 convert_element_type.179
  6.7 1.3 %copy-done.1 = bf16[1920,320]{0,1:T(8,128)(2,1)S(1)} copy-done((bf16[1920,320]{0,1:T(8,128)(2,1)S(1)}, bf16[1920,320]{0,1:T(8,128)(2,1)}, u32[]{:S(2)}) %copy-start.1) | copy-done | bytes 1228824
  8.0 0.7 shard_map.56
  8.7 9.6 %collective-permute-done.3 = bf16[128,1920]{1,0:T(8,128)(2,1)S(1)} collective-permute-done((bf16[128,1920]{1,0:T(8,128)(2,1)S(1)}, bf16[128,1920]{1,0:T(8,128)(2,1)S(1)}, u32[]{:S(2)}, u32[]{:S(2)}) %collective-permute-start.3) | collective-permute-done | bytes 491552 | tf_op jit(solution)/shard_map/ppermute | solution.py:212
  18.7 2.0 %collective-permute-start.1 = (bf16[64,1920]{1,0:T(8,128)(2,1)S(1)}, bf16[64,1920]{1,0:T(8,128)(2,1)S(1)}, u32[]{:S(2)}, u32[]{:S(2)}) collective-permute-start(bf16[64,1920]{1,0:T(8,128)(2,1)S(1)} %get-tuple-element.24), channel_id=1, source_target_pairs={{0,3},{1,2},{2,1},{3,0},{4,7},{5,6},{6,5},{7,4},{8,11},{9,10},{10,... | collective-permute-start | bytes 737288 | tf_op jit(solution)/shard_map/ppermute | solution.py:229
  20.6 4.7 %collective-permute-done.4 = bf16[64,1920]{1,0:T(8,128)(2,1)S(1)} collective-permute-done((bf16[64,1920]{1,0:T(8,128)(2,1)S(1)}, bf16[64,1920]{1,0:T(8,128)(2,1)S(1)}, u32[]{:S(2)}, u32[]{:S(2)}) %collective-permute-start.4) | collective-permute-done | bytes 245792 | tf_op jit(solution)/shard_map/ppermute | solution.py:230
  25.4 6.4 %collective-permute-start.5 = (bf16[32,1920]{1,0:T(8,128)(2,1)S(1)}, bf16[32,1920]{1,0:T(8,128)(2,1)S(1)}, u32[]{:S(2)}, u32[]{:S(2)}) collective-permute-start(bf16[32,1920]{1,0:T(8,128)(2,1)S(1)} %get-tuple-element.30), channel_id=1, source_target_pairs={{0,12},{1,13},{2,14},{3,15},{4,8},{5,9},{6,10},{7,11},{8,4},{9,5},... | collective-permute-start | bytes 368648 | tf_op jit(solution)/shard_map/ppermute | solution.py:230
  31.9 1.5 %collective-permute-start.2 = (bf16[32,1920]{1,0:T(8,128)(2,1)S(1)}, bf16[32,1920]{1,0:T(8,128)(2,1)S(1)}, u32[]{:S(2)}, u32[]{:S(2)}) collective-permute-start(bf16[32,1920]{1,0:T(8,128)(2,1)S(1)} %get-tuple-element.28), channel_id=1, source_target_pairs={{0,4},{1,5},{2,6},{3,7},{4,0},{5,1},{6,2},{7,3},{8,12},{9,13},{10,... | collective-permute-start | bytes 368648 | tf_op jit(solution)/shard_map/ppermute | solution.py:229
  33.4 2.2 %collective-permute-done.5 = bf16[32,1920]{1,0:T(8,128)(2,1)S(1)} collective-permute-done((bf16[32,1920]{1,0:T(8,128)(2,1)S(1)}, bf16[32,1920]{1,0:T(8,128)(2,1)S(1)}, u32[]{:S(2)}, u32[]{:S(2)}) %collective-permute-start.5) | collective-permute-done | bytes 122912 | tf_op jit(solution)/shard_map/ppermute | solution.py:230
  35.7 0.6 collective-permute-start.7
  36.3 5.1 %collective-permute-done.2 = bf16[32,1920]{1,0:T(8,128)(2,1)S(1)} collective-permute-done((bf16[32,1920]{1,0:T(8,128)(2,1)S(1)}, bf16[32,1920]{1,0:T(8,128)(2,1)S(1)}, u32[]{:S(2)}, u32[]{:S(2)}) %collective-permute-start.2) | collective-permute-done | bytes 122912 | tf_op jit(solution)/shard_map/ppermute | solution.py:229
  42.0 7.4 %collective-permute-done.6 = bf16[16,1920]{1,0:T(8,128)(2,1)S(1)} collective-permute-done((bf16[16,1920]{1,0:T(8,128)(2,1)S(1)}, bf16[16,1920]{1,0:T(8,128)(2,1)S(1)}, u32[]{:S(2)}, u32[]{:S(2)}) %collective-permute-start.6) | collective-permute-done | bytes 61472 | tf_op jit(solution)/shard_map/ppermute | solution.py:229
  49.6 1.7 %collective-permute-start.9 = (bf16[32,1920]{1,0:T(8,128)(2,1)S(1)}, bf16[32,1920]{1,0:T(8,128)(2,1)S(1)}, u32[]{:S(2)}, u32[]{:S(2)}) collective-permute-start(bf16[32,1920]{1,0:T(8,128)(2,1)S(1)} %fusion.2.own), channel_id=1, source_target_pairs={{0,4},{1,5},{2,6},{3,7},{4,8},{5,9},{6,10},{7,11},{8,12},{9,13},{1... | collective-permute-start | bytes 368648 | tf_op jit(solution)/shard_map/ppermute | solution.py:253
  51.3 2.5 %collective-permute-start.8 = (bf16[32,1920]{1,0:T(8,128)(2,1)S(1)}, bf16[32,1920]{1,0:T(8,128)(2,1)S(1)}, u32[]{:S(2)}, u32[]{:S(2)}) collective-permute-start(bf16[32,1920]{1,0:T(8,128)(2,1)S(1)} %fusion.2.own), channel_id=1, source_target_pairs={{0,12},{1,13},{2,14},{3,15},{4,0},{5,1},{6,2},{7,3},{8,4},{9,5},{1... | collective-permute-start | bytes 368648 | tf_op jit(solution)/shard_map/ppermute | solution.py:254
  53.8 5.0 %collective-permute-start.15 = (bf16[32,1920]{1,0:T(8,128)(2,1)S(1)}, bf16[32,1920]{1,0:T(8,128)(2,1)S(1)}, u32[]{:S(2)}, u32[]{:S(2)}) collective-permute-start(bf16[32,1920]{1,0:T(8,128)(2,1)S(1)} %fusion.2.own), channel_id=1, source_target_pairs={{0,0},{1,32},{2,64},{3,96},{4,16},{5,48},{6,80},{7,112},{8,128},{9... | collective-permute-start | bytes 368648 | tf_op jit(solution)/shard_map/ppermute | solution.py:255
  58.9 0.9 collective-permute-done.10.far
  59.8 1.1 %collective-permute-done.8.right = bf16[32,1920]{1,0:T(8,128)(2,1)S(1)} collective-permute-done((bf16[32,1920]{1,0:T(8,128)(2,1)S(1)}, bf16[32,1920]{1,0:T(8,128)(2,1)S(1)}, u32[]{:S(2)}, u32[]{:S(2)}) %collective-permute-start.8) | collective-permute-done | bytes 122912 | tf_op jit(solution)/shard_map/ppermute | solution.py:254
  60.8 0.6 shard_map.57.own
  61.7 3.0 %collective-permute-start.11 = (bf16[128,1920]{1,0:T(8,128)(2,1)S(1)}, bf16[128,1920]{1,0:T(8,128)(2,1)S(1)}, u32[]{:S(2)}, u32[]{:S(2)}) collective-permute-start(bf16[128,1920]{1,0:T(8,128)(2,1)S(1)} %shard_map.57.own), channel_id=1, source_target_pairs={{0,1},{1,2},{2,3},{3,0},{4,5},{5,6},{6,7},{7,4},{8,9},{9,10},{10,1... | collective-permute-start | bytes 1474568 | tf_op jit(solution)/shard_map/ppermute | solution.py:264
  64.8 2.6 %collective-permute-start.16 = (bf16[32,1920]{1,0:T(8,128)(2,1)S(1)}, bf16[32,1920]{1,0:T(8,128)(2,1)S(1)}, u32[]{:S(2)}, u32[]{:S(2)}) collective-permute-start(bf16[32,1920]{1,0:T(8,128)(2,1)S(1)} %collective-permute-done.15.flipped), channel_id=1, source_target_pairs={{0,128},{16,144},{32,160},{48,176},{64,192},{80,208},{96,224},{112... | collective-permute-start | bytes 368648 | tf_op jit(solution)/shard_map/ppermute | solution.py:266
  67.3 2.9 %collective-permute-done.16.pair = bf16[32,1920]{1,0:T(8,128)(2,1)S(1)} collective-permute-done((bf16[32,1920]{1,0:T(8,128)(2,1)S(1)}, bf16[32,1920]{1,0:T(8,128)(2,1)S(1)}, u32[]{:S(2)}, u32[]{:S(2)}) %collective-permute-start.16) | collective-permute-done | bytes 122912 | tf_op jit(solution)/shard_map/ppermute | solution.py:266
  70.7 4.0 %collective-permute-start.18 = (bf16[64,1920]{1,0:T(8,128)(2,1)S(1)}, bf16[64,1920]{1,0:T(8,128)(2,1)S(1)}, u32[]{:S(2)}, u32[]{:S(2)}) collective-permute-start(bf16[64,1920]{1,0:T(8,128)(2,1)S(1)} %shard_map.60.near), channel_id=1, source_target_pairs={{0,96},{16,112},{32,0},{48,16},{64,32},{80,48},{96,64},{112,80},{1... | collective-permute-start | bytes 737288 | tf_op jit(solution)/shard_map/ppermute | solution.py:275
  74.8 3.2 %collective-permute-start.13 = (bf16[64,1920]{1,0:T(8,128)(2,1)S(1)}, bf16[64,1920]{1,0:T(8,128)(2,1)S(1)}, u32[]{:S(2)}, u32[]{:S(2)}) collective-permute-start(bf16[64,1920]{1,0:T(8,128)(2,1)S(1)} %get-tuple-element.19.after), channel_id=1, source_target_pairs={{0,1},{1,2},{2,3},{3,0},{4,5},{5,6},{6,7},{7,4},{8,9},{9,10},{10,1... | collective-permute-start | bytes 737288 | tf_op jit(solution)/shard_map/ppermute | solution.py:277
  78.4 5.0 %collective-permute-done.17.left.x_left = bf16[64,1920]{1,0:T(8,128)(2,1)S(1)} collective-permute-done((bf16[64,1920]{1,0:T(8,128)(2,1)S(1)}, bf16[64,1920]{1,0:T(8,128)(2,1)S(1)}, u32[]{:S(2)}, u32[]{:S(2)}) %collective-permute-start.17) | collective-permute-done | bytes 245792 | tf_op jit(solution)/shard_map/ppermute | solution.py:274
  83.5 3.2 %collective-permute-start.20 = (bf16[32,1920]{1,0:T(8,128)(2,1)S(1)}, bf16[32,1920]{1,0:T(8,128)(2,1)S(1)}, u32[]{:S(2)}, u32[]{:S(2)}) collective-permute-start(bf16[32,1920]{1,0:T(8,128)(2,1)S(1)} %get-tuple-element.22), channel_id=1, source_target_pairs={{0,96},{16,112},{32,0},{48,16},{64,32},{80,48},{96,64},{112,80},{1... | collective-permute-start | bytes 368648 | tf_op jit(solution)/shard_map/ppermute | solution.py:288
  86.8 2.9 %collective-permute-done.19.x_far_a = bf16[32,1920]{1,0:T(8,128)(2,1)S(1)} collective-permute-done((bf16[32,1920]{1,0:T(8,128)(2,1)S(1)}, bf16[32,1920]{1,0:T(8,128)(2,1)S(1)}, u32[]{:S(2)}, u32[]{:S(2)}) %collective-permute-start.19) | collective-permute-done | bytes 122912 | tf_op jit(solution)/shard_map/ppermute | solution.py:287
  89.9 2.5 %collective-permute-done.21.other = bf16[256,1920]{1,0:T(8,128)(2,1)S(1)} collective-permute-done((bf16[256,1920]{1,0:T(8,128)(2,1)S(1)}, bf16[256,1920]{1,0:T(8,128)(2,1)S(1)}, u32[]{:S(2)}, u32[]{:S(2)}) %collective-permute-start.21) | collective-permute-done | bytes 983072 | tf_op jit(solution)/shard_map/ppermute | solution.py:292
  92.3 6.0 %shard_map.63 = bf16[1920,1920]{1,0:T(8,128)(2,1)} custom-call(s32[2]{0:T(128)S(1)} %pad_add_fusion.at_ref, bf16[128,1920]{1,0:T(8,128)(2,1)S(1)} %shard_map.57.own, bf16[128,1920]{1,0:T(8,128)(2,1)S(1)} %collective-permute-done.11.left, bf16[128,1920]{1,0:T(8,128)(2,1)S(1)} %collective-permute-done.12.right, bf16[128,1920]{1,0:T(8,128)(2,1)S(1)} %shard_map.59.far, ...), custom_call_target="tpu_custom_call" | custom-call | flops 3774873600 | bytes 7372800 | tf_op jit(solution)/shard_map/pallas_call | solution.py:293
  (42 shorter events, 3.1 us)
Async XLA Ops:
  0.0 41.6 %copy-start.4 = (s32[32]{0:T(128)S(1)}, s32[32]{0:T(128)}, u32[]{:S(2)}) copy-start(s32[32]{0:T(128)} %param.9) | copy-start | bytes 388
  0.1 1.3 %copy-start = (bf16[1920,320]{0,1:T(8,128)(2,1)S(1)}, bf16[1920,320]{0,1:T(8,128)(2,1)}, u32[]{:S(2)}) copy-start(bf16[1920,320]{0,1:T(8,128)(2,1)} %param.6) | copy-start | bytes 3686404
  1.4 1.0 copy-start.2
  2.3 47.1 %copy-start.3 = (bf16[1920,32]{0,1:T(8,128)(2,1)S(1)}, bf16[1920,32]{0,1:T(8,128)(2,1)}, u32[]{:S(2)}) copy-start(bf16[1920,32]{0,1:T(8,128)(2,1)} %param.5) | copy-start | bytes 368644
  4.0 14.3 %collective-permute-start.3 = (bf16[128,1920]{1,0:T(8,128)(2,1)S(1)}, bf16[128,1920]{1,0:T(8,128)(2,1)S(1)}, u32[]{:S(2)}, u32[]{:S(2)}) collective-permute-start(bf16[128,1920]{1,0:T(8,128)(2,1)S(1)} %get-tuple-element.18), channel_id=1, source_target_pairs={{0,3},{1,2},{2,1},{3,0},{4,7},{5,6},{6,5},{7,4},{8,11},{9,10},{10,... | collective-permute-start | bytes 1474568 | tf_op jit(solution)/shard_map/ppermute | solution.py:212
  6.1 12.4 %collective-permute-start = (bf16[128,1920]{1,0:T(8,128)(2,1)S(1)}, bf16[128,1920]{1,0:T(8,128)(2,1)S(1)}, u32[]{:S(2)}, u32[]{:S(2)}) collective-permute-start(bf16[128,1920]{1,0:T(8,128)(2,1)S(1)} %get-tuple-element.16), channel_id=1, source_target_pairs={{0,1},{1,0},{2,3},{3,2},{4,5},{5,4},{6,7},{7,6},{8,9},{9,8},{10,11... | collective-permute-start | bytes 1474568 | tf_op jit(solution)/shard_map/ppermute | solution.py:211
  6.7 1.3 %copy-start.1 = (bf16[1920,320]{0,1:T(8,128)(2,1)S(1)}, bf16[1920,320]{0,1:T(8,128)(2,1)}, u32[]{:S(2)}) copy-start(bf16[1920,320]{0,1:T(8,128)(2,1)} %param.6) | copy-start | bytes 3686404
  18.4 6.9 %collective-permute-start.4 = (bf16[64,1920]{1,0:T(8,128)(2,1)S(1)}, bf16[64,1920]{1,0:T(8,128)(2,1)S(1)}, u32[]{:S(2)}, u32[]{:S(2)}) collective-permute-start(bf16[64,1920]{1,0:T(8,128)(2,1)S(1)} %get-tuple-element.26), channel_id=1, source_target_pairs={{0,1},{1,0},{2,3},{3,2},{4,5},{5,4},{6,7},{7,6},{8,9},{9,8},{10,11... | collective-permute-start | bytes 737288 | tf_op jit(solution)/shard_map/ppermute | solution.py:230
  18.7 13.1 %collective-permute-start.1 = (bf16[64,1920]{1,0:T(8,128)(2,1)S(1)}, bf16[64,1920]{1,0:T(8,128)(2,1)S(1)}, u32[]{:S(2)}, u32[]{:S(2)}) collective-permute-start(bf16[64,1920]{1,0:T(8,128)(2,1)S(1)} %get-tuple-element.24), channel_id=1, source_target_pairs={{0,3},{1,2},{2,1},{3,0},{4,7},{5,6},{6,5},{7,4},{8,11},{9,10},{10,... | collective-permute-start | bytes 737288 | tf_op jit(solution)/shard_map/ppermute | solution.py:229
  25.4 10.2 %collective-permute-start.5 = (bf16[32,1920]{1,0:T(8,128)(2,1)S(1)}, bf16[32,1920]{1,0:T(8,128)(2,1)S(1)}, u32[]{:S(2)}, u32[]{:S(2)}) collective-permute-start(bf16[32,1920]{1,0:T(8,128)(2,1)S(1)} %get-tuple-element.30), channel_id=1, source_target_pairs={{0,12},{1,13},{2,14},{3,15},{4,8},{5,9},{6,10},{7,11},{8,4},{9,5},... | collective-permute-start | bytes 368648 | tf_op jit(solution)/shard_map/ppermute | solution.py:230
  31.9 9.5 %collective-permute-start.2 = (bf16[32,1920]{1,0:T(8,128)(2,1)S(1)}, bf16[32,1920]{1,0:T(8,128)(2,1)S(1)}, u32[]{:S(2)}, u32[]{:S(2)}) collective-permute-start(bf16[32,1920]{1,0:T(8,128)(2,1)S(1)} %get-tuple-element.28), channel_id=1, source_target_pairs={{0,4},{1,5},{2,6},{3,7},{4,0},{5,1},{6,2},{7,3},{8,12},{9,13},{10,... | collective-permute-start | bytes 368648 | tf_op jit(solution)/shard_map/ppermute | solution.py:229
  35.7 6.4 %collective-permute-start.7 = (bf16[16,1920]{1,0:T(8,128)(2,1)S(1)}, bf16[16,1920]{1,0:T(8,128)(2,1)S(1)}, u32[]{:S(2)}, u32[]{:S(2)}) collective-permute-start(bf16[16,1920]{1,0:T(8,128)(2,1)S(1)} %get-tuple-element.33), channel_id=1, source_target_pairs={{0,4},{1,5},{2,6},{3,7},{4,0},{5,1},{6,2},{7,3},{8,12},{9,13},{10,... | collective-permute-start | bytes 184328 | tf_op jit(solution)/shard_map/ppermute | solution.py:230
  41.4 8.0 %collective-permute-start.6 = (bf16[16,1920]{1,0:T(8,128)(2,1)S(1)}, bf16[16,1920]{1,0:T(8,128)(2,1)S(1)}, u32[]{:S(2)}, u32[]{:S(2)}) collective-permute-start(bf16[16,1920]{1,0:T(8,128)(2,1)S(1)} %get-tuple-element.31), channel_id=1, source_target_pairs={{0,12},{1,13},{2,14},{3,15},{4,8},{5,9},{6,10},{7,11},{8,4},{9,5},... | collective-permute-start | bytes 184328 | tf_op jit(solution)/shard_map/ppermute | solution.py:229
  49.5 10.3 %collective-permute-start.10 = (bf16[32,1920]{1,0:T(8,128)(2,1)S(1)}, bf16[32,1920]{1,0:T(8,128)(2,1)S(1)}, u32[]{:S(2)}, u32[]{:S(2)}) collective-permute-start(bf16[32,1920]{1,0:T(8,128)(2,1)S(1)} %fusion.2.own), channel_id=1, source_target_pairs={{0,8},{1,9},{2,10},{3,11},{4,12},{5,13},{6,14},{7,15},{8,0},{9,1},... | collective-permute-start | bytes 368648 | tf_op jit(solution)/shard_map/ppermute | solution.py:256
  49.6 10.2 %collective-permute-start.9 = (bf16[32,1920]{1,0:T(8,128)(2,1)S(1)}, bf16[32,1920]{1,0:T(8,128)(2,1)S(1)}, u32[]{:S(2)}, u32[]{:S(2)}) collective-permute-start(bf16[32,1920]{1,0:T(8,128)(2,1)S(1)} %fusion.2.own), channel_id=1, source_target_pairs={{0,4},{1,5},{2,6},{3,7},{4,8},{5,9},{6,10},{7,11},{8,12},{9,13},{1... | collective-permute-start | bytes 368648 | tf_op jit(solution)/shard_map/ppermute | solution.py:253
  51.3 9.5 %collective-permute-start.8 = (bf16[32,1920]{1,0:T(8,128)(2,1)S(1)}, bf16[32,1920]{1,0:T(8,128)(2,1)S(1)}, u32[]{:S(2)}, u32[]{:S(2)}) collective-permute-start(bf16[32,1920]{1,0:T(8,128)(2,1)S(1)} %fusion.2.own), channel_id=1, source_target_pairs={{0,12},{1,13},{2,14},{3,15},{4,0},{5,1},{6,2},{7,3},{8,4},{9,5},{1... | collective-permute-start | bytes 368648 | tf_op jit(solution)/shard_map/ppermute | solution.py:254
  53.8 10.9 %collective-permute-start.15 = (bf16[32,1920]{1,0:T(8,128)(2,1)S(1)}, bf16[32,1920]{1,0:T(8,128)(2,1)S(1)}, u32[]{:S(2)}, u32[]{:S(2)}) collective-permute-start(bf16[32,1920]{1,0:T(8,128)(2,1)S(1)} %fusion.2.own), channel_id=1, source_target_pairs={{0,0},{1,32},{2,64},{3,96},{4,16},{5,48},{6,80},{7,112},{8,128},{9... | collective-permute-start | bytes 368648 | tf_op jit(solution)/shard_map/ppermute | solution.py:255
  61.4 13.3 %collective-permute-start.12 = (bf16[128,1920]{1,0:T(8,128)(2,1)S(1)}, bf16[128,1920]{1,0:T(8,128)(2,1)S(1)}, u32[]{:S(2)}, u32[]{:S(2)}) collective-permute-start(bf16[128,1920]{1,0:T(8,128)(2,1)S(1)} %shard_map.57.own), channel_id=1, source_target_pairs={{0,3},{1,0},{2,1},{3,2},{4,7},{5,4},{6,5},{7,6},{8,11},{9,8},{10,9... | collective-permute-start | bytes 1474568 | tf_op jit(solution)/shard_map/ppermute | solution.py:265
  61.7 13.0 %collective-permute-start.11 = (bf16[128,1920]{1,0:T(8,128)(2,1)S(1)}, bf16[128,1920]{1,0:T(8,128)(2,1)S(1)}, u32[]{:S(2)}, u32[]{:S(2)}) collective-permute-start(bf16[128,1920]{1,0:T(8,128)(2,1)S(1)} %shard_map.57.own), channel_id=1, source_target_pairs={{0,1},{1,2},{2,3},{3,0},{4,5},{5,6},{6,7},{7,4},{8,9},{9,10},{10,1... | collective-permute-start | bytes 1474568 | tf_op jit(solution)/shard_map/ppermute | solution.py:264
  64.8 5.4 %collective-permute-start.16 = (bf16[32,1920]{1,0:T(8,128)(2,1)S(1)}, bf16[32,1920]{1,0:T(8,128)(2,1)S(1)}, u32[]{:S(2)}, u32[]{:S(2)}) collective-permute-start(bf16[32,1920]{1,0:T(8,128)(2,1)S(1)} %collective-permute-done.15.flipped), channel_id=1, source_target_pairs={{0,128},{16,144},{32,160},{48,176},{64,192},{80,208},{96,224},{112... | collective-permute-start | bytes 368648 | tf_op jit(solution)/shard_map/ppermute | solution.py:266
  70.7 7.7 %collective-permute-start.18 = (bf16[64,1920]{1,0:T(8,128)(2,1)S(1)}, bf16[64,1920]{1,0:T(8,128)(2,1)S(1)}, u32[]{:S(2)}, u32[]{:S(2)}) collective-permute-start(bf16[64,1920]{1,0:T(8,128)(2,1)S(1)} %shard_map.60.near), channel_id=1, source_target_pairs={{0,96},{16,112},{32,0},{48,16},{64,32},{80,48},{96,64},{112,80},{1... | collective-permute-start | bytes 737288 | tf_op jit(solution)/shard_map/ppermute | solution.py:275
  74.7 8.7 %collective-permute-start.17 = (bf16[64,1920]{1,0:T(8,128)(2,1)S(1)}, bf16[64,1920]{1,0:T(8,128)(2,1)S(1)}, u32[]{:S(2)}, u32[]{:S(2)}) collective-permute-start(bf16[64,1920]{1,0:T(8,128)(2,1)S(1)} %shard_map.60.near), channel_id=1, source_target_pairs={{0,32},{16,48},{32,64},{48,80},{64,96},{80,112},{96,0},{112,16},{1... | collective-permute-start | bytes 737288 | tf_op jit(solution)/shard_map/ppermute | solution.py:274
  74.8 15.0 %collective-permute-start.14 = (bf16[64,1920]{1,0:T(8,128)(2,1)S(1)}, bf16[64,1920]{1,0:T(8,128)(2,1)S(1)}, u32[]{:S(2)}, u32[]{:S(2)}) collective-permute-start(bf16[64,1920]{1,0:T(8,128)(2,1)S(1)} %get-tuple-element.20), channel_id=1, source_target_pairs={{0,3},{1,0},{2,1},{3,2},{4,7},{5,4},{6,5},{7,6},{8,11},{9,8},{10,9... | collective-permute-start | bytes 737288 | tf_op jit(solution)/shard_map/ppermute | solution.py:278
  74.8 15.0 %collective-permute-start.13 = (bf16[64,1920]{1,0:T(8,128)(2,1)S(1)}, bf16[64,1920]{1,0:T(8,128)(2,1)S(1)}, u32[]{:S(2)}, u32[]{:S(2)}) collective-permute-start(bf16[64,1920]{1,0:T(8,128)(2,1)S(1)} %get-tuple-element.19.after), channel_id=1, source_target_pairs={{0,1},{1,2},{2,3},{3,0},{4,5},{5,6},{6,7},{7,4},{8,9},{9,10},{10,1... | collective-permute-start | bytes 737288 | tf_op jit(solution)/shard_map/ppermute | solution.py:277
  83.4 6.2 %collective-permute-start.19 = (bf16[32,1920]{1,0:T(8,128)(2,1)S(1)}, bf16[32,1920]{1,0:T(8,128)(2,1)S(1)}, u32[]{:S(2)}, u32[]{:S(2)}) collective-permute-start(bf16[32,1920]{1,0:T(8,128)(2,1)S(1)} %get-tuple-element.21), channel_id=1, source_target_pairs={{0,32},{16,48},{32,64},{48,80},{64,96},{80,112},{96,0},{112,16},{1... | collective-permute-start | bytes 368648 | tf_op jit(solution)/shard_map/ppermute | solution.py:287
  83.5 6.1 %collective-permute-start.20 = (bf16[32,1920]{1,0:T(8,128)(2,1)S(1)}, bf16[32,1920]{1,0:T(8,128)(2,1)S(1)}, u32[]{:S(2)}, u32[]{:S(2)}) collective-permute-start(bf16[32,1920]{1,0:T(8,128)(2,1)S(1)} %get-tuple-element.22), channel_id=1, source_target_pairs={{0,96},{16,112},{32,0},{48,16},{64,32},{80,48},{96,64},{112,80},{1... | collective-permute-start | bytes 368648 | tf_op jit(solution)/shard_map/ppermute | solution.py:288
  89.7 2.7 %collective-permute-start.21 = (bf16[256,1920]{1,0:T(8,128)(2,1)S(1)}, bf16[256,1920]{1,0:T(8,128)(2,1)S(1)}, u32[]{:S(2)}, u32[]{:S(2)}) collective-permute-start(bf16[256,1920]{1,0:T(8,128)(2,1)S(1)} %shard_map.62.near), channel_id=1, source_target_pairs={{0,16},{16,0},{32,48},{48,32},{64,80},{80,64},{96,112},{112,96},{1... | collective-permute-start | bytes 2949128 | tf_op jit(solution)/shard_map/ppermute | solution.py:292

commit v12 on v11

--- a/solution.py
+++ b/solution.py
@@ -120,7 +120,7 @@
     out[half:] = two[...]
 
 
-BLOCKS = ((0, 480), (480, 960), (960, 1440), (1440, 1760), (1760, 1920))
+BLOCKS = ((0, 640), (640, 1280), (1280, 1792), (1792, 1920))
 
 
 def last_kernel(
@@ -184,7 +184,7 @@
 
     @pl.when(row > col)
     def _():
-        held[:480] = jnp.zeros((480, columns), BF16)
+        held[:640] = jnp.zeros((640, columns), BF16)
         for at, (first, end) in enumerate(BLOCKS):
             sent(at, held.at[: end - first]).start()
 

time: 99.3 us -> 99.5 us (level)
  no operation moved by 1% of the time
where the time goes in v12:
time: 99.5 us; the launch traced here: 98.7 us
  waiting for transfers between devices  45 us (45%)
  starting transfers between devices  38.6 us (39%)
  Pallas kernels  9.92 us (10%)
  local copies, waits for them, and re-layouts  3.62 us (4%)
  other arithmetic  1.25 us (1%)
    ppermute x3, waiting for transfers between devices, per_device(): next_a = lax.ppermute(sent_a, 'col', swap_a)  12.4 us
    ppermute x1, waiting for transfers between devices, per_device(): got_b = lax.ppermute(sent_b, 'col', y_swap(3))  9.57 us
    ppermute x3, waiting for transfers between devices, per_device(): next_b = lax.ppermute(sent_b, 'col', swap_b)  7.38 us
    ppermute x3, starting transfers between devices, per_device(): next_b = lax.ppermute(sent_b, 'col', swap_b)  7.11 us
    pallas_call x1, Pallas kernels, per_device(): call(last_kernel, out_shape=shape(rows, rows), in_specs=[SCALAR] + [WHOLE...  6.23 us
    ppermute x1, starting transfers between devices, per_device(): flipped = lax.ppermute(slopes, ('row', 'col'), flip_pairs())  5.04 us
    ppermute x1, waiting for transfers between devices, per_device(): x_left = lax.ppermute(near, 'row', x_turn(1))  5.01 us
    ppermute x1, starting transfers between devices, per_device(): x_right = lax.ppermute(near, 'row', x_turn(-1))  3.96 us
  transfers between devices with their start and end apart: 22, of which 13 were waited for; matrix products, arithmetic and copies ran while one was open for 1% of the time, Pallas kernels for 2%

profile of v12, /device:TPU:24, one launch (start us, length us, event | category | flops | bytes accessed | tf_op | source)
XLA Modules:
  0.0 98.7 jit_solution(5723414266941338702)
XLA Ops:
  0.1 1.3 %copy-done = bf16[1920,320]{0,1:T(8,128)(2,1)S(1)} copy-done((bf16[1920,320]{0,1:T(8,128)(2,1)S(1)}, bf16[1920,320]{0,1:T(8,128)(2,1)}, u32[]{:S(2)}) %copy-start) | copy-done | bytes 1228824
  1.4 1.0 copy-done.2
  2.3 1.7 %shard_map.55 = (bf16[128,1920]{1,0:T(8,128)(2,1)S(1)}, bf16[128,1920]{1,0:T(8,128)(2,1)S(1)}, bf16[256,320]{1,0:T(8,128)(2,1)S(1)}) custom-call(s32[2]{0:T(128)S(1)} %pad_add_fusion.at_ref, bf16[320,512]{1,0:T(8,128)(2,1)S(1)} %copy-done.2, bf16[320,1920]{1,0:T(8,128)(2,1)S(1)} %bitcast.13), custom_call_target="tpu_custom_call" | custom-call | flops 314572800 | bytes 1600000 | tf_op jit(solution)/shard_map/pallas_call | solution.py:202
  4.0 2.0 %collective-permute-start.3 = (bf16[128,1920]{1,0:T(8,128)(2,1)S(1)}, bf16[128,1920]{1,0:T(8,128)(2,1)S(1)}, u32[]{:S(2)}, u32[]{:S(2)}) collective-permute-start(bf16[128,1920]{1,0:T(8,128)(2,1)S(1)} %get-tuple-element.18), channel_id=1, source_target_pairs={{0,3},{1,2},{2,1},{3,0},{4,7},{5,6},{6,5},{7,4},{8,11},{9,10},{10,... | collective-permute-start | bytes 1474568 | tf_op jit(solution)/shard_map/ppermute | solution.py:212
  6.1 0.7 convert_element_type.179
  6.7 1.3 %copy-done.1 = bf16[1920,320]{0,1:T(8,128)(2,1)S(1)} copy-done((bf16[1920,320]{0,1:T(8,128)(2,1)S(1)}, bf16[1920,320]{0,1:T(8,128)(2,1)}, u32[]{:S(2)}) %copy-start.1) | copy-done | bytes 1228824
  8.0 0.7 shard_map.56
  8.7 9.6 %collective-permute-done.3 = bf16[128,1920]{1,0:T(8,128)(2,1)S(1)} collective-permute-done((bf16[128,1920]{1,0:T(8,128)(2,1)S(1)}, bf16[128,1920]{1,0:T(8,128)(2,1)S(1)}, u32[]{:S(2)}, u32[]{:S(2)}) %collective-permute-start.3) | collective-permute-done | bytes 491552 | tf_op jit(solution)/shard_map/ppermute | solution.py:212
  18.7 2.0 %collective-permute-start.1 = (bf16[64,1920]{1,0:T(8,128)(2,1)S(1)}, bf16[64,1920]{1,0:T(8,128)(2,1)S(1)}, u32[]{:S(2)}, u32[]{:S(2)}) collective-permute-start(bf16[64,1920]{1,0:T(8,128)(2,1)S(1)} %get-tuple-element.24), channel_id=1, source_target_pairs={{0,3},{1,2},{2,1},{3,0},{4,7},{5,6},{6,5},{7,4},{8,11},{9,10},{10,... | collective-permute-start | bytes 737288 | tf_op jit(solution)/shard_map/ppermute | solution.py:229
  20.6 4.7 %collective-permute-done.4 = bf16[64,1920]{1,0:T(8,128)(2,1)S(1)} collective-permute-done((bf16[64,1920]{1,0:T(8,128)(2,1)S(1)}, bf16[64,1920]{1,0:T(8,128)(2,1)S(1)}, u32[]{:S(2)}, u32[]{:S(2)}) %collective-permute-start.4) | collective-permute-done | bytes 245792 | tf_op jit(solution)/shard_map/ppermute | solution.py:230
  25.4 6.4 %collective-permute-start.5 = (bf16[32,1920]{1,0:T(8,128)(2,1)S(1)}, bf16[32,1920]{1,0:T(8,128)(2,1)S(1)}, u32[]{:S(2)}, u32[]{:S(2)}) collective-permute-start(bf16[32,1920]{1,0:T(8,128)(2,1)S(1)} %get-tuple-element.30), channel_id=1, source_target_pairs={{0,12},{1,13},{2,14},{3,15},{4,8},{5,9},{6,10},{7,11},{8,4},{9,5},... | collective-permute-start | bytes 368648 | tf_op jit(solution)/shard_map/ppermute | solution.py:230
  31.9 1.5 %collective-permute-start.2 = (bf16[32,1920]{1,0:T(8,128)(2,1)S(1)}, bf16[32,1920]{1,0:T(8,128)(2,1)S(1)}, u32[]{:S(2)}, u32[]{:S(2)}) collective-permute-start(bf16[32,1920]{1,0:T(8,128)(2,1)S(1)} %get-tuple-element.28), channel_id=1, source_target_pairs={{0,4},{1,5},{2,6},{3,7},{4,0},{5,1},{6,2},{7,3},{8,12},{9,13},{10,... | collective-permute-start | bytes 368648 | tf_op jit(solution)/shard_map/ppermute | solution.py:229
  33.4 2.2 %collective-permute-done.5 = bf16[32,1920]{1,0:T(8,128)(2,1)S(1)} collective-permute-done((bf16[32,1920]{1,0:T(8,128)(2,1)S(1)}, bf16[32,1920]{1,0:T(8,128)(2,1)S(1)}, u32[]{:S(2)}, u32[]{:S(2)}) %collective-permute-start.5) | collective-permute-done | bytes 122912 | tf_op jit(solution)/shard_map/ppermute | solution.py:230
  35.7 0.6 collective-permute-start.7
  36.3 5.1 %collective-permute-done.2 = bf16[32,1920]{1,0:T(8,128)(2,1)S(1)} collective-permute-done((bf16[32,1920]{1,0:T(8,128)(2,1)S(1)}, bf16[32,1920]{1,0:T(8,128)(2,1)S(1)}, u32[]{:S(2)}, u32[]{:S(2)}) %collective-permute-start.2) | collective-permute-done | bytes 122912 | tf_op jit(solution)/shard_map/ppermute | solution.py:229
  42.0 7.4 %collective-permute-done.6 = bf16[16,1920]{1,0:T(8,128)(2,1)S(1)} collective-permute-done((bf16[16,1920]{1,0:T(8,128)(2,1)S(1)}, bf16[16,1920]{1,0:T(8,128)(2,1)S(1)}, u32[]{:S(2)}, u32[]{:S(2)}) %collective-permute-start.6) | collective-permute-done | bytes 61472 | tf_op jit(solution)/shard_map/ppermute | solution.py:229
  49.6 1.7 %collective-permute-start.9 = (bf16[32,1920]{1,0:T(8,128)(2,1)S(1)}, bf16[32,1920]{1,0:T(8,128)(2,1)S(1)}, u32[]{:S(2)}, u32[]{:S(2)}) collective-permute-start(bf16[32,1920]{1,0:T(8,128)(2,1)S(1)} %fusion.2.own), channel_id=1, source_target_pairs={{0,4},{1,5},{2,6},{3,7},{4,8},{5,9},{6,10},{7,11},{8,12},{9,13},{1... | collective-permute-start | bytes 368648 | tf_op jit(solution)/shard_map/ppermute | solution.py:253
  51.3 2.5 %collective-permute-start.8 = (bf16[32,1920]{1,0:T(8,128)(2,1)S(1)}, bf16[32,1920]{1,0:T(8,128)(2,1)S(1)}, u32[]{:S(2)}, u32[]{:S(2)}) collective-permute-start(bf16[32,1920]{1,0:T(8,128)(2,1)S(1)} %fusion.2.own), channel_id=1, source_target_pairs={{0,12},{1,13},{2,14},{3,15},{4,0},{5,1},{6,2},{7,3},{8,4},{9,5},{1... | collective-permute-start | bytes 368648 | tf_op jit(solution)/shard_map/ppermute | solution.py:254
  53.8 5.0 %collective-permute-start.15 = (bf16[32,1920]{1,0:T(8,128)(2,1)S(1)}, bf16[32,1920]{1,0:T(8,128)(2,1)S(1)}, u32[]{:S(2)}, u32[]{:S(2)}) collective-permute-start(bf16[32,1920]{1,0:T(8,128)(2,1)S(1)} %fusion.2.own), channel_id=1, source_target_pairs={{0,0},{1,32},{2,64},{3,96},{4,16},{5,48},{6,80},{7,112},{8,128},{9... | collective-permute-start | bytes 368648 | tf_op jit(solution)/shard_map/ppermute | solution.py:255
  58.9 0.9 collective-permute-done.10.far
  59.8 1.1 %collective-permute-done.8.right = bf16[32,1920]{1,0:T(8,128)(2,1)S(1)} collective-permute-done((bf16[32,1920]{1,0:T(8,128)(2,1)S(1)}, bf16[32,1920]{1,0:T(8,128)(2,1)S(1)}, u32[]{:S(2)}, u32[]{:S(2)}) %collective-permute-start.8) | collective-permute-done | bytes 122912 | tf_op jit(solution)/shard_map/ppermute | solution.py:254
  60.8 0.6 shard_map.57.own
  61.7 3.0 %collective-permute-start.11 = (bf16[128,1920]{1,0:T(8,128)(2,1)S(1)}, bf16[128,1920]{1,0:T(8,128)(2,1)S(1)}, u32[]{:S(2)}, u32[]{:S(2)}) collective-permute-start(bf16[128,1920]{1,0:T(8,128)(2,1)S(1)} %shard_map.57.own), channel_id=1, source_target_pairs={{0,1},{1,2},{2,3},{3,0},{4,5},{5,6},{6,7},{7,4},{8,9},{9,10},{10,1... | collective-permute-start | bytes 1474568 | tf_op jit(solution)/shard_map/ppermute | solution.py:264
  64.8 2.6 %collective-permute-start.16 = (bf16[32,1920]{1,0:T(8,128)(2,1)S(1)}, bf16[32,1920]{1,0:T(8,128)(2,1)S(1)}, u32[]{:S(2)}, u32[]{:S(2)}) collective-permute-start(bf16[32,1920]{1,0:T(8,128)(2,1)S(1)} %collective-permute-done.15.flipped), channel_id=1, source_target_pairs={{0,128},{16,144},{32,160},{48,176},{64,192},{80,208},{96,224},{112... | collective-permute-start | bytes 368648 | tf_op jit(solution)/shard_map/ppermute | solution.py:266
  67.3 2.9 %collective-permute-done.16.pair = bf16[32,1920]{1,0:T(8,128)(2,1)S(1)} collective-permute-done((bf16[32,1920]{1,0:T(8,128)(2,1)S(1)}, bf16[32,1920]{1,0:T(8,128)(2,1)S(1)}, u32[]{:S(2)}, u32[]{:S(2)}) %collective-permute-start.16) | collective-permute-done | bytes 122912 | tf_op jit(solution)/shard_map/ppermute | solution.py:266
  70.7 4.0 %collective-permute-start.18 = (bf16[64,1920]{1,0:T(8,128)(2,1)S(1)}, bf16[64,1920]{1,0:T(8,128)(2,1)S(1)}, u32[]{:S(2)}, u32[]{:S(2)}) collective-permute-start(bf16[64,1920]{1,0:T(8,128)(2,1)S(1)} %shard_map.60.near), channel_id=1, source_target_pairs={{0,96},{16,112},{32,0},{48,16},{64,32},{80,48},{96,64},{112,80},{1... | collective-permute-start | bytes 737288 | tf_op jit(solution)/shard_map/ppermute | solution.py:275
  74.8 3.2 %collective-permute-start.13 = (bf16[64,1920]{1,0:T(8,128)(2,1)S(1)}, bf16[64,1920]{1,0:T(8,128)(2,1)S(1)}, u32[]{:S(2)}, u32[]{:S(2)}) collective-permute-start(bf16[64,1920]{1,0:T(8,128)(2,1)S(1)} %get-tuple-element.19.after), channel_id=1, source_target_pairs={{0,1},{1,2},{2,3},{3,0},{4,5},{5,6},{6,7},{7,4},{8,9},{9,10},{10,1... | collective-permute-start | bytes 737288 | tf_op jit(solution)/shard_map/ppermute | solution.py:277
  78.4 5.0 %collective-permute-done.17.left.x_left = bf16[64,1920]{1,0:T(8,128)(2,1)S(1)} collective-permute-done((bf16[64,1920]{1,0:T(8,128)(2,1)S(1)}, bf16[64,1920]{1,0:T(8,128)(2,1)S(1)}, u32[]{:S(2)}, u32[]{:S(2)}) %collective-permute-start.17) | collective-permute-done | bytes 245792 | tf_op jit(solution)/shard_map/ppermute | solution.py:274
  83.5 3.2 %collective-permute-start.20 = (bf16[32,1920]{1,0:T(8,128)(2,1)S(1)}, bf16[32,1920]{1,0:T(8,128)(2,1)S(1)}, u32[]{:S(2)}, u32[]{:S(2)}) collective-permute-start(bf16[32,1920]{1,0:T(8,128)(2,1)S(1)} %get-tuple-element.22), channel_id=1, source_target_pairs={{0,96},{16,112},{32,0},{48,16},{64,32},{80,48},{96,64},{112,80},{1... | collective-permute-start | bytes 368648 | tf_op jit(solution)/shard_map/ppermute | solution.py:288
  86.8 2.9 %collective-permute-done.19.x_far_a = bf16[32,1920]{1,0:T(8,128)(2,1)S(1)} collective-permute-done((bf16[32,1920]{1,0:T(8,128)(2,1)S(1)}, bf16[32,1920]{1,0:T(8,128)(2,1)S(1)}, u32[]{:S(2)}, u32[]{:S(2)}) %collective-permute-start.19) | collective-permute-done | bytes 122912 | tf_op jit(solution)/shard_map/ppermute | solution.py:287
  89.9 2.5 %collective-permute-done.21.other = bf16[256,1920]{1,0:T(8,128)(2,1)S(1)} collective-permute-done((bf16[256,1920]{1,0:T(8,128)(2,1)S(1)}, bf16[256,1920]{1,0:T(8,128)(2,1)S(1)}, u32[]{:S(2)}, u32[]{:S(2)}) %collective-permute-start.21) | collective-permute-done | bytes 983072 | tf_op jit(solution)/shard_map/ppermute | solution.py:292
  92.3 6.2 %shard_map.63 = bf16[1920,1920]{1,0:T(8,128)(2,1)} custom-call(s32[2]{0:T(128)S(1)} %pad_add_fusion.at_ref, bf16[128,1920]{1,0:T(8,128)(2,1)S(1)} %shard_map.57.own, bf16[128,1920]{1,0:T(8,128)(2,1)S(1)} %collective-permute-done.11.left, bf16[128,1920]{1,0:T(8,128)(2,1)S(1)} %collective-permute-done.12.right, bf16[128,1920]{1,0:T(8,128)(2,1)S(1)} %shard_map.59.far, ...), custom_call_target="tpu_custom_call" | custom-call | flops 3774873600 | bytes 7372800 | tf_op jit(solution)/shard_map/pallas_call | solution.py:293
  (42 shorter events, 3.1 us)
Async XLA Ops:
  0.0 41.6 %copy-start.4 = (s32[32]{0:T(128)S(1)}, s32[32]{0:T(128)}, u32[]{:S(2)}) copy-start(s32[32]{0:T(128)} %param.9) | copy-start | bytes 388
  0.1 1.3 %copy-start = (bf16[1920,320]{0,1:T(8,128)(2,1)S(1)}, bf16[1920,320]{0,1:T(8,128)(2,1)}, u32[]{:S(2)}) copy-start(bf16[1920,320]{0,1:T(8,128)(2,1)} %param.6) | copy-start | bytes 3686404
  1.4 1.0 copy-start.2
  2.3 47.1 %copy-start.3 = (bf16[1920,32]{0,1:T(8,128)(2,1)S(1)}, bf16[1920,32]{0,1:T(8,128)(2,1)}, u32[]{:S(2)}) copy-start(bf16[1920,32]{0,1:T(8,128)(2,1)} %param.5) | copy-start | bytes 368644
  4.0 14.3 %collective-permute-start.3 = (bf16[128,1920]{1,0:T(8,128)(2,1)S(1)}, bf16[128,1920]{1,0:T(8,128)(2,1)S(1)}, u32[]{:S(2)}, u32[]{:S(2)}) collective-permute-start(bf16[128,1920]{1,0:T(8,128)(2,1)S(1)} %get-tuple-element.18), channel_id=1, source_target_pairs={{0,3},{1,2},{2,1},{3,0},{4,7},{5,6},{6,5},{7,4},{8,11},{9,10},{10,... | collective-permute-start | bytes 1474568 | tf_op jit(solution)/shard_map/ppermute | solution.py:212
  6.1 12.4 %collective-permute-start = (bf16[128,1920]{1,0:T(8,128)(2,1)S(1)}, bf16[128,1920]{1,0:T(8,128)(2,1)S(1)}, u32[]{:S(2)}, u32[]{:S(2)}) collective-permute-start(bf16[128,1920]{1,0:T(8,128)(2,1)S(1)} %get-tuple-element.16), channel_id=1, source_target_pairs={{0,1},{1,0},{2,3},{3,2},{4,5},{5,4},{6,7},{7,6},{8,9},{9,8},{10,11... | collective-permute-start | bytes 1474568 | tf_op jit(solution)/shard_map/ppermute | solution.py:211
  6.7 1.3 %copy-start.1 = (bf16[1920,320]{0,1:T(8,128)(2,1)S(1)}, bf16[1920,320]{0,1:T(8,128)(2,1)}, u32[]{:S(2)}) copy-start(bf16[1920,320]{0,1:T(8,128)(2,1)} %param.6) | copy-start | bytes 3686404
  18.4 6.9 %collective-permute-start.4 = (bf16[64,1920]{1,0:T(8,128)(2,1)S(1)}, bf16[64,1920]{1,0:T(8,128)(2,1)S(1)}, u32[]{:S(2)}, u32[]{:S(2)}) collective-permute-start(bf16[64,1920]{1,0:T(8,128)(2,1)S(1)} %get-tuple-element.26), channel_id=1, source_target_pairs={{0,1},{1,0},{2,3},{3,2},{4,5},{5,4},{6,7},{7,6},{8,9},{9,8},{10,11... | collective-permute-start | bytes 737288 | tf_op jit(solution)/shard_map/ppermute | solution.py:230
  18.7 13.1 %collective-permute-start.1 = (bf16[64,1920]{1,0:T(8,128)(2,1)S(1)}, bf16[64,1920]{1,0:T(8,128)(2,1)S(1)}, u32[]{:S(2)}, u32[]{:S(2)}) collective-permute-start(bf16[64,1920]{1,0:T(8,128)(2,1)S(1)} %get-tuple-element.24), channel_id=1, source_target_pairs={{0,3},{1,2},{2,1},{3,0},{4,7},{5,6},{6,5},{7,4},{8,11},{9,10},{10,... | collective-permute-start | bytes 737288 | tf_op jit(solution)/shard_map/ppermute | solution.py:229
  25.4 10.2 %collective-permute-start.5 = (bf16[32,1920]{1,0:T(8,128)(2,1)S(1)}, bf16[32,1920]{1,0:T(8,128)(2,1)S(1)}, u32[]{:S(2)}, u32[]{:S(2)}) collective-permute-start(bf16[32,1920]{1,0:T(8,128)(2,1)S(1)} %get-tuple-element.30), channel_id=1, source_target_pairs={{0,12},{1,13},{2,14},{3,15},{4,8},{5,9},{6,10},{7,11},{8,4},{9,5},... | collective-permute-start | bytes 368648 | tf_op jit(solution)/shard_map/ppermute | solution.py:230
  31.9 9.5 %collective-permute-start.2 = (bf16[32,1920]{1,0:T(8,128)(2,1)S(1)}, bf16[32,1920]{1,0:T(8,128)(2,1)S(1)}, u32[]{:S(2)}, u32[]{:S(2)}) collective-permute-start(bf16[32,1920]{1,0:T(8,128)(2,1)S(1)} %get-tuple-element.28), channel_id=1, source_target_pairs={{0,4},{1,5},{2,6},{3,7},{4,0},{5,1},{6,2},{7,3},{8,12},{9,13},{10,... | collective-permute-start | bytes 368648 | tf_op jit(solution)/shard_map/ppermute | solution.py:229
  35.7 6.4 %collective-permute-start.7 = (bf16[16,1920]{1,0:T(8,128)(2,1)S(1)}, bf16[16,1920]{1,0:T(8,128)(2,1)S(1)}, u32[]{:S(2)}, u32[]{:S(2)}) collective-permute-start(bf16[16,1920]{1,0:T(8,128)(2,1)S(1)} %get-tuple-element.33), channel_id=1, source_target_pairs={{0,4},{1,5},{2,6},{3,7},{4,0},{5,1},{6,2},{7,3},{8,12},{9,13},{10,... | collective-permute-start | bytes 184328 | tf_op jit(solution)/shard_map/ppermute | solution.py:230
  41.4 8.0 %collective-permute-start.6 = (bf16[16,1920]{1,0:T(8,128)(2,1)S(1)}, bf16[16,1920]{1,0:T(8,128)(2,1)S(1)}, u32[]{:S(2)}, u32[]{:S(2)}) collective-permute-start(bf16[16,1920]{1,0:T(8,128)(2,1)S(1)} %get-tuple-element.31), channel_id=1, source_target_pairs={{0,12},{1,13},{2,14},{3,15},{4,8},{5,9},{6,10},{7,11},{8,4},{9,5},... | collective-permute-start | bytes 184328 | tf_op jit(solution)/shard_map/ppermute | solution.py:229
  49.5 10.3 %collective-permute-start.10 = (bf16[32,1920]{1,0:T(8,128)(2,1)S(1)}, bf16[32,1920]{1,0:T(8,128)(2,1)S(1)}, u32[]{:S(2)}, u32[]{:S(2)}) collective-permute-start(bf16[32,1920]{1,0:T(8,128)(2,1)S(1)} %fusion.2.own), channel_id=1, source_target_pairs={{0,8},{1,9},{2,10},{3,11},{4,12},{5,13},{6,14},{7,15},{8,0},{9,1},... | collective-permute-start | bytes 368648 | tf_op jit(solution)/shard_map/ppermute | solution.py:256
  49.6 10.2 %collective-permute-start.9 = (bf16[32,1920]{1,0:T(8,128)(2,1)S(1)}, bf16[32,1920]{1,0:T(8,128)(2,1)S(1)}, u32[]{:S(2)}, u32[]{:S(2)}) collective-permute-start(bf16[32,1920]{1,0:T(8,128)(2,1)S(1)} %fusion.2.own), channel_id=1, source_target_pairs={{0,4},{1,5},{2,6},{3,7},{4,8},{5,9},{6,10},{7,11},{8,12},{9,13},{1... | collective-permute-start | bytes 368648 | tf_op jit(solution)/shard_map/ppermute | solution.py:253
  51.3 9.5 %collective-permute-start.8 = (bf16[32,1920]{1,0:T(8,128)(2,1)S(1)}, bf16[32,1920]{1,0:T(8,128)(2,1)S(1)}, u32[]{:S(2)}, u32[]{:S(2)}) collective-permute-start(bf16[32,1920]{1,0:T(8,128)(2,1)S(1)} %fusion.2.own), channel_id=1, source_target_pairs={{0,12},{1,13},{2,14},{3,15},{4,0},{5,1},{6,2},{7,3},{8,4},{9,5},{1... | collective-permute-start | bytes 368648 | tf_op jit(solution)/shard_map/ppermute | solution.py:254
  53.8 10.9 %collective-permute-start.15 = (bf16[32,1920]{1,0:T(8,128)(2,1)S(1)}, bf16[32,1920]{1,0:T(8,128)(2,1)S(1)}, u32[]{:S(2)}, u32[]{:S(2)}) collective-permute-start(bf16[32,1920]{1,0:T(8,128)(2,1)S(1)} %fusion.2.own), channel_id=1, source_target_pairs={{0,0},{1,32},{2,64},{3,96},{4,16},{5,48},{6,80},{7,112},{8,128},{9... | collective-permute-start | bytes 368648 | tf_op jit(solution)/shard_map/ppermute | solution.py:255
  61.4 13.3 %collective-permute-start.12 = (bf16[128,1920]{1,0:T(8,128)(2,1)S(1)}, bf16[128,1920]{1,0:T(8,128)(2,1)S(1)}, u32[]{:S(2)}, u32[]{:S(2)}) collective-permute-start(bf16[128,1920]{1,0:T(8,128)(2,1)S(1)} %shard_map.57.own), channel_id=1, source_target_pairs={{0,3},{1,0},{2,1},{3,2},{4,7},{5,4},{6,5},{7,6},{8,11},{9,8},{10,9... | collective-permute-start | bytes 1474568 | tf_op jit(solution)/shard_map/ppermute | solution.py:265
  61.7 13.0 %collective-permute-start.11 = (bf16[128,1920]{1,0:T(8,128)(2,1)S(1)}, bf16[128,1920]{1,0:T(8,128)(2,1)S(1)}, u32[]{:S(2)}, u32[]{:S(2)}) collective-permute-start(bf16[128,1920]{1,0:T(8,128)(2,1)S(1)} %shard_map.57.own), channel_id=1, source_target_pairs={{0,1},{1,2},{2,3},{3,0},{4,5},{5,6},{6,7},{7,4},{8,9},{9,10},{10,1... | collective-permute-start | bytes 1474568 | tf_op jit(solution)/shard_map/ppermute | solution.py:264
  64.8 5.4 %collective-permute-start.16 = (bf16[32,1920]{1,0:T(8,128)(2,1)S(1)}, bf16[32,1920]{1,0:T(8,128)(2,1)S(1)}, u32[]{:S(2)}, u32[]{:S(2)}) collective-permute-start(bf16[32,1920]{1,0:T(8,128)(2,1)S(1)} %collective-permute-done.15.flipped), channel_id=1, source_target_pairs={{0,128},{16,144},{32,160},{48,176},{64,192},{80,208},{96,224},{112... | collective-permute-start | bytes 368648 | tf_op jit(solution)/shard_map/ppermute | solution.py:266
  70.7 7.7 %collective-permute-start.18 = (bf16[64,1920]{1,0:T(8,128)(2,1)S(1)}, bf16[64,1920]{1,0:T(8,128)(2,1)S(1)}, u32[]{:S(2)}, u32[]{:S(2)}) collective-permute-start(bf16[64,1920]{1,0:T(8,128)(2,1)S(1)} %shard_map.60.near), channel_id=1, source_target_pairs={{0,96},{16,112},{32,0},{48,16},{64,32},{80,48},{96,64},{112,80},{1... | collective-permute-start | bytes 737288 | tf_op jit(solution)/shard_map/ppermute | solution.py:275
  74.7 8.7 %collective-permute-start.17 = (bf16[64,1920]{1,0:T(8,128)(2,1)S(1)}, bf16[64,1920]{1,0:T(8,128)(2,1)S(1)}, u32[]{:S(2)}, u32[]{:S(2)}) collective-permute-start(bf16[64,1920]{1,0:T(8,128)(2,1)S(1)} %shard_map.60.near), channel_id=1, source_target_pairs={{0,32},{16,48},{32,64},{48,80},{64,96},{80,112},{96,0},{112,16},{1... | collective-permute-start | bytes 737288 | tf_op jit(solution)/shard_map/ppermute | solution.py:274
  74.8 15.0 %collective-permute-start.14 = (bf16[64,1920]{1,0:T(8,128)(2,1)S(1)}, bf16[64,1920]{1,0:T(8,128)(2,1)S(1)}, u32[]{:S(2)}, u32[]{:S(2)}) collective-permute-start(bf16[64,1920]{1,0:T(8,128)(2,1)S(1)} %get-tuple-element.20), channel_id=1, source_target_pairs={{0,3},{1,0},{2,1},{3,2},{4,7},{5,4},{6,5},{7,6},{8,11},{9,8},{10,9... | collective-permute-start | bytes 737288 | tf_op jit(solution)/shard_map/ppermute | solution.py:278
  74.8 15.0 %collective-permute-start.13 = (bf16[64,1920]{1,0:T(8,128)(2,1)S(1)}, bf16[64,1920]{1,0:T(8,128)(2,1)S(1)}, u32[]{:S(2)}, u32[]{:S(2)}) collective-permute-start(bf16[64,1920]{1,0:T(8,128)(2,1)S(1)} %get-tuple-element.19.after), channel_id=1, source_target_pairs={{0,1},{1,2},{2,3},{3,0},{4,5},{5,6},{6,7},{7,4},{8,9},{9,10},{10,1... | collective-permute-start | bytes 737288 | tf_op jit(solution)/shard_map/ppermute | solution.py:277
  83.4 6.2 %collective-permute-start.19 = (bf16[32,1920]{1,0:T(8,128)(2,1)S(1)}, bf16[32,1920]{1,0:T(8,128)(2,1)S(1)}, u32[]{:S(2)}, u32[]{:S(2)}) collective-permute-start(bf16[32,1920]{1,0:T(8,128)(2,1)S(1)} %get-tuple-element.21), channel_id=1, source_target_pairs={{0,32},{16,48},{32,64},{48,80},{64,96},{80,112},{96,0},{112,16},{1... | collective-permute-start | bytes 368648 | tf_op jit(solution)/shard_map/ppermute | solution.py:287
  83.5 6.1 %collective-permute-start.20 = (bf16[32,1920]{1,0:T(8,128)(2,1)S(1)}, bf16[32,1920]{1,0:T(8,128)(2,1)S(1)}, u32[]{:S(2)}, u32[]{:S(2)}) collective-permute-start(bf16[32,1920]{1,0:T(8,128)(2,1)S(1)} %get-tuple-element.22), channel_id=1, source_target_pairs={{0,96},{16,112},{32,0},{48,16},{64,32},{80,48},{96,64},{112,80},{1... | collective-permute-start | bytes 368648 | tf_op jit(solution)/shard_map/ppermute | solution.py:288
  89.7 2.7 %collective-permute-start.21 = (bf16[256,1920]{1,0:T(8,128)(2,1)S(1)}, bf16[256,1920]{1,0:T(8,128)(2,1)S(1)}, u32[]{:S(2)}, u32[]{:S(2)}) collective-permute-start(bf16[256,1920]{1,0:T(8,128)(2,1)S(1)} %shard_map.62.near), channel_id=1, source_target_pairs={{0,16},{16,0},{32,48},{48,32},{64,80},{80,64},{96,112},{112,96},{1... | collective-permute-start | bytes 2949128 | tf_op jit(solution)/shard_map/ppermute | solution.py:292
